TPU v7x, 256 devices: a whole 4x4x8 slice. The times are simulated.
256 devices in a mesh: seg: 32 (over x, z), head: 8 (over y, core).
Axes of the slice: x: 4, y: 4, z: 8, core: 2. Of those that a mesh axis runs over, the one named last changes fastest.
Arguments:
- q_heads: bfloat16 [24576, 4096], P('seg', 'head'), may hold values from -6 to 6
- k_heads: bfloat16 [24576, 4096], P('seg', 'head'), may hold values from -6 to 6
- v_heads: bfloat16 [24576, 4096], P('seg', 'head'), may hold values from -600 to 600
- log_decay: float32 [32, 24576], P('head', 'seg'), may hold values from -1 to 0
- parent: int32 [32], replicated, may hold values from -1 to 31, as said below
- norm_gain: float32 [4096], P('head'), may hold values from 0.1 to 1.9
- w_out: bfloat16 [4096, 6144], P('head'), may hold values from -0.09375 to 0.09375
Outputs:
- mixed: bfloat16 [24576, 6144], P(('seg', 'head'))
Inputs may be any that keep to these rules, and one draw needn't show every extreme that they name: A segment's parent is a root or a segment whose parent is a root; the tree has three levels, and the third is never empty.
All inputs are finite; a program needn't handle non-finite values.
Results may differ from a plain program's by a relative error of at most 0.0051.
Values sent between devices are 32-bit elements; how exact they have to be, the bound alone decides.
No kernel may reach another device: no remote copies, remote signals or barrier semaphores. Data moves between devices by JAX's collectives and lax.ppermute only.
A program may use at most 128 MiB of HBM per device.

v0:
```python
import jax
import jax.numpy as jnp
from jax import lax
from jax.sharding import PartitionSpec as P


def per_device(q_heads, k_heads, v_heads, log_decay, parent, norm_gain, w_out):
    segment_len = q_heads.shape[0]
    head_count = log_decay.shape[0]
    head_width = q_heads.shape[1] // head_count
    queries = q_heads.reshape(segment_len, head_count, head_width)
    key_rows = k_heads.reshape(segment_len, head_count, head_width)
    values = v_heads.reshape(segment_len, head_count, head_width)
    running = jnp.cumsum(log_decay, axis=1)
    segment_total = running[:, -1]
    key_weight = jnp.exp(segment_total[:, None] - running)
    weighted = key_rows.astype(jnp.float32) * key_weight.T[:, :, None]
    local_state = jnp.einsum(
        "shd,she->hde", weighted, values.astype(jnp.float32), precision=lax.Precision.HIGHEST
    )
    scores = jnp.einsum("thd,shd->hts", queries, key_rows, preferred_element_type=jnp.float32)
    row_index = lax.broadcasted_iota(jnp.int32, (segment_len, segment_len), 0)
    col_index = lax.broadcasted_iota(jnp.int32, (segment_len, segment_len), 1)
    causal = row_index >= col_index
    log_gap = running[:, :, None] - running[:, None, :]
    decay_factor = jnp.where(causal[None], jnp.exp(jnp.minimum(log_gap, 0.0)), 0.0)
    weights = (scores * head_width ** (-0.5) * decay_factor).astype(jnp.bfloat16)
    within = jnp.einsum("hts,she->the", weights, values, preferred_element_type=jnp.float32)
    own_index = lax.axis_index("seg")
    parent_id = parent[own_index]
    end_state = local_state
    prefix = jnp.zeros_like(local_state)
    for step_index in range(2):
        gathered = lax.all_gather(end_state[None], "seg", axis=0, tiled=True)
        segment_ids = jnp.arange(gathered.shape[0], dtype=jnp.int32)
        is_parent = segment_ids == parent_id
        prefix = jnp.sum(jnp.where(is_parent[:, None, None, None], gathered, 0.0), axis=0)
        end_state = jnp.exp(segment_total)[:, None, None] * prefix + local_state
    prefix_term = (
        jnp.einsum(
            "thd,hde->the", queries.astype(jnp.float32), prefix, precision=lax.Precision.HIGHEST
        )
        * jnp.exp(running).T[:, :, None]
    )
    attention = (prefix_term + within).reshape(segment_len, head_count * head_width)
    squares = lax.psum(jnp.sum(attention * attention, axis=1), "head")
    total_features = head_count * head_width * lax.axis_size("head")
    inverse = 1.0 / jnp.sqrt(squares / total_features + 1e-06)
    normed = (attention * inverse[:, None] * norm_gain[None, :]).astype(jnp.bfloat16)
    mixed = lax.psum_scatter(
        jnp.dot(normed, w_out, preferred_element_type=jnp.float32),
        "head",
        scatter_dimension=0,
        tiled=True,
    )
    return mixed.astype(jnp.bfloat16)


def solution(mesh):
    return jax.shard_map(
        per_device,
        mesh=mesh,
        in_specs=(
            P("seg", "head"),
            P("seg", "head"),
            P("seg", "head"),
            P("head", "seg"),
            P(),
            P("head"),
            P("head", None),
        ),
        out_specs=P(("seg", "head"), None),
        check_vma=False,
    )
```

profile of v0, /device:TPU:1, one launch (start us, length us, event | category | flops | bytes accessed | tf_op | source)
XLA Modules:
  0.0 356.8 jit_solution(15222258950869572937)
XLA Ops:
  6.5 0.0 copy-start
  6.5 0.0 copy-start.4
  6.5 0.0 all-gather.5.cloned.1.call-start
  6.5 0.8 reshape.66
  7.3 1.1 reduce-window.6
  8.5 0.2 slice_reduce_fusion
  8.6 0.2 reduce-window.9
  8.8 0.1 add_bitcast_fusion
  8.9 0.2 slice_reduce_fusion.1
  9.1 0.1 exponential_bitcast_fusion.1
  9.2 1.4 copy.31
  10.6 1.4 copy.32
  12.0 1.6 fusion.6
  13.6 0.0 copy-start.1
  13.6 0.0 all-gather.5.cloned.1.call-update
  13.7 0.0 all-gather.7.cloned.1.call-start
  13.7 0.0 copy-done.4
  13.7 0.6 dynamic_slice.3
  14.3 0.6 iota_compare_fusion.1
  14.9 100.6 %all-gather.5.cloned.1.call-done = f32[128,128,128]{2,1,0:T(8,128)} async-done(((f32[4,128,128]{2,1,0:T(8,128)}), f32[128,128,128]{2,1,0:T(8,128)}) %all-gather.5.cloned.1.call-update) | async-done | bytes 8388624 | tf_op jit(solution)/shard_map/all_gather | solution.py:34
  115.5 4.5 %select_reduce_fusion.1 = f32[4,128,128]{2,1,0:T(8,128)S(1)} fusion(f32[32,4,128,128]{3,2,1,0:T(8,128)} %bitcast.49, pred[32]{0:T(512)(128)(4,1)S(1)} %iota_compare_fusion.1), kind=kLoop, calls=%fused_computation.2 | loop fusion | flops 4128768 | bytes 8650784 | tf_op jit(solution)/shard_map/reduce_sum | solution.py:37
  120.0 0.0 copy-done.1
  120.0 0.8 multiply_add_fusion
  120.8 0.0 all-gather.7.cloned.1.call-update
  120.8 0.0 reduce-scatter.2.cloned.1.call-start
  120.9 0.2 iota_compare_fusion
  121.0 0.0 copy-done
  121.1 5.6 %fusion = f32[4,768,128]{1,2,0:T(8,128)} fusion(bf16[768,4,128]{0,2,1:T(8,128)(2,1)S(1)} %bitcast.54, f32[4,768]{1,0:T(4,128)S(1)} %get-tuple-element.6, pred[768,768]{1,0:T(8,128)(4,1)S(1)} %iota_compare_fusion, bf16[768,4,128]{0,2,1:T(8,128)(2,1)S(1)} %bitcast.52, bf16[768,512]{1,0:T(8,128)(2,1)S(1)} %copy-done), kind=kOutput, calls=%fused_computation.3 | convolution fusion | flops 1222115328 | bytes 4534272 | tf_op jit(solution)/shard_map/hts,she->the/dot_general | solution.py:28
  126.7 89.7 %all-gather.7.cloned.1.call-done = f32[128,128,128]{2,1,0:T(8,128)} async-done(((f32[4,128,128]{2,1,0:T(8,128)}), f32[128,128,128]{2,1,0:T(8,128)}) %all-gather.7.cloned.1.call-update) | async-done | bytes 8388624 | tf_op jit(solution)/shard_map/all_gather | solution.py:34
  216.3 0.0 copy-start.2
  216.4 0.0 copy-start.3
  216.4 4.6 %select_reduce_fusion = f32[4,128,128]{2,1,0:T(8,128)S(1)} fusion(f32[32,4,128,128]{3,2,1,0:T(8,128)} %bitcast.50, pred[32]{0:T(512)(128)(4,1)S(1)} %iota_compare_fusion.1), kind=kLoop, calls=%fused_computation.1 | loop fusion | flops 4128768 | bytes 8650784 | tf_op jit(solution)/shard_map/reduce_sum | solution.py:37
  221.0 0.0 copy-done.2
  221.0 1.0 multiply_reduce_fusion
  222.0 13.0 %psum.7 = f32[768]{0:T(1024)S(1)} all-reduce(f32[768]{0:T(1024)S(1)} %get-tuple-element.7), channel_id=1, replica_groups=mesh['seg'=32,'head'=8] {'head'}, use_global_device_ids=true, to_apply=%region_5.6 | all-reduce | flops 768 | bytes 6144 | tf_op jit(solution)/shard_map/psum | solution.py:46
  235.1 0.0 copy-done.3
  235.1 0.2 fusion.5
  235.3 12.0 %fusion.18 = f32[768,6144]{1,0:T(8,128)} fusion(bf16[768,512]{0,1:T(8,128)(2,1)S(1)} %fusion.5, bf16[512,6144]{1,0:T(8,128)(2,1)} %param.13), kind=kOutput, calls=%fused_computation.32 | convolution fusion | flops 4831838208 | bytes 25952256 | tf_op jit(solution)/shard_map/dot_general | solution.py:51
  247.2 0.0 reduce-scatter.2.cloned.1.call-update
  247.2 100.2 %reduce-scatter.2.cloned.1.call-done = f32[96,6144]{1,0:T(8,128)} async-done(((f32[768,6144]{1,0:T(8,128)}), f32[96,6144]{1,0:T(8,128)}) %reduce-scatter.2.cloned.1.call-update) | async-done | bytes 2359312 | tf_op jit(solution)/shard_map/reduce_scatter | solution.py:50
  347.4 2.8 convert_element_type.17
  (3 shorter events, 0.0 us)
Async XLA Ops:
  6.5 114.5 %copy-start = (bf16[768,512]{1,0:T(8,128)(2,1)S(1)}, bf16[768,512]{1,0:T(8,128)(2,1)}, u32[]{:S(2)}) copy-start(bf16[768,512]{1,0:T(8,128)(2,1)} %param.7) | copy-start | bytes 2359300
  6.5 7.2 %copy-start.4 = (s32[32]{0:T(128)S(1)}, s32[32]{0:T(128)}, u32[]{:S(2)}) copy-start(s32[32]{0:T(128)} %param.11) | copy-start | bytes 388
  6.5 108.9 %all-gather.5.cloned.1.call-start = ((), (), s32[]{:S(2)}) async-start(), calls=%async_computation.2 | async-start | bytes 8650752 | tf_op jit(solution)/shard_map/all_gather | solution.py:34
  13.6 106.3 %copy-start.1 = (f32[4,128,128]{2,1,0:T(8,128)S(1)}, f32[4,128,128]{2,1,0:T(8,128)}, u32[]{:S(2)}) copy-start(f32[4,128,128]{2,1,0:T(8,128)} %fusion.6) | copy-start | bytes 786436
  13.7 202.7 %all-gather.7.cloned.1.call-start = ((), (), s32[]{:S(2)}) async-start(), calls=%async_computation.3 | async-start | bytes 8650752 | tf_op jit(solution)/shard_map/all_gather | solution.py:34
  120.8 226.6 %reduce-scatter.2.cloned.1.call-start = ((), (), s32[]{:S(2)}) async-start(), calls=%async_computation.1 | async-start | bytes 21233664 | tf_op jit(solution)/shard_map/reduce_scatter | solution.py:50
  216.3 4.6 %copy-start.2 = (f32[4,768,128]{1,2,0:T(8,128)S(1)}, f32[4,768,128]{1,2,0:T(8,128)}, u32[]{:S(2)}) copy-start(f32[4,768,128]{1,2,0:T(8,128)} %fusion) | copy-start | bytes 4718596
  216.4 18.7 %copy-start.3 = (f32[512]{0:T(512)S(1)}, f32[512]{0:T(512)}, u32[]{:S(2)}) copy-start(f32[512]{0:T(512)} %param.12) | copy-start | bytes 6148
Sparse Core Ops, SparseCore 0:
  13.8 101.6 all-gather.4
  120.9 95.3 all-gather.6
  247.4 100.0 reduce-scatter.1
where the time goes:
time: 357 us
  waiting for transfers between devices  290 us (81%)
  matrix products  20.3 us (6%)
  other arithmetic  15.1 us (4%)
  between operations  13.2 us (4%)
  blocking collectives  13 us (4%)
  local copies, waits for them, and re-layouts  4.55 us (1%)
    all_gather x2, waiting for transfers between devices, per_device(): gathered = lax.all_gather(end_state[None], 'seg', axis=0, tiled=True)  190 us
    reduce_scatter x1, waiting for transfers between devices, per_device(): lax.psum_scatter(jnp.dot(normed, w_out, preferred_element_type=jnp.float3...  100 us
    psum x1, blocking collectives, per_device(): squares = lax.psum(jnp.sum(attention * attention, axis=1), 'head')  13 us
    dot_general x1, matrix products, per_device(): jnp.dot(normed, w_out, preferred_element_type=jnp.float32)  12 us
    reduce_sum x2, other arithmetic, per_device(): jnp.sum(jnp.where(is_parent[:, None, None, None], gathered, 0.0), axis=0)  9.08 us
  transfers between devices with their start and end apart: 3, of which 3 were waited for; matrix products, arithmetic and copies ran while one was open for 2% of the time, Pallas kernels for 0%

commit v1 on v0

v1 whole, which is shorter than its diff:
```python
import functools
import jax
import jax.numpy as jnp
from jax import lax
from jax.experimental import pallas as pl
from jax.experimental.pallas import tpu as pltpu
from jax.sharding import PartitionSpec as P

F32, BF16 = jnp.float32, jnp.bfloat16
NT = (((1,), (1,)), ((), ()))
TN = (((0,), (0,)), ((), ()))
NN = (((1,), (0,)), ((), ()))


def dot(a, b, dims=NN):
    return lax.dot_general(a, b, dims, preferred_element_type=F32)


def split(x):
    high = x.astype(BF16)
    return high, (x - high.astype(F32)).astype(BF16)


def state_kernel(decay_ref, k_ref, v_ref, chunks_ref, running_ref, column_ref):
    heads, length = decay_ref.shape
    running = jnp.concatenate([decay_ref[...]] * (8 // heads), axis=0)
    lane = lax.broadcasted_iota(jnp.int32, running.shape, 1)
    shift = 1
    while shift < length:
        running += jnp.where(lane >= shift, pltpu.roll(running, shift, 1), 0.0)
        shift *= 2
    running_ref[...] = running
    column = running.T
    column_ref[...] = column
    for h in range(heads):
        cols = slice(128 * h, 128 * h + 128)
        total = column[length - 1 : length, h : h + 1]
        weight = jnp.exp(total - column[:, h : h + 1])
        high, low = split(k_ref[:, cols].astype(F32) * weight)
        values = v_ref[:, cols]
        state = dot(high, values, TN) + dot(low, values, TN)
        chunks_ref[8 * h : 8 * h + 8, 0:16, :] = state.reshape(8, 16, 128)
        chunks_ref[8 * h : 8 * h + 8, 16:24, :] = jnp.broadcast_to(total.reshape(1, 1, 1), (8, 8, 128))


def prefix_kernel(parent_ref, all_ref, out_ref):
    segments = all_ref.shape[0]

    def body(s, carry):
        first = parent_ref[s]
        p = jnp.clip(first, 0, segments - 1)
        second = parent_ref[p]
        g = jnp.clip(second, 0, segments - 1)
        own = all_ref[p, 0:16, :]
        factor = jnp.exp(all_ref[p, 16:24, :])
        factor = jnp.concatenate([factor, factor], axis=0)
        older = jnp.where(second >= 0, factor * all_ref[g, 0:16, :], 0.0)
        out_ref[s] = jnp.where(first >= 0, own + older, 0.0)
        return carry

    lax.fori_loop(0, segments, body, 0)


def within_kernel(q_ref, k_ref, v_ref, running_ref, column_ref, out_ref):
    length = q_ref.shape[0]
    size = 256
    scale = 128 ** (-0.5)
    causal = lax.broadcasted_iota(jnp.int32, (size, size), 0) >= lax.broadcasted_iota(jnp.int32, (size, size), 1)
    for h in range(4):
        cols = slice(128 * h, 128 * h + 128)
        for i in range(length // size):
            rows = slice(size * i, size * i + size)
            q = q_ref[rows, cols]
            total = None
            for j in range(i + 1):
                inner = slice(size * j, size * j + size)
                scores = dot(q, k_ref[inner, cols], NT)
                gap = column_ref[rows, h : h + 1] - running_ref[h : h + 1, inner]
                factor = jnp.exp(jnp.minimum(gap, 0.0))
                if i == j:
                    factor = jnp.where(causal, factor, 0.0)
                weights = (scores * scale * factor).astype(BF16)
                term = dot(weights, v_ref[inner, cols])
                total = term if total is None else total + term
            out_ref[rows, cols] = total


def mix_kernel(q_ref, prefix_ref, within_ref, column_ref, gain_ref, out_ref, squares_ref):
    squares = None
    for h in range(4):
        cols = slice(128 * h, 128 * h + 128)
        high, low = split(prefix_ref[h])
        q = q_ref[:, cols]
        grown = (dot(q, high) + dot(q, low)) * jnp.exp(column_ref[:, h : h + 1])
        attention = grown + within_ref[:, cols]
        term = jnp.sum(attention * attention, axis=1, keepdims=True)
        squares = term if squares is None else squares + term
        out_ref[:, cols] = (attention * gain_ref[:, cols]).astype(BF16)
    squares_ref[...] = jnp.broadcast_to(squares, squares_ref.shape)


VMEM = pl.BlockSpec(memory_space=pltpu.VMEM)
SMEM = pl.BlockSpec(memory_space=pltpu.SMEM)


def call(kernel, shapes, count, scalars=0, flops=0):
    return pl.pallas_call(
        kernel,
        out_shape=[jax.ShapeDtypeStruct(s, d) for s, d in shapes],
        in_specs=[SMEM] * scalars + [VMEM] * (count - scalars),
        out_specs=[VMEM] * len(shapes),
        compiler_params=pltpu.CompilerParams(vmem_limit_bytes=48 * 2**20),
        cost_estimate=pl.CostEstimate(flops=flops, bytes_accessed=6 * 2**20, transcendentals=0),
    )


def per_device(q, k, v, log_decay, parent, gain, w):
    length, width = q.shape
    chunks, running, column = call(
        state_kernel, [((32, 24, 128), F32), ((8, length), F32), ((length, 8), F32)], 3, flops=2**28
    )(log_decay, k, v)
    everyone = lax.all_to_all(chunks, "seg", 0, 0, tiled=True)
    (within,) = call(within_kernel, [((length, width), F32)], 5, flops=2**31)(q, k, v, running, column)
    (mine,) = call(prefix_kernel, [((32, 16, 128), F32)], 2, scalars=1)(parent, everyone)
    prefix = lax.all_to_all(mine, "seg", 0, 0, tiled=True).reshape(4, 128, 128)
    features, squares = call(mix_kernel, [((length, width), BF16), ((length, 128), F32)], 5, flops=2**28)(
        q, prefix, within, column, gain.reshape(1, width)
    )
    part = jnp.dot(features, w, preferred_element_type=F32)
    mixed = lax.psum_scatter(part, "head", scatter_dimension=0, tiled=True)
    squares = lax.psum_scatter(squares, "head", scatter_dimension=0, tiled=True)
    inverse = 1.0 / jnp.sqrt(squares[:, :1] / (width * lax.axis_size("head")) + 1e-06)
    return (mixed * inverse).astype(BF16)


def solution(mesh):
    return jax.shard_map(
        per_device,
        mesh=mesh,
        in_specs=(P("seg", "head"), P("seg", "head"), P("seg", "head"), P("head", "seg"), P(), P("head"), P("head", None)),
        out_specs=P(("seg", "head"), None),
        check_vma=False,
    )
```

time: 357 us -> 207 us (0.58)
  waiting for transfers between devices: 290 us -> 130 us
  other arithmetic: 15.1 us -> 3.83 us
  blocking collectives: 13 us -> 23.3 us
  Pallas kernels: 0 us -> 8.47 us
  matrix products: 20.3 us -> 11.9 us
  starting transfers between devices: 0.09 us -> 7.54 us
    all_gather x2 -> x0, waiting for transfers between devices: 190 us -> none  [per_device(): gathered = lax.all_gather(end_state[None], 'seg', axis=0, tiled=True)]
    reduce_scatter x1 -> x2, waiting for transfers between devices: 100 us -> 125 us  [the longest x1 107 us: per_device(): mixed = lax.psum_scatter(part, 'head', scatter_dimension=0, tiled=True)]
    all_to_all x0 -> x1, blocking collectives: none -> 23.3 us  [per_device(): everyone = lax.all_to_all(chunks, 'seg', 0, 0, tiled=True)]
    psum x1 -> x0, blocking collectives: 13 us -> none  [per_device(): squares = lax.psum(jnp.sum(attention * attention, axis=1), 'head')]
    reduce_sum x2 -> x0, other arithmetic: 9.08 us -> none  [per_device(): jnp.sum(jnp.where(is_parent[:, None, None, None], gathered, 0.0), axis=0)]
    pallas_call x0 -> x4, Pallas kernels: none -> 8.47 us  [the longest x1 2.91 us: per_device(): call(within_kernel, [((length, width), F32)], 5, flops=2 ** 31)]
    dot_general x4 -> x1, matrix products: 20.3 us -> 11.9 us  [per_device(): part = jnp.dot(features, w, preferred_element_type=F32)]
    unnamed x10 -> x24, local copies, waits for them, and re-layouts: 0.02 us -> 7.98 us
  transfers between devices with their start and end apart: 3 -> 3, of which waited for: 3 -> 3; matrix products, arithmetic and copies ran while one was open for 2% -> 6% of each run, Pallas kernels for 0% -> 1%
where the time goes in v1:
time: 207 us; the launch traced here: 206 us
  waiting for transfers between devices  130 us (63%)
  blocking collectives  23.3 us (11%)
  between operations  13.5 us (7%)
  matrix products  11.9 us (6%)
  Pallas kernels  8.47 us (4%)
  local copies, waits for them, and re-layouts  7.98 us (4%)
  starting transfers between devices  7.54 us (4%)
  other arithmetic  3.83 us (2%)
    reduce_scatter x1, waiting for transfers between devices, per_device(): mixed = lax.psum_scatter(part, 'head', scatter_dimension=0, tiled=True)  107 us
    all_to_all x1, blocking collectives, per_device(): everyone = lax.all_to_all(chunks, 'seg', 0, 0, tiled=True)  23.3 us
    reduce_scatter x1, waiting for transfers between devices, per_device(): squares = lax.psum_scatter(squares, 'head', scatter_dimension=0, tiled=True)  18.3 us
    dot_general x1, matrix products, per_device(): part = jnp.dot(features, w, preferred_element_type=F32)  11.9 us
    unnamed x24, local copies, waits for them, and re-layouts  7.98 us
    all_to_all x1, starting transfers between devices, per_device(): prefix = lax.all_to_all(mine, 'seg', 0, 0, tiled=True).reshape(4, 128, 128)  7.46 us
    all_to_all x1, waiting for transfers between devices, per_device(): prefix = lax.all_to_all(mine, 'seg', 0, 0, tiled=True).reshape(4, 128, 128)  4.54 us
  transfers between devices with their start and end apart: 3, of which 3 were waited for; matrix products, arithmetic and copies ran while one was open for 6% of the time, Pallas kernels for 1%

profile of v1, /device:TPU:1, one launch (start us, length us, event | category | flops | bytes accessed | tf_op | source)
XLA Modules:
  0.0 206.1 jit_solution(16160650165868123141)
XLA Ops:
  6.5 0.0 copy-start
  6.5 1.1 copy-done
  7.7 0.0 copy-start.2
  7.7 1.1 copy-done.2
  8.8 0.0 copy-start.9
  8.8 0.7 copy-done.9
  9.5 0.0 copy-start.11
  9.5 0.0 copy-start.1
  9.5 0.0 copy-start.3
  9.5 1.9 shard_map.73
  11.4 0.0 copy-start.6
  11.4 0.7 copy-done.6
  12.1 23.3 %all_to_all.10.all_ref = f32[32,24,128]{2,1,0:T(8,128)S(1)} all-to-all(f32[32,24,128]{2,1,0:T(8,128)S(1)} %get-tuple-element.10), channel_id=1, replica_groups=mesh['seg'=32,'head'=8] {'seg'}, dimensions={0} | all-to-all | bytes 786432 | tf_op jit(solution)/shard_map/all_to_all | solution.py:122
  35.4 0.0 copy-done.11
  35.4 1.8 shard_map.74
  37.2 7.5 %all-to-all-start.1 = ((f32[32,16,128]{2,1,0:T(8,128)}), f32[32,16,128]{2,1,0:T(8,128)S(1)}, u32[]{:S(2)}, u32[]{:S(2)}) async-start(f32[32,16,128]{2,1,0:T(8,128)} %shard_map.74), calls=%async_computation.1 | async-start | bytes 524288 | tf_op jit(solution)/shard_map/all_to_all | solution.py:125
  44.7 0.0 reduce-scatter.5.cloned.1.call-start
  44.8 0.0 copy-done.1
  44.8 0.0 copy-done.3
  44.8 0.0 copy-start.4
  44.8 1.1 copy-done.4
  45.9 0.0 copy-start.7
  45.9 1.0 copy-done.7
  46.9 0.0 copy-start.10
  46.9 2.9 %shard_map.75.within_ref = f32[768,512]{1,0:T(8,128)S(1)} custom-call(bf16[768,512]{1,0:T(8,128)(2,1)S(1)} %copy-done.4, bf16[768,512]{1,0:T(8,128)(2,1)S(1)} %copy-done.1, bf16[768,512]{1,0:T(8,128)(2,1)S(1)} %copy-done.3, f32[8,768]{1,0:T(8,128)S(1)} %get-tuple-element.11.running_ref, f32[768,8]{1,0:T(8,128)S(1)} %copy-done.7), custom_call_target="tpu_custom_call" | custom-call | flops 2147483648 | bytes 6291456 | tf_op jit(solution)/shard_map/pallas_call | solution.py:123
  49.8 4.5 %all-to-all-done.1 = f32[32,16,128]{2,1,0:T(8,128)S(1)} async-done(((f32[32,16,128]{2,1,0:T(8,128)}), f32[32,16,128]{2,1,0:T(8,128)S(1)}, u32[]{:S(2)}, u32[]{:S(2)}) %all-to-all-start.1) | async-done | bytes 262176 | tf_op jit(solution)/shard_map/all_to_all | solution.py:125
  54.4 0.0 copy-done.10
  54.4 0.0 copy-start.5
  54.4 1.1 copy-done.5
  55.5 0.0 copy-start.8
  55.5 1.0 copy-done.8
  56.5 1.9 shard_map.76
  58.4 0.0 reduce-scatter.5.cloned.1.call-update
  58.4 0.0 reduce-scatter.3.cloned.1.call-start
  58.5 11.9 %fusion.3 = f32[768,6144]{1,0:T(8,128)} fusion(bf16[768,512]{1,0:T(8,128)(2,1)S(1)} %get-tuple-element.13, bf16[512,6144]{1,0:T(8,128)(2,1)} %param.13), kind=kOutput, calls=%fused_computation.5 | convolution fusion | flops 4831838208 | bytes 25952256 | tf_op jit(solution)/shard_map/dot_general | solution.py:129
  70.4 0.0 reduce-scatter.3.cloned.1.call-update
  70.4 18.3 %reduce-scatter.5.cloned.1.call-done = f32[96,128]{1,0:T(8,128)} async-done(((f32[768,128]{1,0:T(8,128)}), f32[96,128]{1,0:T(8,128)}) %reduce-scatter.5.cloned.1.call-update) | async-done | bytes 49168 | tf_op jit(solution)/shard_map/reduce_scatter | solution.py:131
  88.7 0.9 fusion.2
  89.6 106.7 %reduce-scatter.3.cloned.1.call-done = f32[96,6144]{1,0:T(8,128)} async-done(((f32[768,6144]{1,0:T(8,128)}), f32[96,6144]{1,0:T(8,128)}) %reduce-scatter.3.cloned.1.call-update) | async-done | bytes 2359312 | tf_op jit(solution)/shard_map/reduce_scatter | solution.py:130
  196.3 2.9 %multiply_convert_fusion = bf16[96,6144]{1,0:T(8,128)(2,1)} fusion(f32[96,6144]{1,0:T(8,128)} %reduce-scatter.3.cloned.1.call-done, f32[96]{0:T(128)S(1)} %fusion.2), kind=kLoop, calls=%fused_computation | loop fusion | flops 1179648 | bytes 3539328 | tf_op jit(solution)/shard_map/convert_element_type | solution.py:133
Async XLA Ops:
  6.5 1.1 copy-start
  7.7 1.1 copy-start.2
  8.8 0.7 copy-start.9
  9.5 25.9 %copy-start.11 = (s32[32]{0:T(128)S(1)}, s32[32]{0:T(128)}, u32[]{:S(2)}) copy-start(s32[32]{0:T(128)} %parent_ref.1) | copy-start | bytes 388
  9.5 35.3 %copy-start.1 = (bf16[768,512]{1,0:T(8,128)(2,1)S(1)}, bf16[768,512]{1,0:T(8,128)(2,1)}, u32[]{:S(2)}) copy-start(bf16[768,512]{1,0:T(8,128)(2,1)} %k_ref.3) | copy-start | bytes 2359300
  9.5 35.3 %copy-start.3 = (bf16[768,512]{1,0:T(8,128)(2,1)S(1)}, bf16[768,512]{1,0:T(8,128)(2,1)}, u32[]{:S(2)}) copy-start(bf16[768,512]{1,0:T(8,128)(2,1)} %v_ref.3) | copy-start | bytes 2359300
  11.4 0.7 copy-start.6
  37.2 17.1 %all-to-all-start.1 = ((f32[32,16,128]{2,1,0:T(8,128)}), f32[32,16,128]{2,1,0:T(8,128)S(1)}, u32[]{:S(2)}, u32[]{:S(2)}) async-start(f32[32,16,128]{2,1,0:T(8,128)} %shard_map.74), calls=%async_computation.1 | async-start | bytes 524288 | tf_op jit(solution)/shard_map/all_to_all | solution.py:125
  44.7 44.0 %reduce-scatter.5.cloned.1.call-start = ((), (), s32[]{:S(2)}) async-start(), calls=%async_computation.5 | async-start | bytes 442368 | tf_op jit(solution)/shard_map/reduce_scatter | solution.py:131
  44.8 1.1 copy-start.4
  45.9 1.0 copy-start.7
  46.9 7.5 %copy-start.10 = (f32[512]{0:T(512)S(1)}, f32[512]{0:T(512)}, u32[]{:S(2)}) copy-start(f32[512]{0:T(512)} %param.12) | copy-start | bytes 6148
  54.4 1.1 copy-start.5
  55.5 1.0 copy-start.8
  58.4 137.9 %reduce-scatter.3.cloned.1.call-start = ((), (), s32[]{:S(2)}) async-start(), calls=%async_computation.4 | async-start | bytes 21233664 | tf_op jit(solution)/shard_map/reduce_scatter | solution.py:130
Sparse Core Ops, SparseCore 0:
  58.5 30.0 reduce-scatter.4
  91.5 104.8 reduce-scatter.2

commit v2 on v1

--- a/solution.py
+++ b/solution.py
@@ -96,7 +96,71 @@
         term = jnp.sum(attention * attention, axis=1, keepdims=True)
         squares = term if squares is None else squares + term
         out_ref[:, cols] = (attention * gain_ref[:, cols]).astype(BF16)
-    squares_ref[...] = jnp.broadcast_to(squares, squares_ref.shape)
+    squares_ref[...] = jnp.broadcast_to(squares, (squares.shape[0], 128)).T[0:8, :]
+
+
+def project_kernel(index_ref, own_ref, other_ref, w_ref, keep_ref, send_ref):
+    keep_ref[...] = dot(own_ref[0], w_ref[...])
+    send_ref[...] = dot(other_ref[0], w_ref[...])
+
+
+def project(blocks, step, features, w, start, width):
+    rows, depth = features.shape[1:]
+    tile = 1024
+    out = pl.BlockSpec((rows, tile), lambda n, index: (0, n))
+    return pl.pallas_call(
+        project_kernel,
+        out_shape=[jax.ShapeDtypeStruct((rows, width), F32)] * 2,
+        grid_spec=pltpu.PrefetchScalarGridSpec(
+            num_scalar_prefetch=1,
+            grid=(width // tile,),
+            in_specs=[
+                pl.BlockSpec((1, rows, depth), lambda n, index: (index[2 * step], 0, 0)),
+                pl.BlockSpec((1, rows, depth), lambda n, index: (index[2 * step + 1], 0, 0)),
+                pl.BlockSpec((depth, tile), lambda n, index: (0, start // tile + n)),
+            ],
+            out_specs=[out, out],
+        ),
+        compiler_params=pltpu.CompilerParams(vmem_limit_bytes=16 * 2**20),
+        cost_estimate=pl.CostEstimate(flops=4 * rows * depth * width, bytes_accessed=8 * rows * width, transcendentals=0),
+    )(blocks, features, features, w)
+
+
+def finish_kernel(inverse_ref, *refs):
+    terms, out_ref = refs[:3], refs[-1]
+    out_ref[...] = ((terms[0][...] + terms[1][...] + terms[2][...]) * inverse_ref[...]).astype(BF16)
+
+
+def finish(inverse, terms, start, columns, out):
+    rows, width = terms[0].shape
+    tile = 1024
+    block = pl.BlockSpec((rows, tile), lambda n: (0, n))
+    args = [inverse, *terms] + ([] if out is None else [out])
+    return pl.pallas_call(
+        finish_kernel,
+        out_shape=jax.ShapeDtypeStruct((rows, columns), BF16),
+        grid=(width // tile,),
+        in_specs=[pl.BlockSpec((rows, 1), lambda n: (0, 0))] + [block] * 3 + [pl.BlockSpec(memory_space=pl.ANY)] * (out is not None),
+        out_specs=pl.BlockSpec((rows, tile), lambda n: (0, start // tile + n)),
+        input_output_aliases={} if out is None else {4: 0},
+        compiler_params=pltpu.CompilerParams(vmem_limit_bytes=16 * 2**20),
+        cost_estimate=pl.CostEstimate(flops=4 * rows * width, bytes_accessed=14 * rows * width, transcendentals=0),
+    )(*args)
+
+
+def head_pairs(target):
+    pairs = []
+    for y in range(4):
+        for core in range(2):
+            to, to_core = target(y, core)
+            pairs.append((2 * y + core, 2 * (to % 4) + to_core))
+    return pairs
+
+
+SWAP = head_pairs(lambda y, core: (y, 1 - core))
+RING = head_pairs(lambda y, core: (y + 1 - 2 * core, core))
+NEAR = head_pairs(lambda y, core: (y ^ 1, core))
+FAR = head_pairs(lambda y, core: (y ^ 2, core))
 
 
 VMEM = pl.BlockSpec(memory_space=pltpu.VMEM)
@@ -109,7 +173,7 @@
         out_shape=[jax.ShapeDtypeStruct(s, d) for s, d in shapes],
         in_specs=[SMEM] * scalars + [VMEM] * (count - scalars),
         out_specs=[VMEM] * len(shapes),
-        compiler_params=pltpu.CompilerParams(vmem_limit_bytes=48 * 2**20),
+        compiler_params=pltpu.CompilerParams(vmem_limit_bytes=16 * 2**20),
         cost_estimate=pl.CostEstimate(flops=flops, bytes_accessed=6 * 2**20, transcendentals=0),
     )
 
@@ -123,14 +187,31 @@
     (within,) = call(within_kernel, [((length, width), F32)], 5, flops=2**31)(q, k, v, running, column)
     (mine,) = call(prefix_kernel, [((32, 16, 128), F32)], 2, scalars=1)(parent, everyone)
     prefix = lax.all_to_all(mine, "seg", 0, 0, tiled=True).reshape(4, 128, 128)
-    features, squares = call(mix_kernel, [((length, width), BF16), ((length, 128), F32)], 5, flops=2**28)(
+    features, squares = call(mix_kernel, [((length, width), BF16), ((8, length), F32)], 5, flops=2**28)(
         q, prefix, within, column, gain.reshape(1, width)
     )
-    part = jnp.dot(features, w, preferred_element_type=F32)
-    mixed = lax.psum_scatter(part, "head", scatter_dimension=0, tiled=True)
-    squares = lax.psum_scatter(squares, "head", scatter_dimension=0, tiled=True)
-    inverse = 1.0 / jnp.sqrt(squares[:, :1] / (width * lax.axis_size("head")) + 1e-06)
-    return (mixed * inverse).astype(BF16)
+    for pairs in (SWAP, NEAR, FAR):
+        squares = squares + lax.ppermute(squares, "head", pairs)
+    me = lax.axis_index("head")
+    y, core = me >> 1, me & 1
+    way = (1 - 2 * core) * jnp.arange(1, 5, dtype=jnp.int32)
+    blocks = jnp.stack([((y - way) & 3) * 2 + core, ((y + way) & 3) * 2 + 1 - core], axis=1).reshape(8)
+    share = length // 8
+    features = features.reshape(8, share, width)
+    chunks = 2
+    part = w.shape[1] // chunks
+    arrived = [None] * chunks
+    for step in range(1, 5):
+        for chunk in range(chunks):
+            keep, send = project(blocks, step - 1, features, w, chunk * part, part)
+            terms = [keep, lax.ppermute(send, "head", SWAP)] + ([arrived[chunk]] if step > 1 else [])
+            arrived[chunk] = lax.ppermute(sum(terms[1:], terms[0]), "head", RING) if step < 4 else terms
+    squares = lax.dynamic_index_in_dim(squares[0].reshape(8, share), me, 0, keepdims=False)
+    inverse = 1.0 / jnp.sqrt(squares / (width * lax.axis_size("head")) + 1e-06)
+    out = None
+    for chunk in range(chunks):
+        out = finish(inverse[:, None], arrived[chunk], chunk * part, w.shape[1], out)
+    return out
 
 
 def solution(mesh):

time: 207 us -> 160 us (0.77)
  waiting for transfers between devices: 130 us -> 51.1 us
  Pallas kernels: 8.47 us -> 34.9 us
  starting transfers between devices: 7.54 us -> 32.2 us
  between operations: 13.5 us -> 0.18 us
  matrix products: 11.9 us -> 0 us
  local copies, waits for them, and re-layouts: 7.98 us -> 12.5 us
    reduce_scatter x2 -> x0, waiting for transfers between devices: 125 us -> none  [the longest x1 107 us: per_device(): mixed = lax.psum_scatter(part, 'head', scatter_dimension=0, tiled=True)]
    ppermute x0 -> x17, waiting for transfers between devices: none -> 46.7 us  [the longest x6 24.1 us: per_device(): lax.ppermute(sum(terms[1:], terms[0]), 'head', RING)]
    pallas_call x1 -> x11, Pallas kernels: 1.89 us -> 28.3 us  [the longest x8 20.7 us: project(): pl.pallas_call(project_kernel, out_shape=[jax.ShapeDtypeStruct((rows, wid...]
    ppermute x0 -> x17, starting transfers between devices: none -> 24.7 us  [the longest x6 16.2 us: per_device(): lax.ppermute(sum(terms[1:], terms[0]), 'head', RING)]
    dot_general x1 -> x0, matrix products: 11.9 us -> none  [per_device(): part = jnp.dot(features, w, preferred_element_type=F32)]
    add x0 -> x8, other arithmetic: none -> 3.77 us  [the longest x6 3.17 us: per_device(): sum(terms[1:], terms[0])]
    unnamed x24 -> x32, local copies, waits for them, and re-layouts: 7.98 us -> 11.6 us
    convert_element_type x1 -> x0, other arithmetic: 2.91 us -> none  [per_device(): return (mixed * inverse).astype(BF16)]
  transfers between devices with their start and end apart: 3 -> 18, of which waited for: 3 -> 8; matrix products, arithmetic and copies ran while one was open for 6% -> 3% of each run, Pallas kernels for 1% -> 15%
where the time goes in v2:
time: 160 us; the launch traced here: 159 us
  waiting for transfers between devices  51.1 us (32%)
  Pallas kernels  34.9 us (22%)
  starting transfers between devices  32.2 us (20%)
  blocking collectives  23.4 us (15%)
  local copies, waits for them, and re-layouts  12.5 us (8%)
  other arithmetic  4.64 us (3%)
    ppermute x6, waiting for transfers between devices, per_device(): lax.ppermute(sum(terms[1:], terms[0]), 'head', RING)  24.1 us
    all_to_all x1, blocking collectives, per_device(): everyone = lax.all_to_all(chunks, 'seg', 0, 0, tiled=True)  23.4 us
    ppermute x3, waiting for transfers between devices, per_device(): squares = squares + lax.ppermute(squares, 'head', pairs)  22.6 us
    pallas_call x8, Pallas kernels, project(): pl.pallas_call(project_kernel, out_shape=[jax.ShapeDtypeStruct((rows, wid...  20.7 us
    ppermute x6, starting transfers between devices, per_device(): lax.ppermute(sum(terms[1:], terms[0]), 'head', RING)  16.2 us
    unnamed x32, local copies, waits for them, and re-layouts  11.6 us
    all_to_all x1, starting transfers between devices, per_device(): prefix = lax.all_to_all(mine, 'seg', 0, 0, tiled=True).reshape(4, 128, 128)  7.46 us
    pallas_call x2, Pallas kernels, finish(): pl.pallas_call(finish_kernel, out_shape=jax.ShapeDtypeStruct((rows, colum...  6.36 us
  transfers between devices with their start and end apart: 18, of which 8 were waited for; matrix products, arithmetic and copies ran while one was open for 3% of the time, Pallas kernels for 15%

profile of v2, /device:TPU:1, one launch (start us, length us, event | category | flops | bytes accessed | tf_op | source)
XLA Modules:
  0.0 158.9 jit_solution(11213142324249871832)
XLA Ops:
  0.0 1.1 copy-done.1
  1.1 1.1 copy-done.3
  2.3 0.7 copy-done.11
  3.0 1.9 %shard_map.73 = (f32[32,24,128]{2,1,0:T(8,128)S(1)}, f32[8,768]{1,0:T(8,128)S(1)}, f32[768,8]{1,0:T(8,128)S(1)}) custom-call(f32[4,768]{1,0:T(4,128)S(1)} %copy-done.11, bf16[768,512]{1,0:T(8,128)(2,1)S(1)} %copy-done.1, bf16[768,512]{1,0:T(8,128)(2,1)S(1)} %copy-done.3), custom_call_target="tpu_custom_call" | custom-call | flops 268435456 | bytes 6291456 | tf_op jit(solution)/shard_map/pallas_call | solution.py:183
  4.8 0.0 copy-start.8
  4.9 0.7 copy-done.8
  5.6 23.4 %all_to_all.10.all_ref = f32[32,24,128]{2,1,0:T(8,128)S(1)} all-to-all(f32[32,24,128]{2,1,0:T(8,128)S(1)} %get-tuple-element.26), channel_id=1, replica_groups=mesh['seg'=32,'head'=8] {'seg'}, dimensions={0} | all-to-all | bytes 786432 | tf_op jit(solution)/shard_map/all_to_all | solution.py:186
  29.0 1.8 %shard_map.74 = f32[32,16,128]{2,1,0:T(8,128)} custom-call(s32[32]{0:T(128)S(1)} %copy-done.13, f32[32,24,128]{2,1,0:T(8,128)S(1)} %all_to_all.10.all_ref), custom_call_target="tpu_custom_call" | custom-call | bytes 6291456 | tf_op jit(solution)/shard_map/pallas_call | solution.py:188
  30.8 7.5 %all-to-all-start.1 = ((f32[32,16,128]{2,1,0:T(8,128)}), f32[32,16,128]{2,1,0:T(8,128)S(1)}, u32[]{:S(2)}, u32[]{:S(2)}) async-start(f32[32,16,128]{2,1,0:T(8,128)} %shard_map.74), calls=%async_computation.1 | async-start | bytes 524288 | tf_op jit(solution)/shard_map/all_to_all | solution.py:189
  38.3 0.1 pad_add_fusion
  38.4 0.1 reshape.73.index_ref
  38.5 1.1 copy-done.5
  39.6 1.0 copy-done.9
  40.6 2.9 %shard_map.75.within_ref = f32[768,512]{1,0:T(8,128)S(1)} custom-call(bf16[768,512]{1,0:T(8,128)(2,1)S(1)} %copy-done.5, bf16[768,512]{1,0:T(8,128)(2,1)S(1)} %copy-done.2, bf16[768,512]{1,0:T(8,128)(2,1)S(1)} %copy-done.4, f32[8,768]{1,0:T(8,128)S(1)} %get-tuple-element.27.running_ref, f32[768,8]{1,0:T(8,128)S(1)} %copy-done.9), custom_call_target="tpu_custom_call" | custom-call | flops 2147483648 | bytes 6291456 | tf_op jit(solution)/shard_map/pallas_call | solution.py:187
  43.6 4.4 %all-to-all-done.1 = f32[32,16,128]{2,1,0:T(8,128)S(1)} async-done(((f32[32,16,128]{2,1,0:T(8,128)}), f32[32,16,128]{2,1,0:T(8,128)S(1)}, u32[]{:S(2)}, u32[]{:S(2)}) %all-to-all-start.1) | async-done | bytes 262176 | tf_op jit(solution)/shard_map/all_to_all | solution.py:189
  48.0 1.1 copy-done.6
  49.1 1.0 copy-done.10
  50.1 1.2 shard_map.76
  51.3 2.8 %copy-done = bf16[512,6144]{1,0:T(8,128)(2,1)S(1)} copy-done((bf16[512,6144]{1,0:T(8,128)(2,1)S(1)}, bf16[512,6144]{1,0:T(8,128)(2,1)}, u32[]{:S(2)}) %copy-start) | copy-done | bytes 6291480
  54.1 2.4 %shard_map.84 = (f32[96,3072]{1,0:T(8,128)S(1)}, f32[96,3072]{1,0:T(8,128)S(1)}) custom-call(s32[8]{0:T(128)S(1)} %reshape.73.index_ref, bf16[8,96,512]{2,1,0:T(8,128)(2,1)S(1)} %bitcast.7, bf16[8,96,512]{2,1,0:T(8,128)(2,1)S(1)} %bitcast.8, bf16[512,6144]{1,0:T(8,128)(2,1)S(1)} %copy-done), custom_call_target="tpu_custom_call" | custom-call | flops 603979776 | bytes 2359296 | tf_op jit(solution)/shard_map/pallas_call | solution.py:111
  56.5 3.7 %collective-permute-start.13 = (f32[96,3072]{1,0:T(8,128)S(1)}, f32[96,3072]{1,0:T(8,128)S(1)}, u32[]{:S(2)}, u32[]{:S(2)}) collective-permute-start(f32[96,3072]{1,0:T(8,128)S(1)} %get-tuple-element.46), channel_id=1, source_target_pairs={{0,1},{1,0},{2,3},{3,2},{4,5},{5,4},{6,7},{7,6},{8,9},{9,8},{10,11... | collective-permute-start | bytes 3538952 | tf_op jit(solution)/shard_map/ppermute | solution.py:207
  60.2 2.4 %shard_map.80 = (f32[96,3072]{1,0:T(8,128)S(1)}, f32[96,3072]{1,0:T(8,128)S(1)}) custom-call(s32[8]{0:T(128)S(1)} %reshape.73.index_ref, bf16[8,96,512]{2,1,0:T(8,128)(2,1)S(1)} %bitcast.9, bf16[8,96,512]{2,1,0:T(8,128)(2,1)S(1)} %bitcast.10, bf16[512,6144]{1,0:T(8,128)(2,1)S(1)} %copy-done), custom_call_target="tpu_custom_call" | custom-call | flops 603979776 | bytes 2359296 | tf_op jit(solution)/shard_map/pallas_call | solution.py:111
  62.6 0.1 collective-permute-start.6
  62.7 2.4 %shard_map.83 = (f32[96,3072]{1,0:T(8,128)S(1)}, f32[96,3072]{1,0:T(8,128)S(1)}) custom-call(s32[8]{0:T(128)S(1)} %reshape.73.index_ref, bf16[8,96,512]{2,1,0:T(8,128)(2,1)S(1)} %bitcast.11, bf16[8,96,512]{2,1,0:T(8,128)(2,1)S(1)} %bitcast.12, bf16[512,6144]{1,0:T(8,128)(2,1)S(1)} %copy-done), custom_call_target="tpu_custom_call" | custom-call | flops 603979776 | bytes 2359296 | tf_op jit(solution)/shard_map/pallas_call | solution.py:111
  65.1 0.6 collective-permute-start.12
  65.7 0.1 add.123
  65.8 2.8 %collective-permute-start.14 = (f32[96,3072]{1,0:T(8,128)S(1)}, f32[96,3072]{1,0:T(8,128)S(1)}, u32[]{:S(2)}, u32[]{:S(2)}) collective-permute-start(f32[96,3072]{1,0:T(8,128)S(1)} %add.123), channel_id=1, source_target_pairs={{0,2},{1,7},{2,4},{3,1},{4,6},{5,3},{6,0},{7,5},{8,10},{9,15},{10,... | collective-permute-start | bytes 3538952 | tf_op jit(solution)/shard_map/ppermute | solution.py:208
  68.7 2.4 %shard_map.79 = (f32[96,3072]{1,0:T(8,128)S(1)}, f32[96,3072]{1,0:T(8,128)S(1)}) custom-call(s32[8]{0:T(128)S(1)} %reshape.73.index_ref, bf16[8,96,512]{2,1,0:T(8,128)(2,1)S(1)} %bitcast.13, bf16[8,96,512]{2,1,0:T(8,128)(2,1)S(1)} %bitcast.14, bf16[512,6144]{1,0:T(8,128)(2,1)S(1)} %copy-done), custom_call_target="tpu_custom_call" | custom-call | flops 603979776 | bytes 2359296 | tf_op jit(solution)/shard_map/pallas_call | solution.py:111
  71.1 0.1 collective-permute-start.5
  71.2 0.0 collective-permute-done.6
  71.2 0.1 add.118
  71.3 0.7 collective-permute-start.7
  72.0 2.4 %shard_map.82 = (f32[96,3072]{1,0:T(8,128)S(1)}, f32[96,3072]{1,0:T(8,128)S(1)}) custom-call(s32[8]{0:T(128)S(1)} %reshape.73.index_ref, bf16[8,96,512]{2,1,0:T(8,128)(2,1)S(1)} %bitcast.15, bf16[8,96,512]{2,1,0:T(8,128)(2,1)S(1)} %bitcast.16, bf16[512,6144]{1,0:T(8,128)(2,1)S(1)} %copy-done), custom_call_target="tpu_custom_call" | custom-call | flops 603979776 | bytes 2359296 | tf_op jit(solution)/shard_map/pallas_call | solution.py:111
  74.4 0.1 collective-permute-start.11
  74.5 2.4 %shard_map.78 = (f32[96,3072]{1,0:T(8,128)S(1)}, f32[96,3072]{1,0:T(8,128)S(1)}) custom-call(s32[8]{0:T(128)S(1)} %reshape.73.index_ref, bf16[8,96,512]{2,1,0:T(8,128)(2,1)S(1)} %bitcast.17, bf16[8,96,512]{2,1,0:T(8,128)(2,1)S(1)} %bitcast.18, bf16[512,6144]{1,0:T(8,128)(2,1)S(1)} %copy-done), custom_call_target="tpu_custom_call" | custom-call | flops 603979776 | bytes 2359296 | tf_op jit(solution)/shard_map/pallas_call | solution.py:111
  76.9 0.5 collective-permute-start.4
  77.5 4.3 %collective-permute-done.14 = f32[96,3072]{1,0:T(8,128)S(1)} collective-permute-done((f32[96,3072]{1,0:T(8,128)S(1)}, f32[96,3072]{1,0:T(8,128)S(1)}, u32[]{:S(2)}, u32[]{:S(2)}) %collective-permute-start.14) | collective-permute-done | bytes 1179680 | tf_op jit(solution)/shard_map/ppermute | solution.py:208
  81.8 0.2 add_add_fusion
  82.0 3.2 %collective-permute-start.15 = (f32[96,3072]{1,0:T(8,128)S(1)}, f32[96,3072]{1,0:T(8,128)S(1)}, u32[]{:S(2)}, u32[]{:S(2)}) collective-permute-start(f32[96,3072]{1,0:T(8,128)S(1)} %add_add_fusion), channel_id=1, source_target_pairs={{0,2},{1,7},{2,4},{3,1},{4,6},{5,3},{6,0},{7,5},{8,10},{9,15},{10,... | collective-permute-start | bytes 3538952 | tf_op jit(solution)/shard_map/ppermute | solution.py:208
  85.2 9.2 %collective-permute-done.7 = f32[96,3072]{1,0:T(8,128)S(1)} collective-permute-done((f32[96,3072]{1,0:T(8,128)S(1)}, f32[96,3072]{1,0:T(8,128)S(1)}, u32[]{:S(2)}, u32[]{:S(2)}) %collective-permute-start.7) | collective-permute-done | bytes 1179680 | tf_op jit(solution)/shard_map/ppermute | solution.py:208
  94.4 0.2 add_add_fusion.2
  94.7 3.2 %collective-permute-start.8 = (f32[96,3072]{1,0:T(8,128)S(1)}, f32[96,3072]{1,0:T(8,128)S(1)}, u32[]{:S(2)}, u32[]{:S(2)}) collective-permute-start(f32[96,3072]{1,0:T(8,128)S(1)} %add_add_fusion.2), channel_id=1, source_target_pairs={{0,2},{1,7},{2,4},{3,1},{4,6},{5,3},{6,0},{7,5},{8,10},{9,15},{10,... | collective-permute-start | bytes 3538952 | tf_op jit(solution)/shard_map/ppermute | solution.py:208
  97.9 3.2 %shard_map.81 = (f32[96,3072]{1,0:T(8,128)S(1)}, f32[96,3072]{1,0:T(8,128)}) custom-call(s32[8]{0:T(128)S(1)} %reshape.73.index_ref, bf16[8,96,512]{2,1,0:T(8,128)(2,1)S(1)} %bitcast.19, bf16[8,96,512]{2,1,0:T(8,128)(2,1)S(1)} %bitcast.20, bf16[512,6144]{1,0:T(8,128)(2,1)S(1)} %bitcast.6), custom_call_target="tpu_custom_call" | custom-call | flops 603979776 | bytes 2359296 | tf_op jit(solution)/shard_map/pallas_call | solution.py:111
  101.1 3.2 %shard_map.77 = (f32[96,3072]{1,0:T(8,128)S(1)}, f32[96,3072]{1,0:T(8,128)}) custom-call(s32[8]{0:T(128)S(1)} %reshape.73.index_ref, bf16[8,96,512]{2,1,0:T(8,128)(2,1)S(1)} %bitcast.21, bf16[8,96,512]{2,1,0:T(8,128)(2,1)S(1)} %bitcast.22, bf16[512,6144]{1,0:T(8,128)(2,1)S(1)} %bitcast.6), custom_call_target="tpu_custom_call" | custom-call | flops 603979776 | bytes 2359296 | tf_op jit(solution)/shard_map/pallas_call | solution.py:111
  104.3 0.0 collective-permute-done.11
  104.3 0.5 collective-permute-start.3
  104.8 2.3 %collective-permute-done.15 = f32[96,3072]{1,0:T(8,128)S(1)} collective-permute-done((f32[96,3072]{1,0:T(8,128)S(1)}, f32[96,3072]{1,0:T(8,128)S(1)}, u32[]{:S(2)}, u32[]{:S(2)}) %collective-permute-start.15) | collective-permute-done | bytes 1179680 | tf_op jit(solution)/shard_map/ppermute | solution.py:208
  107.1 1.2 add_add_fusion.1
  108.3 3.1 %collective-permute-start.16 = (f32[96,3072]{1,0:T(8,128)}, f32[96,3072]{1,0:T(8,128)}, u32[]{:S(2)}, u32[]{:S(2)}) collective-permute-start(f32[96,3072]{1,0:T(8,128)} %add_add_fusion.1), channel_id=1, source_target_pairs={{0,2},{1,7},{2,4},{3,1},{4,6},{5,3},{6,0},{7,5},{8,10},{9,15},{10,... | collective-permute-start | bytes 3538952 | tf_op jit(solution)/shard_map/ppermute | solution.py:208
  111.4 0.0 collective-permute-done.4
  111.4 8.3 %collective-permute-done.8 = f32[96,3072]{1,0:T(8,128)S(1)} collective-permute-done((f32[96,3072]{1,0:T(8,128)S(1)}, f32[96,3072]{1,0:T(8,128)S(1)}, u32[]{:S(2)}, u32[]{:S(2)}) %collective-permute-start.8) | collective-permute-done | bytes 1179680 | tf_op jit(solution)/shard_map/ppermute | solution.py:208
  119.7 1.2 add_add_fusion.3
  120.9 3.1 %collective-permute-start.9 = (f32[96,3072]{1,0:T(8,128)}, f32[96,3072]{1,0:T(8,128)}, u32[]{:S(2)}, u32[]{:S(2)}) collective-permute-start(f32[96,3072]{1,0:T(8,128)} %add_add_fusion.3), channel_id=1, source_target_pairs={{0,2},{1,7},{2,4},{3,1},{4,6},{5,3},{6,0},{7,5},{8,10},{9,15},{10,... | collective-permute-start | bytes 3538952 | tf_op jit(solution)/shard_map/ppermute | solution.py:208
  124.1 1.2 collective-permute-done
  125.3 19.8 %collective-permute-done.1 = f32[8,768]{1,0:T(8,128)S(1)} collective-permute-done((f32[8,768]{1,0:T(8,128)S(1)}, f32[8,768]{1,0:T(8,128)S(1)}, u32[]{:S(2)}, u32[]{:S(2)}) %collective-permute-start.1) | collective-permute-done | bytes 24608 | tf_op jit(solution)/shard_map/ppermute | solution.py:194
  145.1 0.6 add.106
  145.7 2.9 %collective-permute-start.2 = (f32[8,768]{1,0:T(8,128)}, f32[8,768]{1,0:T(8,128)}, u32[]{:S(2)}, u32[]{:S(2)}) collective-permute-start(f32[8,768]{1,0:T(8,128)} %add.106), channel_id=1, source_target_pairs={{0,4},{1,5},{2,6},{3,7},{4,0},{5,1},{6,2},{7,3},{8,12},{9,13},{10,... | collective-permute-start | bytes 73736 | tf_op jit(solution)/shard_map/ppermute | solution.py:194
  148.6 1.6 %collective-permute-done.2 = f32[8,768]{1,0:T(8,128)} collective-permute-done((f32[8,768]{1,0:T(8,128)}, f32[8,768]{1,0:T(8,128)}, u32[]{:S(2)}, u32[]{:S(2)}) %collective-permute-start.2) | collective-permute-done | bytes 24608 | tf_op jit(solution)/shard_map/ppermute | solution.py:194
  150.2 0.8 fusion
  151.0 0.1 reshape_squeeze.3
  151.1 0.7 copy.12.inverse_ref
  151.8 0.8 copy-done.7
  152.6 3.0 %shard_map.85.refs_3_ = bf16[96,6144]{1,0:T(8,128)(2,1)} custom-call(f32[96,1]{1,0:T(8,128)S(1)} %copy-done.7, f32[96,3072]{1,0:T(8,128)S(1)} %get-tuple-element.39.refs_0_, f32[96,3072]{1,0:T(8,128)S(1)} %collective-permute-done.10.refs_1_, f32[96,3072]{1,0:T(8,128)} %collective-permute-done.16.refs_2_), custom_call_target="tpu_custom_call" | custom-call | flops 1179648 | bytes 4128768 | tf_op jit(solution)/shard_map/pallas_call | solution.py:139
  155.6 3.3 %shard_map.86 = bf16[96,6144]{1,0:T(8,128)(2,1)} custom-call(f32[96,1]{1,0:T(8,128)S(1)} %copy-done.7, f32[96,3072]{1,0:T(8,128)S(1)} %get-tuple-element.31.refs_0_, f32[96,3072]{1,0:T(8,128)} %collective-permute-done.3.refs_1_, f32[96,3072]{1,0:T(8,128)} %collective-permute-done.9.refs_2_, ...), custom_call_target="tpu_custom_call", output_to_operand_aliasing={{}: (4, {})} | custom-call | flops 1179648 | bytes 4128768 | tf_op jit(solution)/shard_map/pallas_call | solution.py:139
  (35 shorter events, 0.1 us)
Async XLA Ops:
  0.0 1.1 copy-start.1
  1.1 1.1 copy-start.3
  2.3 0.7 copy-start.11
  3.0 26.1 %copy-start.13 = (s32[32]{0:T(128)S(1)}, s32[32]{0:T(128)}, u32[]{:S(2)}) copy-start(s32[32]{0:T(128)} %parent_ref.1) | copy-start | bytes 388
  4.8 0.7 copy-start.8
  5.6 32.9 %copy-start.2 = (bf16[768,512]{1,0:T(8,128)(2,1)S(1)}, bf16[768,512]{1,0:T(8,128)(2,1)}, u32[]{:S(2)}) copy-start(bf16[768,512]{1,0:T(8,128)(2,1)} %k_ref.3) | copy-start | bytes 2359300
  5.6 32.9 %copy-start.4 = (bf16[768,512]{1,0:T(8,128)(2,1)S(1)}, bf16[768,512]{1,0:T(8,128)(2,1)}, u32[]{:S(2)}) copy-start(bf16[768,512]{1,0:T(8,128)(2,1)} %v_ref.3) | copy-start | bytes 2359300
  30.8 17.1 %all-to-all-start.1 = ((f32[32,16,128]{2,1,0:T(8,128)}), f32[32,16,128]{2,1,0:T(8,128)S(1)}, u32[]{:S(2)}, u32[]{:S(2)}) async-start(f32[32,16,128]{2,1,0:T(8,128)} %shard_map.74), calls=%async_computation.1 | async-start | bytes 524288 | tf_op jit(solution)/shard_map/all_to_all | solution.py:189
  38.5 1.1 copy-start.5
  39.6 1.0 copy-start.9
  40.6 7.3 %copy-start.12 = (f32[512]{0:T(512)S(1)}, f32[512]{0:T(512)}, u32[]{:S(2)}) copy-start(f32[512]{0:T(512)} %param.12) | copy-start | bytes 6148
  48.0 1.1 copy-start.6
  49.1 1.0 copy-start.10
  51.3 2.8 %copy-start = (bf16[512,6144]{1,0:T(8,128)(2,1)S(1)}, bf16[512,6144]{1,0:T(8,128)(2,1)}, u32[]{:S(2)}) copy-start(bf16[512,6144]{1,0:T(8,128)(2,1)} %w_ref.15) | copy-start | bytes 18874372
  56.5 9.2 %collective-permute-start.13 = (f32[96,3072]{1,0:T(8,128)S(1)}, f32[96,3072]{1,0:T(8,128)S(1)}, u32[]{:S(2)}, u32[]{:S(2)}) collective-permute-start(f32[96,3072]{1,0:T(8,128)S(1)} %get-tuple-element.46), channel_id=1, source_target_pairs={{0,1},{1,0},{2,3},{3,2},{4,5},{5,4},{6,7},{7,6},{8,9},{9,8},{10,11... | collective-permute-start | bytes 3538952 | tf_op jit(solution)/shard_map/ppermute | solution.py:207
  62.6 8.5 %collective-permute-start.6 = (f32[96,3072]{1,0:T(8,128)S(1)}, f32[96,3072]{1,0:T(8,128)S(1)}, u32[]{:S(2)}, u32[]{:S(2)}) collective-permute-start(f32[96,3072]{1,0:T(8,128)S(1)} %get-tuple-element.38), channel_id=1, source_target_pairs={{0,1},{1,0},{2,3},{3,2},{4,5},{5,4},{6,7},{7,6},{8,9},{9,8},{10,11... | collective-permute-start | bytes 3538952 | tf_op jit(solution)/shard_map/ppermute | solution.py:207
  65.1 11.8 %collective-permute-start.12 = (f32[96,3072]{1,0:T(8,128)S(1)}, f32[96,3072]{1,0:T(8,128)S(1)}, u32[]{:S(2)}, u32[]{:S(2)}) collective-permute-start(f32[96,3072]{1,0:T(8,128)S(1)} %get-tuple-element.44), channel_id=1, source_target_pairs={{0,1},{1,0},{2,3},{3,2},{4,5},{5,4},{6,7},{7,6},{8,9},{9,8},{10,11... | collective-permute-start | bytes 3538952 | tf_op jit(solution)/shard_map/ppermute | solution.py:207
  65.8 16.0 %collective-permute-start.14 = (f32[96,3072]{1,0:T(8,128)S(1)}, f32[96,3072]{1,0:T(8,128)S(1)}, u32[]{:S(2)}, u32[]{:S(2)}) collective-permute-start(f32[96,3072]{1,0:T(8,128)S(1)} %add.123), channel_id=1, source_target_pairs={{0,2},{1,7},{2,4},{3,1},{4,6},{5,3},{6,0},{7,5},{8,10},{9,15},{10,... | collective-permute-start | bytes 3538952 | tf_op jit(solution)/shard_map/ppermute | solution.py:208
  71.1 14.2 %collective-permute-start.5 = (f32[96,3072]{1,0:T(8,128)S(1)}, f32[96,3072]{1,0:T(8,128)S(1)}, u32[]{:S(2)}, u32[]{:S(2)}) collective-permute-start(f32[96,3072]{1,0:T(8,128)S(1)} %get-tuple-element.36), channel_id=1, source_target_pairs={{0,1},{1,0},{2,3},{3,2},{4,5},{5,4},{6,7},{7,6},{8,9},{9,8},{10,11... | collective-permute-start | bytes 3538952 | tf_op jit(solution)/shard_map/ppermute | solution.py:207
  71.3 23.1 %collective-permute-start.7 = (f32[96,3072]{1,0:T(8,128)S(1)}, f32[96,3072]{1,0:T(8,128)S(1)}, u32[]{:S(2)}, u32[]{:S(2)}) collective-permute-start(f32[96,3072]{1,0:T(8,128)S(1)} %add.118), channel_id=1, source_target_pairs={{0,2},{1,7},{2,4},{3,1},{4,6},{5,3},{6,0},{7,5},{8,10},{9,15},{10,... | collective-permute-start | bytes 3538952 | tf_op jit(solution)/shard_map/ppermute | solution.py:208
  74.4 29.9 %collective-permute-start.11 = (f32[96,3072]{1,0:T(8,128)S(1)}, f32[96,3072]{1,0:T(8,128)S(1)}, u32[]{:S(2)}, u32[]{:S(2)}) collective-permute-start(f32[96,3072]{1,0:T(8,128)S(1)} %get-tuple-element.42), channel_id=1, source_target_pairs={{0,1},{1,0},{2,3},{3,2},{4,5},{5,4},{6,7},{7,6},{8,9},{9,8},{10,11... | collective-permute-start | bytes 3538952 | tf_op jit(solution)/shard_map/ppermute | solution.py:207
  74.5 23.4 %slice-start = ((s8[6291456]{0:T(1024)(128)(4,1)}), s8[4194304]{0:T(1024)(128)(4,1)S(1)}, s32[]{:S(2)}) async-start(s8[6291456]{0:T(1024)(128)(4,1)} %bitcast.5), calls=%async_computation.2 | async-start | bytes 8388608
  76.9 34.5 %collective-permute-start.4 = (f32[96,3072]{1,0:T(8,128)S(1)}, f32[96,3072]{1,0:T(8,128)S(1)}, u32[]{:S(2)}, u32[]{:S(2)}) collective-permute-start(f32[96,3072]{1,0:T(8,128)S(1)} %get-tuple-element.34), channel_id=1, source_target_pairs={{0,1},{1,0},{2,3},{3,2},{4,5},{5,4},{6,7},{7,6},{8,9},{9,8},{10,11... | collective-permute-start | bytes 3538952 | tf_op jit(solution)/shard_map/ppermute | solution.py:207
  81.8 16.1 %slice-start.1 = ((s8[6291456]{0:T(1024)(128)(4,1)}), s8[2097152]{0:T(1024)(128)(4,1)S(1)}, s32[]{:S(2)}) async-start(s8[6291456]{0:T(1024)(128)(4,1)} %bitcast.5), calls=%async_computation.3 | async-start | bytes 4194304
  82.0 25.0 %collective-permute-start.15 = (f32[96,3072]{1,0:T(8,128)S(1)}, f32[96,3072]{1,0:T(8,128)S(1)}, u32[]{:S(2)}, u32[]{:S(2)}) collective-permute-start(f32[96,3072]{1,0:T(8,128)S(1)} %add_add_fusion), channel_id=1, source_target_pairs={{0,2},{1,7},{2,4},{3,1},{4,6},{5,3},{6,0},{7,5},{8,10},{9,15},{10,... | collective-permute-start | bytes 3538952 | tf_op jit(solution)/shard_map/ppermute | solution.py:208
  94.7 25.0 %collective-permute-start.8 = (f32[96,3072]{1,0:T(8,128)S(1)}, f32[96,3072]{1,0:T(8,128)S(1)}, u32[]{:S(2)}, u32[]{:S(2)}) collective-permute-start(f32[96,3072]{1,0:T(8,128)S(1)} %add_add_fusion.2), channel_id=1, source_target_pairs={{0,2},{1,7},{2,4},{3,1},{4,6},{5,3},{6,0},{7,5},{8,10},{9,15},{10,... | collective-permute-start | bytes 3538952 | tf_op jit(solution)/shard_map/ppermute | solution.py:208
  101.1 50.7 %collective-permute-start.10 = (f32[96,3072]{1,0:T(8,128)}, f32[96,3072]{1,0:T(8,128)S(1)}, u32[]{:S(2)}, u32[]{:S(2)}) collective-permute-start(f32[96,3072]{1,0:T(8,128)} %get-tuple-element.40), channel_id=1, source_target_pairs={{0,1},{1,0},{2,3},{3,2},{4,5},{5,4},{6,7},{7,6},{8,9},{9,8},{10,11... | collective-permute-start | bytes 3538952 | tf_op jit(solution)/shard_map/ppermute | solution.py:207
  104.3 51.3 %collective-permute-start.3 = (f32[96,3072]{1,0:T(8,128)}, f32[96,3072]{1,0:T(8,128)}, u32[]{:S(2)}, u32[]{:S(2)}) collective-permute-start(f32[96,3072]{1,0:T(8,128)} %get-tuple-element.32), channel_id=1, source_target_pairs={{0,1},{1,0},{2,3},{3,2},{4,5},{5,4},{6,7},{7,6},{8,9},{9,8},{10,11... | collective-permute-start | bytes 3538952 | tf_op jit(solution)/shard_map/ppermute | solution.py:207
  108.3 43.5 %collective-permute-start.16 = (f32[96,3072]{1,0:T(8,128)}, f32[96,3072]{1,0:T(8,128)}, u32[]{:S(2)}, u32[]{:S(2)}) collective-permute-start(f32[96,3072]{1,0:T(8,128)} %add_add_fusion.1), channel_id=1, source_target_pairs={{0,2},{1,7},{2,4},{3,1},{4,6},{5,3},{6,0},{7,5},{8,10},{9,15},{10,... | collective-permute-start | bytes 3538952 | tf_op jit(solution)/shard_map/ppermute | solution.py:208
  120.9 34.7 %collective-permute-start.9 = (f32[96,3072]{1,0:T(8,128)}, f32[96,3072]{1,0:T(8,128)}, u32[]{:S(2)}, u32[]{:S(2)}) collective-permute-start(f32[96,3072]{1,0:T(8,128)} %add_add_fusion.3), channel_id=1, source_target_pairs={{0,2},{1,7},{2,4},{3,1},{4,6},{5,3},{6,0},{7,5},{8,10},{9,15},{10,... | collective-permute-start | bytes 3538952 | tf_op jit(solution)/shard_map/ppermute | solution.py:208
  124.1 1.2 collective-permute-start
  125.3 19.8 %collective-permute-start.1 = (f32[8,768]{1,0:T(8,128)S(1)}, f32[8,768]{1,0:T(8,128)S(1)}, u32[]{:S(2)}, u32[]{:S(2)}) collective-permute-start(f32[8,768]{1,0:T(8,128)S(1)} %add.105), channel_id=1, source_target_pairs={{0,2},{1,3},{2,0},{3,1},{4,6},{5,7},{6,4},{7,5},{8,10},{9,11},{10,... | collective-permute-start | bytes 73736 | tf_op jit(solution)/shard_map/ppermute | solution.py:194
  145.7 4.5 %collective-permute-start.2 = (f32[8,768]{1,0:T(8,128)}, f32[8,768]{1,0:T(8,128)}, u32[]{:S(2)}, u32[]{:S(2)}) collective-permute-start(f32[8,768]{1,0:T(8,128)} %add.106), channel_id=1, source_target_pairs={{0,4},{1,5},{2,6},{3,7},{4,0},{5,1},{6,2},{7,3},{8,12},{9,13},{10,... | collective-permute-start | bytes 73736 | tf_op jit(solution)/shard_map/ppermute | solution.py:194
  151.8 0.8 copy-start.7

commit v3 on v1

v3 whole, which is shorter than its diff:
```python
import functools
import jax
import jax.numpy as jnp
from jax import lax
from jax.experimental import pallas as pl
from jax.experimental.pallas import tpu as pltpu
from jax.sharding import PartitionSpec as P

F32, BF16 = jnp.float32, jnp.bfloat16
NT = (((1,), (1,)), ((), ()))
TN = (((0,), (0,)), ((), ()))
NN = (((1,), (0,)), ((), ()))


def dot(a, b, dims=NN):
    return lax.dot_general(a, b, dims, preferred_element_type=F32)


def split(x):
    high = x.astype(BF16)
    return high, (x - high.astype(F32)).astype(BF16)


def load(sems, *pairs):
    copies = [pltpu.make_async_copy(source, target, sems.at[i]) for i, (source, target) in enumerate(pairs)]
    for copy in copies:
        copy.start()
    return copies


def state_kernel(decay_hbm, k_hbm, v_hbm, chunks_ref, running_ref, decay_ref, k_ref, v_ref, sems):
    copies = load(sems, (decay_hbm, decay_ref), (k_hbm, k_ref), (v_hbm, v_ref))
    copies[0].wait()
    heads, length = decay_ref.shape
    running = jnp.concatenate([decay_ref[...]] * (8 // heads), axis=0)
    lane = lax.broadcasted_iota(jnp.int32, running.shape, 1)
    shift = 1
    while shift < length:
        running += jnp.where(lane >= shift, pltpu.roll(running, shift, 1), 0.0)
        shift *= 2
    running_ref[...] = running
    column = running.T
    copies[1].wait()
    copies[2].wait()
    for h in range(heads):
        cols = slice(128 * h, 128 * h + 128)
        total = column[length - 1 : length, h : h + 1]
        weight = jnp.exp(total - column[:, h : h + 1])
        high, low = split(k_ref[:, cols].astype(F32) * weight)
        values = v_ref[:, cols]
        state = dot(high, values, TN) + dot(low, values, TN)
        chunks_ref[8 * h : 8 * h + 8, 0:16, :] = state.reshape(8, 16, 128)
        chunks_ref[8 * h : 8 * h + 8, 16:24, :] = jnp.broadcast_to(total.reshape(1, 1, 1), (8, 8, 128))


def prefix_kernel(parent_ref, all_ref, out_ref):
    segments = all_ref.shape[0]
    for s in range(segments):
        first = parent_ref[s]
        p = jnp.clip(first, 0, segments - 1)
        second = parent_ref[p]
        g = jnp.clip(second, 0, segments - 1)
        own = all_ref[p, 0:16, :]
        factor = jnp.exp(all_ref[p, 16:24, :])
        factor = jnp.concatenate([factor, factor], axis=0)
        older = jnp.where(second >= 0, factor * all_ref[g, 0:16, :], 0.0)
        out_ref[s] = jnp.where(first >= 0, own + older, 0.0)


def within_kernel(first, q_hbm, k_hbm, v_hbm, running_ref, out_ref, *rest):
    q_ref, k_ref, v_ref, sems = rest[-4:]
    copies = load(sems, (q_hbm, q_ref), (k_hbm, k_ref), (v_hbm, v_ref))
    length = q_ref.shape[0]
    size = 256
    scale = 128 ** (-0.5)
    causal = lax.broadcasted_iota(jnp.int32, (size, size), 0) >= lax.broadcasted_iota(jnp.int32, (size, size), 1)
    column = running_ref[...].T
    for copy in copies:
        copy.wait()
    for h in range(first, first + 2):
        cols = slice(128 * h, 128 * h + 128)
        for i in range(length // size):
            rows = slice(size * i, size * i + size)
            q = q_ref[rows, cols]
            total = None
            for j in range(i + 1):
                inner = slice(size * j, size * j + size)
                scores = dot(q, k_ref[inner, cols], NT)
                gap = column[rows, h : h + 1] - running_ref[h : h + 1, inner]
                factor = jnp.exp(jnp.minimum(gap, 0.0))
                if i == j:
                    factor = jnp.where(causal, factor, 0.0)
                weights = (scores * scale * factor).astype(BF16)
                term = dot(weights, v_ref[inner, cols])
                total = term if total is None else total + term
            out_ref[rows, cols.start - 128 * first : cols.stop - 128 * first] = total
    if len(rest) > 4:
        rest[0][...] = q_ref[...]


def mix_kernel(q_ref, prefix_ref, early_ref, late_ref, running_ref, gain_ref, out_ref, squares_ref):
    parts, share = out_ref.shape[:2]
    growth = jnp.exp(running_ref[...].T)
    squares = None
    for h in range(4):
        cols = slice(128 * h, 128 * h + 128)
        high, low = split(prefix_ref[h])
        q = q_ref[:, cols]
        inner = (early_ref if h < 2 else late_ref)[:, 128 * (h % 2) : 128 * (h % 2) + 128]
        attention = (dot(q, high) + dot(q, low)) * growth[:, h : h + 1] + inner
        term = jnp.sum(attention * attention, axis=1, keepdims=True)
        squares = term if squares is None else squares + term
        out_ref[:, :, cols] = (attention * gain_ref[:, cols]).astype(BF16).reshape(parts, share, 128)
    squares_ref[...] = jnp.broadcast_to(squares, (parts * share, 128)).reshape(parts, share, 128)


def project_kernel(step, start, index_ref, features_ref, squares_ref, w_hbm, keep_ref, send_ref, w_ref, sems):
    own, other = index_ref[2 * step], index_ref[2 * step + 1]
    rows = features_ref.shape[1]
    width = keep_ref.shape[1] - (128 if start == 0 else 0)
    tiles = [slice(n, n + 512) for n in range(0, width, 512)]
    copies = load(sems, *[(w_hbm.at[:, start + t.start : start + t.stop], w_ref.at[:, t]) for t in tiles])
    left = jnp.concatenate([features_ref[own], features_ref[other]], axis=0)
    for copy, t in zip(copies, tiles):
        copy.wait()
        both = dot(left, w_ref[:, t])
        keep_ref[:, t] = both[:rows]
        send_ref[:, t] = both[rows:]
    if start == 0:
        keep_ref[:, width:] = squares_ref[own]
        send_ref[:, width:] = squares_ref[other]


def add_kernel(index_ref, keep_ref, arrived_ref, total_ref, next_ref):
    total_ref[...] = keep_ref[...] + arrived_ref[...]
    for i in range(8):
        next_ref[i] = index_ref[i]


def finish_kernel(start, features, *refs):
    terms = refs[:3]
    if start == 0:
        out_hbm, inverse_ref, buffer, sems = refs[3:]
        width = terms[0].shape[1] - 128
        squares = terms[0][:, width:] + terms[1][:, width:] + terms[2][:, width:]
        inverse_ref[...] = 1.0 / jnp.sqrt(squares / features + 1e-06)
    else:
        inverse_ref, _, out_hbm, buffer, sems = refs[3:]
        width = terms[0].shape[1]
    inverse = inverse_ref[:, 0:1]
    tile = 1024
    copies = []
    for i, n in enumerate(range(0, width, tile)):
        cols = slice(n, n + tile)
        buffer[:, cols] = ((terms[0][:, cols] + terms[1][:, cols] + terms[2][:, cols]) * inverse).astype(BF16)
        copy = pltpu.make_async_copy(buffer.at[:, cols], out_hbm.at[:, start + n : start + n + tile], sems.at[i])
        copy.start()
        copies.append(copy)
    for copy in copies:
        copy.wait()


VMEM = pl.BlockSpec(memory_space=pltpu.VMEM)
SMEM = pl.BlockSpec(memory_space=pltpu.SMEM)
ANY = pl.BlockSpec(memory_space=pl.ANY)
HBM = pl.BlockSpec(memory_space=pltpu.HBM)


def call(kernel, shapes, ins, outs=None, scratch=(), aliases=None, flops=2**28, moved=2**20, vmem=16 * 2**20):
    return pl.pallas_call(
        kernel,
        out_shape=[jax.ShapeDtypeStruct(s, d) for s, d in shapes],
        in_specs=ins,
        out_specs=outs or [VMEM] * len(shapes),
        scratch_shapes=list(scratch),
        input_output_aliases=aliases or {},
        compiler_params=pltpu.CompilerParams(vmem_limit_bytes=vmem),
        cost_estimate=pl.CostEstimate(flops=flops, bytes_accessed=moved, transcendentals=0),
    )


def head_pairs(target):
    pairs = []
    for y in range(4):
        for core in range(2):
            to, to_core = target(y, core)
            pairs.append((2 * y + core, 2 * (to % 4) + to_core))
    return pairs


SWAP = head_pairs(lambda y, core: (y, 1 - core))
RING = head_pairs(lambda y, core: (y + 1 - 2 * core, core))

def per_device(q, k, v, log_decay, parent, gain, w):
    length, width = q.shape
    dma = pltpu.SemaphoreType.DMA
    chunks, running = call(
        state_kernel,
        [((32, 24, 128), F32), ((8, length), F32)],
        [HBM] * 3,
        scratch=[pltpu.VMEM(log_decay.shape, F32), pltpu.VMEM(k.shape, BF16), pltpu.VMEM(v.shape, BF16), dma((3,))],
        vmem=253 * 2**18,
    )(log_decay, k, v)
    everyone = lax.all_to_all(chunks, "seg", 0, 0, tiled=True)
    inputs = [pltpu.VMEM(q.shape, BF16)] * 3 + [dma((3,))]
    (early,) = call(
        functools.partial(within_kernel, 0), [((length, width // 2), F32)], [HBM] * 3 + [VMEM], scratch=inputs, flops=2**30
    )(q, k, v, running)
    everyone, early, running = lax.optimization_barrier((everyone, early, running))
    (mine,) = call(prefix_kernel, [((32, 16, 128), F32)], [SMEM, VMEM])(parent, everyone)
    prefix = lax.all_to_all(mine, "seg", 0, 0, tiled=True).reshape(4, 128, 128)
    late, q_near = call(
        functools.partial(within_kernel, 2),
        [((length, width // 2), F32), (q.shape, BF16)],
        [HBM] * 3 + [VMEM],
        scratch=inputs,
        flops=2**30,
    )(q, k, v, running)
    me = lax.axis_index("head")
    y, core = me >> 1, me & 1
    way = (1 - 2 * core) * jnp.arange(1, 5, dtype=jnp.int32)
    blocks = jnp.stack([((y - way) & 3) * 2 + core, ((y + way) & 3) * 2 + 1 - core], axis=1).reshape(8)
    share = length // 8
    features, squares = call(mix_kernel, [((8, share, width), BF16), ((8, share, 128), F32)], [VMEM] * 6)(
        q_near, prefix, early, late, running, gain.reshape(1, width)
    )
    chunks = 2
    part = w.shape[1] // chunks
    arrived = [None] * chunks
    for step in range(1, 5):
        terms = []
        for chunk in range(chunks):
            start = chunk * part
            shape = ((share, part + (128 if chunk == 0 else 0)), F32)
            keep, send = call(
                functools.partial(project_kernel, step - 1, start),
                [shape, shape],
                [SMEM, VMEM, VMEM, HBM],
                scratch=[pltpu.VMEM((width, part), BF16), dma((part // 512,))],
                flops=2**22,
                moved=2**14,
                vmem=(50 if step == 1 else 16) * 2**20,
            )(blocks, features, squares, w)
            terms.append([keep, lax.ppermute(send, "head", SWAP)] + ([arrived[chunk]] if step > 1 else []))
        if step < 4:
            totals = [None] * chunks
            for chunk in reversed(range(chunks)):
                t = terms[chunk]
                if step == 1:
                    totals[chunk], blocks = call(
                        add_kernel, [(t[0].shape, F32), ((8,), jnp.int32)], [SMEM, VMEM, VMEM], outs=[VMEM, SMEM], flops=2**20, moved=2**14
                    )(blocks, *t)
                else:
                    totals[chunk] = sum(t[1:], t[0])
            arrived = [lax.ppermute(total, "head", RING) for total in totals]
    out = ((share, w.shape[1]), BF16)
    scratch = [pltpu.VMEM((share, part), BF16), dma((part // 1024,))]
    total_features = width * lax.axis_size("head")
    half, inverse = call(
        functools.partial(finish_kernel, 0, total_features),
        [out, ((share, 128), F32)],
        [VMEM] * 3,
        outs=[ANY, VMEM],
        scratch=scratch,
    )(*terms[0])
    (mixed,) = call(
        functools.partial(finish_kernel, part, total_features),
        [out],
        [VMEM] * 4 + [ANY],
        outs=[ANY],
        scratch=scratch,
        aliases={4: 0},
    )(*terms[1], inverse, half)
    return mixed


def solution(mesh):
    return jax.shard_map(
        per_device,
        mesh=mesh,
        in_specs=(P("seg", "head"), P("seg", "head"), P("seg", "head"), P("head", "seg"), P(), P("head"), P("head", None)),
        out_specs=P(("seg", "head"), None),
        check_vma=False,
    )
```

time: 207 us -> 149 us (0.72)
  waiting for transfers between devices: 130 us -> 60.8 us
  starting transfers between devices: 7.54 us -> 41.3 us
  Pallas kernels: 8.47 us -> 37.9 us
  blocking collectives: 23.3 us -> 0 us
  between operations: 13.5 us -> 0.46 us
  matrix products: 11.9 us -> 0 us
  other arithmetic: 3.83 us -> 0.79 us
    reduce_scatter x2 -> x0, waiting for transfers between devices: 125 us -> none  [the longest x1 107 us: per_device(): mixed = lax.psum_scatter(part, 'head', scatter_dimension=0, tiled=True)]
    ppermute x0 -> x14, waiting for transfers between devices: none -> 49.8 us  [the longest x6 47.3 us: per_device(): arrived = [lax.ppermute(total, 'head', RING) for total in totals]]
    pallas_call x4 -> x17, Pallas kernels: 8.47 us -> 37.9 us  [the longest x8 23.5 us: per_device(): call(functools.partial(project_kernel, step - 1, start), [shape, shape],...]
    all_to_all x1 -> x0, blocking collectives: 23.3 us -> none  [per_device(): everyone = lax.all_to_all(chunks, 'seg', 0, 0, tiled=True)]
    ppermute x0 -> x14, starting transfers between devices: none -> 22 us  [the longest x6 16 us: per_device(): arrived = [lax.ppermute(total, 'head', RING) for total in totals]]
    dot_general x1 -> x0, matrix products: 11.9 us -> none  [per_device(): part = jnp.dot(features, w, preferred_element_type=F32)]
    all_to_all x0 -> x1, starting transfers between devices: none -> 11.9 us  [per_device(): everyone = lax.all_to_all(chunks, 'seg', 0, 0, tiled=True)]
    all_to_all x0 -> x1, waiting for transfers between devices: none -> 5.52 us  [per_device(): everyone = lax.all_to_all(chunks, 'seg', 0, 0, tiled=True)]
  transfers between devices with their start and end apart: 3 -> 16, of which waited for: 3 -> 9; matrix products, arithmetic and copies ran while one was open for 6% -> 1% of each run, Pallas kernels for 1% -> 16%
where the time goes in v3:
time: 149 us
  waiting for transfers between devices  60.8 us (41%)
  starting transfers between devices  41.3 us (28%)
  Pallas kernels  37.9 us (25%)
  local copies, waits for them, and re-layouts  7.39 us (5%)
    ppermute x6, waiting for transfers between devices, per_device(): arrived = [lax.ppermute(total, 'head', RING) for total in totals]  47.3 us
    pallas_call x8, Pallas kernels, per_device(): call(functools.partial(project_kernel, step - 1, start), [shape, shape],...  23.5 us
    ppermute x6, starting transfers between devices, per_device(): arrived = [lax.ppermute(total, 'head', RING) for total in totals]  16 us
    all_to_all x1, starting transfers between devices, per_device(): everyone = lax.all_to_all(chunks, 'seg', 0, 0, tiled=True)  11.9 us
    all_to_all x1, starting transfers between devices, per_device(): prefix = lax.all_to_all(mine, 'seg', 0, 0, tiled=True).reshape(4, 128, 128)  7.46 us
    unnamed x28, local copies, waits for them, and re-layouts  7.3 us
    ppermute x8, starting transfers between devices, per_device(): lax.ppermute(send, 'head', SWAP)  6.01 us
    all_to_all x1, waiting for transfers between devices, per_device(): everyone = lax.all_to_all(chunks, 'seg', 0, 0, tiled=True)  5.52 us
  transfers between devices with their start and end apart: 16, of which 9 were waited for; matrix products, arithmetic and copies ran while one was open for 1% of the time, Pallas kernels for 16%

profile of v3, /device:TPU:1, one launch (start us, length us, event | category | flops | bytes accessed | tf_op | source)
XLA Modules:
  0.0 148.6 jit_solution(3038208309911346410)
XLA Ops:
  0.0 3.3 %shard_map.73 = (f32[32,24,128]{2,1,0:T(8,128)}, f32[8,768]{1,0:T(8,128)}) custom-call(f32[4,768]{1,0:T(4,128)} %decay_hbm.1, bf16[768,512]{1,0:T(8,128)(2,1)} %k_hbm.5, bf16[768,512]{1,0:T(8,128)(2,1)} %v_hbm.5), custom_call_target="tpu_custom_call" | custom-call | flops 268435456 | bytes 1048576 | tf_op jit(solution)/shard_map/pallas_call | solution.py:197
  3.3 11.9 %all-to-all-start = ((f32[32,24,128]{2,1,0:T(8,128)}), f32[32,24,128]{2,1,0:T(8,128)S(1)}, u32[]{:S(2)}, u32[]{:S(2)}) async-start(f32[32,24,128]{2,1,0:T(8,128)} %get-tuple-element.36), calls=%async_computation | async-start | bytes 786432 | tf_op jit(solution)/shard_map/all_to_all | solution.py:204
  15.2 0.0 copy-start
  15.2 1.1 copy-done
  16.4 1.1 copy-done.2
  17.5 0.7 copy-done.6
  18.2 1.1 copy-done.9
  19.4 2.0 %shard_map.74.early_ref = f32[768,256]{1,0:T(8,128)S(1)} custom-call(bf16[768,512]{1,0:T(8,128)(2,1)S(1)} %copy-done.9, bf16[768,512]{1,0:T(8,128)(2,1)S(1)} %copy-done, bf16[768,512]{1,0:T(8,128)(2,1)S(1)} %copy-done.2, f32[8,768]{1,0:T(8,128)S(1)} %copy-done.6), custom_call_target="tpu_custom_call" | custom-call | flops 1073741824 | bytes 1048576 | tf_op jit(solution)/shard_map/pallas_call | solution.py:206
  21.3 0.0 copy-start.1
  21.4 5.5 %all-to-all-done.all_ref = f32[32,24,128]{2,1,0:T(8,128)S(1)} async-done(((f32[32,24,128]{2,1,0:T(8,128)}), f32[32,24,128]{2,1,0:T(8,128)S(1)}, u32[]{:S(2)}, u32[]{:S(2)}) %all-to-all-start) | async-done | bytes 393248 | tf_op jit(solution)/shard_map/all_to_all | solution.py:204
  26.9 1.4 shard_map.76
  28.3 7.5 %all-to-all-start.1 = ((f32[32,16,128]{2,1,0:T(8,128)}), f32[32,16,128]{2,1,0:T(8,128)S(1)}, u32[]{:S(2)}, u32[]{:S(2)}) async-start(f32[32,16,128]{2,1,0:T(8,128)} %shard_map.76), calls=%async_computation.1 | async-start | bytes 524288 | tf_op jit(solution)/shard_map/all_to_all | solution.py:211
  35.8 0.1 pad_add_fusion
  35.9 0.1 reshape.47.index_ref
  36.0 0.0 copy-start.10
  36.0 1.1 copy-done.10
  37.1 2.0 %shard_map.75 = (f32[768,256]{1,0:T(8,128)S(1)}, bf16[768,512]{1,0:T(8,128)(2,1)S(1)}) custom-call(bf16[768,512]{1,0:T(8,128)(2,1)S(1)} %copy-done.10, bf16[768,512]{1,0:T(8,128)(2,1)S(1)} %copy-done.1, bf16[768,512]{1,0:T(8,128)(2,1)S(1)} %copy-done.3, f32[8,768]{1,0:T(8,128)S(1)} %copy-done.7), custom_call_target="tpu_custom_call" | custom-call | flops 1073741824 | bytes 1048576 | tf_op jit(solution)/shard_map/pallas_call | solution.py:212
  39.1 0.0 copy-start.4
  39.1 0.9 copy-done.4
  40.0 5.5 %all-to-all-done.1 = f32[32,16,128]{2,1,0:T(8,128)S(1)} async-done(((f32[32,16,128]{2,1,0:T(8,128)}), f32[32,16,128]{2,1,0:T(8,128)S(1)}, u32[]{:S(2)}, u32[]{:S(2)}) %all-to-all-start.1) | async-done | bytes 262176 | tf_op jit(solution)/shard_map/all_to_all | solution.py:211
  45.4 1.1 copy-done.5
  46.6 1.3 shard_map.77
  47.9 0.0 slice-start
  47.9 3.3 %shard_map.80 = (f32[96,3200]{1,0:T(8,128)S(1)}, f32[96,3200]{1,0:T(8,128)S(1)}) custom-call(s32[8]{0:T(128)S(1)} %reshape.47.index_ref, bf16[8,96,512]{2,1,0:T(8,128)(2,1)S(1)} %get-tuple-element.43.features_ref, f32[8,96,128]{2,1,0:T(8,128)S(1)} %get-tuple-element.44.squares_ref, bf16[512,6144]{1,0:T(8,128)(2,1)} %w_hbm.15), custom_call_target="tpu_custom_call" | custom-call | flops 4194304 | bytes 16384 | tf_op jit(solution)/shard_map/pallas_call | solution.py:235
  51.2 0.0 slice-start.1
  51.2 3.7 %collective-permute-start.1 = (f32[96,3200]{1,0:T(8,128)S(1)}, f32[96,3200]{1,0:T(8,128)S(1)}, u32[]{:S(2)}, u32[]{:S(2)}) collective-permute-start(f32[96,3200]{1,0:T(8,128)S(1)} %get-tuple-element.49), channel_id=1, source_target_pairs={{0,1},{1,0},{2,3},{3,2},{4,5},{5,4},{6,7},{7,6},{8,9},{9,8},{10,11... | collective-permute-start | bytes 3686408 | tf_op jit(solution)/shard_map/ppermute | solution.py:244
  55.0 3.3 %shard_map.78 = (f32[96,3072]{1,0:T(8,128)S(1)}, f32[96,3072]{1,0:T(8,128)S(1)}) custom-call(s32[8]{0:T(128)S(1)} %reshape.47.index_ref, bf16[8,96,512]{2,1,0:T(8,128)(2,1)S(1)} %get-tuple-element.43.features_ref, f32[8,96,128]{2,1,0:T(8,128)S(1)} %get-tuple-element.44.squares_ref, bf16[512,6144]{1,0:T(8,128)(2,1)} %w_hbm.15), custom_call_target="tpu_custom_call" | custom-call | flops 4194304 | bytes 16384 | tf_op jit(solution)/shard_map/pallas_call | solution.py:235
  58.2 0.4 collective-permute-start
  58.6 2.5 %collective-permute-done.arrived_ref = f32[96,3072]{1,0:T(8,128)S(1)} collective-permute-done((f32[96,3072]{1,0:T(8,128)S(1)}, f32[96,3072]{1,0:T(8,128)S(1)}, u32[]{:S(2)}, u32[]{:S(2)}) %collective-permute-start) | collective-permute-done | bytes 1179680 | tf_op jit(solution)/shard_map/ppermute | solution.py:244
  61.2 1.1 shard_map.79
  62.3 1.1 shard_map.81
  63.5 2.8 %shard_map.87 = (f32[96,3200]{1,0:T(8,128)S(1)}, f32[96,3200]{1,0:T(8,128)S(1)}) custom-call(s32[8]{0:T(128)S(1)} %get-tuple-element.50.index_ref, bf16[8,96,512]{2,1,0:T(8,128)(2,1)S(1)} %get-tuple-element.43.features_ref, f32[8,96,128]{2,1,0:T(8,128)S(1)} %get-tuple-element.44.squares_ref, bf16[512,6144]{1,0:T(8,128)(2,1)S(1)} %bitcast.3), custom_call_target="tpu_custom_call" | custom-call | flops 4194304 | bytes 16384 | tf_op jit(solution)/shard_map/pallas_call | solution.py:235
  66.3 0.4 collective-permute-start.10
  66.8 2.7 %collective-permute-start.11 = (f32[96,3200]{1,0:T(8,128)S(1)}, f32[96,3200]{1,0:T(8,128)S(1)}, u32[]{:S(2)}, u32[]{:S(2)}) collective-permute-start(f32[96,3200]{1,0:T(8,128)S(1)} %get-tuple-element.64), channel_id=1, source_target_pairs={{0,2},{1,7},{2,4},{3,1},{4,6},{5,3},{6,0},{7,5},{8,10},{9,15},{10,... | collective-permute-start | bytes 3686408 | tf_op jit(solution)/shard_map/ppermute | solution.py:255
  69.5 0.5 collective-permute-start.5
  70.0 2.8 %shard_map.86 = (f32[96,3200]{1,0:T(8,128)S(1)}, f32[96,3200]{1,0:T(8,128)S(1)}) custom-call(s32[8]{0:T(128)S(1)} %get-tuple-element.50.index_ref, bf16[8,96,512]{2,1,0:T(8,128)(2,1)S(1)} %get-tuple-element.43.features_ref, f32[8,96,128]{2,1,0:T(8,128)S(1)} %get-tuple-element.44.squares_ref, bf16[512,6144]{1,0:T(8,128)(2,1)S(1)} %bitcast.3), custom_call_target="tpu_custom_call" | custom-call | flops 4194304 | bytes 16384 | tf_op jit(solution)/shard_map/pallas_call | solution.py:235
  72.8 0.3 collective-permute-start.9
  73.1 2.8 %shard_map.84 = (f32[96,3072]{1,0:T(8,128)S(1)}, f32[96,3072]{1,0:T(8,128)S(1)}) custom-call(s32[8]{0:T(128)S(1)} %get-tuple-element.50.index_ref, bf16[8,96,512]{2,1,0:T(8,128)(2,1)S(1)} %get-tuple-element.43.features_ref, f32[8,96,128]{2,1,0:T(8,128)S(1)} %get-tuple-element.44.squares_ref, bf16[512,6144]{1,0:T(8,128)(2,1)S(1)} %bitcast.3), custom_call_target="tpu_custom_call" | custom-call | flops 4194304 | bytes 16384 | tf_op jit(solution)/shard_map/pallas_call | solution.py:235
  75.9 0.4 collective-permute-start.4
  76.3 0.0 collective-permute-done.10
  76.3 6.9 %collective-permute-done.11 = f32[96,3200]{1,0:T(8,128)S(1)} collective-permute-done((f32[96,3200]{1,0:T(8,128)S(1)}, f32[96,3200]{1,0:T(8,128)S(1)}, u32[]{:S(2)}, u32[]{:S(2)}) %collective-permute-start.11) | collective-permute-done | bytes 1228832 | tf_op jit(solution)/shard_map/ppermute | solution.py:255
  83.2 0.2 add_add_fusion
  83.3 3.2 %collective-permute-start.12 = (f32[96,3200]{1,0:T(8,128)S(1)}, f32[96,3200]{1,0:T(8,128)S(1)}, u32[]{:S(2)}, u32[]{:S(2)}) collective-permute-start(f32[96,3200]{1,0:T(8,128)S(1)} %add_add_fusion), channel_id=1, source_target_pairs={{0,2},{1,7},{2,4},{3,1},{4,6},{5,3},{6,0},{7,5},{8,10},{9,15},{10,... | collective-permute-start | bytes 3686408 | tf_op jit(solution)/shard_map/ppermute | solution.py:255
  86.5 2.8 %shard_map.83 = (f32[96,3072]{1,0:T(8,128)S(1)}, f32[96,3072]{1,0:T(8,128)S(1)}) custom-call(s32[8]{0:T(128)S(1)} %get-tuple-element.50.index_ref, bf16[8,96,512]{2,1,0:T(8,128)(2,1)S(1)} %get-tuple-element.43.features_ref, f32[8,96,128]{2,1,0:T(8,128)S(1)} %get-tuple-element.44.squares_ref, bf16[512,6144]{1,0:T(8,128)(2,1)S(1)} %bitcast.3), custom_call_target="tpu_custom_call" | custom-call | flops 4194304 | bytes 16384 | tf_op jit(solution)/shard_map/pallas_call | solution.py:235
  89.4 0.1 collective-permute-start.3
  89.5 6.3 %collective-permute-done.5 = f32[96,3072]{1,0:T(8,128)S(1)} collective-permute-done((f32[96,3072]{1,0:T(8,128)S(1)}, f32[96,3072]{1,0:T(8,128)S(1)}, u32[]{:S(2)}, u32[]{:S(2)}) %collective-permute-start.5) | collective-permute-done | bytes 1179680 | tf_op jit(solution)/shard_map/ppermute | solution.py:255
  95.8 0.2 add_add_fusion.2
  96.0 3.2 %collective-permute-start.6 = (f32[96,3072]{1,0:T(8,128)S(1)}, f32[96,3072]{1,0:T(8,128)S(1)}, u32[]{:S(2)}, u32[]{:S(2)}) collective-permute-start(f32[96,3072]{1,0:T(8,128)S(1)} %add_add_fusion.2), channel_id=1, source_target_pairs={{0,2},{1,7},{2,4},{3,1},{4,6},{5,3},{6,0},{7,5},{8,10},{9,15},{10,... | collective-permute-start | bytes 3538952 | tf_op jit(solution)/shard_map/ppermute | solution.py:255
  99.2 2.8 %shard_map.85 = (f32[96,3200]{1,0:T(8,128)S(1)}, f32[96,3200]{1,0:T(8,128)S(1)}) custom-call(s32[8]{0:T(128)S(1)} %get-tuple-element.50.index_ref, bf16[8,96,512]{2,1,0:T(8,128)(2,1)S(1)} %get-tuple-element.43.features_ref, f32[8,96,128]{2,1,0:T(8,128)S(1)} %get-tuple-element.44.squares_ref, bf16[512,6144]{1,0:T(8,128)(2,1)S(1)} %bitcast.3), custom_call_target="tpu_custom_call" | custom-call | flops 4194304 | bytes 16384 | tf_op jit(solution)/shard_map/pallas_call | solution.py:235
  102.0 0.1 collective-permute-start.8
  102.1 2.8 %shard_map.82 = (f32[96,3072]{1,0:T(8,128)S(1)}, f32[96,3072]{1,0:T(8,128)S(1)}) custom-call(s32[8]{0:T(128)S(1)} %get-tuple-element.50.index_ref, bf16[8,96,512]{2,1,0:T(8,128)(2,1)S(1)} %get-tuple-element.43.features_ref, f32[8,96,128]{2,1,0:T(8,128)S(1)} %get-tuple-element.44.squares_ref, bf16[512,6144]{1,0:T(8,128)(2,1)S(1)} %bitcast.3), custom_call_target="tpu_custom_call" | custom-call | flops 4194304 | bytes 16384 | tf_op jit(solution)/shard_map/pallas_call | solution.py:235
  104.9 0.0 collective-permute-done.9
  104.9 0.6 collective-permute-start.2
  105.5 3.4 %collective-permute-done.12 = f32[96,3200]{1,0:T(8,128)S(1)} collective-permute-done((f32[96,3200]{1,0:T(8,128)S(1)}, f32[96,3200]{1,0:T(8,128)S(1)}, u32[]{:S(2)}, u32[]{:S(2)}) %collective-permute-start.12) | collective-permute-done | bytes 1228832 | tf_op jit(solution)/shard_map/ppermute | solution.py:255
  109.0 0.2 add_add_fusion.1
  109.2 3.2 %collective-permute-start.13 = (f32[96,3200]{1,0:T(8,128)S(1)}, f32[96,3200]{1,0:T(8,128)S(1)}, u32[]{:S(2)}, u32[]{:S(2)}) collective-permute-start(f32[96,3200]{1,0:T(8,128)S(1)} %add_add_fusion.1), channel_id=1, source_target_pairs={{0,2},{1,7},{2,4},{3,1},{4,6},{5,3},{6,0},{7,5},{8,10},{9,15},{10,... | collective-permute-start | bytes 3686408 | tf_op jit(solution)/shard_map/ppermute | solution.py:255
  112.3 9.3 %collective-permute-done.6 = f32[96,3072]{1,0:T(8,128)S(1)} collective-permute-done((f32[96,3072]{1,0:T(8,128)S(1)}, f32[96,3072]{1,0:T(8,128)S(1)}, u32[]{:S(2)}, u32[]{:S(2)}) %collective-permute-start.6) | collective-permute-done | bytes 1179680 | tf_op jit(solution)/shard_map/ppermute | solution.py:255
  121.6 0.2 add_add_fusion.3
  121.8 3.2 %collective-permute-start.7 = (f32[96,3072]{1,0:T(8,128)S(1)}, f32[96,3072]{1,0:T(8,128)S(1)}, u32[]{:S(2)}, u32[]{:S(2)}) collective-permute-start(f32[96,3072]{1,0:T(8,128)S(1)} %add_add_fusion.3), channel_id=1, source_target_pairs={{0,2},{1,7},{2,4},{3,1},{4,6},{5,3},{6,0},{7,5},{8,10},{9,15},{10,... | collective-permute-start | bytes 3538952 | tf_op jit(solution)/shard_map/ppermute | solution.py:255
  125.0 9.8 %collective-permute-done.13.refs_2_ = f32[96,3200]{1,0:T(8,128)S(1)} collective-permute-done((f32[96,3200]{1,0:T(8,128)S(1)}, f32[96,3200]{1,0:T(8,128)S(1)}, u32[]{:S(2)}, u32[]{:S(2)}) %collective-permute-start.13) | collective-permute-done | bytes 1228832 | tf_op jit(solution)/shard_map/ppermute | solution.py:255
  134.8 1.0 shard_map.88
  135.8 0.0 collective-permute-done.2.refs_1_
  135.8 11.6 %collective-permute-done.7.refs_2_ = f32[96,3072]{1,0:T(8,128)S(1)} collective-permute-done((f32[96,3072]{1,0:T(8,128)S(1)}, f32[96,3072]{1,0:T(8,128)S(1)}, u32[]{:S(2)}, u32[]{:S(2)}) %collective-permute-start.7) | collective-permute-done | bytes 1179680 | tf_op jit(solution)/shard_map/ppermute | solution.py:255
  147.4 1.0 shard_map.89
  (21 shorter events, 0.1 us)
Async XLA Ops:
  3.3 23.5 %all-to-all-start = ((f32[32,24,128]{2,1,0:T(8,128)}), f32[32,24,128]{2,1,0:T(8,128)S(1)}, u32[]{:S(2)}, u32[]{:S(2)}) async-start(f32[32,24,128]{2,1,0:T(8,128)} %get-tuple-element.36), calls=%async_computation | async-start | bytes 786432 | tf_op jit(solution)/shard_map/all_to_all | solution.py:204
  15.2 1.1 copy-start
  16.4 1.1 copy-start.2
  17.5 0.7 copy-start.6
  18.2 1.1 copy-start.9
  19.4 7.5 %copy-start.11 = (s32[32]{0:T(128)S(1)}, s32[32]{0:T(128)}, u32[]{:S(2)}) copy-start(s32[32]{0:T(128)} %parent_ref.1) | copy-start | bytes 388
  19.4 16.6 %copy-start.3 = (bf16[768,512]{1,0:T(8,128)(2,1)S(1)}, bf16[768,512]{1,0:T(8,128)(2,1)}, u32[]{:S(2)}) copy-start(bf16[768,512]{1,0:T(8,128)(2,1)} %v_hbm.5) | copy-start | bytes 2359300
  21.3 14.6 %copy-start.1 = (bf16[768,512]{1,0:T(8,128)(2,1)S(1)}, bf16[768,512]{1,0:T(8,128)(2,1)}, u32[]{:S(2)}) copy-start(bf16[768,512]{1,0:T(8,128)(2,1)} %k_hbm.5) | copy-start | bytes 2359300
  21.3 14.6 %copy-start.7 = (f32[8,768]{1,0:T(8,128)S(1)}, f32[8,768]{1,0:T(8,128)}, u32[]{:S(2)}) copy-start(f32[8,768]{1,0:T(8,128)} %get-tuple-element.38.running_ref) | copy-start | bytes 73732
  28.3 17.1 %all-to-all-start.1 = ((f32[32,16,128]{2,1,0:T(8,128)}), f32[32,16,128]{2,1,0:T(8,128)S(1)}, u32[]{:S(2)}, u32[]{:S(2)}) async-start(f32[32,16,128]{2,1,0:T(8,128)} %shard_map.76), calls=%async_computation.1 | async-start | bytes 524288 | tf_op jit(solution)/shard_map/all_to_all | solution.py:211
  36.0 1.1 copy-start.10
  37.1 8.3 %copy-start.8 = (f32[512]{0:T(512)S(1)}, f32[512]{0:T(512)}, u32[]{:S(2)}) copy-start(f32[512]{0:T(512)} %param.12) | copy-start | bytes 6148
  39.1 0.9 copy-start.4
  45.4 1.1 copy-start.5
  47.9 15.6 %slice-start = ((s8[6291456]{0:T(1024)(128)(4,1)}), s8[2097152]{0:T(1024)(128)(4,1)S(1)}, s32[]{:S(2)}) async-start(s8[6291456]{0:T(1024)(128)(4,1)} %bitcast.2), calls=%async_computation.2 | async-start | bytes 4194304
  51.2 12.3 %slice-start.1 = ((s8[6291456]{0:T(1024)(128)(4,1)}), s8[4194304]{0:T(1024)(128)(4,1)S(1)}, s32[]{:S(2)}) async-start(s8[6291456]{0:T(1024)(128)(4,1)} %bitcast.2), calls=%async_computation.3 | async-start | bytes 8388608
  51.2 11.1 %collective-permute-start.1 = (f32[96,3200]{1,0:T(8,128)S(1)}, f32[96,3200]{1,0:T(8,128)S(1)}, u32[]{:S(2)}, u32[]{:S(2)}) collective-permute-start(f32[96,3200]{1,0:T(8,128)S(1)} %get-tuple-element.49), channel_id=1, source_target_pairs={{0,1},{1,0},{2,3},{3,2},{4,5},{5,4},{6,7},{7,6},{8,9},{9,8},{10,11... | collective-permute-start | bytes 3686408 | tf_op jit(solution)/shard_map/ppermute | solution.py:244
  58.2 2.9 %collective-permute-start = (f32[96,3072]{1,0:T(8,128)S(1)}, f32[96,3072]{1,0:T(8,128)S(1)}, u32[]{:S(2)}, u32[]{:S(2)}) collective-permute-start(f32[96,3072]{1,0:T(8,128)S(1)} %get-tuple-element.46), channel_id=1, source_target_pairs={{0,1},{1,0},{2,3},{3,2},{4,5},{5,4},{6,7},{7,6},{8,9},{9,8},{10,11... | collective-permute-start | bytes 3538952 | tf_op jit(solution)/shard_map/ppermute | solution.py:244
  66.3 10.0 %collective-permute-start.10 = (f32[96,3200]{1,0:T(8,128)S(1)}, f32[96,3200]{1,0:T(8,128)S(1)}, u32[]{:S(2)}, u32[]{:S(2)}) collective-permute-start(f32[96,3200]{1,0:T(8,128)S(1)} %get-tuple-element.63), channel_id=1, source_target_pairs={{0,1},{1,0},{2,3},{3,2},{4,5},{5,4},{6,7},{7,6},{8,9},{9,8},{10,11... | collective-permute-start | bytes 3686408 | tf_op jit(solution)/shard_map/ppermute | solution.py:244
  66.8 16.4 %collective-permute-start.11 = (f32[96,3200]{1,0:T(8,128)S(1)}, f32[96,3200]{1,0:T(8,128)S(1)}, u32[]{:S(2)}, u32[]{:S(2)}) collective-permute-start(f32[96,3200]{1,0:T(8,128)S(1)} %get-tuple-element.64), channel_id=1, source_target_pairs={{0,2},{1,7},{2,4},{3,1},{4,6},{5,3},{6,0},{7,5},{8,10},{9,15},{10,... | collective-permute-start | bytes 3686408 | tf_op jit(solution)/shard_map/ppermute | solution.py:255
  69.5 26.3 %collective-permute-start.5 = (f32[96,3072]{1,0:T(8,128)S(1)}, f32[96,3072]{1,0:T(8,128)S(1)}, u32[]{:S(2)}, u32[]{:S(2)}) collective-permute-start(f32[96,3072]{1,0:T(8,128)S(1)} %get-tuple-element.57), channel_id=1, source_target_pairs={{0,2},{1,7},{2,4},{3,1},{4,6},{5,3},{6,0},{7,5},{8,10},{9,15},{10,... | collective-permute-start | bytes 3538952 | tf_op jit(solution)/shard_map/ppermute | solution.py:255
  72.8 32.2 %collective-permute-start.9 = (f32[96,3200]{1,0:T(8,128)S(1)}, f32[96,3200]{1,0:T(8,128)S(1)}, u32[]{:S(2)}, u32[]{:S(2)}) collective-permute-start(f32[96,3200]{1,0:T(8,128)S(1)} %get-tuple-element.61), channel_id=1, source_target_pairs={{0,1},{1,0},{2,3},{3,2},{4,5},{5,4},{6,7},{7,6},{8,9},{9,8},{10,11... | collective-permute-start | bytes 3686408 | tf_op jit(solution)/shard_map/ppermute | solution.py:244
  75.9 19.9 %collective-permute-start.4 = (f32[96,3072]{1,0:T(8,128)S(1)}, f32[96,3072]{1,0:T(8,128)S(1)}, u32[]{:S(2)}, u32[]{:S(2)}) collective-permute-start(f32[96,3072]{1,0:T(8,128)S(1)} %get-tuple-element.56), channel_id=1, source_target_pairs={{0,1},{1,0},{2,3},{3,2},{4,5},{5,4},{6,7},{7,6},{8,9},{9,8},{10,11... | collective-permute-start | bytes 3538952 | tf_op jit(solution)/shard_map/ppermute | solution.py:244
  83.3 25.6 %collective-permute-start.12 = (f32[96,3200]{1,0:T(8,128)S(1)}, f32[96,3200]{1,0:T(8,128)S(1)}, u32[]{:S(2)}, u32[]{:S(2)}) collective-permute-start(f32[96,3200]{1,0:T(8,128)S(1)} %add_add_fusion), channel_id=1, source_target_pairs={{0,2},{1,7},{2,4},{3,1},{4,6},{5,3},{6,0},{7,5},{8,10},{9,15},{10,... | collective-permute-start | bytes 3686408 | tf_op jit(solution)/shard_map/ppermute | solution.py:255
  89.4 23.0 %collective-permute-start.3 = (f32[96,3072]{1,0:T(8,128)S(1)}, f32[96,3072]{1,0:T(8,128)S(1)}, u32[]{:S(2)}, u32[]{:S(2)}) collective-permute-start(f32[96,3072]{1,0:T(8,128)S(1)} %get-tuple-element.54), channel_id=1, source_target_pairs={{0,1},{1,0},{2,3},{3,2},{4,5},{5,4},{6,7},{7,6},{8,9},{9,8},{10,11... | collective-permute-start | bytes 3538952 | tf_op jit(solution)/shard_map/ppermute | solution.py:244
  96.0 25.6 %collective-permute-start.6 = (f32[96,3072]{1,0:T(8,128)S(1)}, f32[96,3072]{1,0:T(8,128)S(1)}, u32[]{:S(2)}, u32[]{:S(2)}) collective-permute-start(f32[96,3072]{1,0:T(8,128)S(1)} %add_add_fusion.2), channel_id=1, source_target_pairs={{0,2},{1,7},{2,4},{3,1},{4,6},{5,3},{6,0},{7,5},{8,10},{9,15},{10,... | collective-permute-start | bytes 3538952 | tf_op jit(solution)/shard_map/ppermute | solution.py:255
  102.0 23.0 %collective-permute-start.8 = (f32[96,3200]{1,0:T(8,128)S(1)}, f32[96,3200]{1,0:T(8,128)S(1)}, u32[]{:S(2)}, u32[]{:S(2)}) collective-permute-start(f32[96,3200]{1,0:T(8,128)S(1)} %get-tuple-element.59), channel_id=1, source_target_pairs={{0,1},{1,0},{2,3},{3,2},{4,5},{5,4},{6,7},{7,6},{8,9},{9,8},{10,11... | collective-permute-start | bytes 3686408 | tf_op jit(solution)/shard_map/ppermute | solution.py:244
  104.9 30.9 %collective-permute-start.2 = (f32[96,3072]{1,0:T(8,128)S(1)}, f32[96,3072]{1,0:T(8,128)S(1)}, u32[]{:S(2)}, u32[]{:S(2)}) collective-permute-start(f32[96,3072]{1,0:T(8,128)S(1)} %get-tuple-element.52), channel_id=1, source_target_pairs={{0,1},{1,0},{2,3},{3,2},{4,5},{5,4},{6,7},{7,6},{8,9},{9,8},{10,11... | collective-permute-start | bytes 3538952 | tf_op jit(solution)/shard_map/ppermute | solution.py:244
  109.2 25.6 %collective-permute-start.13 = (f32[96,3200]{1,0:T(8,128)S(1)}, f32[96,3200]{1,0:T(8,128)S(1)}, u32[]{:S(2)}, u32[]{:S(2)}) collective-permute-start(f32[96,3200]{1,0:T(8,128)S(1)} %add_add_fusion.1), channel_id=1, source_target_pairs={{0,2},{1,7},{2,4},{3,1},{4,6},{5,3},{6,0},{7,5},{8,10},{9,15},{10,... | collective-permute-start | bytes 3686408 | tf_op jit(solution)/shard_map/ppermute | solution.py:255
  121.8 25.6 %collective-permute-start.7 = (f32[96,3072]{1,0:T(8,128)S(1)}, f32[96,3072]{1,0:T(8,128)S(1)}, u32[]{:S(2)}, u32[]{:S(2)}) collective-permute-start(f32[96,3072]{1,0:T(8,128)S(1)} %add_add_fusion.3), channel_id=1, source_target_pairs={{0,2},{1,7},{2,4},{3,1},{4,6},{5,3},{6,0},{7,5},{8,10},{9,15},{10,... | collective-permute-start | bytes 3538952 | tf_op jit(solution)/shard_map/ppermute | solution.py:255

commit v4 on v3

--- a/solution.py
+++ b/solution.py
@@ -67,8 +67,7 @@
         out_ref[s] = jnp.where(first >= 0, own + older, 0.0)
 
 
-def within_kernel(first, q_hbm, k_hbm, v_hbm, running_ref, out_ref, *rest):
-    q_ref, k_ref, v_ref, sems = rest[-4:]
+def within_kernel(first, q_hbm, k_hbm, v_hbm, running_ref, out_ref, q_ref, k_ref, v_ref, sems):
     copies = load(sems, (q_hbm, q_ref), (k_hbm, k_ref), (v_hbm, v_ref))
     length = q_ref.shape[0]
     size = 256
@@ -94,65 +93,65 @@
                 term = dot(weights, v_ref[inner, cols])
                 total = term if total is None else total + term
             out_ref[rows, cols.start - 128 * first : cols.stop - 128 * first] = total
-    if len(rest) > 4:
-        rest[0][...] = q_ref[...]
-
-
-def mix_kernel(q_ref, prefix_ref, early_ref, late_ref, running_ref, gain_ref, out_ref, squares_ref):
-    parts, share = out_ref.shape[:2]
+
+
+def mix_kernel(
+    index_ref, q_hbm, prefix_ref, early_ref, late_ref, running_ref, gain_ref, _,
+    out_ref, squares_out_ref,
+    features_ref, squares_ref, q_ref, sems,
+):
+    heads = [slice(128 * h, 128 * h + 128) for h in range(4)]
+    inputs = load(sems, *[(q_hbm.at[:, cols], q_ref.at[:, cols]) for cols in heads])
+    parts, share, width = out_ref.shape
     growth = jnp.exp(running_ref[...].T)
     squares = None
     for h in range(4):
         cols = slice(128 * h, 128 * h + 128)
         high, low = split(prefix_ref[h])
+        inputs[h].wait()
         q = q_ref[:, cols]
         inner = (early_ref if h < 2 else late_ref)[:, 128 * (h % 2) : 128 * (h % 2) + 128]
         attention = (dot(q, high) + dot(q, low)) * growth[:, h : h + 1] + inner
         term = jnp.sum(attention * attention, axis=1, keepdims=True)
         squares = term if squares is None else squares + term
-        out_ref[:, :, cols] = (attention * gain_ref[:, cols]).astype(BF16).reshape(parts, share, 128)
+        features_ref[:, :, cols] = (attention * gain_ref[:, cols]).astype(BF16).reshape(parts, share, 128)
     squares_ref[...] = jnp.broadcast_to(squares, (parts * share, 128)).reshape(parts, share, 128)
-
-
-def project_kernel(step, start, index_ref, features_ref, squares_ref, w_hbm, keep_ref, send_ref, w_ref, sems):
-    own, other = index_ref[2 * step], index_ref[2 * step + 1]
-    rows = features_ref.shape[1]
-    width = keep_ref.shape[1] - (128 if start == 0 else 0)
-    tiles = [slice(n, n + 512) for n in range(0, width, 512)]
-    copies = load(sems, *[(w_hbm.at[:, start + t.start : start + t.stop], w_ref.at[:, t]) for t in tiles])
-    left = jnp.concatenate([features_ref[own], features_ref[other]], axis=0)
-    for copy, t in zip(copies, tiles):
-        copy.wait()
-        both = dot(left, w_ref[:, t])
-        keep_ref[:, t] = both[:rows]
-        send_ref[:, t] = both[rows:]
+    for i in range(parts):
+        out_ref[i] = features_ref[index_ref[i]]
+        squares_out_ref[i] = squares_ref[index_ref[i]]
+
+
+def project_kernel(start, first, features_ref, squares_ref, w_ref, *refs):
+    keep_ref, send_ref = refs[-2:]
+    count, rows = keep_ref.shape[:2]
+    width = keep_ref.shape[2] - (128 if start == 0 else 0)
+    sides = [slice(first, first + count), slice(4 + first, 4 + first + count)]
+    left = jnp.concatenate([features_ref[side].reshape(count * rows, -1) for side in sides], axis=0)
+    for n in range(0, width, 512):
+        t = slice(n, n + 512)
+        both = dot(left, w_ref[:, start + n : start + n + 512])
+        keep_ref[:, :, t] = both[: count * rows].reshape(count, rows, 512)
+        send_ref[:, :, t] = both[count * rows :].reshape(count, rows, 512)
     if start == 0:
-        keep_ref[:, width:] = squares_ref[own]
-        send_ref[:, width:] = squares_ref[other]
-
-
-def add_kernel(index_ref, keep_ref, arrived_ref, total_ref, next_ref):
-    total_ref[...] = keep_ref[...] + arrived_ref[...]
-    for i in range(8):
-        next_ref[i] = index_ref[i]
+        keep_ref[:, :, width:] = squares_ref[sides[0]]
+        send_ref[:, :, width:] = squares_ref[sides[1]]
 
 
 def finish_kernel(start, features, *refs):
-    terms = refs[:3]
+    mine_ref, arrived_ref = refs[:2]
     if start == 0:
-        out_hbm, inverse_ref, buffer, sems = refs[3:]
-        width = terms[0].shape[1] - 128
-        squares = terms[0][:, width:] + terms[1][:, width:] + terms[2][:, width:]
-        inverse_ref[...] = 1.0 / jnp.sqrt(squares / features + 1e-06)
+        out_hbm, inverse_ref, buffer, sems = refs[2:]
+        width = mine_ref.shape[1] - 128
+        inverse_ref[...] = 1.0 / jnp.sqrt((mine_ref[:, width:] + arrived_ref[:, width:]) / features + 1e-06)
     else:
-        inverse_ref, _, out_hbm, buffer, sems = refs[3:]
-        width = terms[0].shape[1]
+        inverse_ref, _, out_hbm, buffer, sems = refs[2:]
+        width = mine_ref.shape[1]
     inverse = inverse_ref[:, 0:1]
-    tile = 1024
+    tile = 512
     copies = []
     for i, n in enumerate(range(0, width, tile)):
         cols = slice(n, n + tile)
-        buffer[:, cols] = ((terms[0][:, cols] + terms[1][:, cols] + terms[2][:, cols]) * inverse).astype(BF16)
+        buffer[:, cols] = ((mine_ref[:, cols] + arrived_ref[:, cols]) * inverse).astype(BF16)
         copy = pltpu.make_async_copy(buffer.at[:, cols], out_hbm.at[:, start + n : start + n + tile], sems.at[i])
         copy.start()
         copies.append(copy)
@@ -166,7 +165,7 @@
 HBM = pl.BlockSpec(memory_space=pltpu.HBM)
 
 
-def call(kernel, shapes, ins, outs=None, scratch=(), aliases=None, flops=2**28, moved=2**20, vmem=16 * 2**20):
+def call(kernel, shapes, ins, outs=None, scratch=(), aliases=None, flops=2**28, moved=2**20, vmem=6 * 2**20):
     return pl.pallas_call(
         kernel,
         out_shape=[jax.ShapeDtypeStruct(s, d) for s, d in shapes],
@@ -209,68 +208,55 @@
     everyone, early, running = lax.optimization_barrier((everyone, early, running))
     (mine,) = call(prefix_kernel, [((32, 16, 128), F32)], [SMEM, VMEM])(parent, everyone)
     prefix = lax.all_to_all(mine, "seg", 0, 0, tiled=True).reshape(4, 128, 128)
-    late, q_near = call(
-        functools.partial(within_kernel, 2),
-        [((length, width // 2), F32), (q.shape, BF16)],
-        [HBM] * 3 + [VMEM],
-        scratch=inputs,
-        flops=2**30,
+    (late,) = call(
+        functools.partial(within_kernel, 2), [((length, width // 2), F32)], [HBM] * 3 + [VMEM], scratch=inputs, flops=2**30
     )(q, k, v, running)
     me = lax.axis_index("head")
     y, core = me >> 1, me & 1
     way = (1 - 2 * core) * jnp.arange(1, 5, dtype=jnp.int32)
-    blocks = jnp.stack([((y - way) & 3) * 2 + core, ((y + way) & 3) * 2 + 1 - core], axis=1).reshape(8)
+    blocks = jnp.concatenate([((y - way) & 3) * 2 + core, ((y + way) & 3) * 2 + 1 - core])
     share = length // 8
-    features, squares = call(mix_kernel, [((8, share, width), BF16), ((8, share, 128), F32)], [VMEM] * 6)(
-        q_near, prefix, early, late, running, gain.reshape(1, width)
-    )
-    chunks = 2
-    part = w.shape[1] // chunks
-    arrived = [None] * chunks
-    for step in range(1, 5):
-        terms = []
-        for chunk in range(chunks):
-            start = chunk * part
-            shape = ((share, part + (128 if chunk == 0 else 0)), F32)
-            keep, send = call(
-                functools.partial(project_kernel, step - 1, start),
-                [shape, shape],
-                [SMEM, VMEM, VMEM, HBM],
-                scratch=[pltpu.VMEM((width, part), BF16), dma((part // 512,))],
-                flops=2**22,
-                moved=2**14,
-                vmem=(50 if step == 1 else 16) * 2**20,
-            )(blocks, features, squares, w)
-            terms.append([keep, lax.ppermute(send, "head", SWAP)] + ([arrived[chunk]] if step > 1 else []))
-        if step < 4:
-            totals = [None] * chunks
-            for chunk in reversed(range(chunks)):
-                t = terms[chunk]
-                if step == 1:
-                    totals[chunk], blocks = call(
-                        add_kernel, [(t[0].shape, F32), ((8,), jnp.int32)], [SMEM, VMEM, VMEM], outs=[VMEM, SMEM], flops=2**20, moved=2**14
-                    )(blocks, *t)
-                else:
-                    totals[chunk] = sum(t[1:], t[0])
+    starts = [0, 2048, 4096]
+    widths = [2048, 2048, 2048]
+
+    features, squares = call(
+        mix_kernel,
+        [((8, share, width), BF16), ((8, share, 128), F32)],
+        [SMEM, HBM, VMEM, VMEM, VMEM, VMEM, VMEM, HBM],
+        scratch=[pltpu.VMEM((8, share, width), BF16), pltpu.VMEM((8, share, 128), F32), pltpu.VMEM(q.shape, BF16)]
+        + [dma((4,))],
+        vmem=50 * 2**20,
+    )(blocks, q, prefix, early, late, running, gain.reshape(1, width), w)
+
+    def project(start, size, first, after):
+        return call(
+            functools.partial(project_kernel, start, first),
+            [((1, share, size + (128 if start == 0 else 0)), F32)] * 2,
+            [VMEM, VMEM, VMEM] + [ANY] * len(after),
+
+        )(features, squares, w, *after)
+
+    before, arrived = [], []
+    for step in range(4):
+        totals = []
+        for i, (start, size) in enumerate(zip(starts, widths)):
+            keep, send = project(start, size, step, before if step == 1 else before[i : i + 1] if step > 1 else [])
+            totals.append(keep[0] + lax.ppermute(send[0], "head", SWAP) + (arrived[i] if step in (1, 2) else 0.0))
+        if step < 3:
+            before = totals if step == 0 else arrived
             arrived = [lax.ppermute(total, "head", RING) for total in totals]
+    total_features = width * lax.axis_size("head")
     out = ((share, w.shape[1]), BF16)
-    scratch = [pltpu.VMEM((share, part), BF16), dma((part // 1024,))]
-    total_features = width * lax.axis_size("head")
-    half, inverse = call(
-        functools.partial(finish_kernel, 0, total_features),
-        [out, ((share, 128), F32)],
-        [VMEM] * 3,
-        outs=[ANY, VMEM],
-        scratch=scratch,
-    )(*terms[0])
-    (mixed,) = call(
-        functools.partial(finish_kernel, part, total_features),
-        [out],
-        [VMEM] * 4 + [ANY],
-        outs=[ANY],
-        scratch=scratch,
-        aliases={4: 0},
-    )(*terms[1], inverse, half)
+    mixed = None
+    for start, size, own, got in zip(starts, widths, totals, arrived):
+        buffers = [pltpu.VMEM((share, size), BF16), dma((size // 512,))]
+        kernel = functools.partial(finish_kernel, start, total_features)
+        if start == 0:
+            mixed, inverse = call(kernel, [out, ((share, 128), F32)], [VMEM] * 2, outs=[ANY, VMEM], scratch=buffers)(own, got)
+        else:
+            (mixed,) = call(kernel, [out], [VMEM] * 3 + [ANY], outs=[ANY], scratch=buffers, aliases={3: 0})(
+                own, got, inverse, mixed
+            )
     return mixed
 
 

time: 149 us -> 141 us (0.946)
  Pallas kernels: 37.9 us -> 21 us
  starting transfers between devices: 41.3 us -> 48.9 us
  local copies, waits for them, and re-layouts: 7.39 us -> 10.5 us
  waiting for transfers between devices: 60.8 us -> 58.1 us
    pallas_call x14 -> x17, Pallas kernels: 31.1 us -> 14.2 us  [the longest x12 7.01 us: project(): call(functools.partial(project_kernel, start, first), [((1, share, size +...]
    ppermute x8 -> x12, starting transfers between devices: 6.01 us -> 11.2 us  [per_device(): lax.ppermute(send[0], 'head', SWAP)]
    unnamed x28 -> x32, local copies, waits for them, and re-layouts: 7.3 us -> 10.5 us
    ppermute x6 -> x9, starting transfers between devices: 16 us -> 18.4 us  [per_device(): arrived = [lax.ppermute(total, 'head', RING) for total in totals]]
    ppermute x6 -> x9, waiting for transfers between devices: 47.3 us -> 46.8 us  [per_device(): arrived = [lax.ppermute(total, 'head', RING) for total in totals]]
  transfers between devices with their start and end apart: 16 -> 23, of which waited for: 9 -> 11; matrix products, arithmetic and copies ran while one was open for 1% -> 1% of each run, Pallas kernels for 16% -> 9%
where the time goes in v4:
time: 141 us; the launch traced here: 140 us
  waiting for transfers between devices  58.1 us (41%)
  starting transfers between devices  48.9 us (35%)
  Pallas kernels  21 us (15%)
  local copies, waits for them, and re-layouts  10.5 us (7%)
    ppermute x9, waiting for transfers between devices, per_device(): arrived = [lax.ppermute(total, 'head', RING) for total in totals]  46.8 us
    ppermute x9, starting transfers between devices, per_device(): arrived = [lax.ppermute(total, 'head', RING) for total in totals]  18.4 us
    all_to_all x1, starting transfers between devices, per_device(): everyone = lax.all_to_all(chunks, 'seg', 0, 0, tiled=True)  11.9 us
    ppermute x12, starting transfers between devices, per_device(): lax.ppermute(send[0], 'head', SWAP)  11.2 us
    unnamed x32, local copies, waits for them, and re-layouts  10.5 us
    all_to_all x1, starting transfers between devices, per_device(): prefix = lax.all_to_all(mine, 'seg', 0, 0, tiled=True).reshape(4, 128, 128)  7.46 us
    pallas_call x12, Pallas kernels, project(): call(functools.partial(project_kernel, start, first), [((1, share, size +...  7.01 us
    all_to_all x1, waiting for transfers between devices, per_device(): everyone = lax.all_to_all(chunks, 'seg', 0, 0, tiled=True)  4.65 us
  transfers between devices with their start and end apart: 23, of which 11 were waited for; matrix products, arithmetic and copies ran while one was open for 1% of the time, Pallas kernels for 9%

profile of v4, /device:TPU:1, one launch (start us, length us, event | category | flops | bytes accessed | tf_op | source)
XLA Modules:
  0.0 140.3 jit_solution(17230737979450716381)
XLA Ops:
  0.0 3.3 %shard_map.73 = (f32[32,24,128]{2,1,0:T(8,128)}, f32[8,768]{1,0:T(8,128)}) custom-call(f32[4,768]{1,0:T(4,128)} %decay_hbm.1, bf16[768,512]{1,0:T(8,128)(2,1)} %k_hbm.5, bf16[768,512]{1,0:T(8,128)(2,1)} %v_hbm.5), custom_call_target="tpu_custom_call" | custom-call | flops 268435456 | bytes 1048576 | tf_op jit(solution)/shard_map/pallas_call | solution.py:196
  3.4 11.9 %all-to-all-start = ((f32[32,24,128]{2,1,0:T(8,128)}), f32[32,24,128]{2,1,0:T(8,128)S(1)}, u32[]{:S(2)}, u32[]{:S(2)}) async-start(f32[32,24,128]{2,1,0:T(8,128)} %get-tuple-element.38), calls=%async_computation | async-start | bytes 786432 | tf_op jit(solution)/shard_map/all_to_all | solution.py:203
  15.2 1.1 copy-done
  16.4 1.1 copy-done.6
  17.5 1.1 copy-done.8
  18.6 0.7 copy-done.10
  19.4 2.0 %shard_map.74.early_ref = f32[768,256]{1,0:T(8,128)S(1)} custom-call(bf16[768,512]{1,0:T(8,128)(2,1)S(1)} %copy-done, bf16[768,512]{1,0:T(8,128)(2,1)S(1)} %copy-done.6, bf16[768,512]{1,0:T(8,128)(2,1)S(1)} %copy-done.8, f32[8,768]{1,0:T(8,128)S(1)} %copy-done.10), custom_call_target="tpu_custom_call" | custom-call | flops 1073741824 | bytes 1048576 | tf_op jit(solution)/shard_map/pallas_call | solution.py:205
  21.4 0.9 copy-done.2
  22.2 4.7 %all-to-all-done.all_ref = f32[32,24,128]{2,1,0:T(8,128)S(1)} async-done(((f32[32,24,128]{2,1,0:T(8,128)}), f32[32,24,128]{2,1,0:T(8,128)S(1)}, u32[]{:S(2)}, u32[]{:S(2)}) %all-to-all-start) | async-done | bytes 393248 | tf_op jit(solution)/shard_map/all_to_all | solution.py:203
  26.9 1.4 %shard_map.75 = f32[32,16,128]{2,1,0:T(8,128)} custom-call(s32[32]{0:T(128)S(1)} %copy-done.13, f32[32,24,128]{2,1,0:T(8,128)S(1)} %all-to-all-done.all_ref), custom_call_target="tpu_custom_call" | custom-call | flops 268435456 | bytes 1048576 | tf_op jit(solution)/shard_map/pallas_call | solution.py:209
  28.3 7.5 %all-to-all-start.1 = ((f32[32,16,128]{2,1,0:T(8,128)}), f32[32,16,128]{2,1,0:T(8,128)S(1)}, u32[]{:S(2)}, u32[]{:S(2)}) async-start(f32[32,16,128]{2,1,0:T(8,128)} %shard_map.75), calls=%async_computation.1 | async-start | bytes 524288 | tf_op jit(solution)/shard_map/all_to_all | solution.py:210
  35.9 1.1 copy-done.7
  37.0 1.1 copy-done.9
  38.2 2.0 %shard_map.76.late_ref = f32[768,256]{1,0:T(8,128)S(1)} custom-call(bf16[768,512]{1,0:T(8,128)(2,1)S(1)} %copy-done.1, bf16[768,512]{1,0:T(8,128)(2,1)S(1)} %copy-done.7, bf16[768,512]{1,0:T(8,128)(2,1)S(1)} %copy-done.9, f32[8,768]{1,0:T(8,128)S(1)} %copy-done.11), custom_call_target="tpu_custom_call" | custom-call | flops 1073741824 | bytes 1048576 | tf_op jit(solution)/shard_map/pallas_call | solution.py:211
  40.1 0.9 copy-done.4
  41.1 4.4 %all-to-all-done.1 = f32[32,16,128]{2,1,0:T(8,128)S(1)} async-done(((f32[32,16,128]{2,1,0:T(8,128)}), f32[32,16,128]{2,1,0:T(8,128)S(1)}, u32[]{:S(2)}, u32[]{:S(2)}) %all-to-all-start.1) | async-done | bytes 262176 | tf_op jit(solution)/shard_map/all_to_all | solution.py:210
  45.4 1.1 copy-done.3
  46.6 1.1 copy-done.5
  47.7 2.6 %shard_map.77 = (bf16[8,96,512]{2,1,0:T(8,128)(2,1)S(1)}, f32[8,96,128]{2,1,0:T(8,128)S(1)}) custom-call(s32[8]{0:T(128)S(1)} %pad_add_fusion.index_ref, bf16[768,512]{1,0:T(8,128)(2,1)S(1)} %copy-done.1, f32[4,128,128]{2,1,0:T(8,128)S(1)} %bitcast.52, f32[768,256]{1,0:T(8,128)S(1)} %copy-done.3, f32[768,256]{1,0:T(8,128)S(1)} %copy-done.5, ...), custom_call_target="tpu_custom_call" | custom-call | flops 268435456 | bytes 1048576 | tf_op jit(solution)/shard_map/pallas_call | solution.py:222
  50.3 0.6 shard_map.79
  50.9 3.7 %collective-permute-start.1 = (f32[96,2048]{1,0:T(8,128)S(1)}, f32[96,2048]{1,0:T(8,128)S(1)}, u32[]{:S(2)}, u32[]{:S(2)}) collective-permute-start(f32[96,2048]{1,0:T(8,128)S(1)} %bitcast.65), channel_id=1, source_target_pairs={{0,1},{1,0},{2,3},{3,2},{4,5},{5,4},{6,7},{7,6},{8,9},{9,8},{10,11... | collective-permute-start | bytes 2359304 | tf_op jit(solution)/shard_map/ppermute | solution.py:244
  54.6 0.6 shard_map.80
  55.2 0.1 collective-permute-start.2
  55.3 0.6 shard_map.78
  55.9 0.6 collective-permute-start
  56.6 2.8 %collective-permute-start.16 = (f32[96,2048]{1,0:T(8,128)S(1)}, f32[96,2048]{1,0:T(8,128)S(1)}, u32[]{:S(2)}, u32[]{:S(2)}) collective-permute-start(f32[96,2048]{1,0:T(8,128)S(1)} %bitcast_add_fusion.11.refs_1_), channel_id=1, source_target_pairs={{0,2},{1,7},{2,4},{3,1},{4,6},{5,3},{6,0},{7,5},{8,10},{9,15},{10,... | collective-permute-start | bytes 2359304 | tf_op jit(solution)/shard_map/ppermute | solution.py:247
  59.6 1.2 collective-permute-start.4
  60.9 0.6 shard_map.88
  61.5 0.6 shard_map.81
  62.1 0.6 collective-permute-start.3
  62.7 0.8 collective-permute-start.10
  63.6 0.6 shard_map.84
  64.2 4.2 %collective-permute-done.16.refs_0_ = f32[96,2048]{1,0:T(8,128)S(1)} collective-permute-done((f32[96,2048]{1,0:T(8,128)S(1)}, f32[96,2048]{1,0:T(8,128)S(1)}, u32[]{:S(2)}, u32[]{:S(2)}) %collective-permute-start.16) | collective-permute-done | bytes 786464 | tf_op jit(solution)/shard_map/ppermute | solution.py:247
  68.4 1.9 %collective-permute-start.9 = (f32[96,2176]{1,0:T(8,128)S(1)}, f32[96,2176]{1,0:T(8,128)S(1)}, u32[]{:S(2)}, u32[]{:S(2)}) collective-permute-start(f32[96,2176]{1,0:T(8,128)S(1)} %bitcast.55), channel_id=1, source_target_pairs={{0,1},{1,0},{2,3},{3,2},{4,5},{5,4},{6,7},{7,6},{8,9},{9,8},{10,11... | collective-permute-start | bytes 2506760 | tf_op jit(solution)/shard_map/ppermute | solution.py:244
  70.3 0.6 shard_map.90
  70.9 5.9 %collective-permute-done.4.refs_0_ = f32[96,2048]{1,0:T(8,128)S(1)} collective-permute-done((f32[96,2048]{1,0:T(8,128)S(1)}, f32[96,2048]{1,0:T(8,128)S(1)}, u32[]{:S(2)}, u32[]{:S(2)}) %collective-permute-start.4) | collective-permute-done | bytes 786464 | tf_op jit(solution)/shard_map/ppermute | solution.py:247
  76.8 1.9 %collective-permute-start.19 = (f32[96,2048]{1,0:T(8,128)S(1)}, f32[96,2048]{1,0:T(8,128)S(1)}, u32[]{:S(2)}, u32[]{:S(2)}) collective-permute-start(f32[96,2048]{1,0:T(8,128)S(1)} %bitcast.59), channel_id=1, source_target_pairs={{0,1},{1,0},{2,3},{3,2},{4,5},{5,4},{6,7},{7,6},{8,9},{9,8},{10,11... | collective-permute-start | bytes 2359304 | tf_op jit(solution)/shard_map/ppermute | solution.py:244
  78.7 0.6 shard_map.83
  79.4 0.1 fusion.3
  79.6 1.8 %collective-permute-start.17 = (f32[96,2048]{1,0:T(8,128)S(1)}, f32[96,2048]{1,0:T(8,128)S(1)}, u32[]{:S(2)}, u32[]{:S(2)}) collective-permute-start(f32[96,2048]{1,0:T(8,128)S(1)} %fusion.3), channel_id=1, source_target_pairs={{0,2},{1,7},{2,4},{3,1},{4,6},{5,3},{6,0},{7,5},{8,10},{9,15},{10,... | collective-permute-start | bytes 2359304 | tf_op jit(solution)/shard_map/ppermute | solution.py:247
  81.3 0.1 fusion.5
  81.5 0.4 collective-permute-start.5
  81.8 3.9 %collective-permute-done.10.refs_0_ = f32[96,2176]{1,0:T(8,128)S(1)} collective-permute-done((f32[96,2176]{1,0:T(8,128)S(1)}, f32[96,2176]{1,0:T(8,128)S(1)}, u32[]{:S(2)}, u32[]{:S(2)}) %collective-permute-start.10) | collective-permute-done | bytes 835616 | tf_op jit(solution)/shard_map/ppermute | solution.py:247
  85.8 0.1 fusion.1
  85.9 3.2 %collective-permute-start.11 = (f32[96,2176]{1,0:T(8,128)S(1)}, f32[96,2176]{1,0:T(8,128)S(1)}, u32[]{:S(2)}, u32[]{:S(2)}) collective-permute-start(f32[96,2176]{1,0:T(8,128)S(1)} %fusion.1), channel_id=1, source_target_pairs={{0,2},{1,7},{2,4},{3,1},{4,6},{5,3},{6,0},{7,5},{8,10},{9,15},{10,... | collective-permute-start | bytes 2506760 | tf_op jit(solution)/shard_map/ppermute | solution.py:247
  89.1 0.6 shard_map.86
  89.8 4.4 %collective-permute-done.17.refs_0_ = f32[96,2048]{1,0:T(8,128)S(1)} collective-permute-done((f32[96,2048]{1,0:T(8,128)S(1)}, f32[96,2048]{1,0:T(8,128)S(1)}, u32[]{:S(2)}, u32[]{:S(2)}) %collective-permute-start.17) | collective-permute-done | bytes 786464 | tf_op jit(solution)/shard_map/ppermute | solution.py:247
  94.2 0.1 fusion.2
  94.3 3.2 %collective-permute-start.20 = (f32[96,2048]{1,0:T(8,128)S(1)}, f32[96,2048]{1,0:T(8,128)S(1)}, u32[]{:S(2)}, u32[]{:S(2)}) collective-permute-start(f32[96,2048]{1,0:T(8,128)S(1)} %fusion.2), channel_id=1, source_target_pairs={{0,2},{1,7},{2,4},{3,1},{4,6},{5,3},{6,0},{7,5},{8,10},{9,15},{10,... | collective-permute-start | bytes 2359304 | tf_op jit(solution)/shard_map/ppermute | solution.py:247
  97.5 0.6 shard_map.89
  98.2 4.4 %collective-permute-done.5.refs_0_ = f32[96,2048]{1,0:T(8,128)S(1)} collective-permute-done((f32[96,2048]{1,0:T(8,128)S(1)}, f32[96,2048]{1,0:T(8,128)S(1)}, u32[]{:S(2)}, u32[]{:S(2)}) %collective-permute-start.5) | collective-permute-done | bytes 786464 | tf_op jit(solution)/shard_map/ppermute | solution.py:247
  102.6 0.1 fusion.4
  102.8 3.4 %collective-permute-start.8 = (f32[96,2048]{1,0:T(8,128)S(1)}, f32[96,2048]{1,0:T(8,128)S(1)}, u32[]{:S(2)}, u32[]{:S(2)}) collective-permute-start(f32[96,2048]{1,0:T(8,128)S(1)} %fusion.4), channel_id=1, source_target_pairs={{0,2},{1,7},{2,4},{3,1},{4,6},{5,3},{6,0},{7,5},{8,10},{9,15},{10,... | collective-permute-start | bytes 2359304 | tf_op jit(solution)/shard_map/ppermute | solution.py:247
  106.2 0.6 shard_map.82
  106.8 4.8 %collective-permute-done.11.refs_0_ = f32[96,2176]{1,0:T(8,128)S(1)} collective-permute-done((f32[96,2176]{1,0:T(8,128)S(1)}, f32[96,2176]{1,0:T(8,128)S(1)}, u32[]{:S(2)}, u32[]{:S(2)}) %collective-permute-start.11) | collective-permute-done | bytes 835616 | tf_op jit(solution)/shard_map/ppermute | solution.py:247
  111.6 1.9 %collective-permute-start.6 = (f32[96,2048]{1,0:T(8,128)S(1)}, f32[96,2048]{1,0:T(8,128)S(1)}, u32[]{:S(2)}, u32[]{:S(2)}) collective-permute-start(f32[96,2048]{1,0:T(8,128)S(1)} %bitcast.63), channel_id=1, source_target_pairs={{0,1},{1,0},{2,3},{3,2},{4,5},{5,4},{6,7},{7,6},{8,9},{9,8},{10,11... | collective-permute-start | bytes 2359304 | tf_op jit(solution)/shard_map/ppermute | solution.py:244
  113.5 0.1 fusion
  113.6 1.6 %collective-permute-start.14 = (f32[96,2176]{1,0:T(8,128)S(1)}, f32[96,2176]{1,0:T(8,128)S(1)}, u32[]{:S(2)}, u32[]{:S(2)}) collective-permute-start(f32[96,2176]{1,0:T(8,128)S(1)} %fusion), channel_id=1, source_target_pairs={{0,2},{1,7},{2,4},{3,1},{4,6},{5,3},{6,0},{7,5},{8,10},{9,15},{10,... | collective-permute-start | bytes 2506760 | tf_op jit(solution)/shard_map/ppermute | solution.py:247
  115.2 0.6 shard_map.85
  116.1 2.1 %collective-permute-done.12 = f32[96,2176]{1,0:T(8,128)S(1)} collective-permute-done((f32[96,2176]{1,0:T(8,128)S(1)}, f32[96,2176]{1,0:T(8,128)S(1)}, u32[]{:S(2)}, u32[]{:S(2)}) %collective-permute-start.12) | collective-permute-done | bytes 835616 | tf_op jit(solution)/shard_map/ppermute | solution.py:244
  118.3 19.0 %collective-permute-done.14.refs_1_ = f32[96,2176]{1,0:T(8,128)S(1)} collective-permute-done((f32[96,2176]{1,0:T(8,128)S(1)}, f32[96,2176]{1,0:T(8,128)S(1)}, u32[]{:S(2)}, u32[]{:S(2)}) %collective-permute-start.14) | collective-permute-done | bytes 835616 | tf_op jit(solution)/shard_map/ppermute | solution.py:247
  137.4 0.9 shard_map.87
  138.3 0.9 shard_map.91.refs_3_
  139.2 0.9 shard_map.92
  (49 shorter events, 1.2 us)
Async XLA Ops:
  3.4 23.5 %all-to-all-start = ((f32[32,24,128]{2,1,0:T(8,128)}), f32[32,24,128]{2,1,0:T(8,128)S(1)}, u32[]{:S(2)}, u32[]{:S(2)}) async-start(f32[32,24,128]{2,1,0:T(8,128)} %get-tuple-element.38), calls=%async_computation | async-start | bytes 786432 | tf_op jit(solution)/shard_map/all_to_all | solution.py:203
  15.2 1.1 copy-start
  16.4 1.1 copy-start.6
  17.5 1.1 copy-start.8
  18.6 0.7 copy-start.10
  19.4 7.5 %copy-start.13 = (s32[32]{0:T(128)S(1)}, s32[32]{0:T(128)}, u32[]{:S(2)}) copy-start(s32[32]{0:T(128)} %parent_ref.1) | copy-start | bytes 388
  21.3 0.9 copy-start.2
  22.2 13.7 %copy-start.1 = (bf16[768,512]{1,0:T(8,128)(2,1)S(1)}, bf16[768,512]{1,0:T(8,128)(2,1)}, u32[]{:S(2)}) copy-start(bf16[768,512]{1,0:T(8,128)(2,1)} %q_hbm.5) | copy-start | bytes 2359300
  22.2 13.7 %copy-start.11 = (f32[8,768]{1,0:T(8,128)S(1)}, f32[8,768]{1,0:T(8,128)}, u32[]{:S(2)}) copy-start(f32[8,768]{1,0:T(8,128)} %get-tuple-element.42.running_ref) | copy-start | bytes 73732
  28.3 17.1 %all-to-all-start.1 = ((f32[32,16,128]{2,1,0:T(8,128)}), f32[32,16,128]{2,1,0:T(8,128)S(1)}, u32[]{:S(2)}, u32[]{:S(2)}) async-start(f32[32,16,128]{2,1,0:T(8,128)} %shard_map.75), calls=%async_computation.1 | async-start | bytes 524288 | tf_op jit(solution)/shard_map/all_to_all | solution.py:210
  35.9 1.1 copy-start.7
  37.0 1.1 copy-start.9
  38.2 7.3 %copy-start.12 = (f32[512]{0:T(512)S(1)}, f32[512]{0:T(512)}, u32[]{:S(2)}) copy-start(f32[512]{0:T(512)} %param.12) | copy-start | bytes 6148
  38.2 12.2 %slice-start = ((s8[6291456]{0:T(1024)(128)(4,1)}), s8[2097152]{0:T(1024)(128)(4,1)S(1)}, s32[]{:S(2)}) async-start(s8[6291456]{0:T(1024)(128)(4,1)} %bitcast.50), calls=%async_computation.2 | async-start | bytes 4194304
  40.1 0.9 copy-start.4
  45.4 1.1 copy-start.3
  46.6 1.1 copy-start.5
  47.7 2.6 %slice-start.1 = ((s8[6291456]{0:T(1024)(128)(4,1)}), s8[4194304]{0:T(1024)(128)(4,1)S(1)}, s32[]{:S(2)}) async-start(s8[6291456]{0:T(1024)(128)(4,1)} %bitcast.50), calls=%async_computation.3 | async-start | bytes 8388608
  50.9 5.6 %collective-permute-start.1 = (f32[96,2048]{1,0:T(8,128)S(1)}, f32[96,2048]{1,0:T(8,128)S(1)}, u32[]{:S(2)}, u32[]{:S(2)}) collective-permute-start(f32[96,2048]{1,0:T(8,128)S(1)} %bitcast.65), channel_id=1, source_target_pairs={{0,1},{1,0},{2,3},{3,2},{4,5},{5,4},{6,7},{7,6},{8,9},{9,8},{10,11... | collective-permute-start | bytes 2359304 | tf_op jit(solution)/shard_map/ppermute | solution.py:244
  55.2 4.2 %collective-permute-start.2 = (f32[96,2048]{1,0:T(8,128)S(1)}, f32[96,2048]{1,0:T(8,128)S(1)}, u32[]{:S(2)}, u32[]{:S(2)}) collective-permute-start(f32[96,2048]{1,0:T(8,128)S(1)} %bitcast.64), channel_id=1, source_target_pairs={{0,1},{1,0},{2,3},{3,2},{4,5},{5,4},{6,7},{7,6},{8,9},{9,8},{10,11... | collective-permute-start | bytes 2359304 | tf_op jit(solution)/shard_map/ppermute | solution.py:244
  55.9 4.8 %collective-permute-start = (f32[96,2176]{1,0:T(8,128)S(1)}, f32[96,2176]{1,0:T(8,128)S(1)}, u32[]{:S(2)}, u32[]{:S(2)}) collective-permute-start(f32[96,2176]{1,0:T(8,128)S(1)} %bitcast.56), channel_id=1, source_target_pairs={{0,1},{1,0},{2,3},{3,2},{4,5},{5,4},{6,7},{7,6},{8,9},{9,8},{10,11... | collective-permute-start | bytes 2506760 | tf_op jit(solution)/shard_map/ppermute | solution.py:244
  56.6 11.7 %collective-permute-start.16 = (f32[96,2048]{1,0:T(8,128)S(1)}, f32[96,2048]{1,0:T(8,128)S(1)}, u32[]{:S(2)}, u32[]{:S(2)}) collective-permute-start(f32[96,2048]{1,0:T(8,128)S(1)} %bitcast_add_fusion.11.refs_1_), channel_id=1, source_target_pairs={{0,2},{1,7},{2,4},{3,1},{4,6},{5,3},{6,0},{7,5},{8,10},{9,15},{10,... | collective-permute-start | bytes 2359304 | tf_op jit(solution)/shard_map/ppermute | solution.py:247
  59.6 17.3 %collective-permute-start.4 = (f32[96,2048]{1,0:T(8,128)S(1)}, f32[96,2048]{1,0:T(8,128)S(1)}, u32[]{:S(2)}, u32[]{:S(2)}) collective-permute-start(f32[96,2048]{1,0:T(8,128)S(1)} %bitcast_add_fusion.10.refs_2_), channel_id=1, source_target_pairs={{0,2},{1,7},{2,4},{3,1},{4,6},{5,3},{6,0},{7,5},{8,10},{9,15},{10,... | collective-permute-start | bytes 2359304 | tf_op jit(solution)/shard_map/ppermute | solution.py:247
  61.4 17.9 %collective-permute-start.15 = (f32[96,2048]{1,0:T(8,128)S(1)}, f32[96,2048]{1,0:T(8,128)S(1)}, u32[]{:S(2)}, u32[]{:S(2)}) collective-permute-start(f32[96,2048]{1,0:T(8,128)S(1)} %bitcast.62), channel_id=1, source_target_pairs={{0,1},{1,0},{2,3},{3,2},{4,5},{5,4},{6,7},{7,6},{8,9},{9,8},{10,11... | collective-permute-start | bytes 2359304 | tf_op jit(solution)/shard_map/ppermute | solution.py:244
  62.1 17.4 %collective-permute-start.3 = (f32[96,2048]{1,0:T(8,128)S(1)}, f32[96,2048]{1,0:T(8,128)S(1)}, u32[]{:S(2)}, u32[]{:S(2)}) collective-permute-start(f32[96,2048]{1,0:T(8,128)S(1)} %bitcast.61), channel_id=1, source_target_pairs={{0,1},{1,0},{2,3},{3,2},{4,5},{5,4},{6,7},{7,6},{8,9},{9,8},{10,11... | collective-permute-start | bytes 2359304 | tf_op jit(solution)/shard_map/ppermute | solution.py:244
  62.7 23.1 %collective-permute-start.10 = (f32[96,2176]{1,0:T(8,128)S(1)}, f32[96,2176]{1,0:T(8,128)S(1)}, u32[]{:S(2)}, u32[]{:S(2)}) collective-permute-start(f32[96,2176]{1,0:T(8,128)S(1)} %bitcast_add_fusion.3.refs_0_), channel_id=1, source_target_pairs={{0,2},{1,7},{2,4},{3,1},{4,6},{5,3},{6,0},{7,5},{8,10},{9,15},{10,... | collective-permute-start | bytes 2506760 | tf_op jit(solution)/shard_map/ppermute | solution.py:247
  68.4 13.1 %collective-permute-start.9 = (f32[96,2176]{1,0:T(8,128)S(1)}, f32[96,2176]{1,0:T(8,128)S(1)}, u32[]{:S(2)}, u32[]{:S(2)}) collective-permute-start(f32[96,2176]{1,0:T(8,128)S(1)} %bitcast.55), channel_id=1, source_target_pairs={{0,1},{1,0},{2,3},{3,2},{4,5},{5,4},{6,7},{7,6},{8,9},{9,8},{10,11... | collective-permute-start | bytes 2506760 | tf_op jit(solution)/shard_map/ppermute | solution.py:244
  76.8 12.9 %collective-permute-start.19 = (f32[96,2048]{1,0:T(8,128)S(1)}, f32[96,2048]{1,0:T(8,128)S(1)}, u32[]{:S(2)}, u32[]{:S(2)}) collective-permute-start(f32[96,2048]{1,0:T(8,128)S(1)} %bitcast.59), channel_id=1, source_target_pairs={{0,1},{1,0},{2,3},{3,2},{4,5},{5,4},{6,7},{7,6},{8,9},{9,8},{10,11... | collective-permute-start | bytes 2359304 | tf_op jit(solution)/shard_map/ppermute | solution.py:244
  79.3 18.8 %collective-permute-start.7 = (f32[96,2048]{1,0:T(8,128)S(1)}, f32[96,2048]{1,0:T(8,128)S(1)}, u32[]{:S(2)}, u32[]{:S(2)}) collective-permute-start(f32[96,2048]{1,0:T(8,128)S(1)} %bitcast.58), channel_id=1, source_target_pairs={{0,1},{1,0},{2,3},{3,2},{4,5},{5,4},{6,7},{7,6},{8,9},{9,8},{10,11... | collective-permute-start | bytes 2359304 | tf_op jit(solution)/shard_map/ppermute | solution.py:244
  79.6 14.6 %collective-permute-start.17 = (f32[96,2048]{1,0:T(8,128)S(1)}, f32[96,2048]{1,0:T(8,128)S(1)}, u32[]{:S(2)}, u32[]{:S(2)}) collective-permute-start(f32[96,2048]{1,0:T(8,128)S(1)} %fusion.3), channel_id=1, source_target_pairs={{0,2},{1,7},{2,4},{3,1},{4,6},{5,3},{6,0},{7,5},{8,10},{9,15},{10,... | collective-permute-start | bytes 2359304 | tf_op jit(solution)/shard_map/ppermute | solution.py:247
  81.5 21.1 %collective-permute-start.5 = (f32[96,2048]{1,0:T(8,128)S(1)}, f32[96,2048]{1,0:T(8,128)S(1)}, u32[]{:S(2)}, u32[]{:S(2)}) collective-permute-start(f32[96,2048]{1,0:T(8,128)S(1)} %fusion.5), channel_id=1, source_target_pairs={{0,2},{1,7},{2,4},{3,1},{4,6},{5,3},{6,0},{7,5},{8,10},{9,15},{10,... | collective-permute-start | bytes 2359304 | tf_op jit(solution)/shard_map/ppermute | solution.py:247
  85.9 25.7 %collective-permute-start.11 = (f32[96,2176]{1,0:T(8,128)S(1)}, f32[96,2176]{1,0:T(8,128)S(1)}, u32[]{:S(2)}, u32[]{:S(2)}) collective-permute-start(f32[96,2176]{1,0:T(8,128)S(1)} %fusion.1), channel_id=1, source_target_pairs={{0,2},{1,7},{2,4},{3,1},{4,6},{5,3},{6,0},{7,5},{8,10},{9,15},{10,... | collective-permute-start | bytes 2506760 | tf_op jit(solution)/shard_map/ppermute | solution.py:247
  89.7 23.8 %collective-permute-start.13 = (f32[96,2176]{1,0:T(8,128)S(1)}, f32[96,2176]{1,0:T(8,128)S(1)}, u32[]{:S(2)}, u32[]{:S(2)}) collective-permute-start(f32[96,2176]{1,0:T(8,128)S(1)} %bitcast.54), channel_id=1, source_target_pairs={{0,1},{1,0},{2,3},{3,2},{4,5},{5,4},{6,7},{7,6},{8,9},{9,8},{10,11... | collective-permute-start | bytes 2506760 | tf_op jit(solution)/shard_map/ppermute | solution.py:244
  94.3 44.0 %collective-permute-start.20 = (f32[96,2048]{1,0:T(8,128)S(1)}, f32[96,2048]{1,0:T(8,128)S(1)}, u32[]{:S(2)}, u32[]{:S(2)}) collective-permute-start(f32[96,2048]{1,0:T(8,128)S(1)} %fusion.2), channel_id=1, source_target_pairs={{0,2},{1,7},{2,4},{3,1},{4,6},{5,3},{6,0},{7,5},{8,10},{9,15},{10,... | collective-permute-start | bytes 2359304 | tf_op jit(solution)/shard_map/ppermute | solution.py:247
  98.1 17.7 %collective-permute-start.18 = (f32[96,2048]{1,0:T(8,128)S(1)}, f32[96,2048]{1,0:T(8,128)S(1)}, u32[]{:S(2)}, u32[]{:S(2)}) collective-permute-start(f32[96,2048]{1,0:T(8,128)S(1)} %bitcast.60), channel_id=1, source_target_pairs={{0,1},{1,0},{2,3},{3,2},{4,5},{5,4},{6,7},{7,6},{8,9},{9,8},{10,11... | collective-permute-start | bytes 2359304 | tf_op jit(solution)/shard_map/ppermute | solution.py:244
  102.8 36.4 %collective-permute-start.8 = (f32[96,2048]{1,0:T(8,128)S(1)}, f32[96,2048]{1,0:T(8,128)S(1)}, u32[]{:S(2)}, u32[]{:S(2)}) collective-permute-start(f32[96,2048]{1,0:T(8,128)S(1)} %fusion.4), channel_id=1, source_target_pairs={{0,2},{1,7},{2,4},{3,1},{4,6},{5,3},{6,0},{7,5},{8,10},{9,15},{10,... | collective-permute-start | bytes 2359304 | tf_op jit(solution)/shard_map/ppermute | solution.py:247
  111.6 4.4 %collective-permute-start.6 = (f32[96,2048]{1,0:T(8,128)S(1)}, f32[96,2048]{1,0:T(8,128)S(1)}, u32[]{:S(2)}, u32[]{:S(2)}) collective-permute-start(f32[96,2048]{1,0:T(8,128)S(1)} %bitcast.63), channel_id=1, source_target_pairs={{0,1},{1,0},{2,3},{3,2},{4,5},{5,4},{6,7},{7,6},{8,9},{9,8},{10,11... | collective-permute-start | bytes 2359304 | tf_op jit(solution)/shard_map/ppermute | solution.py:244
  113.6 23.8 %collective-permute-start.14 = (f32[96,2176]{1,0:T(8,128)S(1)}, f32[96,2176]{1,0:T(8,128)S(1)}, u32[]{:S(2)}, u32[]{:S(2)}) collective-permute-start(f32[96,2176]{1,0:T(8,128)S(1)} %fusion), channel_id=1, source_target_pairs={{0,2},{1,7},{2,4},{3,1},{4,6},{5,3},{6,0},{7,5},{8,10},{9,15},{10,... | collective-permute-start | bytes 2506760 | tf_op jit(solution)/shard_map/ppermute | solution.py:247
  115.8 2.4 %collective-permute-start.12 = (f32[96,2176]{1,0:T(8,128)S(1)}, f32[96,2176]{1,0:T(8,128)S(1)}, u32[]{:S(2)}, u32[]{:S(2)}) collective-permute-start(f32[96,2176]{1,0:T(8,128)S(1)} %bitcast.57), channel_id=1, source_target_pairs={{0,1},{1,0},{2,3},{3,2},{4,5},{5,4},{6,7},{7,6},{8,9},{9,8},{10,11... | collective-permute-start | bytes 2506760 | tf_op jit(solution)/shard_map/ppermute | solution.py:244

commit v5 on v4

--- a/solution.py
+++ b/solution.py
@@ -49,8 +49,8 @@
         high, low = split(k_ref[:, cols].astype(F32) * weight)
         values = v_ref[:, cols]
         state = dot(high, values, TN) + dot(low, values, TN)
-        chunks_ref[8 * h : 8 * h + 8, 0:16, :] = state.reshape(8, 16, 128)
-        chunks_ref[8 * h : 8 * h + 8, 16:24, :] = jnp.broadcast_to(total.reshape(1, 1, 1), (8, 8, 128))
+        chunks_ref[8 * h : 8 * h + 8, 0:16, 0, :] = state.reshape(8, 16, 128)
+        chunks_ref[8 * h : 8 * h + 8, 16, 0, :] = jnp.broadcast_to(total, (8, 128))
 
 
 def prefix_kernel(parent_ref, all_ref, out_ref):
@@ -60,10 +60,9 @@
         p = jnp.clip(first, 0, segments - 1)
         second = parent_ref[p]
         g = jnp.clip(second, 0, segments - 1)
-        own = all_ref[p, 0:16, :]
-        factor = jnp.exp(all_ref[p, 16:24, :])
-        factor = jnp.concatenate([factor, factor], axis=0)
-        older = jnp.where(second >= 0, factor * all_ref[g, 0:16, :], 0.0)
+        own = all_ref[p, 0:16, 0, :]
+        factor = jnp.exp(all_ref[p, 16:17, 0, :])
+        older = jnp.where(second >= 0, factor * all_ref[g, 0:16, 0, :], 0.0)
         out_ref[s] = jnp.where(first >= 0, own + older, 0.0)
 
 
@@ -121,27 +120,26 @@
         squares_out_ref[i] = squares_ref[index_ref[i]]
 
 
-def project_kernel(start, first, features_ref, squares_ref, w_ref, *refs):
+def project_kernel(start, size, first, features_ref, squares_ref, w_ref, *refs):
     keep_ref, send_ref = refs[-2:]
     count, rows = keep_ref.shape[:2]
-    width = keep_ref.shape[2] - (128 if start == 0 else 0)
     sides = [slice(first, first + count), slice(4 + first, 4 + first + count)]
     left = jnp.concatenate([features_ref[side].reshape(count * rows, -1) for side in sides], axis=0)
-    for n in range(0, width, 512):
+    for n in range(0, size, 512):
         t = slice(n, n + 512)
         both = dot(left, w_ref[:, start + n : start + n + 512])
         keep_ref[:, :, t] = both[: count * rows].reshape(count, rows, 512)
         send_ref[:, :, t] = both[count * rows :].reshape(count, rows, 512)
-    if start == 0:
-        keep_ref[:, :, width:] = squares_ref[sides[0]]
-        send_ref[:, :, width:] = squares_ref[sides[1]]
-
-
-def finish_kernel(start, features, *refs):
+    if keep_ref.shape[2] > size:
+        keep_ref[:, :, size:] = squares_ref[sides[0]]
+        send_ref[:, :, size:] = squares_ref[sides[1]]
+
+
+def finish_kernel(start, extra, features, *refs):
     mine_ref, arrived_ref = refs[:2]
-    if start == 0:
+    if extra:
         out_hbm, inverse_ref, buffer, sems = refs[2:]
-        width = mine_ref.shape[1] - 128
+        width = mine_ref.shape[1] - extra
         inverse_ref[...] = 1.0 / jnp.sqrt((mine_ref[:, width:] + arrived_ref[:, width:]) / features + 1e-06)
     else:
         inverse_ref, _, out_hbm, buffer, sems = refs[2:]
@@ -195,7 +193,7 @@
     dma = pltpu.SemaphoreType.DMA
     chunks, running = call(
         state_kernel,
-        [((32, 24, 128), F32), ((8, length), F32)],
+        [((32, 17, 1, 128), F32), ((8, length), F32)],
         [HBM] * 3,
         scratch=[pltpu.VMEM(log_decay.shape, F32), pltpu.VMEM(k.shape, BF16), pltpu.VMEM(v.shape, BF16), dma((3,))],
         vmem=253 * 2**18,
@@ -216,8 +214,9 @@
     way = (1 - 2 * core) * jnp.arange(1, 5, dtype=jnp.int32)
     blocks = jnp.concatenate([((y - way) & 3) * 2 + core, ((y + way) & 3) * 2 + 1 - core])
     share = length // 8
-    starts = [0, 2048, 4096]
-    widths = [2048, 2048, 2048]
+    starts = [0, 1536, 3584]
+    widths = [1536, 2048, 2560]
+    extras = [128, 0, 0]
 
     features, squares = call(
         mix_kernel,
@@ -228,10 +227,10 @@
         vmem=50 * 2**20,
     )(blocks, q, prefix, early, late, running, gain.reshape(1, width), w)
 
-    def project(start, size, first, after):
+    def project(start, size, extra, first, after):
         return call(
-            functools.partial(project_kernel, start, first),
-            [((1, share, size + (128 if start == 0 else 0)), F32)] * 2,
+            functools.partial(project_kernel, start, size, first),
+            [((1, share, size + extra), F32)] * 2,
             [VMEM, VMEM, VMEM] + [ANY] * len(after),
 
         )(features, squares, w, *after)
@@ -239,23 +238,23 @@
     before, arrived = [], []
     for step in range(4):
         totals = []
-        for i, (start, size) in enumerate(zip(starts, widths)):
-            keep, send = project(start, size, step, before if step == 1 else before[i : i + 1] if step > 1 else [])
+        for i, (start, size, extra) in enumerate(zip(starts, widths, extras)):
+            keep, send = project(start, size, extra, step, before if step == 1 else before[i : i + 1] if step > 1 else [])
             totals.append(keep[0] + lax.ppermute(send[0], "head", SWAP) + (arrived[i] if step in (1, 2) else 0.0))
         if step < 3:
             before = totals if step == 0 else arrived
             arrived = [lax.ppermute(total, "head", RING) for total in totals]
     total_features = width * lax.axis_size("head")
     out = ((share, w.shape[1]), BF16)
-    mixed = None
-    for start, size, own, got in zip(starts, widths, totals, arrived):
+    for extra, start, size, i in sorted(zip(extras, starts, widths, range(len(starts))), key=lambda c: -c[0]):
         buffers = [pltpu.VMEM((share, size), BF16), dma((size // 512,))]
-        kernel = functools.partial(finish_kernel, start, total_features)
-        if start == 0:
-            mixed, inverse = call(kernel, [out, ((share, 128), F32)], [VMEM] * 2, outs=[ANY, VMEM], scratch=buffers)(own, got)
+        kernel = functools.partial(finish_kernel, start, extra, total_features)
+        terms = [totals[i], arrived[i]]
+        if extra:
+            mixed, inverse = call(kernel, [out, ((share, 128), F32)], [VMEM] * 2, outs=[ANY, VMEM], scratch=buffers)(*terms)
         else:
             (mixed,) = call(kernel, [out], [VMEM] * 3 + [ANY], outs=[ANY], scratch=buffers, aliases={3: 0})(
-                own, got, inverse, mixed
+                *terms, inverse, mixed
             )
     return mixed
 

time: 141 us -> 136 us (0.965)
  waiting for transfers between devices: 58.1 us -> 54.6 us
    ppermute x12, waiting for transfers between devices: 2.23 us -> 0.03 us  [per_device(): lax.ppermute(send[0], 'head', SWAP)]
    all_to_all x1, waiting for transfers between devices: 4.65 us -> 2.77 us  [per_device(): everyone = lax.all_to_all(chunks, 'seg', 0, 0, tiled=True)]
  transfers between devices with their start and end apart: 23 -> 23, of which waited for: 11 -> 10; matrix products, arithmetic and copies ran while one was open for 1% -> 1% of each run, Pallas kernels for 9% -> 9%
where the time goes in v5:
time: 136 us
  waiting for transfers between devices  54.6 us (40%)
  starting transfers between devices  47.7 us (35%)
  Pallas kernels  21.1 us (16%)
  local copies, waits for them, and re-layouts  10.5 us (8%)
    ppermute x9, waiting for transfers between devices, per_device(): arrived = [lax.ppermute(total, 'head', RING) for total in totals]  47.4 us
    ppermute x9, starting transfers between devices, per_device(): arrived = [lax.ppermute(total, 'head', RING) for total in totals]  17.4 us
    ppermute x12, starting transfers between devices, per_device(): lax.ppermute(send[0], 'head', SWAP)  12 us
    all_to_all x1, starting transfers between devices, per_device(): everyone = lax.all_to_all(chunks, 'seg', 0, 0, tiled=True)  11.9 us
    unnamed x32, local copies, waits for them, and re-layouts  10.5 us
    pallas_call x12, Pallas kernels, project(): call(functools.partial(project_kernel, start, size, first), [((1, share,...  7.03 us
    all_to_all x1, starting transfers between devices, per_device(): prefix = lax.all_to_all(mine, 'seg', 0, 0, tiled=True).reshape(4, 128, 128)  6.46 us
    all_to_all x1, waiting for transfers between devices, per_device(): prefix = lax.all_to_all(mine, 'seg', 0, 0, tiled=True).reshape(4, 128, 128)  4.4 us
  transfers between devices with their start and end apart: 23, of which 10 were waited for; matrix products, arithmetic and copies ran while one was open for 1% of the time, Pallas kernels for 9%

profile of v5, /device:TPU:1, one launch (start us, length us, event | category | flops | bytes accessed | tf_op | source)
XLA Modules:
  0.0 135.7 jit_solution(14684418378042740512)
XLA Ops:
  0.0 3.3 %shard_map.73 = (f32[32,17,1,128]{3,2,1,0:T(1,128)}, f32[8,768]{1,0:T(8,128)}) custom-call(f32[4,768]{1,0:T(4,128)} %decay_hbm.1, bf16[768,512]{1,0:T(8,128)(2,1)} %k_hbm.5, bf16[768,512]{1,0:T(8,128)(2,1)} %v_hbm.5), custom_call_target="tpu_custom_call" | custom-call | flops 268435456 | bytes 1048576 | tf_op jit(solution)/shard_map/pallas_call | solution.py:194
  3.3 11.9 %all-to-all-start = ((f32[32,17,1,128]{3,2,1,0:T(1,128)}), f32[32,17,1,128]{3,2,1,0:T(1,128)S(1)}, u32[]{:S(2)}, u32[]{:S(2)}) async-start(f32[32,17,1,128]{3,2,1,0:T(1,128)} %get-tuple-element.38), calls=%async_computation | async-start | bytes 557056 | tf_op jit(solution)/shard_map/all_to_all | solution.py:201
  15.2 1.1 copy-done
  16.3 1.1 copy-done.6
  17.5 1.1 copy-done.8
  18.6 0.7 copy-done.10
  19.3 2.0 %shard_map.74.early_ref = f32[768,256]{1,0:T(8,128)S(1)} custom-call(bf16[768,512]{1,0:T(8,128)(2,1)S(1)} %copy-done, bf16[768,512]{1,0:T(8,128)(2,1)S(1)} %copy-done.6, bf16[768,512]{1,0:T(8,128)(2,1)S(1)} %copy-done.8, f32[8,768]{1,0:T(8,128)S(1)} %copy-done.10), custom_call_target="tpu_custom_call" | custom-call | flops 1073741824 | bytes 1048576 | tf_op jit(solution)/shard_map/pallas_call | solution.py:203
  21.3 0.9 copy-done.2
  22.2 2.8 %all-to-all-done.all_ref = f32[32,17,1,128]{3,2,1,0:T(1,128)S(1)} async-done(((f32[32,17,1,128]{3,2,1,0:T(1,128)}), f32[32,17,1,128]{3,2,1,0:T(1,128)S(1)}, u32[]{:S(2)}, u32[]{:S(2)}) %all-to-all-start) | async-done | bytes 278560 | tf_op jit(solution)/shard_map/all_to_all | solution.py:201
  25.0 1.6 %shard_map.75 = f32[32,16,128]{2,1,0:T(8,128)} custom-call(s32[32]{0:T(128)S(1)} %copy-done.13, f32[32,17,1,128]{3,2,1,0:T(1,128)S(1)} %all-to-all-done.all_ref), custom_call_target="tpu_custom_call" | custom-call | flops 268435456 | bytes 1048576 | tf_op jit(solution)/shard_map/pallas_call | solution.py:207
  26.5 6.5 %all-to-all-start.1 = ((f32[32,16,128]{2,1,0:T(8,128)}), f32[32,16,128]{2,1,0:T(8,128)S(1)}, u32[]{:S(2)}, u32[]{:S(2)}) async-start(f32[32,16,128]{2,1,0:T(8,128)} %shard_map.75), calls=%async_computation.1 | async-start | bytes 524288 | tf_op jit(solution)/shard_map/all_to_all | solution.py:208
  33.1 1.1 copy-done.7
  34.2 1.1 copy-done.9
  35.4 2.0 %shard_map.76.late_ref = f32[768,256]{1,0:T(8,128)S(1)} custom-call(bf16[768,512]{1,0:T(8,128)(2,1)S(1)} %copy-done.1, bf16[768,512]{1,0:T(8,128)(2,1)S(1)} %copy-done.7, bf16[768,512]{1,0:T(8,128)(2,1)S(1)} %copy-done.9, f32[8,768]{1,0:T(8,128)S(1)} %copy-done.11), custom_call_target="tpu_custom_call" | custom-call | flops 1073741824 | bytes 1048576 | tf_op jit(solution)/shard_map/pallas_call | solution.py:209
  37.4 0.9 copy-done.4
  38.3 4.4 %all-to-all-done.1 = f32[32,16,128]{2,1,0:T(8,128)S(1)} async-done(((f32[32,16,128]{2,1,0:T(8,128)}), f32[32,16,128]{2,1,0:T(8,128)S(1)}, u32[]{:S(2)}, u32[]{:S(2)}) %all-to-all-start.1) | async-done | bytes 262176 | tf_op jit(solution)/shard_map/all_to_all | solution.py:208
  42.7 1.1 copy-done.3
  43.8 1.1 copy-done.5
  44.9 2.6 %shard_map.77 = (bf16[8,96,512]{2,1,0:T(8,128)(2,1)S(1)}, f32[8,96,128]{2,1,0:T(8,128)S(1)}) custom-call(s32[8]{0:T(128)S(1)} %pad_add_fusion.index_ref, bf16[768,512]{1,0:T(8,128)(2,1)S(1)} %copy-done.1, f32[4,128,128]{2,1,0:T(8,128)S(1)} %bitcast.52, f32[768,256]{1,0:T(8,128)S(1)} %copy-done.3, f32[768,256]{1,0:T(8,128)S(1)} %copy-done.5, ...), custom_call_target="tpu_custom_call" | custom-call | flops 268435456 | bytes 1048576 | tf_op jit(solution)/shard_map/pallas_call | solution.py:221
  47.6 0.5 shard_map.78
  48.1 3.7 %collective-permute-start = (f32[96,1664]{1,0:T(8,128)S(1)}, f32[96,1664]{1,0:T(8,128)S(1)}, u32[]{:S(2)}, u32[]{:S(2)}) collective-permute-start(f32[96,1664]{1,0:T(8,128)S(1)} %bitcast.65), channel_id=1, source_target_pairs={{0,1},{1,0},{2,3},{3,2},{4,5},{5,4},{6,7},{7,6},{8,9},{9,8},{10,11... | collective-permute-start | bytes 1916936 | tf_op jit(solution)/shard_map/ppermute | solution.py:243
  51.8 0.6 shard_map.79
  52.4 0.1 collective-permute-start.1
  52.5 0.7 shard_map.80
  53.2 0.6 collective-permute-start.2
  53.8 2.8 %collective-permute-start.10 = (f32[96,1664]{1,0:T(8,128)S(1)}, f32[96,1664]{1,0:T(8,128)S(1)}, u32[]{:S(2)}, u32[]{:S(2)}) collective-permute-start(f32[96,1664]{1,0:T(8,128)S(1)} %bitcast_add_fusion.11.refs_0_), channel_id=1, source_target_pairs={{0,2},{1,7},{2,4},{3,1},{4,6},{5,3},{6,0},{7,5},{8,10},{9,15},{10,... | collective-permute-start | bytes 1916936 | tf_op jit(solution)/shard_map/ppermute | solution.py:246
  56.7 1.1 collective-permute-start.16
  57.9 0.1 bitcast_add_fusion.3.refs_2_
  58.0 0.5 shard_map.84
  58.5 0.6 shard_map.88
  59.1 0.6 collective-permute-start.15
  59.7 1.1 collective-permute-start.4
  60.8 0.7 shard_map.81
  61.5 2.5 %collective-permute-done.10.refs_0_ = f32[96,1664]{1,0:T(8,128)S(1)} collective-permute-done((f32[96,1664]{1,0:T(8,128)S(1)}, f32[96,1664]{1,0:T(8,128)S(1)}, u32[]{:S(2)}, u32[]{:S(2)}) %collective-permute-start.10) | collective-permute-done | bytes 639008 | tf_op jit(solution)/shard_map/ppermute | solution.py:246
  64.0 1.6 %collective-permute-start.3 = (f32[96,2560]{1,0:T(8,128)S(1)}, f32[96,2560]{1,0:T(8,128)S(1)}, u32[]{:S(2)}, u32[]{:S(2)}) collective-permute-start(f32[96,2560]{1,0:T(8,128)S(1)} %bitcast.55), channel_id=1, source_target_pairs={{0,1},{1,0},{2,3},{3,2},{4,5},{5,4},{6,7},{7,6},{8,9},{9,8},{10,11... | collective-permute-start | bytes 2949128 | tf_op jit(solution)/shard_map/ppermute | solution.py:243
  65.7 0.5 shard_map.86
  66.1 6.3 %collective-permute-done.16.refs_0_ = f32[96,2048]{1,0:T(8,128)S(1)} collective-permute-done((f32[96,2048]{1,0:T(8,128)S(1)}, f32[96,2048]{1,0:T(8,128)S(1)}, u32[]{:S(2)}, u32[]{:S(2)}) %collective-permute-start.16) | collective-permute-done | bytes 786464 | tf_op jit(solution)/shard_map/ppermute | solution.py:246
  72.4 1.6 %collective-permute-start.13 = (f32[96,1664]{1,0:T(8,128)S(1)}, f32[96,1664]{1,0:T(8,128)S(1)}, u32[]{:S(2)}, u32[]{:S(2)}) collective-permute-start(f32[96,1664]{1,0:T(8,128)S(1)} %bitcast.62), channel_id=1, source_target_pairs={{0,1},{1,0},{2,3},{3,2},{4,5},{5,4},{6,7},{7,6},{8,9},{9,8},{10,11... | collective-permute-start | bytes 1916936 | tf_op jit(solution)/shard_map/ppermute | solution.py:243
  74.1 0.6 shard_map.90
  74.9 2.0 %collective-permute-start.11 = (f32[96,1664]{1,0:T(8,128)S(1)}, f32[96,1664]{1,0:T(8,128)S(1)}, u32[]{:S(2)}, u32[]{:S(2)}) collective-permute-start(f32[96,1664]{1,0:T(8,128)S(1)} %fusion.5), channel_id=1, source_target_pairs={{0,2},{1,7},{2,4},{3,1},{4,6},{5,3},{6,0},{7,5},{8,10},{9,15},{10,... | collective-permute-start | bytes 1916936 | tf_op jit(solution)/shard_map/ppermute | solution.py:246
  76.9 0.1 fusion.3
  77.2 5.8 %collective-permute-done.4.refs_0_ = f32[96,2560]{1,0:T(8,128)S(1)} collective-permute-done((f32[96,2560]{1,0:T(8,128)S(1)}, f32[96,2560]{1,0:T(8,128)S(1)}, u32[]{:S(2)}, u32[]{:S(2)}) %collective-permute-start.4) | collective-permute-done | bytes 983072 | tf_op jit(solution)/shard_map/ppermute | solution.py:246
  83.0 0.1 fusion.1
  83.1 3.2 %collective-permute-start.5 = (f32[96,2560]{1,0:T(8,128)S(1)}, f32[96,2560]{1,0:T(8,128)S(1)}, u32[]{:S(2)}, u32[]{:S(2)}) collective-permute-start(f32[96,2560]{1,0:T(8,128)S(1)} %fusion.1), channel_id=1, source_target_pairs={{0,2},{1,7},{2,4},{3,1},{4,6},{5,3},{6,0},{7,5},{8,10},{9,15},{10,... | collective-permute-start | bytes 2949128 | tf_op jit(solution)/shard_map/ppermute | solution.py:246
  86.3 0.7 shard_map.83
  87.0 2.8 %collective-permute-done.11.refs_0_ = f32[96,1664]{1,0:T(8,128)S(1)} collective-permute-done((f32[96,1664]{1,0:T(8,128)S(1)}, f32[96,1664]{1,0:T(8,128)S(1)}, u32[]{:S(2)}, u32[]{:S(2)}) %collective-permute-start.11) | collective-permute-done | bytes 639008 | tf_op jit(solution)/shard_map/ppermute | solution.py:246
  89.8 1.6 %collective-permute-start.7 = (f32[96,2560]{1,0:T(8,128)S(1)}, f32[96,2560]{1,0:T(8,128)S(1)}, u32[]{:S(2)}, u32[]{:S(2)}) collective-permute-start(f32[96,2560]{1,0:T(8,128)S(1)} %bitcast.54), channel_id=1, source_target_pairs={{0,1},{1,0},{2,3},{3,2},{4,5},{5,4},{6,7},{7,6},{8,9},{9,8},{10,11... | collective-permute-start | bytes 2949128 | tf_op jit(solution)/shard_map/ppermute | solution.py:243
  91.5 0.5 shard_map.85
  92.2 2.0 %collective-permute-start.14 = (f32[96,1664]{1,0:T(8,128)S(1)}, f32[96,1664]{1,0:T(8,128)S(1)}, u32[]{:S(2)}, u32[]{:S(2)}) collective-permute-start(f32[96,1664]{1,0:T(8,128)S(1)} %fusion.4), channel_id=1, source_target_pairs={{0,2},{1,7},{2,4},{3,1},{4,6},{5,3},{6,0},{7,5},{8,10},{9,15},{10,... | collective-permute-start | bytes 1916936 | tf_op jit(solution)/shard_map/ppermute | solution.py:246
  94.2 4.0 %collective-permute-done.17.refs_0_ = f32[96,2048]{1,0:T(8,128)S(1)} collective-permute-done((f32[96,2048]{1,0:T(8,128)S(1)}, f32[96,2048]{1,0:T(8,128)S(1)}, u32[]{:S(2)}, u32[]{:S(2)}) %collective-permute-start.17) | collective-permute-done | bytes 786464 | tf_op jit(solution)/shard_map/ppermute | solution.py:246
  98.2 0.1 fusion.2
  98.4 3.4 %collective-permute-start.20 = (f32[96,2048]{1,0:T(8,128)S(1)}, f32[96,2048]{1,0:T(8,128)S(1)}, u32[]{:S(2)}, u32[]{:S(2)}) collective-permute-start(f32[96,2048]{1,0:T(8,128)S(1)} %fusion.2), channel_id=1, source_target_pairs={{0,2},{1,7},{2,4},{3,1},{4,6},{5,3},{6,0},{7,5},{8,10},{9,15},{10,... | collective-permute-start | bytes 2359304 | tf_op jit(solution)/shard_map/ppermute | solution.py:246
  101.8 0.6 shard_map.89
  102.6 13.1 %collective-permute-done.14.refs_1_ = f32[96,1664]{1,0:T(8,128)S(1)} collective-permute-done((f32[96,1664]{1,0:T(8,128)S(1)}, f32[96,1664]{1,0:T(8,128)S(1)}, u32[]{:S(2)}, u32[]{:S(2)}) %collective-permute-start.14) | collective-permute-done | bytes 639008 | tf_op jit(solution)/shard_map/ppermute | solution.py:246
  115.6 0.8 shard_map.87
  116.5 0.7 shard_map.82
  117.2 1.7 %collective-permute-start.6 = (f32[96,2560]{1,0:T(8,128)S(1)}, f32[96,2560]{1,0:T(8,128)S(1)}, u32[]{:S(2)}, u32[]{:S(2)}) collective-permute-start(f32[96,2560]{1,0:T(8,128)S(1)} %bitcast.56), channel_id=1, source_target_pairs={{0,1},{1,0},{2,3},{3,2},{4,5},{5,4},{6,7},{7,6},{8,9},{9,8},{10,11... | collective-permute-start | bytes 2949128 | tf_op jit(solution)/shard_map/ppermute | solution.py:243
  118.9 0.1 fusion
  119.1 1.6 %collective-permute-start.8 = (f32[96,2560]{1,0:T(8,128)S(1)}, f32[96,2560]{1,0:T(8,128)S(1)}, u32[]{:S(2)}, u32[]{:S(2)}) collective-permute-start(f32[96,2560]{1,0:T(8,128)S(1)} %fusion), channel_id=1, source_target_pairs={{0,2},{1,7},{2,4},{3,1},{4,6},{5,3},{6,0},{7,5},{8,10},{9,15},{10,... | collective-permute-start | bytes 2949128 | tf_op jit(solution)/shard_map/ppermute | solution.py:246
  120.8 3.3 %collective-permute-done.20.refs_1_ = f32[96,2048]{1,0:T(8,128)S(1)} collective-permute-done((f32[96,2048]{1,0:T(8,128)S(1)}, f32[96,2048]{1,0:T(8,128)S(1)}, u32[]{:S(2)}, u32[]{:S(2)}) %collective-permute-start.20) | collective-permute-done | bytes 786464 | tf_op jit(solution)/shard_map/ppermute | solution.py:246
  124.1 0.9 shard_map.91.refs_3_
  125.0 0.1 bitcast_add_fusion.1.refs_0_
  125.1 9.5 %collective-permute-done.8.refs_1_ = f32[96,2560]{1,0:T(8,128)S(1)} collective-permute-done((f32[96,2560]{1,0:T(8,128)S(1)}, f32[96,2560]{1,0:T(8,128)S(1)}, u32[]{:S(2)}, u32[]{:S(2)}) %collective-permute-start.8) | collective-permute-done | bytes 983072 | tf_op jit(solution)/shard_map/ppermute | solution.py:246
  134.6 0.9 shard_map.92
  (49 shorter events, 1.1 us)
Async XLA Ops:
  3.3 21.7 %all-to-all-start = ((f32[32,17,1,128]{3,2,1,0:T(1,128)}), f32[32,17,1,128]{3,2,1,0:T(1,128)S(1)}, u32[]{:S(2)}, u32[]{:S(2)}) async-start(f32[32,17,1,128]{3,2,1,0:T(1,128)} %get-tuple-element.38), calls=%async_computation | async-start | bytes 557056 | tf_op jit(solution)/shard_map/all_to_all | solution.py:201
  15.2 1.1 copy-start
  16.3 1.1 copy-start.6
  17.5 1.1 copy-start.8
  18.6 0.7 copy-start.10
  19.3 5.6 %copy-start.13 = (s32[32]{0:T(128)S(1)}, s32[32]{0:T(128)}, u32[]{:S(2)}) copy-start(s32[32]{0:T(128)} %parent_ref.1) | copy-start | bytes 388
  21.3 0.9 copy-start.2
  22.2 10.9 %copy-start.1 = (bf16[768,512]{1,0:T(8,128)(2,1)S(1)}, bf16[768,512]{1,0:T(8,128)(2,1)}, u32[]{:S(2)}) copy-start(bf16[768,512]{1,0:T(8,128)(2,1)} %q_hbm.5) | copy-start | bytes 2359300
  22.2 10.9 %copy-start.11 = (f32[8,768]{1,0:T(8,128)S(1)}, f32[8,768]{1,0:T(8,128)}, u32[]{:S(2)}) copy-start(f32[8,768]{1,0:T(8,128)} %get-tuple-element.42.running_ref) | copy-start | bytes 73732
  26.5 16.1 %all-to-all-start.1 = ((f32[32,16,128]{2,1,0:T(8,128)}), f32[32,16,128]{2,1,0:T(8,128)S(1)}, u32[]{:S(2)}, u32[]{:S(2)}) async-start(f32[32,16,128]{2,1,0:T(8,128)} %shard_map.75), calls=%async_computation.1 | async-start | bytes 524288 | tf_op jit(solution)/shard_map/all_to_all | solution.py:208
  33.1 1.1 copy-start.7
  34.2 1.1 copy-start.9
  35.4 7.3 %copy-start.12 = (f32[512]{0:T(512)S(1)}, f32[512]{0:T(512)}, u32[]{:S(2)}) copy-start(f32[512]{0:T(512)} %param.12) | copy-start | bytes 6148
  35.4 12.2 %slice-start = ((s8[6291456]{0:T(1024)(128)(4,1)}), s8[2097152]{0:T(1024)(128)(4,1)S(1)}, s32[]{:S(2)}) async-start(s8[6291456]{0:T(1024)(128)(4,1)} %bitcast.50), calls=%async_computation.2 | async-start | bytes 4194304
  37.3 0.9 copy-start.4
  42.7 1.1 copy-start.3
  43.8 1.1 copy-start.5
  44.9 2.6 %slice-start.1 = ((s8[6291456]{0:T(1024)(128)(4,1)}), s8[4194304]{0:T(1024)(128)(4,1)S(1)}, s32[]{:S(2)}) async-start(s8[6291456]{0:T(1024)(128)(4,1)} %bitcast.50), calls=%async_computation.3 | async-start | bytes 8388608
  48.1 5.7 %collective-permute-start = (f32[96,1664]{1,0:T(8,128)S(1)}, f32[96,1664]{1,0:T(8,128)S(1)}, u32[]{:S(2)}, u32[]{:S(2)}) collective-permute-start(f32[96,1664]{1,0:T(8,128)S(1)} %bitcast.65), channel_id=1, source_target_pairs={{0,1},{1,0},{2,3},{3,2},{4,5},{5,4},{6,7},{7,6},{8,9},{9,8},{10,11... | collective-permute-start | bytes 1916936 | tf_op jit(solution)/shard_map/ppermute | solution.py:243
  52.4 4.3 %collective-permute-start.1 = (f32[96,2048]{1,0:T(8,128)S(1)}, f32[96,2048]{1,0:T(8,128)S(1)}, u32[]{:S(2)}, u32[]{:S(2)}) collective-permute-start(f32[96,2048]{1,0:T(8,128)S(1)} %bitcast.61), channel_id=1, source_target_pairs={{0,1},{1,0},{2,3},{3,2},{4,5},{5,4},{6,7},{7,6},{8,9},{9,8},{10,11... | collective-permute-start | bytes 2359304 | tf_op jit(solution)/shard_map/ppermute | solution.py:243
  53.2 4.7 %collective-permute-start.2 = (f32[96,2560]{1,0:T(8,128)S(1)}, f32[96,2560]{1,0:T(8,128)S(1)}, u32[]{:S(2)}, u32[]{:S(2)}) collective-permute-start(f32[96,2560]{1,0:T(8,128)S(1)} %bitcast.57), channel_id=1, source_target_pairs={{0,1},{1,0},{2,3},{3,2},{4,5},{5,4},{6,7},{7,6},{8,9},{9,8},{10,11... | collective-permute-start | bytes 2949128 | tf_op jit(solution)/shard_map/ppermute | solution.py:243
  53.8 10.2 %collective-permute-start.10 = (f32[96,1664]{1,0:T(8,128)S(1)}, f32[96,1664]{1,0:T(8,128)S(1)}, u32[]{:S(2)}, u32[]{:S(2)}) collective-permute-start(f32[96,1664]{1,0:T(8,128)S(1)} %bitcast_add_fusion.11.refs_0_), channel_id=1, source_target_pairs={{0,2},{1,7},{2,4},{3,1},{4,6},{5,3},{6,0},{7,5},{8,10},{9,15},{10,... | collective-permute-start | bytes 1916936 | tf_op jit(solution)/shard_map/ppermute | solution.py:246
  56.7 15.7 %collective-permute-start.16 = (f32[96,2048]{1,0:T(8,128)S(1)}, f32[96,2048]{1,0:T(8,128)S(1)}, u32[]{:S(2)}, u32[]{:S(2)}) collective-permute-start(f32[96,2048]{1,0:T(8,128)S(1)} %bitcast_add_fusion.7.refs_1_), channel_id=1, source_target_pairs={{0,2},{1,7},{2,4},{3,1},{4,6},{5,3},{6,0},{7,5},{8,10},{9,15},{10,... | collective-permute-start | bytes 2359304 | tf_op jit(solution)/shard_map/ppermute | solution.py:246
  58.4 16.2 %collective-permute-start.9 = (f32[96,1664]{1,0:T(8,128)S(1)}, f32[96,1664]{1,0:T(8,128)S(1)}, u32[]{:S(2)}, u32[]{:S(2)}) collective-permute-start(f32[96,1664]{1,0:T(8,128)S(1)} %bitcast.63), channel_id=1, source_target_pairs={{0,1},{1,0},{2,3},{3,2},{4,5},{5,4},{6,7},{7,6},{8,9},{9,8},{10,11... | collective-permute-start | bytes 1916936 | tf_op jit(solution)/shard_map/ppermute | solution.py:243
  59.1 15.7 %collective-permute-start.15 = (f32[96,2048]{1,0:T(8,128)S(1)}, f32[96,2048]{1,0:T(8,128)S(1)}, u32[]{:S(2)}, u32[]{:S(2)}) collective-permute-start(f32[96,2048]{1,0:T(8,128)S(1)} %bitcast.60), channel_id=1, source_target_pairs={{0,1},{1,0},{2,3},{3,2},{4,5},{5,4},{6,7},{7,6},{8,9},{9,8},{10,11... | collective-permute-start | bytes 2359304 | tf_op jit(solution)/shard_map/ppermute | solution.py:243
  59.7 23.3 %collective-permute-start.4 = (f32[96,2560]{1,0:T(8,128)S(1)}, f32[96,2560]{1,0:T(8,128)S(1)}, u32[]{:S(2)}, u32[]{:S(2)}) collective-permute-start(f32[96,2560]{1,0:T(8,128)S(1)} %bitcast_add_fusion.3.refs_2_), channel_id=1, source_target_pairs={{0,2},{1,7},{2,4},{3,1},{4,6},{5,3},{6,0},{7,5},{8,10},{9,15},{10,... | collective-permute-start | bytes 2949128 | tf_op jit(solution)/shard_map/ppermute | solution.py:246
  64.0 13.1 %collective-permute-start.3 = (f32[96,2560]{1,0:T(8,128)S(1)}, f32[96,2560]{1,0:T(8,128)S(1)}, u32[]{:S(2)}, u32[]{:S(2)}) collective-permute-start(f32[96,2560]{1,0:T(8,128)S(1)} %bitcast.55), channel_id=1, source_target_pairs={{0,1},{1,0},{2,3},{3,2},{4,5},{5,4},{6,7},{7,6},{8,9},{9,8},{10,11... | collective-permute-start | bytes 2949128 | tf_op jit(solution)/shard_map/ppermute | solution.py:243
  72.4 19.5 %collective-permute-start.13 = (f32[96,1664]{1,0:T(8,128)S(1)}, f32[96,1664]{1,0:T(8,128)S(1)}, u32[]{:S(2)}, u32[]{:S(2)}) collective-permute-start(f32[96,1664]{1,0:T(8,128)S(1)} %bitcast.62), channel_id=1, source_target_pairs={{0,1},{1,0},{2,3},{3,2},{4,5},{5,4},{6,7},{7,6},{8,9},{9,8},{10,11... | collective-permute-start | bytes 1916936 | tf_op jit(solution)/shard_map/ppermute | solution.py:243
  74.7 17.5 %collective-permute-start.19 = (f32[96,2048]{1,0:T(8,128)S(1)}, f32[96,2048]{1,0:T(8,128)S(1)}, u32[]{:S(2)}, u32[]{:S(2)}) collective-permute-start(f32[96,2048]{1,0:T(8,128)S(1)} %bitcast.58), channel_id=1, source_target_pairs={{0,1},{1,0},{2,3},{3,2},{4,5},{5,4},{6,7},{7,6},{8,9},{9,8},{10,11... | collective-permute-start | bytes 2359304 | tf_op jit(solution)/shard_map/ppermute | solution.py:243
  74.9 14.9 %collective-permute-start.11 = (f32[96,1664]{1,0:T(8,128)S(1)}, f32[96,1664]{1,0:T(8,128)S(1)}, u32[]{:S(2)}, u32[]{:S(2)}) collective-permute-start(f32[96,1664]{1,0:T(8,128)S(1)} %fusion.5), channel_id=1, source_target_pairs={{0,2},{1,7},{2,4},{3,1},{4,6},{5,3},{6,0},{7,5},{8,10},{9,15},{10,... | collective-permute-start | bytes 1916936 | tf_op jit(solution)/shard_map/ppermute | solution.py:246
  77.1 21.2 %collective-permute-start.17 = (f32[96,2048]{1,0:T(8,128)S(1)}, f32[96,2048]{1,0:T(8,128)S(1)}, u32[]{:S(2)}, u32[]{:S(2)}) collective-permute-start(f32[96,2048]{1,0:T(8,128)S(1)} %fusion.3), channel_id=1, source_target_pairs={{0,2},{1,7},{2,4},{3,1},{4,6},{5,3},{6,0},{7,5},{8,10},{9,15},{10,... | collective-permute-start | bytes 2359304 | tf_op jit(solution)/shard_map/ppermute | solution.py:246
  83.1 33.4 %collective-permute-start.5 = (f32[96,2560]{1,0:T(8,128)S(1)}, f32[96,2560]{1,0:T(8,128)S(1)}, u32[]{:S(2)}, u32[]{:S(2)}) collective-permute-start(f32[96,2560]{1,0:T(8,128)S(1)} %fusion.1), channel_id=1, source_target_pairs={{0,2},{1,7},{2,4},{3,1},{4,6},{5,3},{6,0},{7,5},{8,10},{9,15},{10,... | collective-permute-start | bytes 2949128 | tf_op jit(solution)/shard_map/ppermute | solution.py:246
  89.8 29.1 %collective-permute-start.7 = (f32[96,2560]{1,0:T(8,128)S(1)}, f32[96,2560]{1,0:T(8,128)S(1)}, u32[]{:S(2)}, u32[]{:S(2)}) collective-permute-start(f32[96,2560]{1,0:T(8,128)S(1)} %bitcast.54), channel_id=1, source_target_pairs={{0,1},{1,0},{2,3},{3,2},{4,5},{5,4},{6,7},{7,6},{8,9},{9,8},{10,11... | collective-permute-start | bytes 2949128 | tf_op jit(solution)/shard_map/ppermute | solution.py:243
  92.0 10.4 %collective-permute-start.12 = (f32[96,1664]{1,0:T(8,128)S(1)}, f32[96,1664]{1,0:T(8,128)S(1)}, u32[]{:S(2)}, u32[]{:S(2)}) collective-permute-start(f32[96,1664]{1,0:T(8,128)S(1)} %bitcast.64), channel_id=1, source_target_pairs={{0,1},{1,0},{2,3},{3,2},{4,5},{5,4},{6,7},{7,6},{8,9},{9,8},{10,11... | collective-permute-start | bytes 1916936 | tf_op jit(solution)/shard_map/ppermute | solution.py:243
  92.2 23.5 %collective-permute-start.14 = (f32[96,1664]{1,0:T(8,128)S(1)}, f32[96,1664]{1,0:T(8,128)S(1)}, u32[]{:S(2)}, u32[]{:S(2)}) collective-permute-start(f32[96,1664]{1,0:T(8,128)S(1)} %fusion.4), channel_id=1, source_target_pairs={{0,2},{1,7},{2,4},{3,1},{4,6},{5,3},{6,0},{7,5},{8,10},{9,15},{10,... | collective-permute-start | bytes 1916936 | tf_op jit(solution)/shard_map/ppermute | solution.py:246
  98.4 25.7 %collective-permute-start.20 = (f32[96,2048]{1,0:T(8,128)S(1)}, f32[96,2048]{1,0:T(8,128)S(1)}, u32[]{:S(2)}, u32[]{:S(2)}) collective-permute-start(f32[96,2048]{1,0:T(8,128)S(1)} %fusion.2), channel_id=1, source_target_pairs={{0,2},{1,7},{2,4},{3,1},{4,6},{5,3},{6,0},{7,5},{8,10},{9,15},{10,... | collective-permute-start | bytes 2359304 | tf_op jit(solution)/shard_map/ppermute | solution.py:246
  102.4 18.3 %collective-permute-start.18 = (f32[96,2048]{1,0:T(8,128)S(1)}, f32[96,2048]{1,0:T(8,128)S(1)}, u32[]{:S(2)}, u32[]{:S(2)}) collective-permute-start(f32[96,2048]{1,0:T(8,128)S(1)} %bitcast.59), channel_id=1, source_target_pairs={{0,1},{1,0},{2,3},{3,2},{4,5},{5,4},{6,7},{7,6},{8,9},{9,8},{10,11... | collective-permute-start | bytes 2359304 | tf_op jit(solution)/shard_map/ppermute | solution.py:243
  117.2 7.8 %collective-permute-start.6 = (f32[96,2560]{1,0:T(8,128)S(1)}, f32[96,2560]{1,0:T(8,128)S(1)}, u32[]{:S(2)}, u32[]{:S(2)}) collective-permute-start(f32[96,2560]{1,0:T(8,128)S(1)} %bitcast.56), channel_id=1, source_target_pairs={{0,1},{1,0},{2,3},{3,2},{4,5},{5,4},{6,7},{7,6},{8,9},{9,8},{10,11... | collective-permute-start | bytes 2949128 | tf_op jit(solution)/shard_map/ppermute | solution.py:243
  119.1 15.5 %collective-permute-start.8 = (f32[96,2560]{1,0:T(8,128)S(1)}, f32[96,2560]{1,0:T(8,128)S(1)}, u32[]{:S(2)}, u32[]{:S(2)}) collective-permute-start(f32[96,2560]{1,0:T(8,128)S(1)} %fusion), channel_id=1, source_target_pairs={{0,2},{1,7},{2,4},{3,1},{4,6},{5,3},{6,0},{7,5},{8,10},{9,15},{10,... | collective-permute-start | bytes 2949128 | tf_op jit(solution)/shard_map/ppermute | solution.py:246

commit v6 on v5

--- a/solution.py
+++ b/solution.py
@@ -29,7 +29,11 @@
 
 
 def state_kernel(decay_hbm, k_hbm, v_hbm, chunks_ref, running_ref, decay_ref, k_ref, v_ref, sems):
-    copies = load(sems, (decay_hbm, decay_ref), (k_hbm, k_ref), (v_hbm, v_ref))
+    blocks = [slice(128 * h, 128 * h + 128) for h in range(decay_ref.shape[0])]
+    pairs = [(decay_hbm, decay_ref)]
+    for cols in blocks:
+        pairs += [(k_hbm.at[:, cols], k_ref.at[:, cols]), (v_hbm.at[:, cols], v_ref.at[:, cols])]
+    copies = load(sems, *pairs)
     copies[0].wait()
     heads, length = decay_ref.shape
     running = jnp.concatenate([decay_ref[...]] * (8 // heads), axis=0)
@@ -39,16 +43,14 @@
         running += jnp.where(lane >= shift, pltpu.roll(running, shift, 1), 0.0)
         shift *= 2
     running_ref[...] = running
-    column = running.T
-    copies[1].wait()
-    copies[2].wait()
-    for h in range(heads):
-        cols = slice(128 * h, 128 * h + 128)
-        total = column[length - 1 : length, h : h + 1]
-        weight = jnp.exp(total - column[:, h : h + 1])
-        high, low = split(k_ref[:, cols].astype(F32) * weight)
-        values = v_ref[:, cols]
-        state = dot(high, values, TN) + dot(low, values, TN)
+    for h, cols in enumerate(blocks):
+        total = running[h : h + 1, length - 1 : length]
+        weight = jnp.exp(total - running[h : h + 1, :])
+        copies[1 + 2 * h].wait()
+        high, low = split(k_ref[:, cols].T.astype(F32) * weight)
+        copies[2 + 2 * h].wait()
+        both = dot(jnp.concatenate([high, low], axis=0), v_ref[:, cols])
+        state = both[:128] + both[128:]
         chunks_ref[8 * h : 8 * h + 8, 0:16, 0, :] = state.reshape(8, 16, 128)
         chunks_ref[8 * h : 8 * h + 8, 16, 0, :] = jnp.broadcast_to(total, (8, 128))
 
@@ -110,7 +112,8 @@
         inputs[h].wait()
         q = q_ref[:, cols]
         inner = (early_ref if h < 2 else late_ref)[:, 128 * (h % 2) : 128 * (h % 2) + 128]
-        attention = (dot(q, high) + dot(q, low)) * growth[:, h : h + 1] + inner
+        both = dot(q, jnp.concatenate([high, low], axis=1))
+        attention = (both[:, :128] + both[:, 128:]) * growth[:, h : h + 1] + inner
         term = jnp.sum(attention * attention, axis=1, keepdims=True)
         squares = term if squares is None else squares + term
         features_ref[:, :, cols] = (attention * gain_ref[:, cols]).astype(BF16).reshape(parts, share, 128)
@@ -195,7 +198,7 @@
         state_kernel,
         [((32, 17, 1, 128), F32), ((8, length), F32)],
         [HBM] * 3,
-        scratch=[pltpu.VMEM(log_decay.shape, F32), pltpu.VMEM(k.shape, BF16), pltpu.VMEM(v.shape, BF16), dma((3,))],
+        scratch=[pltpu.VMEM(log_decay.shape, F32), pltpu.VMEM(k.shape, BF16), pltpu.VMEM(v.shape, BF16), dma((9,))],
         vmem=253 * 2**18,
     )(log_decay, k, v)
     everyone = lax.all_to_all(chunks, "seg", 0, 0, tiled=True)
@@ -207,7 +210,7 @@
     (mine,) = call(prefix_kernel, [((32, 16, 128), F32)], [SMEM, VMEM])(parent, everyone)
     prefix = lax.all_to_all(mine, "seg", 0, 0, tiled=True).reshape(4, 128, 128)
     (late,) = call(
-        functools.partial(within_kernel, 2), [((length, width // 2), F32)], [HBM] * 3 + [VMEM], scratch=inputs, flops=2**30
+        functools.partial(within_kernel, 2), [((length, width // 2), F32)], [HBM] * 3 + [VMEM], scratch=inputs, flops=2**30, vmem=6*2**20
     )(q, k, v, running)
     me = lax.axis_index("head")
     y, core = me >> 1, me & 1

time: 136 us -> 137 us (level)
  no operation moved by 1% of the time
where the time goes in v6:
time: 137 us; the launch traced here: 136 us
  waiting for transfers between devices  54.6 us (40%)
  starting transfers between devices  47.7 us (35%)
  Pallas kernels  21.5 us (16%)
  local copies, waits for them, and re-layouts  10.5 us (8%)
    ppermute x9, waiting for transfers between devices, per_device(): arrived = [lax.ppermute(total, 'head', RING) for total in totals]  47.4 us
    ppermute x9, starting transfers between devices, per_device(): arrived = [lax.ppermute(total, 'head', RING) for total in totals]  17.4 us
    ppermute x12, starting transfers between devices, per_device(): lax.ppermute(send[0], 'head', SWAP)  12 us
    all_to_all x1, starting transfers between devices, per_device(): everyone = lax.all_to_all(chunks, 'seg', 0, 0, tiled=True)  11.9 us
    unnamed x32, local copies, waits for them, and re-layouts  10.5 us
    pallas_call x12, Pallas kernels, project(): call(functools.partial(project_kernel, start, size, first), [((1, share,...  7.03 us
    all_to_all x1, starting transfers between devices, per_device(): prefix = lax.all_to_all(mine, 'seg', 0, 0, tiled=True).reshape(4, 128, 128)  6.46 us
    all_to_all x1, waiting for transfers between devices, per_device(): prefix = lax.all_to_all(mine, 'seg', 0, 0, tiled=True).reshape(4, 128, 128)  4.4 us
  transfers between devices with their start and end apart: 23, of which 10 were waited for; matrix products, arithmetic and copies ran while one was open for 1% of the time, Pallas kernels for 9%

profile of v6, /device:TPU:1, one launch (start us, length us, event | category | flops | bytes accessed | tf_op | source)
XLA Modules:
  0.0 136.1 jit_solution(449476014436487655)
XLA Ops:
  0.0 3.7 %shard_map.73 = (f32[32,17,1,128]{3,2,1,0:T(1,128)}, f32[8,768]{1,0:T(8,128)}) custom-call(f32[4,768]{1,0:T(4,128)} %decay_hbm.1, bf16[768,512]{1,0:T(8,128)(2,1)} %k_hbm.5, bf16[768,512]{1,0:T(8,128)(2,1)} %v_hbm.5), custom_call_target="tpu_custom_call" | custom-call | flops 268435456 | bytes 1048576 | tf_op jit(solution)/shard_map/pallas_call | solution.py:197
  3.7 11.9 %all-to-all-start = ((f32[32,17,1,128]{3,2,1,0:T(1,128)}), f32[32,17,1,128]{3,2,1,0:T(1,128)S(1)}, u32[]{:S(2)}, u32[]{:S(2)}) async-start(f32[32,17,1,128]{3,2,1,0:T(1,128)} %get-tuple-element.38), calls=%async_computation | async-start | bytes 557056 | tf_op jit(solution)/shard_map/all_to_all | solution.py:204
  15.6 1.1 copy-done
  16.8 1.1 copy-done.6
  17.9 1.1 copy-done.8
  19.0 0.7 copy-done.10
  19.8 2.0 %shard_map.74.early_ref = f32[768,256]{1,0:T(8,128)S(1)} custom-call(bf16[768,512]{1,0:T(8,128)(2,1)S(1)} %copy-done, bf16[768,512]{1,0:T(8,128)(2,1)S(1)} %copy-done.6, bf16[768,512]{1,0:T(8,128)(2,1)S(1)} %copy-done.8, f32[8,768]{1,0:T(8,128)S(1)} %copy-done.10), custom_call_target="tpu_custom_call" | custom-call | flops 1073741824 | bytes 1048576 | tf_op jit(solution)/shard_map/pallas_call | solution.py:206
  21.7 0.9 copy-done.2
  22.6 2.8 %all-to-all-done.all_ref = f32[32,17,1,128]{3,2,1,0:T(1,128)S(1)} async-done(((f32[32,17,1,128]{3,2,1,0:T(1,128)}), f32[32,17,1,128]{3,2,1,0:T(1,128)S(1)}, u32[]{:S(2)}, u32[]{:S(2)}) %all-to-all-start) | async-done | bytes 278560 | tf_op jit(solution)/shard_map/all_to_all | solution.py:204
  25.4 1.6 %shard_map.75 = f32[32,16,128]{2,1,0:T(8,128)} custom-call(s32[32]{0:T(128)S(1)} %copy-done.13, f32[32,17,1,128]{3,2,1,0:T(1,128)S(1)} %all-to-all-done.all_ref), custom_call_target="tpu_custom_call" | custom-call | flops 268435456 | bytes 1048576 | tf_op jit(solution)/shard_map/pallas_call | solution.py:210
  27.0 6.5 %all-to-all-start.1 = ((f32[32,16,128]{2,1,0:T(8,128)}), f32[32,16,128]{2,1,0:T(8,128)S(1)}, u32[]{:S(2)}, u32[]{:S(2)}) async-start(f32[32,16,128]{2,1,0:T(8,128)} %shard_map.75), calls=%async_computation.1 | async-start | bytes 524288 | tf_op jit(solution)/shard_map/all_to_all | solution.py:211
  33.5 1.1 copy-done.7
  34.7 1.1 copy-done.9
  35.8 2.0 %shard_map.76.late_ref = f32[768,256]{1,0:T(8,128)S(1)} custom-call(bf16[768,512]{1,0:T(8,128)(2,1)S(1)} %copy-done.1, bf16[768,512]{1,0:T(8,128)(2,1)S(1)} %copy-done.7, bf16[768,512]{1,0:T(8,128)(2,1)S(1)} %copy-done.9, f32[8,768]{1,0:T(8,128)S(1)} %copy-done.11), custom_call_target="tpu_custom_call" | custom-call | flops 1073741824 | bytes 1048576 | tf_op jit(solution)/shard_map/pallas_call | solution.py:212
  37.8 0.9 copy-done.4
  38.7 4.4 %all-to-all-done.1 = f32[32,16,128]{2,1,0:T(8,128)S(1)} async-done(((f32[32,16,128]{2,1,0:T(8,128)}), f32[32,16,128]{2,1,0:T(8,128)S(1)}, u32[]{:S(2)}, u32[]{:S(2)}) %all-to-all-start.1) | async-done | bytes 262176 | tf_op jit(solution)/shard_map/all_to_all | solution.py:211
  43.1 1.1 copy-done.3
  44.2 1.1 copy-done.5
  45.4 2.6 %shard_map.77 = (bf16[8,96,512]{2,1,0:T(8,128)(2,1)S(1)}, f32[8,96,128]{2,1,0:T(8,128)S(1)}) custom-call(s32[8]{0:T(128)S(1)} %pad_add_fusion.index_ref, bf16[768,512]{1,0:T(8,128)(2,1)S(1)} %copy-done.1, f32[4,128,128]{2,1,0:T(8,128)S(1)} %bitcast.52, f32[768,256]{1,0:T(8,128)S(1)} %copy-done.3, f32[768,256]{1,0:T(8,128)S(1)} %copy-done.5, ...), custom_call_target="tpu_custom_call" | custom-call | flops 268435456 | bytes 1048576 | tf_op jit(solution)/shard_map/pallas_call | solution.py:224
  48.0 0.5 shard_map.78
  48.5 3.7 %collective-permute-start = (f32[96,1664]{1,0:T(8,128)S(1)}, f32[96,1664]{1,0:T(8,128)S(1)}, u32[]{:S(2)}, u32[]{:S(2)}) collective-permute-start(f32[96,1664]{1,0:T(8,128)S(1)} %bitcast.65), channel_id=1, source_target_pairs={{0,1},{1,0},{2,3},{3,2},{4,5},{5,4},{6,7},{7,6},{8,9},{9,8},{10,11... | collective-permute-start | bytes 1916936 | tf_op jit(solution)/shard_map/ppermute | solution.py:246
  52.2 0.6 shard_map.79
  52.8 0.1 collective-permute-start.1
  52.9 0.7 shard_map.80
  53.6 0.6 collective-permute-start.2
  54.2 2.8 %collective-permute-start.10 = (f32[96,1664]{1,0:T(8,128)S(1)}, f32[96,1664]{1,0:T(8,128)S(1)}, u32[]{:S(2)}, u32[]{:S(2)}) collective-permute-start(f32[96,1664]{1,0:T(8,128)S(1)} %bitcast_add_fusion.11.refs_0_), channel_id=1, source_target_pairs={{0,2},{1,7},{2,4},{3,1},{4,6},{5,3},{6,0},{7,5},{8,10},{9,15},{10,... | collective-permute-start | bytes 1916936 | tf_op jit(solution)/shard_map/ppermute | solution.py:249
  57.2 1.1 collective-permute-start.16
  58.3 0.1 bitcast_add_fusion.3.refs_2_
  58.4 0.5 shard_map.84
  59.0 0.6 shard_map.88
  59.5 0.6 collective-permute-start.15
  60.1 1.1 collective-permute-start.4
  61.2 0.7 shard_map.81
  61.9 2.5 %collective-permute-done.10.refs_0_ = f32[96,1664]{1,0:T(8,128)S(1)} collective-permute-done((f32[96,1664]{1,0:T(8,128)S(1)}, f32[96,1664]{1,0:T(8,128)S(1)}, u32[]{:S(2)}, u32[]{:S(2)}) %collective-permute-start.10) | collective-permute-done | bytes 639008 | tf_op jit(solution)/shard_map/ppermute | solution.py:249
  64.4 1.6 %collective-permute-start.3 = (f32[96,2560]{1,0:T(8,128)S(1)}, f32[96,2560]{1,0:T(8,128)S(1)}, u32[]{:S(2)}, u32[]{:S(2)}) collective-permute-start(f32[96,2560]{1,0:T(8,128)S(1)} %bitcast.55), channel_id=1, source_target_pairs={{0,1},{1,0},{2,3},{3,2},{4,5},{5,4},{6,7},{7,6},{8,9},{9,8},{10,11... | collective-permute-start | bytes 2949128 | tf_op jit(solution)/shard_map/ppermute | solution.py:246
  66.1 0.5 shard_map.86
  66.5 6.3 %collective-permute-done.16.refs_0_ = f32[96,2048]{1,0:T(8,128)S(1)} collective-permute-done((f32[96,2048]{1,0:T(8,128)S(1)}, f32[96,2048]{1,0:T(8,128)S(1)}, u32[]{:S(2)}, u32[]{:S(2)}) %collective-permute-start.16) | collective-permute-done | bytes 786464 | tf_op jit(solution)/shard_map/ppermute | solution.py:249
  72.8 1.6 %collective-permute-start.13 = (f32[96,1664]{1,0:T(8,128)S(1)}, f32[96,1664]{1,0:T(8,128)S(1)}, u32[]{:S(2)}, u32[]{:S(2)}) collective-permute-start(f32[96,1664]{1,0:T(8,128)S(1)} %bitcast.62), channel_id=1, source_target_pairs={{0,1},{1,0},{2,3},{3,2},{4,5},{5,4},{6,7},{7,6},{8,9},{9,8},{10,11... | collective-permute-start | bytes 1916936 | tf_op jit(solution)/shard_map/ppermute | solution.py:246
  74.5 0.6 shard_map.90
  75.3 2.1 %collective-permute-start.11 = (f32[96,1664]{1,0:T(8,128)S(1)}, f32[96,1664]{1,0:T(8,128)S(1)}, u32[]{:S(2)}, u32[]{:S(2)}) collective-permute-start(f32[96,1664]{1,0:T(8,128)S(1)} %fusion.5), channel_id=1, source_target_pairs={{0,2},{1,7},{2,4},{3,1},{4,6},{5,3},{6,0},{7,5},{8,10},{9,15},{10,... | collective-permute-start | bytes 1916936 | tf_op jit(solution)/shard_map/ppermute | solution.py:249
  77.3 0.1 fusion.3
  77.6 5.8 %collective-permute-done.4.refs_0_ = f32[96,2560]{1,0:T(8,128)S(1)} collective-permute-done((f32[96,2560]{1,0:T(8,128)S(1)}, f32[96,2560]{1,0:T(8,128)S(1)}, u32[]{:S(2)}, u32[]{:S(2)}) %collective-permute-start.4) | collective-permute-done | bytes 983072 | tf_op jit(solution)/shard_map/ppermute | solution.py:249
  83.4 0.1 fusion.1
  83.5 3.2 %collective-permute-start.5 = (f32[96,2560]{1,0:T(8,128)S(1)}, f32[96,2560]{1,0:T(8,128)S(1)}, u32[]{:S(2)}, u32[]{:S(2)}) collective-permute-start(f32[96,2560]{1,0:T(8,128)S(1)} %fusion.1), channel_id=1, source_target_pairs={{0,2},{1,7},{2,4},{3,1},{4,6},{5,3},{6,0},{7,5},{8,10},{9,15},{10,... | collective-permute-start | bytes 2949128 | tf_op jit(solution)/shard_map/ppermute | solution.py:249
  86.7 0.7 shard_map.83
  87.4 2.8 %collective-permute-done.11.refs_0_ = f32[96,1664]{1,0:T(8,128)S(1)} collective-permute-done((f32[96,1664]{1,0:T(8,128)S(1)}, f32[96,1664]{1,0:T(8,128)S(1)}, u32[]{:S(2)}, u32[]{:S(2)}) %collective-permute-start.11) | collective-permute-done | bytes 639008 | tf_op jit(solution)/shard_map/ppermute | solution.py:249
  90.2 1.6 %collective-permute-start.7 = (f32[96,2560]{1,0:T(8,128)S(1)}, f32[96,2560]{1,0:T(8,128)S(1)}, u32[]{:S(2)}, u32[]{:S(2)}) collective-permute-start(f32[96,2560]{1,0:T(8,128)S(1)} %bitcast.54), channel_id=1, source_target_pairs={{0,1},{1,0},{2,3},{3,2},{4,5},{5,4},{6,7},{7,6},{8,9},{9,8},{10,11... | collective-permute-start | bytes 2949128 | tf_op jit(solution)/shard_map/ppermute | solution.py:246
  91.9 0.5 shard_map.85
  92.6 2.0 %collective-permute-start.14 = (f32[96,1664]{1,0:T(8,128)S(1)}, f32[96,1664]{1,0:T(8,128)S(1)}, u32[]{:S(2)}, u32[]{:S(2)}) collective-permute-start(f32[96,1664]{1,0:T(8,128)S(1)} %fusion.4), channel_id=1, source_target_pairs={{0,2},{1,7},{2,4},{3,1},{4,6},{5,3},{6,0},{7,5},{8,10},{9,15},{10,... | collective-permute-start | bytes 1916936 | tf_op jit(solution)/shard_map/ppermute | solution.py:249
  94.6 4.0 %collective-permute-done.17.refs_0_ = f32[96,2048]{1,0:T(8,128)S(1)} collective-permute-done((f32[96,2048]{1,0:T(8,128)S(1)}, f32[96,2048]{1,0:T(8,128)S(1)}, u32[]{:S(2)}, u32[]{:S(2)}) %collective-permute-start.17) | collective-permute-done | bytes 786464 | tf_op jit(solution)/shard_map/ppermute | solution.py:249
  98.7 0.1 fusion.2
  98.8 3.4 %collective-permute-start.20 = (f32[96,2048]{1,0:T(8,128)S(1)}, f32[96,2048]{1,0:T(8,128)S(1)}, u32[]{:S(2)}, u32[]{:S(2)}) collective-permute-start(f32[96,2048]{1,0:T(8,128)S(1)} %fusion.2), channel_id=1, source_target_pairs={{0,2},{1,7},{2,4},{3,1},{4,6},{5,3},{6,0},{7,5},{8,10},{9,15},{10,... | collective-permute-start | bytes 2359304 | tf_op jit(solution)/shard_map/ppermute | solution.py:249
  102.2 0.6 shard_map.89
  103.0 13.1 %collective-permute-done.14.refs_1_ = f32[96,1664]{1,0:T(8,128)S(1)} collective-permute-done((f32[96,1664]{1,0:T(8,128)S(1)}, f32[96,1664]{1,0:T(8,128)S(1)}, u32[]{:S(2)}, u32[]{:S(2)}) %collective-permute-start.14) | collective-permute-done | bytes 639008 | tf_op jit(solution)/shard_map/ppermute | solution.py:249
  116.0 0.8 shard_map.87
  116.9 0.7 shard_map.82
  117.6 1.7 %collective-permute-start.6 = (f32[96,2560]{1,0:T(8,128)S(1)}, f32[96,2560]{1,0:T(8,128)S(1)}, u32[]{:S(2)}, u32[]{:S(2)}) collective-permute-start(f32[96,2560]{1,0:T(8,128)S(1)} %bitcast.56), channel_id=1, source_target_pairs={{0,1},{1,0},{2,3},{3,2},{4,5},{5,4},{6,7},{7,6},{8,9},{9,8},{10,11... | collective-permute-start | bytes 2949128 | tf_op jit(solution)/shard_map/ppermute | solution.py:246
  119.3 0.1 fusion
  119.5 1.6 %collective-permute-start.8 = (f32[96,2560]{1,0:T(8,128)S(1)}, f32[96,2560]{1,0:T(8,128)S(1)}, u32[]{:S(2)}, u32[]{:S(2)}) collective-permute-start(f32[96,2560]{1,0:T(8,128)S(1)} %fusion), channel_id=1, source_target_pairs={{0,2},{1,7},{2,4},{3,1},{4,6},{5,3},{6,0},{7,5},{8,10},{9,15},{10,... | collective-permute-start | bytes 2949128 | tf_op jit(solution)/shard_map/ppermute | solution.py:249
  121.2 3.3 %collective-permute-done.20.refs_1_ = f32[96,2048]{1,0:T(8,128)S(1)} collective-permute-done((f32[96,2048]{1,0:T(8,128)S(1)}, f32[96,2048]{1,0:T(8,128)S(1)}, u32[]{:S(2)}, u32[]{:S(2)}) %collective-permute-start.20) | collective-permute-done | bytes 786464 | tf_op jit(solution)/shard_map/ppermute | solution.py:249
  124.5 0.9 shard_map.91.refs_3_
  125.4 0.1 bitcast_add_fusion.1.refs_0_
  125.5 9.5 %collective-permute-done.8.refs_1_ = f32[96,2560]{1,0:T(8,128)S(1)} collective-permute-done((f32[96,2560]{1,0:T(8,128)S(1)}, f32[96,2560]{1,0:T(8,128)S(1)}, u32[]{:S(2)}, u32[]{:S(2)}) %collective-permute-start.8) | collective-permute-done | bytes 983072 | tf_op jit(solution)/shard_map/ppermute | solution.py:249
  135.0 0.9 shard_map.92
  (49 shorter events, 1.1 us)
Async XLA Ops:
  3.7 21.6 %all-to-all-start = ((f32[32,17,1,128]{3,2,1,0:T(1,128)}), f32[32,17,1,128]{3,2,1,0:T(1,128)S(1)}, u32[]{:S(2)}, u32[]{:S(2)}) async-start(f32[32,17,1,128]{3,2,1,0:T(1,128)} %get-tuple-element.38), calls=%async_computation | async-start | bytes 557056 | tf_op jit(solution)/shard_map/all_to_all | solution.py:204
  15.6 1.1 copy-start
  16.8 1.1 copy-start.6
  17.9 1.1 copy-start.8
  19.0 0.7 copy-start.10
  19.8 5.6 %copy-start.13 = (s32[32]{0:T(128)S(1)}, s32[32]{0:T(128)}, u32[]{:S(2)}) copy-start(s32[32]{0:T(128)} %parent_ref.1) | copy-start | bytes 388
  21.7 0.9 copy-start.2
  22.6 10.9 %copy-start.1 = (bf16[768,512]{1,0:T(8,128)(2,1)S(1)}, bf16[768,512]{1,0:T(8,128)(2,1)}, u32[]{:S(2)}) copy-start(bf16[768,512]{1,0:T(8,128)(2,1)} %q_hbm.5) | copy-start | bytes 2359300
  22.6 10.9 %copy-start.11 = (f32[8,768]{1,0:T(8,128)S(1)}, f32[8,768]{1,0:T(8,128)}, u32[]{:S(2)}) copy-start(f32[8,768]{1,0:T(8,128)} %get-tuple-element.42.running_ref) | copy-start | bytes 73732
  27.0 16.1 %all-to-all-start.1 = ((f32[32,16,128]{2,1,0:T(8,128)}), f32[32,16,128]{2,1,0:T(8,128)S(1)}, u32[]{:S(2)}, u32[]{:S(2)}) async-start(f32[32,16,128]{2,1,0:T(8,128)} %shard_map.75), calls=%async_computation.1 | async-start | bytes 524288 | tf_op jit(solution)/shard_map/all_to_all | solution.py:211
  33.5 1.1 copy-start.7
  34.7 1.1 copy-start.9
  35.8 7.3 %copy-start.12 = (f32[512]{0:T(512)S(1)}, f32[512]{0:T(512)}, u32[]{:S(2)}) copy-start(f32[512]{0:T(512)} %param.12) | copy-start | bytes 6148
  35.8 12.1 %slice-start = ((s8[6291456]{0:T(1024)(128)(4,1)}), s8[2097152]{0:T(1024)(128)(4,1)S(1)}, s32[]{:S(2)}) async-start(s8[6291456]{0:T(1024)(128)(4,1)} %bitcast.50), calls=%async_computation.2 | async-start | bytes 4194304
  37.8 0.9 copy-start.4
  43.1 1.1 copy-start.3
  44.2 1.1 copy-start.5
  45.4 2.6 %slice-start.1 = ((s8[6291456]{0:T(1024)(128)(4,1)}), s8[4194304]{0:T(1024)(128)(4,1)S(1)}, s32[]{:S(2)}) async-start(s8[6291456]{0:T(1024)(128)(4,1)} %bitcast.50), calls=%async_computation.3 | async-start | bytes 8388608
  48.5 5.7 %collective-permute-start = (f32[96,1664]{1,0:T(8,128)S(1)}, f32[96,1664]{1,0:T(8,128)S(1)}, u32[]{:S(2)}, u32[]{:S(2)}) collective-permute-start(f32[96,1664]{1,0:T(8,128)S(1)} %bitcast.65), channel_id=1, source_target_pairs={{0,1},{1,0},{2,3},{3,2},{4,5},{5,4},{6,7},{7,6},{8,9},{9,8},{10,11... | collective-permute-start | bytes 1916936 | tf_op jit(solution)/shard_map/ppermute | solution.py:246
  52.8 4.3 %collective-permute-start.1 = (f32[96,2048]{1,0:T(8,128)S(1)}, f32[96,2048]{1,0:T(8,128)S(1)}, u32[]{:S(2)}, u32[]{:S(2)}) collective-permute-start(f32[96,2048]{1,0:T(8,128)S(1)} %bitcast.61), channel_id=1, source_target_pairs={{0,1},{1,0},{2,3},{3,2},{4,5},{5,4},{6,7},{7,6},{8,9},{9,8},{10,11... | collective-permute-start | bytes 2359304 | tf_op jit(solution)/shard_map/ppermute | solution.py:246
  53.6 4.7 %collective-permute-start.2 = (f32[96,2560]{1,0:T(8,128)S(1)}, f32[96,2560]{1,0:T(8,128)S(1)}, u32[]{:S(2)}, u32[]{:S(2)}) collective-permute-start(f32[96,2560]{1,0:T(8,128)S(1)} %bitcast.57), channel_id=1, source_target_pairs={{0,1},{1,0},{2,3},{3,2},{4,5},{5,4},{6,7},{7,6},{8,9},{9,8},{10,11... | collective-permute-start | bytes 2949128 | tf_op jit(solution)/shard_map/ppermute | solution.py:246
  54.2 10.2 %collective-permute-start.10 = (f32[96,1664]{1,0:T(8,128)S(1)}, f32[96,1664]{1,0:T(8,128)S(1)}, u32[]{:S(2)}, u32[]{:S(2)}) collective-permute-start(f32[96,1664]{1,0:T(8,128)S(1)} %bitcast_add_fusion.11.refs_0_), channel_id=1, source_target_pairs={{0,2},{1,7},{2,4},{3,1},{4,6},{5,3},{6,0},{7,5},{8,10},{9,15},{10,... | collective-permute-start | bytes 1916936 | tf_op jit(solution)/shard_map/ppermute | solution.py:249
  57.2 15.7 %collective-permute-start.16 = (f32[96,2048]{1,0:T(8,128)S(1)}, f32[96,2048]{1,0:T(8,128)S(1)}, u32[]{:S(2)}, u32[]{:S(2)}) collective-permute-start(f32[96,2048]{1,0:T(8,128)S(1)} %bitcast_add_fusion.7.refs_1_), channel_id=1, source_target_pairs={{0,2},{1,7},{2,4},{3,1},{4,6},{5,3},{6,0},{7,5},{8,10},{9,15},{10,... | collective-permute-start | bytes 2359304 | tf_op jit(solution)/shard_map/ppermute | solution.py:249
  58.9 16.2 %collective-permute-start.9 = (f32[96,1664]{1,0:T(8,128)S(1)}, f32[96,1664]{1,0:T(8,128)S(1)}, u32[]{:S(2)}, u32[]{:S(2)}) collective-permute-start(f32[96,1664]{1,0:T(8,128)S(1)} %bitcast.63), channel_id=1, source_target_pairs={{0,1},{1,0},{2,3},{3,2},{4,5},{5,4},{6,7},{7,6},{8,9},{9,8},{10,11... | collective-permute-start | bytes 1916936 | tf_op jit(solution)/shard_map/ppermute | solution.py:246
  59.5 15.7 %collective-permute-start.15 = (f32[96,2048]{1,0:T(8,128)S(1)}, f32[96,2048]{1,0:T(8,128)S(1)}, u32[]{:S(2)}, u32[]{:S(2)}) collective-permute-start(f32[96,2048]{1,0:T(8,128)S(1)} %bitcast.60), channel_id=1, source_target_pairs={{0,1},{1,0},{2,3},{3,2},{4,5},{5,4},{6,7},{7,6},{8,9},{9,8},{10,11... | collective-permute-start | bytes 2359304 | tf_op jit(solution)/shard_map/ppermute | solution.py:246
  60.1 23.2 %collective-permute-start.4 = (f32[96,2560]{1,0:T(8,128)S(1)}, f32[96,2560]{1,0:T(8,128)S(1)}, u32[]{:S(2)}, u32[]{:S(2)}) collective-permute-start(f32[96,2560]{1,0:T(8,128)S(1)} %bitcast_add_fusion.3.refs_2_), channel_id=1, source_target_pairs={{0,2},{1,7},{2,4},{3,1},{4,6},{5,3},{6,0},{7,5},{8,10},{9,15},{10,... | collective-permute-start | bytes 2949128 | tf_op jit(solution)/shard_map/ppermute | solution.py:249
  64.4 13.1 %collective-permute-start.3 = (f32[96,2560]{1,0:T(8,128)S(1)}, f32[96,2560]{1,0:T(8,128)S(1)}, u32[]{:S(2)}, u32[]{:S(2)}) collective-permute-start(f32[96,2560]{1,0:T(8,128)S(1)} %bitcast.55), channel_id=1, source_target_pairs={{0,1},{1,0},{2,3},{3,2},{4,5},{5,4},{6,7},{7,6},{8,9},{9,8},{10,11... | collective-permute-start | bytes 2949128 | tf_op jit(solution)/shard_map/ppermute | solution.py:246
  72.8 19.5 %collective-permute-start.13 = (f32[96,1664]{1,0:T(8,128)S(1)}, f32[96,1664]{1,0:T(8,128)S(1)}, u32[]{:S(2)}, u32[]{:S(2)}) collective-permute-start(f32[96,1664]{1,0:T(8,128)S(1)} %bitcast.62), channel_id=1, source_target_pairs={{0,1},{1,0},{2,3},{3,2},{4,5},{5,4},{6,7},{7,6},{8,9},{9,8},{10,11... | collective-permute-start | bytes 1916936 | tf_op jit(solution)/shard_map/ppermute | solution.py:246
  75.1 17.5 %collective-permute-start.19 = (f32[96,2048]{1,0:T(8,128)S(1)}, f32[96,2048]{1,0:T(8,128)S(1)}, u32[]{:S(2)}, u32[]{:S(2)}) collective-permute-start(f32[96,2048]{1,0:T(8,128)S(1)} %bitcast.58), channel_id=1, source_target_pairs={{0,1},{1,0},{2,3},{3,2},{4,5},{5,4},{6,7},{7,6},{8,9},{9,8},{10,11... | collective-permute-start | bytes 2359304 | tf_op jit(solution)/shard_map/ppermute | solution.py:246
  75.3 14.9 %collective-permute-start.11 = (f32[96,1664]{1,0:T(8,128)S(1)}, f32[96,1664]{1,0:T(8,128)S(1)}, u32[]{:S(2)}, u32[]{:S(2)}) collective-permute-start(f32[96,1664]{1,0:T(8,128)S(1)} %fusion.5), channel_id=1, source_target_pairs={{0,2},{1,7},{2,4},{3,1},{4,6},{5,3},{6,0},{7,5},{8,10},{9,15},{10,... | collective-permute-start | bytes 1916936 | tf_op jit(solution)/shard_map/ppermute | solution.py:249
  77.5 21.2 %collective-permute-start.17 = (f32[96,2048]{1,0:T(8,128)S(1)}, f32[96,2048]{1,0:T(8,128)S(1)}, u32[]{:S(2)}, u32[]{:S(2)}) collective-permute-start(f32[96,2048]{1,0:T(8,128)S(1)} %fusion.3), channel_id=1, source_target_pairs={{0,2},{1,7},{2,4},{3,1},{4,6},{5,3},{6,0},{7,5},{8,10},{9,15},{10,... | collective-permute-start | bytes 2359304 | tf_op jit(solution)/shard_map/ppermute | solution.py:249
  83.5 33.4 %collective-permute-start.5 = (f32[96,2560]{1,0:T(8,128)S(1)}, f32[96,2560]{1,0:T(8,128)S(1)}, u32[]{:S(2)}, u32[]{:S(2)}) collective-permute-start(f32[96,2560]{1,0:T(8,128)S(1)} %fusion.1), channel_id=1, source_target_pairs={{0,2},{1,7},{2,4},{3,1},{4,6},{5,3},{6,0},{7,5},{8,10},{9,15},{10,... | collective-permute-start | bytes 2949128 | tf_op jit(solution)/shard_map/ppermute | solution.py:249
  90.2 29.1 %collective-permute-start.7 = (f32[96,2560]{1,0:T(8,128)S(1)}, f32[96,2560]{1,0:T(8,128)S(1)}, u32[]{:S(2)}, u32[]{:S(2)}) collective-permute-start(f32[96,2560]{1,0:T(8,128)S(1)} %bitcast.54), channel_id=1, source_target_pairs={{0,1},{1,0},{2,3},{3,2},{4,5},{5,4},{6,7},{7,6},{8,9},{9,8},{10,11... | collective-permute-start | bytes 2949128 | tf_op jit(solution)/shard_map/ppermute | solution.py:246
  92.4 10.4 %collective-permute-start.12 = (f32[96,1664]{1,0:T(8,128)S(1)}, f32[96,1664]{1,0:T(8,128)S(1)}, u32[]{:S(2)}, u32[]{:S(2)}) collective-permute-start(f32[96,1664]{1,0:T(8,128)S(1)} %bitcast.64), channel_id=1, source_target_pairs={{0,1},{1,0},{2,3},{3,2},{4,5},{5,4},{6,7},{7,6},{8,9},{9,8},{10,11... | collective-permute-start | bytes 1916936 | tf_op jit(solution)/shard_map/ppermute | solution.py:246
  92.6 23.5 %collective-permute-start.14 = (f32[96,1664]{1,0:T(8,128)S(1)}, f32[96,1664]{1,0:T(8,128)S(1)}, u32[]{:S(2)}, u32[]{:S(2)}) collective-permute-start(f32[96,1664]{1,0:T(8,128)S(1)} %fusion.4), channel_id=1, source_target_pairs={{0,2},{1,7},{2,4},{3,1},{4,6},{5,3},{6,0},{7,5},{8,10},{9,15},{10,... | collective-permute-start | bytes 1916936 | tf_op jit(solution)/shard_map/ppermute | solution.py:249
  98.8 25.7 %collective-permute-start.20 = (f32[96,2048]{1,0:T(8,128)S(1)}, f32[96,2048]{1,0:T(8,128)S(1)}, u32[]{:S(2)}, u32[]{:S(2)}) collective-permute-start(f32[96,2048]{1,0:T(8,128)S(1)} %fusion.2), channel_id=1, source_target_pairs={{0,2},{1,7},{2,4},{3,1},{4,6},{5,3},{6,0},{7,5},{8,10},{9,15},{10,... | collective-permute-start | bytes 2359304 | tf_op jit(solution)/shard_map/ppermute | solution.py:249
  102.8 18.3 %collective-permute-start.18 = (f32[96,2048]{1,0:T(8,128)S(1)}, f32[96,2048]{1,0:T(8,128)S(1)}, u32[]{:S(2)}, u32[]{:S(2)}) collective-permute-start(f32[96,2048]{1,0:T(8,128)S(1)} %bitcast.59), channel_id=1, source_target_pairs={{0,1},{1,0},{2,3},{3,2},{4,5},{5,4},{6,7},{7,6},{8,9},{9,8},{10,11... | collective-permute-start | bytes 2359304 | tf_op jit(solution)/shard_map/ppermute | solution.py:246
  117.6 7.8 %collective-permute-start.6 = (f32[96,2560]{1,0:T(8,128)S(1)}, f32[96,2560]{1,0:T(8,128)S(1)}, u32[]{:S(2)}, u32[]{:S(2)}) collective-permute-start(f32[96,2560]{1,0:T(8,128)S(1)} %bitcast.56), channel_id=1, source_target_pairs={{0,1},{1,0},{2,3},{3,2},{4,5},{5,4},{6,7},{7,6},{8,9},{9,8},{10,11... | collective-permute-start | bytes 2949128 | tf_op jit(solution)/shard_map/ppermute | solution.py:246
  119.5 15.5 %collective-permute-start.8 = (f32[96,2560]{1,0:T(8,128)S(1)}, f32[96,2560]{1,0:T(8,128)S(1)}, u32[]{:S(2)}, u32[]{:S(2)}) collective-permute-start(f32[96,2560]{1,0:T(8,128)S(1)} %fusion), channel_id=1, source_target_pairs={{0,2},{1,7},{2,4},{3,1},{4,6},{5,3},{6,0},{7,5},{8,10},{9,15},{10,... | collective-permute-start | bytes 2949128 | tf_op jit(solution)/shard_map/ppermute | solution.py:249

commit v7 on v5

--- a/solution.py
+++ b/solution.py
@@ -95,9 +95,9 @@
 
 
 def mix_kernel(
-    index_ref, q_hbm, prefix_ref, early_ref, late_ref, running_ref, gain_ref, _,
+    place_ref, q_hbm, prefix_ref, early_ref, late_ref, running_ref, gain_ref, _,
     out_ref, squares_out_ref,
-    features_ref, squares_ref, q_ref, sems,
+    q_ref, sems,
 ):
     heads = [slice(128 * h, 128 * h + 128) for h in range(4)]
     inputs = load(sems, *[(q_hbm.at[:, cols], q_ref.at[:, cols]) for cols in heads])
@@ -110,14 +110,16 @@
         inputs[h].wait()
         q = q_ref[:, cols]
         inner = (early_ref if h < 2 else late_ref)[:, 128 * (h % 2) : 128 * (h % 2) + 128]
-        attention = (dot(q, high) + dot(q, low)) * growth[:, h : h + 1] + inner
+        both = dot(q, jnp.concatenate([high, low], axis=1))
+        attention = (both[:, :128] + both[:, 128:]) * growth[:, h : h + 1] + inner
         term = jnp.sum(attention * attention, axis=1, keepdims=True)
         squares = term if squares is None else squares + term
-        features_ref[:, :, cols] = (attention * gain_ref[:, cols]).astype(BF16).reshape(parts, share, 128)
-    squares_ref[...] = jnp.broadcast_to(squares, (parts * share, 128)).reshape(parts, share, 128)
+        features = (attention * gain_ref[:, cols]).astype(BF16).reshape(parts, share, 128)
+        for i in range(parts):
+            out_ref[place_ref[i], :, cols] = features[i]
+    squares = jnp.broadcast_to(squares, (parts * share, 128)).reshape(parts, share, 128)
     for i in range(parts):
-        out_ref[i] = features_ref[index_ref[i]]
-        squares_out_ref[i] = squares_ref[index_ref[i]]
+        squares_out_ref[place_ref[i]] = squares[i]
 
 
 def project_kernel(start, size, first, features_ref, squares_ref, w_ref, *refs):
@@ -207,12 +209,13 @@
     (mine,) = call(prefix_kernel, [((32, 16, 128), F32)], [SMEM, VMEM])(parent, everyone)
     prefix = lax.all_to_all(mine, "seg", 0, 0, tiled=True).reshape(4, 128, 128)
     (late,) = call(
-        functools.partial(within_kernel, 2), [((length, width // 2), F32)], [HBM] * 3 + [VMEM], scratch=inputs, flops=2**30
+        functools.partial(within_kernel, 2), [((length, width // 2), F32)], [HBM] * 3 + [VMEM], scratch=inputs, flops=2**30, vmem=62*2**20
     )(q, k, v, running)
     me = lax.axis_index("head")
     y, core = me >> 1, me & 1
-    way = (1 - 2 * core) * jnp.arange(1, 5, dtype=jnp.int32)
-    blocks = jnp.concatenate([((y - way) & 3) * 2 + core, ((y + way) & 3) * 2 + 1 - core])
+    block = jnp.arange(8, dtype=jnp.int32)
+    steps = (y - (block >> 1)) * (1 - 2 * core)
+    places = jnp.where((block & 1) == core, (steps - 1) & 3, 4 + ((-steps - 1) & 3))
     share = length // 8
     starts = [0, 1536, 3584]
     widths = [1536, 2048, 2560]
@@ -222,10 +225,10 @@
         mix_kernel,
         [((8, share, width), BF16), ((8, share, 128), F32)],
         [SMEM, HBM, VMEM, VMEM, VMEM, VMEM, VMEM, HBM],
-        scratch=[pltpu.VMEM((8, share, width), BF16), pltpu.VMEM((8, share, 128), F32), pltpu.VMEM(q.shape, BF16)]
-        + [dma((4,))],
+        scratch=[pltpu.VMEM(q.shape, BF16), dma((4,))],
+        flops=2**34,
         vmem=50 * 2**20,
-    )(blocks, q, prefix, early, late, running, gain.reshape(1, width), w)
+    )(places, q, prefix, early, late, running, gain.reshape(1, width), w)
 
     def project(start, size, extra, first, after):
         return call(

time: 136 us -> 135 us (level)
  local copies, waits for them, and re-layouts: 10.5 us -> 5.44 us
  Pallas kernels: 21.1 us -> 24 us
    unnamed x32 -> x22, local copies, waits for them, and re-layouts: 10.5 us -> 5.44 us
    pallas_call x1, Pallas kernels: 1.96 us -> 4.92 us  [per_device(): call(functools.partial(within_kernel, 2), [((length, width // 2), F32)],...]
  transfers between devices with their start and end apart: 23 -> 23, of which waited for: 10 -> 10; matrix products, arithmetic and copies ran while one was open for 1% -> 1% of each run, Pallas kernels for 9% -> 11%
where the time goes in v7:
time: 135 us
  waiting for transfers between devices  55.7 us (41%)
  starting transfers between devices  47.8 us (35%)
  Pallas kernels  24 us (18%)
  local copies, waits for them, and re-layouts  5.44 us (4%)
    ppermute x9, waiting for transfers between devices, per_device(): arrived = [lax.ppermute(total, 'head', RING) for total in totals]  47.3 us
    ppermute x9, starting transfers between devices, per_device(): arrived = [lax.ppermute(total, 'head', RING) for total in totals]  17.4 us
    ppermute x12, starting transfers between devices, per_device(): lax.ppermute(send[0], 'head', SWAP)  12 us
    all_to_all x1, starting transfers between devices, per_device(): everyone = lax.all_to_all(chunks, 'seg', 0, 0, tiled=True)  11.9 us
    pallas_call x12, Pallas kernels, project(): call(functools.partial(project_kernel, start, size, first), [((1, share,...  7.01 us
    all_to_all x1, starting transfers between devices, per_device(): prefix = lax.all_to_all(mine, 'seg', 0, 0, tiled=True).reshape(4, 128, 128)  6.46 us
    unnamed x22, local copies, waits for them, and re-layouts  5.44 us
    pallas_call x1, Pallas kernels, per_device(): call(functools.partial(within_kernel, 2), [((length, width // 2), F32)],...  4.92 us
  transfers between devices with their start and end apart: 23, of which 10 were waited for; matrix products, arithmetic and copies ran while one was open for 1% of the time, Pallas kernels for 11%

profile of v7, /device:TPU:1, one launch (start us, length us, event | category | flops | bytes accessed | tf_op | source)
XLA Modules:
  0.0 134.7 jit_solution(12667468121108985198)
XLA Ops:
  0.0 3.3 %shard_map.73 = (f32[32,17,1,128]{3,2,1,0:T(1,128)}, f32[8,768]{1,0:T(8,128)}) custom-call(f32[4,768]{1,0:T(4,128)} %decay_hbm.1, bf16[768,512]{1,0:T(8,128)(2,1)} %k_hbm.5, bf16[768,512]{1,0:T(8,128)(2,1)} %v_hbm.5), custom_call_target="tpu_custom_call" | custom-call | flops 268435456 | bytes 1048576 | tf_op jit(solution)/shard_map/pallas_call | solution.py:196
  3.3 11.9 %all-to-all-start = ((f32[32,17,1,128]{3,2,1,0:T(1,128)}), f32[32,17,1,128]{3,2,1,0:T(1,128)S(1)}, u32[]{:S(2)}, u32[]{:S(2)}) async-start(f32[32,17,1,128]{3,2,1,0:T(1,128)} %get-tuple-element.38), calls=%async_computation | async-start | bytes 557056 | tf_op jit(solution)/shard_map/all_to_all | solution.py:203
  15.2 1.1 copy-done
  16.3 1.1 copy-done.1
  17.5 1.1 copy-done.2
  18.6 0.7 copy-done.4
  19.3 2.0 %shard_map.74.early_ref = f32[768,256]{1,0:T(8,128)S(1)} custom-call(bf16[768,512]{1,0:T(8,128)(2,1)S(1)} %copy-done.2, bf16[768,512]{1,0:T(8,128)(2,1)S(1)} %copy-done, bf16[768,512]{1,0:T(8,128)(2,1)S(1)} %copy-done.1, f32[8,768]{1,0:T(8,128)S(1)} %copy-done.4), custom_call_target="tpu_custom_call" | custom-call | flops 1073741824 | bytes 1048576 | tf_op jit(solution)/shard_map/pallas_call | solution.py:205
  21.3 3.7 %all-to-all-done.all_ref = f32[32,17,1,128]{3,2,1,0:T(1,128)S(1)} async-done(((f32[32,17,1,128]{3,2,1,0:T(1,128)}), f32[32,17,1,128]{3,2,1,0:T(1,128)S(1)}, u32[]{:S(2)}, u32[]{:S(2)}) %all-to-all-start) | async-done | bytes 278560 | tf_op jit(solution)/shard_map/all_to_all | solution.py:203
  25.0 1.6 %shard_map.75 = f32[32,16,128]{2,1,0:T(8,128)} custom-call(s32[32]{0:T(128)S(1)} %copy-done.7, f32[32,17,1,128]{3,2,1,0:T(1,128)S(1)} %all-to-all-done.all_ref), custom_call_target="tpu_custom_call" | custom-call | flops 268435456 | bytes 1048576 | tf_op jit(solution)/shard_map/pallas_call | solution.py:209
  26.5 6.5 %all-to-all-start.1 = ((f32[32,16,128]{2,1,0:T(8,128)}), f32[32,16,128]{2,1,0:T(8,128)S(1)}, u32[]{:S(2)}, u32[]{:S(2)}) async-start(f32[32,16,128]{2,1,0:T(8,128)} %shard_map.75), calls=%async_computation.1 | async-start | bytes 524288 | tf_op jit(solution)/shard_map/all_to_all | solution.py:210
  33.1 4.9 %shard_map.76.late_ref = f32[768,256]{1,0:T(8,128)} custom-call(bf16[768,512]{1,0:T(8,128)(2,1)} %q_hbm.5, bf16[768,512]{1,0:T(8,128)(2,1)} %k_hbm.5, bf16[768,512]{1,0:T(8,128)(2,1)} %v_hbm.5, f32[8,768]{1,0:T(8,128)} %get-tuple-element.42.running_ref), custom_call_target="tpu_custom_call" | custom-call | flops 1073741824 | bytes 1048576 | tf_op jit(solution)/shard_map/pallas_call | solution.py:211
  38.0 4.7 %all-to-all-done.1 = f32[32,16,128]{2,1,0:T(8,128)S(1)} async-done(((f32[32,16,128]{2,1,0:T(8,128)}), f32[32,16,128]{2,1,0:T(8,128)S(1)}, u32[]{:S(2)}, u32[]{:S(2)}) %all-to-all-start.1) | async-done | bytes 262176 | tf_op jit(solution)/shard_map/all_to_all | solution.py:210
  42.7 1.3 copy-done.8
  44.0 2.5 %shard_map.77 = (bf16[8,96,512]{2,1,0:T(8,128)(2,1)S(1)}, f32[8,96,128]{2,1,0:T(8,128)S(1)}) custom-call(s32[8]{0:T(128)S(1)} %compare_select_fusion.place_ref, bf16[768,512]{1,0:T(8,128)(2,1)S(1)} %copy-done.3, f32[4,128,128]{2,1,0:T(8,128)S(1)} %bitcast.52, f32[768,256]{1,0:T(8,128)S(1)} %shard_map.74.early_ref, f32[768,256]{1,0:T(8,128)S(1)} %copy-done.8, ...), custom_call_target="tpu_custom_call" | custom-call | flops 17179869184 | bytes 1048576 | tf_op jit(solution)/shard_map/pallas_call | solution.py:224
  46.6 0.5 shard_map.78
  47.0 3.8 %collective-permute-start = (f32[96,1664]{1,0:T(8,128)S(1)}, f32[96,1664]{1,0:T(8,128)S(1)}, u32[]{:S(2)}, u32[]{:S(2)}) collective-permute-start(f32[96,1664]{1,0:T(8,128)S(1)} %bitcast.64), channel_id=1, source_target_pairs={{0,1},{1,0},{2,3},{3,2},{4,5},{5,4},{6,7},{7,6},{8,9},{9,8},{10,11... | collective-permute-start | bytes 1916936 | tf_op jit(solution)/shard_map/ppermute | solution.py:246
  50.8 0.6 shard_map.79
  51.4 0.1 collective-permute-start.1
  51.5 0.7 shard_map.80
  52.2 0.6 collective-permute-start.2
  52.8 2.8 %collective-permute-start.10 = (f32[96,1664]{1,0:T(8,128)S(1)}, f32[96,1664]{1,0:T(8,128)S(1)}, u32[]{:S(2)}, u32[]{:S(2)}) collective-permute-start(f32[96,1664]{1,0:T(8,128)S(1)} %bitcast_add_fusion.11.refs_0_), channel_id=1, source_target_pairs={{0,2},{1,7},{2,4},{3,1},{4,6},{5,3},{6,0},{7,5},{8,10},{9,15},{10,... | collective-permute-start | bytes 1916936 | tf_op jit(solution)/shard_map/ppermute | solution.py:249
  55.7 1.1 collective-permute-start.16
  56.8 0.1 bitcast_add_fusion.3.refs_2_
  56.9 0.5 shard_map.84
  57.4 0.1 collective-permute-start.9
  57.5 0.6 shard_map.88
  58.1 0.6 collective-permute-start.15
  58.7 1.1 collective-permute-start.4
  59.8 0.7 shard_map.81
  60.5 2.5 %collective-permute-done.10.refs_0_ = f32[96,1664]{1,0:T(8,128)S(1)} collective-permute-done((f32[96,1664]{1,0:T(8,128)S(1)}, f32[96,1664]{1,0:T(8,128)S(1)}, u32[]{:S(2)}, u32[]{:S(2)}) %collective-permute-start.10) | collective-permute-done | bytes 639008 | tf_op jit(solution)/shard_map/ppermute | solution.py:249
  63.0 1.6 %collective-permute-start.3 = (f32[96,2560]{1,0:T(8,128)S(1)}, f32[96,2560]{1,0:T(8,128)S(1)}, u32[]{:S(2)}, u32[]{:S(2)}) collective-permute-start(f32[96,2560]{1,0:T(8,128)S(1)} %bitcast.54), channel_id=1, source_target_pairs={{0,1},{1,0},{2,3},{3,2},{4,5},{5,4},{6,7},{7,6},{8,9},{9,8},{10,11... | collective-permute-start | bytes 2949128 | tf_op jit(solution)/shard_map/ppermute | solution.py:246
  64.6 0.5 shard_map.86
  65.1 6.3 %collective-permute-done.16.refs_0_ = f32[96,2048]{1,0:T(8,128)S(1)} collective-permute-done((f32[96,2048]{1,0:T(8,128)S(1)}, f32[96,2048]{1,0:T(8,128)S(1)}, u32[]{:S(2)}, u32[]{:S(2)}) %collective-permute-start.16) | collective-permute-done | bytes 786464 | tf_op jit(solution)/shard_map/ppermute | solution.py:249
  71.4 1.6 %collective-permute-start.13 = (f32[96,1664]{1,0:T(8,128)S(1)}, f32[96,1664]{1,0:T(8,128)S(1)}, u32[]{:S(2)}, u32[]{:S(2)}) collective-permute-start(f32[96,1664]{1,0:T(8,128)S(1)} %bitcast.61), channel_id=1, source_target_pairs={{0,1},{1,0},{2,3},{3,2},{4,5},{5,4},{6,7},{7,6},{8,9},{9,8},{10,11... | collective-permute-start | bytes 1916936 | tf_op jit(solution)/shard_map/ppermute | solution.py:246
  73.1 0.6 shard_map.90
  73.8 0.1 fusion.5
  73.9 2.0 %collective-permute-start.11 = (f32[96,1664]{1,0:T(8,128)S(1)}, f32[96,1664]{1,0:T(8,128)S(1)}, u32[]{:S(2)}, u32[]{:S(2)}) collective-permute-start(f32[96,1664]{1,0:T(8,128)S(1)} %fusion.5), channel_id=1, source_target_pairs={{0,2},{1,7},{2,4},{3,1},{4,6},{5,3},{6,0},{7,5},{8,10},{9,15},{10,... | collective-permute-start | bytes 1916936 | tf_op jit(solution)/shard_map/ppermute | solution.py:249
  75.9 0.1 fusion.3
  76.0 0.1 collective-permute-start.17
  76.2 5.8 %collective-permute-done.4.refs_0_ = f32[96,2560]{1,0:T(8,128)S(1)} collective-permute-done((f32[96,2560]{1,0:T(8,128)S(1)}, f32[96,2560]{1,0:T(8,128)S(1)}, u32[]{:S(2)}, u32[]{:S(2)}) %collective-permute-start.4) | collective-permute-done | bytes 983072 | tf_op jit(solution)/shard_map/ppermute | solution.py:249
  82.0 0.1 fusion.1
  82.1 3.2 %collective-permute-start.5 = (f32[96,2560]{1,0:T(8,128)S(1)}, f32[96,2560]{1,0:T(8,128)S(1)}, u32[]{:S(2)}, u32[]{:S(2)}) collective-permute-start(f32[96,2560]{1,0:T(8,128)S(1)} %fusion.1), channel_id=1, source_target_pairs={{0,2},{1,7},{2,4},{3,1},{4,6},{5,3},{6,0},{7,5},{8,10},{9,15},{10,... | collective-permute-start | bytes 2949128 | tf_op jit(solution)/shard_map/ppermute | solution.py:249
  85.3 0.7 shard_map.83
  86.0 2.8 %collective-permute-done.11.refs_0_ = f32[96,1664]{1,0:T(8,128)S(1)} collective-permute-done((f32[96,1664]{1,0:T(8,128)S(1)}, f32[96,1664]{1,0:T(8,128)S(1)}, u32[]{:S(2)}, u32[]{:S(2)}) %collective-permute-start.11) | collective-permute-done | bytes 639008 | tf_op jit(solution)/shard_map/ppermute | solution.py:249
  88.8 1.6 %collective-permute-start.7 = (f32[96,2560]{1,0:T(8,128)S(1)}, f32[96,2560]{1,0:T(8,128)S(1)}, u32[]{:S(2)}, u32[]{:S(2)}) collective-permute-start(f32[96,2560]{1,0:T(8,128)S(1)} %bitcast.53), channel_id=1, source_target_pairs={{0,1},{1,0},{2,3},{3,2},{4,5},{5,4},{6,7},{7,6},{8,9},{9,8},{10,11... | collective-permute-start | bytes 2949128 | tf_op jit(solution)/shard_map/ppermute | solution.py:246
  90.4 0.5 shard_map.85
  90.9 0.1 collective-permute-start.12
  91.0 0.1 fusion.4
  91.1 2.0 %collective-permute-start.14 = (f32[96,1664]{1,0:T(8,128)S(1)}, f32[96,1664]{1,0:T(8,128)S(1)}, u32[]{:S(2)}, u32[]{:S(2)}) collective-permute-start(f32[96,1664]{1,0:T(8,128)S(1)} %fusion.4), channel_id=1, source_target_pairs={{0,2},{1,7},{2,4},{3,1},{4,6},{5,3},{6,0},{7,5},{8,10},{9,15},{10,... | collective-permute-start | bytes 1916936 | tf_op jit(solution)/shard_map/ppermute | solution.py:249
  93.2 4.0 %collective-permute-done.17.refs_0_ = f32[96,2048]{1,0:T(8,128)S(1)} collective-permute-done((f32[96,2048]{1,0:T(8,128)S(1)}, f32[96,2048]{1,0:T(8,128)S(1)}, u32[]{:S(2)}, u32[]{:S(2)}) %collective-permute-start.17) | collective-permute-done | bytes 786464 | tf_op jit(solution)/shard_map/ppermute | solution.py:249
  97.2 0.1 fusion.2
  97.3 3.4 %collective-permute-start.20 = (f32[96,2048]{1,0:T(8,128)S(1)}, f32[96,2048]{1,0:T(8,128)S(1)}, u32[]{:S(2)}, u32[]{:S(2)}) collective-permute-start(f32[96,2048]{1,0:T(8,128)S(1)} %fusion.2), channel_id=1, source_target_pairs={{0,2},{1,7},{2,4},{3,1},{4,6},{5,3},{6,0},{7,5},{8,10},{9,15},{10,... | collective-permute-start | bytes 2359304 | tf_op jit(solution)/shard_map/ppermute | solution.py:249
  100.8 0.6 shard_map.89
  101.5 13.1 %collective-permute-done.14.refs_1_ = f32[96,1664]{1,0:T(8,128)S(1)} collective-permute-done((f32[96,1664]{1,0:T(8,128)S(1)}, f32[96,1664]{1,0:T(8,128)S(1)}, u32[]{:S(2)}, u32[]{:S(2)}) %collective-permute-start.14) | collective-permute-done | bytes 639008 | tf_op jit(solution)/shard_map/ppermute | solution.py:249
  114.6 0.8 shard_map.87
  115.5 0.7 shard_map.82
  116.2 1.7 %collective-permute-start.6 = (f32[96,2560]{1,0:T(8,128)S(1)}, f32[96,2560]{1,0:T(8,128)S(1)}, u32[]{:S(2)}, u32[]{:S(2)}) collective-permute-start(f32[96,2560]{1,0:T(8,128)S(1)} %bitcast.55), channel_id=1, source_target_pairs={{0,1},{1,0},{2,3},{3,2},{4,5},{5,4},{6,7},{7,6},{8,9},{9,8},{10,11... | collective-permute-start | bytes 2949128 | tf_op jit(solution)/shard_map/ppermute | solution.py:246
  117.9 0.2 fusion
  118.1 1.6 %collective-permute-start.8 = (f32[96,2560]{1,0:T(8,128)S(1)}, f32[96,2560]{1,0:T(8,128)S(1)}, u32[]{:S(2)}, u32[]{:S(2)}) collective-permute-start(f32[96,2560]{1,0:T(8,128)S(1)} %fusion), channel_id=1, source_target_pairs={{0,2},{1,7},{2,4},{3,1},{4,6},{5,3},{6,0},{7,5},{8,10},{9,15},{10,... | collective-permute-start | bytes 2949128 | tf_op jit(solution)/shard_map/ppermute | solution.py:249
  119.8 3.2 %collective-permute-done.20.refs_1_ = f32[96,2048]{1,0:T(8,128)S(1)} collective-permute-done((f32[96,2048]{1,0:T(8,128)S(1)}, f32[96,2048]{1,0:T(8,128)S(1)}, u32[]{:S(2)}, u32[]{:S(2)}) %collective-permute-start.20) | collective-permute-done | bytes 786464 | tf_op jit(solution)/shard_map/ppermute | solution.py:249
  123.0 0.9 shard_map.91.refs_3_
  123.9 0.2 bitcast_add_fusion.1.refs_0_
  124.1 9.5 %collective-permute-done.8.refs_1_ = f32[96,2560]{1,0:T(8,128)S(1)} collective-permute-done((f32[96,2560]{1,0:T(8,128)S(1)}, f32[96,2560]{1,0:T(8,128)S(1)}, u32[]{:S(2)}, u32[]{:S(2)}) %collective-permute-start.8) | collective-permute-done | bytes 983072 | tf_op jit(solution)/shard_map/ppermute | solution.py:249
  133.6 0.9 shard_map.92
  (38 shorter events, 0.6 us)
Async XLA Ops:
  3.3 21.7 %all-to-all-start = ((f32[32,17,1,128]{3,2,1,0:T(1,128)}), f32[32,17,1,128]{3,2,1,0:T(1,128)S(1)}, u32[]{:S(2)}, u32[]{:S(2)}) async-start(f32[32,17,1,128]{3,2,1,0:T(1,128)} %get-tuple-element.38), calls=%async_computation | async-start | bytes 557056 | tf_op jit(solution)/shard_map/all_to_all | solution.py:203
  15.2 1.1 copy-start
  16.3 1.1 copy-start.1
  17.5 1.1 copy-start.2
  18.6 0.7 copy-start.4
  19.3 5.6 %copy-start.7 = (s32[32]{0:T(128)S(1)}, s32[32]{0:T(128)}, u32[]{:S(2)}) copy-start(s32[32]{0:T(128)} %parent_ref.1) | copy-start | bytes 388
  26.5 16.1 %all-to-all-start.1 = ((f32[32,16,128]{2,1,0:T(8,128)}), f32[32,16,128]{2,1,0:T(8,128)S(1)}, u32[]{:S(2)}, u32[]{:S(2)}) async-start(f32[32,16,128]{2,1,0:T(8,128)} %shard_map.75), calls=%async_computation.1 | async-start | bytes 524288 | tf_op jit(solution)/shard_map/all_to_all | solution.py:210
  33.0 9.6 %copy-start.3 = (bf16[768,512]{1,0:T(8,128)(2,1)S(1)}, bf16[768,512]{1,0:T(8,128)(2,1)}, u32[]{:S(2)}) copy-start(bf16[768,512]{1,0:T(8,128)(2,1)} %q_hbm.5) | copy-start | bytes 2359300
  33.0 9.6 %copy-start.5 = (f32[8,768]{1,0:T(8,128)S(1)}, f32[8,768]{1,0:T(8,128)}, u32[]{:S(2)}) copy-start(f32[8,768]{1,0:T(8,128)} %get-tuple-element.42.running_ref) | copy-start | bytes 73732
  33.0 9.6 %copy-start.6 = (f32[512]{0:T(512)S(1)}, f32[512]{0:T(512)}, u32[]{:S(2)}) copy-start(f32[512]{0:T(512)} %param.12) | copy-start | bytes 6148
  42.7 3.9 %slice-start = ((s8[6291456]{0:T(1024)(128)(4,1)}), s8[4194304]{0:T(1024)(128)(4,1)S(1)}, s32[]{:S(2)}) async-start(s8[6291456]{0:T(1024)(128)(4,1)} %bitcast.50), calls=%async_computation.2 | async-start | bytes 8388608
  42.7 1.3 copy-start.8
  44.0 2.6 %slice-start.1 = ((s8[6291456]{0:T(1024)(128)(4,1)}), s8[2097152]{0:T(1024)(128)(4,1)S(1)}, s32[]{:S(2)}) async-start(s8[6291456]{0:T(1024)(128)(4,1)} %bitcast.50), calls=%async_computation.3 | async-start | bytes 4194304
  47.0 5.7 %collective-permute-start = (f32[96,1664]{1,0:T(8,128)S(1)}, f32[96,1664]{1,0:T(8,128)S(1)}, u32[]{:S(2)}, u32[]{:S(2)}) collective-permute-start(f32[96,1664]{1,0:T(8,128)S(1)} %bitcast.64), channel_id=1, source_target_pairs={{0,1},{1,0},{2,3},{3,2},{4,5},{5,4},{6,7},{7,6},{8,9},{9,8},{10,11... | collective-permute-start | bytes 1916936 | tf_op jit(solution)/shard_map/ppermute | solution.py:246
  51.4 4.3 %collective-permute-start.1 = (f32[96,2048]{1,0:T(8,128)S(1)}, f32[96,2048]{1,0:T(8,128)S(1)}, u32[]{:S(2)}, u32[]{:S(2)}) collective-permute-start(f32[96,2048]{1,0:T(8,128)S(1)} %bitcast.60), channel_id=1, source_target_pairs={{0,1},{1,0},{2,3},{3,2},{4,5},{5,4},{6,7},{7,6},{8,9},{9,8},{10,11... | collective-permute-start | bytes 2359304 | tf_op jit(solution)/shard_map/ppermute | solution.py:246
  52.2 4.7 %collective-permute-start.2 = (f32[96,2560]{1,0:T(8,128)S(1)}, f32[96,2560]{1,0:T(8,128)S(1)}, u32[]{:S(2)}, u32[]{:S(2)}) collective-permute-start(f32[96,2560]{1,0:T(8,128)S(1)} %bitcast.56), channel_id=1, source_target_pairs={{0,1},{1,0},{2,3},{3,2},{4,5},{5,4},{6,7},{7,6},{8,9},{9,8},{10,11... | collective-permute-start | bytes 2949128 | tf_op jit(solution)/shard_map/ppermute | solution.py:246
  52.8 10.2 %collective-permute-start.10 = (f32[96,1664]{1,0:T(8,128)S(1)}, f32[96,1664]{1,0:T(8,128)S(1)}, u32[]{:S(2)}, u32[]{:S(2)}) collective-permute-start(f32[96,1664]{1,0:T(8,128)S(1)} %bitcast_add_fusion.11.refs_0_), channel_id=1, source_target_pairs={{0,2},{1,7},{2,4},{3,1},{4,6},{5,3},{6,0},{7,5},{8,10},{9,15},{10,... | collective-permute-start | bytes 1916936 | tf_op jit(solution)/shard_map/ppermute | solution.py:249
  55.7 15.7 %collective-permute-start.16 = (f32[96,2048]{1,0:T(8,128)S(1)}, f32[96,2048]{1,0:T(8,128)S(1)}, u32[]{:S(2)}, u32[]{:S(2)}) collective-permute-start(f32[96,2048]{1,0:T(8,128)S(1)} %bitcast_add_fusion.7.refs_1_), channel_id=1, source_target_pairs={{0,2},{1,7},{2,4},{3,1},{4,6},{5,3},{6,0},{7,5},{8,10},{9,15},{10,... | collective-permute-start | bytes 2359304 | tf_op jit(solution)/shard_map/ppermute | solution.py:249
  57.4 16.2 %collective-permute-start.9 = (f32[96,1664]{1,0:T(8,128)S(1)}, f32[96,1664]{1,0:T(8,128)S(1)}, u32[]{:S(2)}, u32[]{:S(2)}) collective-permute-start(f32[96,1664]{1,0:T(8,128)S(1)} %bitcast.62), channel_id=1, source_target_pairs={{0,1},{1,0},{2,3},{3,2},{4,5},{5,4},{6,7},{7,6},{8,9},{9,8},{10,11... | collective-permute-start | bytes 1916936 | tf_op jit(solution)/shard_map/ppermute | solution.py:246
  58.1 15.8 %collective-permute-start.15 = (f32[96,2048]{1,0:T(8,128)S(1)}, f32[96,2048]{1,0:T(8,128)S(1)}, u32[]{:S(2)}, u32[]{:S(2)}) collective-permute-start(f32[96,2048]{1,0:T(8,128)S(1)} %bitcast.59), channel_id=1, source_target_pairs={{0,1},{1,0},{2,3},{3,2},{4,5},{5,4},{6,7},{7,6},{8,9},{9,8},{10,11... | collective-permute-start | bytes 2359304 | tf_op jit(solution)/shard_map/ppermute | solution.py:246
  58.7 23.2 %collective-permute-start.4 = (f32[96,2560]{1,0:T(8,128)S(1)}, f32[96,2560]{1,0:T(8,128)S(1)}, u32[]{:S(2)}, u32[]{:S(2)}) collective-permute-start(f32[96,2560]{1,0:T(8,128)S(1)} %bitcast_add_fusion.3.refs_2_), channel_id=1, source_target_pairs={{0,2},{1,7},{2,4},{3,1},{4,6},{5,3},{6,0},{7,5},{8,10},{9,15},{10,... | collective-permute-start | bytes 2949128 | tf_op jit(solution)/shard_map/ppermute | solution.py:249
  63.0 13.1 %collective-permute-start.3 = (f32[96,2560]{1,0:T(8,128)S(1)}, f32[96,2560]{1,0:T(8,128)S(1)}, u32[]{:S(2)}, u32[]{:S(2)}) collective-permute-start(f32[96,2560]{1,0:T(8,128)S(1)} %bitcast.54), channel_id=1, source_target_pairs={{0,1},{1,0},{2,3},{3,2},{4,5},{5,4},{6,7},{7,6},{8,9},{9,8},{10,11... | collective-permute-start | bytes 2949128 | tf_op jit(solution)/shard_map/ppermute | solution.py:246
  71.4 19.5 %collective-permute-start.13 = (f32[96,1664]{1,0:T(8,128)S(1)}, f32[96,1664]{1,0:T(8,128)S(1)}, u32[]{:S(2)}, u32[]{:S(2)}) collective-permute-start(f32[96,1664]{1,0:T(8,128)S(1)} %bitcast.61), channel_id=1, source_target_pairs={{0,1},{1,0},{2,3},{3,2},{4,5},{5,4},{6,7},{7,6},{8,9},{9,8},{10,11... | collective-permute-start | bytes 1916936 | tf_op jit(solution)/shard_map/ppermute | solution.py:246
  73.7 17.5 %collective-permute-start.19 = (f32[96,2048]{1,0:T(8,128)S(1)}, f32[96,2048]{1,0:T(8,128)S(1)}, u32[]{:S(2)}, u32[]{:S(2)}) collective-permute-start(f32[96,2048]{1,0:T(8,128)S(1)} %bitcast.57), channel_id=1, source_target_pairs={{0,1},{1,0},{2,3},{3,2},{4,5},{5,4},{6,7},{7,6},{8,9},{9,8},{10,11... | collective-permute-start | bytes 2359304 | tf_op jit(solution)/shard_map/ppermute | solution.py:246
  73.9 14.9 %collective-permute-start.11 = (f32[96,1664]{1,0:T(8,128)S(1)}, f32[96,1664]{1,0:T(8,128)S(1)}, u32[]{:S(2)}, u32[]{:S(2)}) collective-permute-start(f32[96,1664]{1,0:T(8,128)S(1)} %fusion.5), channel_id=1, source_target_pairs={{0,2},{1,7},{2,4},{3,1},{4,6},{5,3},{6,0},{7,5},{8,10},{9,15},{10,... | collective-permute-start | bytes 1916936 | tf_op jit(solution)/shard_map/ppermute | solution.py:249
  76.0 21.2 %collective-permute-start.17 = (f32[96,2048]{1,0:T(8,128)S(1)}, f32[96,2048]{1,0:T(8,128)S(1)}, u32[]{:S(2)}, u32[]{:S(2)}) collective-permute-start(f32[96,2048]{1,0:T(8,128)S(1)} %fusion.3), channel_id=1, source_target_pairs={{0,2},{1,7},{2,4},{3,1},{4,6},{5,3},{6,0},{7,5},{8,10},{9,15},{10,... | collective-permute-start | bytes 2359304 | tf_op jit(solution)/shard_map/ppermute | solution.py:249
  82.1 33.4 %collective-permute-start.5 = (f32[96,2560]{1,0:T(8,128)S(1)}, f32[96,2560]{1,0:T(8,128)S(1)}, u32[]{:S(2)}, u32[]{:S(2)}) collective-permute-start(f32[96,2560]{1,0:T(8,128)S(1)} %fusion.1), channel_id=1, source_target_pairs={{0,2},{1,7},{2,4},{3,1},{4,6},{5,3},{6,0},{7,5},{8,10},{9,15},{10,... | collective-permute-start | bytes 2949128 | tf_op jit(solution)/shard_map/ppermute | solution.py:249
  88.8 29.1 %collective-permute-start.7 = (f32[96,2560]{1,0:T(8,128)S(1)}, f32[96,2560]{1,0:T(8,128)S(1)}, u32[]{:S(2)}, u32[]{:S(2)}) collective-permute-start(f32[96,2560]{1,0:T(8,128)S(1)} %bitcast.53), channel_id=1, source_target_pairs={{0,1},{1,0},{2,3},{3,2},{4,5},{5,4},{6,7},{7,6},{8,9},{9,8},{10,11... | collective-permute-start | bytes 2949128 | tf_op jit(solution)/shard_map/ppermute | solution.py:246
  90.9 10.4 %collective-permute-start.12 = (f32[96,1664]{1,0:T(8,128)S(1)}, f32[96,1664]{1,0:T(8,128)S(1)}, u32[]{:S(2)}, u32[]{:S(2)}) collective-permute-start(f32[96,1664]{1,0:T(8,128)S(1)} %bitcast.63), channel_id=1, source_target_pairs={{0,1},{1,0},{2,3},{3,2},{4,5},{5,4},{6,7},{7,6},{8,9},{9,8},{10,11... | collective-permute-start | bytes 1916936 | tf_op jit(solution)/shard_map/ppermute | solution.py:246
  91.1 23.5 %collective-permute-start.14 = (f32[96,1664]{1,0:T(8,128)S(1)}, f32[96,1664]{1,0:T(8,128)S(1)}, u32[]{:S(2)}, u32[]{:S(2)}) collective-permute-start(f32[96,1664]{1,0:T(8,128)S(1)} %fusion.4), channel_id=1, source_target_pairs={{0,2},{1,7},{2,4},{3,1},{4,6},{5,3},{6,0},{7,5},{8,10},{9,15},{10,... | collective-permute-start | bytes 1916936 | tf_op jit(solution)/shard_map/ppermute | solution.py:249
  97.3 25.7 %collective-permute-start.20 = (f32[96,2048]{1,0:T(8,128)S(1)}, f32[96,2048]{1,0:T(8,128)S(1)}, u32[]{:S(2)}, u32[]{:S(2)}) collective-permute-start(f32[96,2048]{1,0:T(8,128)S(1)} %fusion.2), channel_id=1, source_target_pairs={{0,2},{1,7},{2,4},{3,1},{4,6},{5,3},{6,0},{7,5},{8,10},{9,15},{10,... | collective-permute-start | bytes 2359304 | tf_op jit(solution)/shard_map/ppermute | solution.py:249
  101.4 18.3 %collective-permute-start.18 = (f32[96,2048]{1,0:T(8,128)S(1)}, f32[96,2048]{1,0:T(8,128)S(1)}, u32[]{:S(2)}, u32[]{:S(2)}) collective-permute-start(f32[96,2048]{1,0:T(8,128)S(1)} %bitcast.58), channel_id=1, source_target_pairs={{0,1},{1,0},{2,3},{3,2},{4,5},{5,4},{6,7},{7,6},{8,9},{9,8},{10,11... | collective-permute-start | bytes 2359304 | tf_op jit(solution)/shard_map/ppermute | solution.py:246
  116.2 7.8 %collective-permute-start.6 = (f32[96,2560]{1,0:T(8,128)S(1)}, f32[96,2560]{1,0:T(8,128)S(1)}, u32[]{:S(2)}, u32[]{:S(2)}) collective-permute-start(f32[96,2560]{1,0:T(8,128)S(1)} %bitcast.55), channel_id=1, source_target_pairs={{0,1},{1,0},{2,3},{3,2},{4,5},{5,4},{6,7},{7,6},{8,9},{9,8},{10,11... | collective-permute-start | bytes 2949128 | tf_op jit(solution)/shard_map/ppermute | solution.py:246
  118.1 15.5 %collective-permute-start.8 = (f32[96,2560]{1,0:T(8,128)S(1)}, f32[96,2560]{1,0:T(8,128)S(1)}, u32[]{:S(2)}, u32[]{:S(2)}) collective-permute-start(f32[96,2560]{1,0:T(8,128)S(1)} %fusion), channel_id=1, source_target_pairs={{0,2},{1,7},{2,4},{3,1},{4,6},{5,3},{6,0},{7,5},{8,10},{9,15},{10,... | collective-permute-start | bytes 2949128 | tf_op jit(solution)/shard_map/ppermute | solution.py:249

commit v8 on v7

--- a/solution.py
+++ b/solution.py
@@ -48,7 +48,8 @@
         weight = jnp.exp(total - column[:, h : h + 1])
         high, low = split(k_ref[:, cols].astype(F32) * weight)
         values = v_ref[:, cols]
-        state = dot(high, values, TN) + dot(low, values, TN)
+        both = dot(values, jnp.concatenate([high, low], axis=1), TN)
+        state = (both[:, :128] + both[:, 128:]).T
         chunks_ref[8 * h : 8 * h + 8, 0:16, 0, :] = state.reshape(8, 16, 128)
         chunks_ref[8 * h : 8 * h + 8, 16, 0, :] = jnp.broadcast_to(total, (8, 128))
 
@@ -117,42 +118,47 @@
         features = (attention * gain_ref[:, cols]).astype(BF16).reshape(parts, share, 128)
         for i in range(parts):
             out_ref[place_ref[i], :, cols] = features[i]
-    squares = jnp.broadcast_to(squares, (parts * share, 128)).reshape(parts, share, 128)
+    squares = jnp.broadcast_to(squares, (parts * share, 128)).T[0:8, :]
+    squares_out_ref[...] = jnp.zeros_like(squares_out_ref)
     for i in range(parts):
-        squares_out_ref[place_ref[i]] = squares[i]
-
-
-def project_kernel(start, size, first, features_ref, squares_ref, w_ref, *refs):
+        squares_out_ref[place_ref[i], :, 0:share] = squares[:, share * i : share * i + share]
+
+
+def project_kernel(start, size, step, features_ref, squares_ref, w_ref, *refs):
     keep_ref, send_ref = refs[-2:]
-    count, rows = keep_ref.shape[:2]
-    sides = [slice(first, first + count), slice(4 + first, 4 + first + count)]
-    left = jnp.concatenate([features_ref[side].reshape(count * rows, -1) for side in sides], axis=0)
+    rows = features_ref.shape[1]
+    left = jnp.concatenate([features_ref[step], features_ref[4 + step]], axis=0)
     for n in range(0, size, 512):
-        t = slice(n, n + 512)
         both = dot(left, w_ref[:, start + n : start + n + 512])
-        keep_ref[:, :, t] = both[: count * rows].reshape(count, rows, 512)
-        send_ref[:, :, t] = both[count * rows :].reshape(count, rows, 512)
-    if keep_ref.shape[2] > size:
-        keep_ref[:, :, size:] = squares_ref[sides[0]]
-        send_ref[:, :, size:] = squares_ref[sides[1]]
+        for m in range(0, 512, 128):
+            place = slice((n + m) // 128 * rows, (n + m) // 128 * rows + rows)
+            keep_ref[place, :] = both[:rows, m : m + 128]
+            send_ref[place, :] = both[rows:, m : m + 128]
+    end = size // 128 * rows
+    if keep_ref.shape[0] > end:
+        keep_ref[end:, :] = squares_ref[step]
+        send_ref[end:, :] = squares_ref[4 + step]
 
 
 def finish_kernel(start, extra, features, *refs):
     mine_ref, arrived_ref = refs[:2]
     if extra:
         out_hbm, inverse_ref, buffer, sems = refs[2:]
-        width = mine_ref.shape[1] - extra
-        inverse_ref[...] = 1.0 / jnp.sqrt((mine_ref[:, width:] + arrived_ref[:, width:]) / features + 1e-06)
+        end = mine_ref.shape[0] - extra
+        squares = mine_ref[end:, :] + arrived_ref[end:, :]
+        column = jnp.broadcast_to(squares[0:1, :], (128, 128)).T[: inverse_ref.shape[0], :]
+        inverse_ref[...] = 1.0 / jnp.sqrt(column / features + 1e-06)
     else:
         inverse_ref, _, out_hbm, buffer, sems = refs[2:]
-        width = mine_ref.shape[1]
-    inverse = inverse_ref[:, 0:1]
+    rows, width = buffer.shape
+    inverse = inverse_ref[...]
     tile = 512
     copies = []
     for i, n in enumerate(range(0, width, tile)):
-        cols = slice(n, n + tile)
-        buffer[:, cols] = ((mine_ref[:, cols] + arrived_ref[:, cols]) * inverse).astype(BF16)
-        copy = pltpu.make_async_copy(buffer.at[:, cols], out_hbm.at[:, start + n : start + n + tile], sems.at[i])
+        for m in range(n, n + tile, 128):
+            place = slice(m // 128 * rows, m // 128 * rows + rows)
+            buffer[:, m : m + 128] = ((mine_ref[place, :] + arrived_ref[place, :]) * inverse).astype(BF16)
+        copy = pltpu.make_async_copy(buffer.at[:, n : n + tile], out_hbm.at[:, start + n : start + n + tile], sems.at[i])
         copy.start()
         copies.append(copy)
     for copy in copies:
@@ -219,21 +225,21 @@
     share = length // 8
     starts = [0, 1536, 3584]
     widths = [1536, 2048, 2560]
-    extras = [128, 0, 0]
+    extras = [8, 0, 0]
 
     features, squares = call(
         mix_kernel,
-        [((8, share, width), BF16), ((8, share, 128), F32)],
+        [((8, share, width), BF16), ((8, 8, 128), F32)],
         [SMEM, HBM, VMEM, VMEM, VMEM, VMEM, VMEM, HBM],
         scratch=[pltpu.VMEM(q.shape, BF16), dma((4,))],
         flops=2**34,
-        vmem=50 * 2**20,
+        vmem=52 * 2**20,
     )(places, q, prefix, early, late, running, gain.reshape(1, width), w)
 
     def project(start, size, extra, first, after):
         return call(
             functools.partial(project_kernel, start, size, first),
-            [((1, share, size + extra), F32)] * 2,
+            [((size // 128 * share + extra, 128), F32)] * 2,
             [VMEM, VMEM, VMEM] + [ANY] * len(after),
 
         )(features, squares, w, *after)
@@ -243,7 +249,7 @@
         totals = []
         for i, (start, size, extra) in enumerate(zip(starts, widths, extras)):
             keep, send = project(start, size, extra, step, before if step == 1 else before[i : i + 1] if step > 1 else [])
-            totals.append(keep[0] + lax.ppermute(send[0], "head", SWAP) + (arrived[i] if step in (1, 2) else 0.0))
+            totals.append(keep + lax.ppermute(send, "head", SWAP) + (arrived[i] if step in (1, 2) else 0.0))
         if step < 3:
             before = totals if step == 0 else arrived
             arrived = [lax.ppermute(total, "head", RING) for total in totals]

time: 135 us -> 138 us (1.022)
    ppermute x12, waiting for transfers between devices: 0.03 us -> 1.59 us  [per_device(): lax.ppermute(send, 'head', SWAP)]
where the time goes in v8:
time: 138 us; the launch traced here: 137 us
  waiting for transfers between devices  56.6 us (41%)
  starting transfers between devices  48 us (35%)
  Pallas kernels  25.3 us (18%)
  local copies, waits for them, and re-layouts  5.03 us (4%)
    ppermute x9, waiting for transfers between devices, per_device(): arrived = [lax.ppermute(total, 'head', RING) for total in totals]  47.6 us
    ppermute x9, starting transfers between devices, per_device(): arrived = [lax.ppermute(total, 'head', RING) for total in totals]  16.7 us
    ppermute x12, starting transfers between devices, per_device(): lax.ppermute(send, 'head', SWAP)  13 us
    all_to_all x1, starting transfers between devices, per_device(): everyone = lax.all_to_all(chunks, 'seg', 0, 0, tiled=True)  11.9 us
    pallas_call x12, Pallas kernels, project(): call(functools.partial(project_kernel, start, size, first), [((size // 12...  7.02 us
    all_to_all x1, starting transfers between devices, per_device(): prefix = lax.all_to_all(mine, 'seg', 0, 0, tiled=True).reshape(4, 128, 128)  6.46 us
    unnamed x22, local copies, waits for them, and re-layouts  5.03 us
    pallas_call x1, Pallas kernels, per_device(): call(functools.partial(within_kernel, 2), [((length, width // 2), F32)],...  4.94 us
  transfers between devices with their start and end apart: 23, of which 10 were waited for; matrix products, arithmetic and copies ran while one was open for 1% of the time, Pallas kernels for 11%

profile of v8, /device:TPU:1, one launch (start us, length us, event | category | flops | bytes accessed | tf_op | source)
XLA Modules:
  0.0 136.8 jit_solution(726937289707588225)
XLA Ops:
  0.0 3.5 %shard_map.73 = (f32[32,17,1,128]{3,2,1,0:T(1,128)}, f32[8,768]{1,0:T(8,128)}) custom-call(f32[4,768]{1,0:T(4,128)} %decay_hbm.1, bf16[768,512]{1,0:T(8,128)(2,1)} %k_hbm.5, bf16[768,512]{1,0:T(8,128)(2,1)} %v_hbm.5), custom_call_target="tpu_custom_call" | custom-call | flops 268435456 | bytes 1048576 | tf_op jit(solution)/shard_map/pallas_call | solution.py:202
  3.5 11.9 %all-to-all-start = ((f32[32,17,1,128]{3,2,1,0:T(1,128)}), f32[32,17,1,128]{3,2,1,0:T(1,128)S(1)}, u32[]{:S(2)}, u32[]{:S(2)}) async-start(f32[32,17,1,128]{3,2,1,0:T(1,128)} %get-tuple-element.38), calls=%async_computation | async-start | bytes 557056 | tf_op jit(solution)/shard_map/all_to_all | solution.py:209
  15.4 1.1 copy-done
  16.5 1.1 copy-done.1
  17.6 1.1 copy-done.2
  18.8 0.7 copy-done.4
  19.5 2.0 %shard_map.74.early_ref = f32[768,256]{1,0:T(8,128)S(1)} custom-call(bf16[768,512]{1,0:T(8,128)(2,1)S(1)} %copy-done.2, bf16[768,512]{1,0:T(8,128)(2,1)S(1)} %copy-done, bf16[768,512]{1,0:T(8,128)(2,1)S(1)} %copy-done.1, f32[8,768]{1,0:T(8,128)S(1)} %copy-done.4), custom_call_target="tpu_custom_call" | custom-call | flops 1073741824 | bytes 1048576 | tf_op jit(solution)/shard_map/pallas_call | solution.py:211
  21.5 0.9 copy-done.8
  22.4 2.8 %all-to-all-done.all_ref = f32[32,17,1,128]{3,2,1,0:T(1,128)S(1)} async-done(((f32[32,17,1,128]{3,2,1,0:T(1,128)}), f32[32,17,1,128]{3,2,1,0:T(1,128)S(1)}, u32[]{:S(2)}, u32[]{:S(2)}) %all-to-all-start) | async-done | bytes 278560 | tf_op jit(solution)/shard_map/all_to_all | solution.py:209
  25.1 1.6 %shard_map.75 = f32[32,16,128]{2,1,0:T(8,128)} custom-call(s32[32]{0:T(128)S(1)} %copy-done.7, f32[32,17,1,128]{3,2,1,0:T(1,128)S(1)} %all-to-all-done.all_ref), custom_call_target="tpu_custom_call" | custom-call | flops 268435456 | bytes 1048576 | tf_op jit(solution)/shard_map/pallas_call | solution.py:215
  26.7 6.5 %all-to-all-start.1 = ((f32[32,16,128]{2,1,0:T(8,128)}), f32[32,16,128]{2,1,0:T(8,128)S(1)}, u32[]{:S(2)}, u32[]{:S(2)}) async-start(f32[32,16,128]{2,1,0:T(8,128)} %shard_map.75), calls=%async_computation.1 | async-start | bytes 524288 | tf_op jit(solution)/shard_map/all_to_all | solution.py:216
  33.2 4.9 %shard_map.76.late_ref = f32[768,256]{1,0:T(8,128)} custom-call(bf16[768,512]{1,0:T(8,128)(2,1)} %q_hbm.5, bf16[768,512]{1,0:T(8,128)(2,1)} %k_hbm.5, bf16[768,512]{1,0:T(8,128)(2,1)} %v_hbm.5, f32[8,768]{1,0:T(8,128)} %get-tuple-element.42.running_ref), custom_call_target="tpu_custom_call" | custom-call | flops 1073741824 | bytes 1048576 | tf_op jit(solution)/shard_map/pallas_call | solution.py:217
  38.2 4.7 %all-to-all-done.1 = f32[32,16,128]{2,1,0:T(8,128)S(1)} async-done(((f32[32,16,128]{2,1,0:T(8,128)}), f32[32,16,128]{2,1,0:T(8,128)S(1)}, u32[]{:S(2)}, u32[]{:S(2)}) %all-to-all-start.1) | async-done | bytes 262176 | tf_op jit(solution)/shard_map/all_to_all | solution.py:216
  42.8 3.8 %shard_map.77 = (bf16[8,96,512]{2,1,0:T(8,128)(2,1)S(1)}, f32[8,8,128]{2,1,0:T(8,128)S(1)}) custom-call(s32[8]{0:T(128)S(1)} %compare_select_fusion.place_ref, bf16[768,512]{1,0:T(8,128)(2,1)S(1)} %copy-done.3, f32[4,128,128]{2,1,0:T(8,128)S(1)} %bitcast.4, f32[768,256]{1,0:T(8,128)} %copy-done.8, f32[768,256]{1,0:T(8,128)} %shard_map.76.late_ref, ...), custom_call_target="tpu_custom_call" | custom-call | flops 17179869184 | bytes 1048576 | tf_op jit(solution)/shard_map/pallas_call | solution.py:230
  46.7 0.7 shard_map.80
  47.4 3.8 %collective-permute-start.2 = (f32[1920,128]{1,0:T(8,128)S(1)}, f32[1920,128]{1,0:T(8,128)S(1)}, u32[]{:S(2)}, u32[]{:S(2)}) collective-permute-start(f32[1920,128]{1,0:T(8,128)S(1)} %get-tuple-element.50), channel_id=1, source_target_pairs={{0,1},{1,0},{2,3},{3,2},{4,5},{5,4},{6,7},{7,6},{8,9},{9,8},{10,11... | collective-permute-start | bytes 2949128 | tf_op jit(solution)/shard_map/ppermute | solution.py:252
  51.1 0.6 shard_map.79
  51.7 0.1 collective-permute-start.1
  51.8 0.5 shard_map.78
  52.3 0.6 collective-permute-start
  52.9 1.6 %collective-permute-done.1 = f32[1536,128]{1,0:T(8,128)S(1)} collective-permute-done((f32[1536,128]{1,0:T(8,128)S(1)}, f32[1536,128]{1,0:T(8,128)S(1)}, u32[]{:S(2)}, u32[]{:S(2)}) %collective-permute-start.1) | collective-permute-done | bytes 786464 | tf_op jit(solution)/shard_map/ppermute | solution.py:252
  54.4 0.1 add.61.refs_1_
  54.6 2.8 %collective-permute-start.16 = (f32[1536,128]{1,0:T(8,128)S(1)}, f32[1536,128]{1,0:T(8,128)S(1)}, u32[]{:S(2)}, u32[]{:S(2)}) collective-permute-start(f32[1536,128]{1,0:T(8,128)S(1)} %add.61.refs_1_), channel_id=1, source_target_pairs={{0,2},{1,7},{2,4},{3,1},{4,6},{5,3},{6,0},{7,5},{8,10},{9,15},{10,... | collective-permute-start | bytes 2359304 | tf_op jit(solution)/shard_map/ppermute | solution.py:255
  57.4 0.9 collective-permute-start.10
  58.4 0.1 add.62.refs_2_
  58.5 0.5 shard_map.84
  59.0 0.2 collective-permute-start.9
  59.2 0.6 shard_map.88
  59.8 0.5 collective-permute-start.15
  60.3 1.1 collective-permute-start.4
  61.4 0.7 shard_map.81
  62.1 4.2 %collective-permute-done.16.refs_0_ = f32[1536,128]{1,0:T(8,128)S(1)} collective-permute-done((f32[1536,128]{1,0:T(8,128)S(1)}, f32[1536,128]{1,0:T(8,128)S(1)}, u32[]{:S(2)}, u32[]{:S(2)}) %collective-permute-start.16) | collective-permute-done | bytes 786464 | tf_op jit(solution)/shard_map/ppermute | solution.py:255
  66.3 1.9 %collective-permute-start.3 = (f32[1920,128]{1,0:T(8,128)S(1)}, f32[1920,128]{1,0:T(8,128)S(1)}, u32[]{:S(2)}, u32[]{:S(2)}) collective-permute-start(f32[1920,128]{1,0:T(8,128)S(1)} %get-tuple-element.52), channel_id=1, source_target_pairs={{0,1},{1,0},{2,3},{3,2},{4,5},{5,4},{6,7},{7,6},{8,9},{9,8},{10,11... | collective-permute-start | bytes 2949128 | tf_op jit(solution)/shard_map/ppermute | solution.py:252
  68.2 0.6 shard_map.90
  68.8 3.9 %collective-permute-done.10.refs_0_ = f32[1160,128]{1,0:T(8,128)S(1)} collective-permute-done((f32[1160,128]{1,0:T(8,128)S(1)}, f32[1160,128]{1,0:T(8,128)S(1)}, u32[]{:S(2)}, u32[]{:S(2)}) %collective-permute-start.10) | collective-permute-done | bytes 593952 | tf_op jit(solution)/shard_map/ppermute | solution.py:255
  72.7 1.9 %collective-permute-start.19 = (f32[1536,128]{1,0:T(8,128)S(1)}, f32[1536,128]{1,0:T(8,128)S(1)}, u32[]{:S(2)}, u32[]{:S(2)}) collective-permute-start(f32[1536,128]{1,0:T(8,128)S(1)} %get-tuple-element.69), channel_id=1, source_target_pairs={{0,1},{1,0},{2,3},{3,2},{4,5},{5,4},{6,7},{7,6},{8,9},{9,8},{10,11... | collective-permute-start | bytes 2359304 | tf_op jit(solution)/shard_map/ppermute | solution.py:252
  74.6 0.1 add_add_fusion.5
  74.7 1.6 %collective-permute-start.11 = (f32[1160,128]{1,0:T(8,128)S(1)}, f32[1160,128]{1,0:T(8,128)S(1)}, u32[]{:S(2)}, u32[]{:S(2)}) collective-permute-start(f32[1160,128]{1,0:T(8,128)S(1)} %add_add_fusion.5), channel_id=1, source_target_pairs={{0,2},{1,7},{2,4},{3,1},{4,6},{5,3},{6,0},{7,5},{8,10},{9,15},{10,... | collective-permute-start | bytes 1781768 | tf_op jit(solution)/shard_map/ppermute | solution.py:255
  76.3 0.1 add_add_fusion.3
  76.4 0.5 collective-permute-start.17
  77.0 6.2 %collective-permute-done.4.refs_0_ = f32[1920,128]{1,0:T(8,128)S(1)} collective-permute-done((f32[1920,128]{1,0:T(8,128)S(1)}, f32[1920,128]{1,0:T(8,128)S(1)}, u32[]{:S(2)}, u32[]{:S(2)}) %collective-permute-start.4) | collective-permute-done | bytes 983072 | tf_op jit(solution)/shard_map/ppermute | solution.py:255
  83.2 0.1 add_add_fusion.1
  83.3 3.2 %collective-permute-start.5 = (f32[1920,128]{1,0:T(8,128)S(1)}, f32[1920,128]{1,0:T(8,128)S(1)}, u32[]{:S(2)}, u32[]{:S(2)}) collective-permute-start(f32[1920,128]{1,0:T(8,128)S(1)} %add_add_fusion.1), channel_id=1, source_target_pairs={{0,2},{1,7},{2,4},{3,1},{4,6},{5,3},{6,0},{7,5},{8,10},{9,15},{10,... | collective-permute-start | bytes 2949128 | tf_op jit(solution)/shard_map/ppermute | solution.py:255
  86.5 0.7 shard_map.83
  87.2 0.1 collective-permute-start.7
  87.3 0.5 shard_map.86
  87.8 1.7 %collective-permute-done.11.refs_0_ = f32[1160,128]{1,0:T(8,128)S(1)} collective-permute-done((f32[1160,128]{1,0:T(8,128)S(1)}, f32[1160,128]{1,0:T(8,128)S(1)}, u32[]{:S(2)}, u32[]{:S(2)}) %collective-permute-start.11) | collective-permute-done | bytes 593952 | tf_op jit(solution)/shard_map/ppermute | solution.py:255
  89.6 1.9 %collective-permute-start.13 = (f32[1160,128]{1,0:T(8,128)S(1)}, f32[1160,128]{1,0:T(8,128)S(1)}, u32[]{:S(2)}, u32[]{:S(2)}) collective-permute-start(f32[1160,128]{1,0:T(8,128)S(1)} %get-tuple-element.62), channel_id=1, source_target_pairs={{0,1},{1,0},{2,3},{3,2},{4,5},{5,4},{6,7},{7,6},{8,9},{9,8},{10,11... | collective-permute-start | bytes 1781768 | tf_op jit(solution)/shard_map/ppermute | solution.py:252
  91.5 0.5 shard_map.85
  92.1 5.9 %collective-permute-done.17.refs_0_ = f32[1536,128]{1,0:T(8,128)S(1)} collective-permute-done((f32[1536,128]{1,0:T(8,128)S(1)}, f32[1536,128]{1,0:T(8,128)S(1)}, u32[]{:S(2)}, u32[]{:S(2)}) %collective-permute-start.17) | collective-permute-done | bytes 786464 | tf_op jit(solution)/shard_map/ppermute | solution.py:255
  98.0 0.1 add_add_fusion.2
  98.1 3.2 %collective-permute-start.20 = (f32[1536,128]{1,0:T(8,128)S(1)}, f32[1536,128]{1,0:T(8,128)S(1)}, u32[]{:S(2)}, u32[]{:S(2)}) collective-permute-start(f32[1536,128]{1,0:T(8,128)S(1)} %add_add_fusion.2), channel_id=1, source_target_pairs={{0,2},{1,7},{2,4},{3,1},{4,6},{5,3},{6,0},{7,5},{8,10},{9,15},{10,... | collective-permute-start | bytes 2359304 | tf_op jit(solution)/shard_map/ppermute | solution.py:255
  101.3 0.6 shard_map.89
  101.9 6.6 %collective-permute-done.5.refs_0_ = f32[1920,128]{1,0:T(8,128)S(1)} collective-permute-done((f32[1920,128]{1,0:T(8,128)S(1)}, f32[1920,128]{1,0:T(8,128)S(1)}, u32[]{:S(2)}, u32[]{:S(2)}) %collective-permute-start.5) | collective-permute-done | bytes 983072 | tf_op jit(solution)/shard_map/ppermute | solution.py:255
  108.5 1.9 %collective-permute-start.18 = (f32[1536,128]{1,0:T(8,128)S(1)}, f32[1536,128]{1,0:T(8,128)S(1)}, u32[]{:S(2)}, u32[]{:S(2)}) collective-permute-start(f32[1536,128]{1,0:T(8,128)S(1)} %get-tuple-element.67), channel_id=1, source_target_pairs={{0,1},{1,0},{2,3},{3,2},{4,5},{5,4},{6,7},{7,6},{8,9},{9,8},{10,11... | collective-permute-start | bytes 2359304 | tf_op jit(solution)/shard_map/ppermute | solution.py:252
  110.4 0.2 add_add_fusion
  110.6 1.8 %collective-permute-start.8 = (f32[1920,128]{1,0:T(8,128)S(1)}, f32[1920,128]{1,0:T(8,128)S(1)}, u32[]{:S(2)}, u32[]{:S(2)}) collective-permute-start(f32[1920,128]{1,0:T(8,128)S(1)} %add_add_fusion), channel_id=1, source_target_pairs={{0,2},{1,7},{2,4},{3,1},{4,6},{5,3},{6,0},{7,5},{8,10},{9,15},{10,... | collective-permute-start | bytes 2949128 | tf_op jit(solution)/shard_map/ppermute | solution.py:255
  112.4 0.7 shard_map.82
  113.3 1.5 %collective-permute-start.14 = (f32[1160,128]{1,0:T(8,128)S(1)}, f32[1160,128]{1,0:T(8,128)S(1)}, u32[]{:S(2)}, u32[]{:S(2)}) collective-permute-start(f32[1160,128]{1,0:T(8,128)S(1)} %add_add_fusion.4), channel_id=1, source_target_pairs={{0,2},{1,7},{2,4},{3,1},{4,6},{5,3},{6,0},{7,5},{8,10},{9,15},{10,... | collective-permute-start | bytes 1781768 | tf_op jit(solution)/shard_map/ppermute | solution.py:255
  114.9 19.0 %collective-permute-done.14.refs_1_ = f32[1160,128]{1,0:T(8,128)S(1)} collective-permute-done((f32[1160,128]{1,0:T(8,128)S(1)}, f32[1160,128]{1,0:T(8,128)S(1)}, u32[]{:S(2)}, u32[]{:S(2)}) %collective-permute-start.14) | collective-permute-done | bytes 593952 | tf_op jit(solution)/shard_map/ppermute | solution.py:255
  133.8 0.9 shard_map.87
  134.9 0.8 shard_map.91.refs_3_
  135.7 0.1 add.65.refs_0_
  135.8 0.8 shard_map.92
  (38 shorter events, 0.6 us)
Async XLA Ops:
  3.5 21.7 %all-to-all-start = ((f32[32,17,1,128]{3,2,1,0:T(1,128)}), f32[32,17,1,128]{3,2,1,0:T(1,128)S(1)}, u32[]{:S(2)}, u32[]{:S(2)}) async-start(f32[32,17,1,128]{3,2,1,0:T(1,128)} %get-tuple-element.38), calls=%async_computation | async-start | bytes 557056 | tf_op jit(solution)/shard_map/all_to_all | solution.py:209
  15.4 1.1 copy-start
  16.5 1.1 copy-start.1
  17.6 1.1 copy-start.2
  18.8 0.7 copy-start.4
  19.5 5.6 %copy-start.7 = (s32[32]{0:T(128)S(1)}, s32[32]{0:T(128)}, u32[]{:S(2)}) copy-start(s32[32]{0:T(128)} %parent_ref.1) | copy-start | bytes 388
  21.5 0.9 copy-start.8
  26.7 16.1 %all-to-all-start.1 = ((f32[32,16,128]{2,1,0:T(8,128)}), f32[32,16,128]{2,1,0:T(8,128)S(1)}, u32[]{:S(2)}, u32[]{:S(2)}) async-start(f32[32,16,128]{2,1,0:T(8,128)} %shard_map.75), calls=%async_computation.1 | async-start | bytes 524288 | tf_op jit(solution)/shard_map/all_to_all | solution.py:216
  33.2 9.6 %copy-start.3 = (bf16[768,512]{1,0:T(8,128)(2,1)S(1)}, bf16[768,512]{1,0:T(8,128)(2,1)}, u32[]{:S(2)}) copy-start(bf16[768,512]{1,0:T(8,128)(2,1)} %q_hbm.5) | copy-start | bytes 2359300
  33.2 9.6 %copy-start.5 = (f32[8,768]{1,0:T(8,128)S(1)}, f32[8,768]{1,0:T(8,128)}, u32[]{:S(2)}) copy-start(f32[8,768]{1,0:T(8,128)} %get-tuple-element.42.running_ref) | copy-start | bytes 73732
  33.2 9.6 %copy-start.6 = (f32[512]{0:T(512)S(1)}, f32[512]{0:T(512)}, u32[]{:S(2)}) copy-start(f32[512]{0:T(512)} %param.12) | copy-start | bytes 6148
  42.8 3.8 %slice-start = ((s8[6291456]{0:T(1024)(128)(4,1)}), s8[4194304]{0:T(1024)(128)(4,1)S(1)}, s32[]{:S(2)}) async-start(s8[6291456]{0:T(1024)(128)(4,1)} %bitcast.2), calls=%async_computation.2 | async-start | bytes 8388608
  42.8 3.8 %slice-start.1 = ((s8[6291456]{0:T(1024)(128)(4,1)}), s8[2097152]{0:T(1024)(128)(4,1)S(1)}, s32[]{:S(2)}) async-start(s8[6291456]{0:T(1024)(128)(4,1)} %bitcast.2), calls=%async_computation.3 | async-start | bytes 4194304
  47.4 11.0 %collective-permute-start.2 = (f32[1920,128]{1,0:T(8,128)S(1)}, f32[1920,128]{1,0:T(8,128)S(1)}, u32[]{:S(2)}, u32[]{:S(2)}) collective-permute-start(f32[1920,128]{1,0:T(8,128)S(1)} %get-tuple-element.50), channel_id=1, source_target_pairs={{0,1},{1,0},{2,3},{3,2},{4,5},{5,4},{6,7},{7,6},{8,9},{9,8},{10,11... | collective-permute-start | bytes 2949128 | tf_op jit(solution)/shard_map/ppermute | solution.py:252
  51.7 2.7 %collective-permute-start.1 = (f32[1536,128]{1,0:T(8,128)S(1)}, f32[1536,128]{1,0:T(8,128)S(1)}, u32[]{:S(2)}, u32[]{:S(2)}) collective-permute-start(f32[1536,128]{1,0:T(8,128)S(1)} %get-tuple-element.48), channel_id=1, source_target_pairs={{0,1},{1,0},{2,3},{3,2},{4,5},{5,4},{6,7},{7,6},{8,9},{9,8},{10,11... | collective-permute-start | bytes 2359304 | tf_op jit(solution)/shard_map/ppermute | solution.py:252
  52.3 5.1 %collective-permute-start = (f32[1160,128]{1,0:T(8,128)S(1)}, f32[1160,128]{1,0:T(8,128)S(1)}, u32[]{:S(2)}, u32[]{:S(2)}) collective-permute-start(f32[1160,128]{1,0:T(8,128)S(1)} %get-tuple-element.46), channel_id=1, source_target_pairs={{0,1},{1,0},{2,3},{3,2},{4,5},{5,4},{6,7},{7,6},{8,9},{9,8},{10,11... | collective-permute-start | bytes 1781768 | tf_op jit(solution)/shard_map/ppermute | solution.py:252
  54.6 11.7 %collective-permute-start.16 = (f32[1536,128]{1,0:T(8,128)S(1)}, f32[1536,128]{1,0:T(8,128)S(1)}, u32[]{:S(2)}, u32[]{:S(2)}) collective-permute-start(f32[1536,128]{1,0:T(8,128)S(1)} %add.61.refs_1_), channel_id=1, source_target_pairs={{0,2},{1,7},{2,4},{3,1},{4,6},{5,3},{6,0},{7,5},{8,10},{9,15},{10,... | collective-permute-start | bytes 2359304 | tf_op jit(solution)/shard_map/ppermute | solution.py:255
  57.4 15.2 %collective-permute-start.10 = (f32[1160,128]{1,0:T(8,128)S(1)}, f32[1160,128]{1,0:T(8,128)S(1)}, u32[]{:S(2)}, u32[]{:S(2)}) collective-permute-start(f32[1160,128]{1,0:T(8,128)S(1)} %add.60.refs_0_), channel_id=1, source_target_pairs={{0,2},{1,7},{2,4},{3,1},{4,6},{5,3},{6,0},{7,5},{8,10},{9,15},{10,... | collective-permute-start | bytes 1781768 | tf_op jit(solution)/shard_map/ppermute | solution.py:255
  59.0 15.6 %collective-permute-start.9 = (f32[1160,128]{1,0:T(8,128)S(1)}, f32[1160,128]{1,0:T(8,128)S(1)}, u32[]{:S(2)}, u32[]{:S(2)}) collective-permute-start(f32[1160,128]{1,0:T(8,128)S(1)} %get-tuple-element.58), channel_id=1, source_target_pairs={{0,1},{1,0},{2,3},{3,2},{4,5},{5,4},{6,7},{7,6},{8,9},{9,8},{10,11... | collective-permute-start | bytes 1781768 | tf_op jit(solution)/shard_map/ppermute | solution.py:252
  59.8 16.5 %collective-permute-start.15 = (f32[1536,128]{1,0:T(8,128)S(1)}, f32[1536,128]{1,0:T(8,128)S(1)}, u32[]{:S(2)}, u32[]{:S(2)}) collective-permute-start(f32[1536,128]{1,0:T(8,128)S(1)} %get-tuple-element.65), channel_id=1, source_target_pairs={{0,1},{1,0},{2,3},{3,2},{4,5},{5,4},{6,7},{7,6},{8,9},{9,8},{10,11... | collective-permute-start | bytes 2359304 | tf_op jit(solution)/shard_map/ppermute | solution.py:252
  60.3 22.9 %collective-permute-start.4 = (f32[1920,128]{1,0:T(8,128)S(1)}, f32[1920,128]{1,0:T(8,128)S(1)}, u32[]{:S(2)}, u32[]{:S(2)}) collective-permute-start(f32[1920,128]{1,0:T(8,128)S(1)} %add.62.refs_2_), channel_id=1, source_target_pairs={{0,2},{1,7},{2,4},{3,1},{4,6},{5,3},{6,0},{7,5},{8,10},{9,15},{10,... | collective-permute-start | bytes 2949128 | tf_op jit(solution)/shard_map/ppermute | solution.py:255
  66.3 10.7 %collective-permute-start.3 = (f32[1920,128]{1,0:T(8,128)S(1)}, f32[1920,128]{1,0:T(8,128)S(1)}, u32[]{:S(2)}, u32[]{:S(2)}) collective-permute-start(f32[1920,128]{1,0:T(8,128)S(1)} %get-tuple-element.52), channel_id=1, source_target_pairs={{0,1},{1,0},{2,3},{3,2},{4,5},{5,4},{6,7},{7,6},{8,9},{9,8},{10,11... | collective-permute-start | bytes 2949128 | tf_op jit(solution)/shard_map/ppermute | solution.py:252
  72.7 19.3 %collective-permute-start.19 = (f32[1536,128]{1,0:T(8,128)S(1)}, f32[1536,128]{1,0:T(8,128)S(1)}, u32[]{:S(2)}, u32[]{:S(2)}) collective-permute-start(f32[1536,128]{1,0:T(8,128)S(1)} %get-tuple-element.69), channel_id=1, source_target_pairs={{0,1},{1,0},{2,3},{3,2},{4,5},{5,4},{6,7},{7,6},{8,9},{9,8},{10,11... | collective-permute-start | bytes 2359304 | tf_op jit(solution)/shard_map/ppermute | solution.py:252
  74.7 14.9 %collective-permute-start.11 = (f32[1160,128]{1,0:T(8,128)S(1)}, f32[1160,128]{1,0:T(8,128)S(1)}, u32[]{:S(2)}, u32[]{:S(2)}) collective-permute-start(f32[1160,128]{1,0:T(8,128)S(1)} %add_add_fusion.5), channel_id=1, source_target_pairs={{0,2},{1,7},{2,4},{3,1},{4,6},{5,3},{6,0},{7,5},{8,10},{9,15},{10,... | collective-permute-start | bytes 1781768 | tf_op jit(solution)/shard_map/ppermute | solution.py:255
  76.4 21.6 %collective-permute-start.17 = (f32[1536,128]{1,0:T(8,128)S(1)}, f32[1536,128]{1,0:T(8,128)S(1)}, u32[]{:S(2)}, u32[]{:S(2)}) collective-permute-start(f32[1536,128]{1,0:T(8,128)S(1)} %add_add_fusion.3), channel_id=1, source_target_pairs={{0,2},{1,7},{2,4},{3,1},{4,6},{5,3},{6,0},{7,5},{8,10},{9,15},{10,... | collective-permute-start | bytes 2359304 | tf_op jit(solution)/shard_map/ppermute | solution.py:255
  83.3 25.2 %collective-permute-start.5 = (f32[1920,128]{1,0:T(8,128)S(1)}, f32[1920,128]{1,0:T(8,128)S(1)}, u32[]{:S(2)}, u32[]{:S(2)}) collective-permute-start(f32[1920,128]{1,0:T(8,128)S(1)} %add_add_fusion.1), channel_id=1, source_target_pairs={{0,2},{1,7},{2,4},{3,1},{4,6},{5,3},{6,0},{7,5},{8,10},{9,15},{10,... | collective-permute-start | bytes 2949128 | tf_op jit(solution)/shard_map/ppermute | solution.py:255
  87.2 23.2 %collective-permute-start.7 = (f32[1920,128]{1,0:T(8,128)S(1)}, f32[1920,128]{1,0:T(8,128)S(1)}, u32[]{:S(2)}, u32[]{:S(2)}) collective-permute-start(f32[1920,128]{1,0:T(8,128)S(1)} %get-tuple-element.56), channel_id=1, source_target_pairs={{0,1},{1,0},{2,3},{3,2},{4,5},{5,4},{6,7},{7,6},{8,9},{9,8},{10,11... | collective-permute-start | bytes 2949128 | tf_op jit(solution)/shard_map/ppermute | solution.py:252
  89.6 23.6 %collective-permute-start.13 = (f32[1160,128]{1,0:T(8,128)S(1)}, f32[1160,128]{1,0:T(8,128)S(1)}, u32[]{:S(2)}, u32[]{:S(2)}) collective-permute-start(f32[1160,128]{1,0:T(8,128)S(1)} %get-tuple-element.62), channel_id=1, source_target_pairs={{0,1},{1,0},{2,3},{3,2},{4,5},{5,4},{6,7},{7,6},{8,9},{9,8},{10,11... | collective-permute-start | bytes 1781768 | tf_op jit(solution)/shard_map/ppermute | solution.py:252
  92.0 21.4 %collective-permute-start.12 = (f32[1160,128]{1,0:T(8,128)S(1)}, f32[1160,128]{1,0:T(8,128)S(1)}, u32[]{:S(2)}, u32[]{:S(2)}) collective-permute-start(f32[1160,128]{1,0:T(8,128)S(1)} %get-tuple-element.60), channel_id=1, source_target_pairs={{0,1},{1,0},{2,3},{3,2},{4,5},{5,4},{6,7},{7,6},{8,9},{9,8},{10,11... | collective-permute-start | bytes 1781768 | tf_op jit(solution)/shard_map/ppermute | solution.py:252
  98.1 36.7 %collective-permute-start.20 = (f32[1536,128]{1,0:T(8,128)S(1)}, f32[1536,128]{1,0:T(8,128)S(1)}, u32[]{:S(2)}, u32[]{:S(2)}) collective-permute-start(f32[1536,128]{1,0:T(8,128)S(1)} %add_add_fusion.2), channel_id=1, source_target_pairs={{0,2},{1,7},{2,4},{3,1},{4,6},{5,3},{6,0},{7,5},{8,10},{9,15},{10,... | collective-permute-start | bytes 2359304 | tf_op jit(solution)/shard_map/ppermute | solution.py:255
  108.5 26.2 %collective-permute-start.18 = (f32[1536,128]{1,0:T(8,128)S(1)}, f32[1536,128]{1,0:T(8,128)S(1)}, u32[]{:S(2)}, u32[]{:S(2)}) collective-permute-start(f32[1536,128]{1,0:T(8,128)S(1)} %get-tuple-element.67), channel_id=1, source_target_pairs={{0,1},{1,0},{2,3},{3,2},{4,5},{5,4},{6,7},{7,6},{8,9},{9,8},{10,11... | collective-permute-start | bytes 2359304 | tf_op jit(solution)/shard_map/ppermute | solution.py:252
  110.6 25.2 %collective-permute-start.8 = (f32[1920,128]{1,0:T(8,128)S(1)}, f32[1920,128]{1,0:T(8,128)S(1)}, u32[]{:S(2)}, u32[]{:S(2)}) collective-permute-start(f32[1920,128]{1,0:T(8,128)S(1)} %add_add_fusion), channel_id=1, source_target_pairs={{0,2},{1,7},{2,4},{3,1},{4,6},{5,3},{6,0},{7,5},{8,10},{9,15},{10,... | collective-permute-start | bytes 2949128 | tf_op jit(solution)/shard_map/ppermute | solution.py:255
  113.1 22.5 %collective-permute-start.6 = (f32[1920,128]{1,0:T(8,128)S(1)}, f32[1920,128]{1,0:T(8,128)S(1)}, u32[]{:S(2)}, u32[]{:S(2)}) collective-permute-start(f32[1920,128]{1,0:T(8,128)S(1)} %get-tuple-element.54), channel_id=1, source_target_pairs={{0,1},{1,0},{2,3},{3,2},{4,5},{5,4},{6,7},{7,6},{8,9},{9,8},{10,11... | collective-permute-start | bytes 2949128 | tf_op jit(solution)/shard_map/ppermute | solution.py:252
  113.3 20.5 %collective-permute-start.14 = (f32[1160,128]{1,0:T(8,128)S(1)}, f32[1160,128]{1,0:T(8,128)S(1)}, u32[]{:S(2)}, u32[]{:S(2)}) collective-permute-start(f32[1160,128]{1,0:T(8,128)S(1)} %add_add_fusion.4), channel_id=1, source_target_pairs={{0,2},{1,7},{2,4},{3,1},{4,6},{5,3},{6,0},{7,5},{8,10},{9,15},{10,... | collective-permute-start | bytes 1781768 | tf_op jit(solution)/shard_map/ppermute | solution.py:255

commit v9 on v8

--- a/solution.py
+++ b/solution.py
@@ -48,8 +48,7 @@
         weight = jnp.exp(total - column[:, h : h + 1])
         high, low = split(k_ref[:, cols].astype(F32) * weight)
         values = v_ref[:, cols]
-        both = dot(values, jnp.concatenate([high, low], axis=1), TN)
-        state = (both[:, :128] + both[:, 128:]).T
+        state = dot(high, values, TN) + dot(low, values, TN)
         chunks_ref[8 * h : 8 * h + 8, 0:16, 0, :] = state.reshape(8, 16, 128)
         chunks_ref[8 * h : 8 * h + 8, 16, 0, :] = jnp.broadcast_to(total, (8, 128))
 
@@ -132,12 +131,12 @@
         both = dot(left, w_ref[:, start + n : start + n + 512])
         for m in range(0, 512, 128):
             place = slice((n + m) // 128 * rows, (n + m) // 128 * rows + rows)
-            keep_ref[place, :] = both[:rows, m : m + 128]
-            send_ref[place, :] = both[rows:, m : m + 128]
+            keep_ref[0, place, :] = both[:rows, m : m + 128]
+            send_ref[0, place, :] = both[rows:, m : m + 128]
     end = size // 128 * rows
-    if keep_ref.shape[0] > end:
-        keep_ref[end:, :] = squares_ref[step]
-        send_ref[end:, :] = squares_ref[4 + step]
+    if keep_ref.shape[1] > end:
+        keep_ref[0, end:, :] = squares_ref[step]
+        send_ref[0, end:, :] = squares_ref[4 + step]
 
 
 def finish_kernel(start, extra, features, *refs):
@@ -233,13 +232,13 @@
         [SMEM, HBM, VMEM, VMEM, VMEM, VMEM, VMEM, HBM],
         scratch=[pltpu.VMEM(q.shape, BF16), dma((4,))],
         flops=2**34,
-        vmem=52 * 2**20,
+        vmem=50 * 2**20,
     )(places, q, prefix, early, late, running, gain.reshape(1, width), w)
 
     def project(start, size, extra, first, after):
         return call(
             functools.partial(project_kernel, start, size, first),
-            [((size // 128 * share + extra, 128), F32)] * 2,
+            [((1, size // 128 * share + extra, 128), F32)] * 2,
             [VMEM, VMEM, VMEM] + [ANY] * len(after),
 
         )(features, squares, w, *after)
@@ -249,7 +248,7 @@
         totals = []
         for i, (start, size, extra) in enumerate(zip(starts, widths, extras)):
             keep, send = project(start, size, extra, step, before if step == 1 else before[i : i + 1] if step > 1 else [])
-            totals.append(keep + lax.ppermute(send, "head", SWAP) + (arrived[i] if step in (1, 2) else 0.0))
+            totals.append(keep[0] + lax.ppermute(send[0], "head", SWAP) + (arrived[i] if step in (1, 2) else 0.0))
         if step < 3:
             before = totals if step == 0 else arrived
             arrived = [lax.ppermute(total, "head", RING) for total in totals]

time: 138 us -> 134 us (0.971)
  waiting for transfers between devices: 56.6 us -> 54.2 us
    ppermute x9, waiting for transfers between devices: 47.6 us -> 45.8 us  [per_device(): arrived = [lax.ppermute(total, 'head', RING) for total in totals]]
    ppermute x12, waiting for transfers between devices: 1.59 us -> 0.03 us  [per_device(): lax.ppermute(send[0], 'head', SWAP)]
where the time goes in v9:
time: 134 us; the launch traced here: 133 us
  waiting for transfers between devices  54.2 us (40%)
  starting transfers between devices  47.6 us (36%)
  Pallas kernels  24.1 us (18%)
  local copies, waits for them, and re-layouts  5.44 us (4%)
  other arithmetic  1.49 us (1%)
    ppermute x9, waiting for transfers between devices, per_device(): arrived = [lax.ppermute(total, 'head', RING) for total in totals]  45.8 us
    ppermute x9, starting transfers between devices, per_device(): arrived = [lax.ppermute(total, 'head', RING) for total in totals]  17.5 us
    all_to_all x1, starting transfers between devices, per_device(): everyone = lax.all_to_all(chunks, 'seg', 0, 0, tiled=True)  11.9 us
    ppermute x12, starting transfers between devices, per_device(): lax.ppermute(send[0], 'head', SWAP)  11.8 us
    pallas_call x12, Pallas kernels, project(): call(functools.partial(project_kernel, start, size, first), [((1, size //...  7.02 us
    all_to_all x1, starting transfers between devices, per_device(): prefix = lax.all_to_all(mine, 'seg', 0, 0, tiled=True).reshape(4, 128, 128)  6.46 us
    unnamed x22, local copies, waits for them, and re-layouts  5.44 us
    pallas_call x1, Pallas kernels, per_device(): call(functools.partial(within_kernel, 2), [((length, width // 2), F32)],...  4.92 us
  transfers between devices with their start and end apart: 23, of which 10 were waited for; matrix products, arithmetic and copies ran while one was open for 1% of the time, Pallas kernels for 11%

profile of v9, /device:TPU:1, one launch (start us, length us, event | category | flops | bytes accessed | tf_op | source)
XLA Modules:
  0.0 133.4 jit_solution(9573959022691941579)
XLA Ops:
  0.0 3.3 %shard_map.73 = (f32[32,17,1,128]{3,2,1,0:T(1,128)}, f32[8,768]{1,0:T(8,128)}) custom-call(f32[4,768]{1,0:T(4,128)} %decay_hbm.1, bf16[768,512]{1,0:T(8,128)(2,1)} %k_hbm.5, bf16[768,512]{1,0:T(8,128)(2,1)} %v_hbm.5), custom_call_target="tpu_custom_call" | custom-call | flops 268435456 | bytes 1048576 | tf_op jit(solution)/shard_map/pallas_call | solution.py:201
  3.3 11.9 %all-to-all-start = ((f32[32,17,1,128]{3,2,1,0:T(1,128)}), f32[32,17,1,128]{3,2,1,0:T(1,128)S(1)}, u32[]{:S(2)}, u32[]{:S(2)}) async-start(f32[32,17,1,128]{3,2,1,0:T(1,128)} %get-tuple-element.38), calls=%async_computation | async-start | bytes 557056 | tf_op jit(solution)/shard_map/all_to_all | solution.py:208
  15.2 1.1 copy-done
  16.3 1.1 copy-done.1
  17.5 1.1 copy-done.2
  18.6 0.7 copy-done.4
  19.3 2.0 %shard_map.74.early_ref = f32[768,256]{1,0:T(8,128)S(1)} custom-call(bf16[768,512]{1,0:T(8,128)(2,1)S(1)} %copy-done.2, bf16[768,512]{1,0:T(8,128)(2,1)S(1)} %copy-done, bf16[768,512]{1,0:T(8,128)(2,1)S(1)} %copy-done.1, f32[8,768]{1,0:T(8,128)S(1)} %copy-done.4), custom_call_target="tpu_custom_call" | custom-call | flops 1073741824 | bytes 1048576 | tf_op jit(solution)/shard_map/pallas_call | solution.py:210
  21.3 3.7 %all-to-all-done.all_ref = f32[32,17,1,128]{3,2,1,0:T(1,128)S(1)} async-done(((f32[32,17,1,128]{3,2,1,0:T(1,128)}), f32[32,17,1,128]{3,2,1,0:T(1,128)S(1)}, u32[]{:S(2)}, u32[]{:S(2)}) %all-to-all-start) | async-done | bytes 278560 | tf_op jit(solution)/shard_map/all_to_all | solution.py:208
  25.0 1.6 %shard_map.75 = f32[32,16,128]{2,1,0:T(8,128)} custom-call(s32[32]{0:T(128)S(1)} %copy-done.7, f32[32,17,1,128]{3,2,1,0:T(1,128)S(1)} %all-to-all-done.all_ref), custom_call_target="tpu_custom_call" | custom-call | flops 268435456 | bytes 1048576 | tf_op jit(solution)/shard_map/pallas_call | solution.py:214
  26.5 6.5 %all-to-all-start.1 = ((f32[32,16,128]{2,1,0:T(8,128)}), f32[32,16,128]{2,1,0:T(8,128)S(1)}, u32[]{:S(2)}, u32[]{:S(2)}) async-start(f32[32,16,128]{2,1,0:T(8,128)} %shard_map.75), calls=%async_computation.1 | async-start | bytes 524288 | tf_op jit(solution)/shard_map/all_to_all | solution.py:215
  33.1 4.9 %shard_map.76.late_ref = f32[768,256]{1,0:T(8,128)} custom-call(bf16[768,512]{1,0:T(8,128)(2,1)} %q_hbm.5, bf16[768,512]{1,0:T(8,128)(2,1)} %k_hbm.5, bf16[768,512]{1,0:T(8,128)(2,1)} %v_hbm.5, f32[8,768]{1,0:T(8,128)} %get-tuple-element.42.running_ref), custom_call_target="tpu_custom_call" | custom-call | flops 1073741824 | bytes 1048576 | tf_op jit(solution)/shard_map/pallas_call | solution.py:216
  38.0 4.7 %all-to-all-done.1 = f32[32,16,128]{2,1,0:T(8,128)S(1)} async-done(((f32[32,16,128]{2,1,0:T(8,128)}), f32[32,16,128]{2,1,0:T(8,128)S(1)}, u32[]{:S(2)}, u32[]{:S(2)}) %all-to-all-start.1) | async-done | bytes 262176 | tf_op jit(solution)/shard_map/all_to_all | solution.py:215
  42.7 1.3 copy-done.8
  44.0 2.8 %shard_map.77 = (bf16[8,96,512]{2,1,0:T(8,128)(2,1)S(1)}, f32[8,8,128]{2,1,0:T(8,128)S(1)}) custom-call(s32[8]{0:T(128)S(1)} %compare_select_fusion.place_ref, bf16[768,512]{1,0:T(8,128)(2,1)S(1)} %copy-done.3, f32[4,128,128]{2,1,0:T(8,128)S(1)} %bitcast.52, f32[768,256]{1,0:T(8,128)S(1)} %shard_map.74.early_ref, f32[768,256]{1,0:T(8,128)S(1)} %copy-done.8, ...), custom_call_target="tpu_custom_call" | custom-call | flops 17179869184 | bytes 1048576 | tf_op jit(solution)/shard_map/pallas_call | solution.py:229
  46.8 0.5 shard_map.78
  47.3 3.8 %collective-permute-start = (f32[1160,128]{1,0:T(8,128)S(1)}, f32[1160,128]{1,0:T(8,128)S(1)}, u32[]{:S(2)}, u32[]{:S(2)}) collective-permute-start(f32[1160,128]{1,0:T(8,128)S(1)} %bitcast.64), channel_id=1, source_target_pairs={{0,1},{1,0},{2,3},{3,2},{4,5},{5,4},{6,7},{7,6},{8,9},{9,8},{10,11... | collective-permute-start | bytes 1781768 | tf_op jit(solution)/shard_map/ppermute | solution.py:251
  51.0 0.6 shard_map.79
  51.6 0.1 collective-permute-start.1
  51.7 0.7 shard_map.80
  52.4 0.6 collective-permute-start.2
  53.1 2.8 %collective-permute-start.10 = (f32[1160,128]{1,0:T(8,128)S(1)}, f32[1160,128]{1,0:T(8,128)S(1)}, u32[]{:S(2)}, u32[]{:S(2)}) collective-permute-start(f32[1160,128]{1,0:T(8,128)S(1)} %bitcast_add_fusion.11.refs_0_), channel_id=1, source_target_pairs={{0,2},{1,7},{2,4},{3,1},{4,6},{5,3},{6,0},{7,5},{8,10},{9,15},{10,... | collective-permute-start | bytes 1781768 | tf_op jit(solution)/shard_map/ppermute | solution.py:254
  56.0 1.1 collective-permute-start.16
  57.1 0.1 bitcast_add_fusion.3.refs_2_
  57.2 0.5 shard_map.84
  57.8 0.6 shard_map.88
  58.4 0.6 collective-permute-start.15
  59.0 1.1 collective-permute-start.4
  60.1 0.7 shard_map.81
  60.7 2.0 %collective-permute-done.10.refs_0_ = f32[1160,128]{1,0:T(8,128)S(1)} collective-permute-done((f32[1160,128]{1,0:T(8,128)S(1)}, f32[1160,128]{1,0:T(8,128)S(1)}, u32[]{:S(2)}, u32[]{:S(2)}) %collective-permute-start.10) | collective-permute-done | bytes 593952 | tf_op jit(solution)/shard_map/ppermute | solution.py:254
  62.8 1.6 %collective-permute-start.3 = (f32[1920,128]{1,0:T(8,128)S(1)}, f32[1920,128]{1,0:T(8,128)S(1)}, u32[]{:S(2)}, u32[]{:S(2)}) collective-permute-start(f32[1920,128]{1,0:T(8,128)S(1)} %bitcast.54), channel_id=1, source_target_pairs={{0,1},{1,0},{2,3},{3,2},{4,5},{5,4},{6,7},{7,6},{8,9},{9,8},{10,11... | collective-permute-start | bytes 2949128 | tf_op jit(solution)/shard_map/ppermute | solution.py:251
  64.4 0.5 shard_map.86
  64.8 6.4 %collective-permute-done.16.refs_0_ = f32[1536,128]{1,0:T(8,128)S(1)} collective-permute-done((f32[1536,128]{1,0:T(8,128)S(1)}, f32[1536,128]{1,0:T(8,128)S(1)}, u32[]{:S(2)}, u32[]{:S(2)}) %collective-permute-start.16) | collective-permute-done | bytes 786464 | tf_op jit(solution)/shard_map/ppermute | solution.py:254
  71.2 1.6 %collective-permute-start.13 = (f32[1160,128]{1,0:T(8,128)S(1)}, f32[1160,128]{1,0:T(8,128)S(1)}, u32[]{:S(2)}, u32[]{:S(2)}) collective-permute-start(f32[1160,128]{1,0:T(8,128)S(1)} %bitcast.61), channel_id=1, source_target_pairs={{0,1},{1,0},{2,3},{3,2},{4,5},{5,4},{6,7},{7,6},{8,9},{9,8},{10,11... | collective-permute-start | bytes 1781768 | tf_op jit(solution)/shard_map/ppermute | solution.py:251
  72.8 0.6 shard_map.90
  73.4 0.1 collective-permute-start.19
  73.5 0.1 fusion.5
  73.6 2.1 %collective-permute-start.11 = (f32[1160,128]{1,0:T(8,128)S(1)}, f32[1160,128]{1,0:T(8,128)S(1)}, u32[]{:S(2)}, u32[]{:S(2)}) collective-permute-start(f32[1160,128]{1,0:T(8,128)S(1)} %fusion.5), channel_id=1, source_target_pairs={{0,2},{1,7},{2,4},{3,1},{4,6},{5,3},{6,0},{7,5},{8,10},{9,15},{10,... | collective-permute-start | bytes 1781768 | tf_op jit(solution)/shard_map/ppermute | solution.py:254
  75.7 0.2 fusion.3
  75.9 0.1 collective-permute-start.17
  76.0 5.8 %collective-permute-done.4.refs_0_ = f32[1920,128]{1,0:T(8,128)S(1)} collective-permute-done((f32[1920,128]{1,0:T(8,128)S(1)}, f32[1920,128]{1,0:T(8,128)S(1)}, u32[]{:S(2)}, u32[]{:S(2)}) %collective-permute-start.4) | collective-permute-done | bytes 983072 | tf_op jit(solution)/shard_map/ppermute | solution.py:254
  81.7 0.2 fusion.1
  81.9 3.2 %collective-permute-start.5 = (f32[1920,128]{1,0:T(8,128)S(1)}, f32[1920,128]{1,0:T(8,128)S(1)}, u32[]{:S(2)}, u32[]{:S(2)}) collective-permute-start(f32[1920,128]{1,0:T(8,128)S(1)} %fusion.1), channel_id=1, source_target_pairs={{0,2},{1,7},{2,4},{3,1},{4,6},{5,3},{6,0},{7,5},{8,10},{9,15},{10,... | collective-permute-start | bytes 2949128 | tf_op jit(solution)/shard_map/ppermute | solution.py:254
  85.1 0.7 shard_map.83
  85.8 2.3 %collective-permute-done.11.refs_0_ = f32[1160,128]{1,0:T(8,128)S(1)} collective-permute-done((f32[1160,128]{1,0:T(8,128)S(1)}, f32[1160,128]{1,0:T(8,128)S(1)}, u32[]{:S(2)}, u32[]{:S(2)}) %collective-permute-start.11) | collective-permute-done | bytes 593952 | tf_op jit(solution)/shard_map/ppermute | solution.py:254
  88.1 1.6 %collective-permute-start.7 = (f32[1920,128]{1,0:T(8,128)S(1)}, f32[1920,128]{1,0:T(8,128)S(1)}, u32[]{:S(2)}, u32[]{:S(2)}) collective-permute-start(f32[1920,128]{1,0:T(8,128)S(1)} %bitcast.53), channel_id=1, source_target_pairs={{0,1},{1,0},{2,3},{3,2},{4,5},{5,4},{6,7},{7,6},{8,9},{9,8},{10,11... | collective-permute-start | bytes 2949128 | tf_op jit(solution)/shard_map/ppermute | solution.py:251
  89.7 0.5 shard_map.85
  90.2 0.1 collective-permute-start.12
  90.4 2.1 %collective-permute-start.14 = (f32[1160,128]{1,0:T(8,128)S(1)}, f32[1160,128]{1,0:T(8,128)S(1)}, u32[]{:S(2)}, u32[]{:S(2)}) collective-permute-start(f32[1160,128]{1,0:T(8,128)S(1)} %fusion.4), channel_id=1, source_target_pairs={{0,2},{1,7},{2,4},{3,1},{4,6},{5,3},{6,0},{7,5},{8,10},{9,15},{10,... | collective-permute-start | bytes 1781768 | tf_op jit(solution)/shard_map/ppermute | solution.py:254
  92.5 4.0 %collective-permute-done.17.refs_0_ = f32[1536,128]{1,0:T(8,128)S(1)} collective-permute-done((f32[1536,128]{1,0:T(8,128)S(1)}, f32[1536,128]{1,0:T(8,128)S(1)}, u32[]{:S(2)}, u32[]{:S(2)}) %collective-permute-start.17) | collective-permute-done | bytes 786464 | tf_op jit(solution)/shard_map/ppermute | solution.py:254
  96.5 0.1 fusion.2
  96.7 3.4 %collective-permute-start.20 = (f32[1536,128]{1,0:T(8,128)S(1)}, f32[1536,128]{1,0:T(8,128)S(1)}, u32[]{:S(2)}, u32[]{:S(2)}) collective-permute-start(f32[1536,128]{1,0:T(8,128)S(1)} %fusion.2), channel_id=1, source_target_pairs={{0,2},{1,7},{2,4},{3,1},{4,6},{5,3},{6,0},{7,5},{8,10},{9,15},{10,... | collective-permute-start | bytes 2359304 | tf_op jit(solution)/shard_map/ppermute | solution.py:254
  100.1 0.6 shard_map.89
  100.7 0.1 collective-permute-start.18
  100.9 12.6 %collective-permute-done.14.refs_1_ = f32[1160,128]{1,0:T(8,128)S(1)} collective-permute-done((f32[1160,128]{1,0:T(8,128)S(1)}, f32[1160,128]{1,0:T(8,128)S(1)}, u32[]{:S(2)}, u32[]{:S(2)}) %collective-permute-start.14) | collective-permute-done | bytes 593952 | tf_op jit(solution)/shard_map/ppermute | solution.py:254
  113.4 0.9 shard_map.87
  114.3 0.7 shard_map.82
  115.0 1.7 %collective-permute-start.6 = (f32[1920,128]{1,0:T(8,128)S(1)}, f32[1920,128]{1,0:T(8,128)S(1)}, u32[]{:S(2)}, u32[]{:S(2)}) collective-permute-start(f32[1920,128]{1,0:T(8,128)S(1)} %bitcast.55), channel_id=1, source_target_pairs={{0,1},{1,0},{2,3},{3,2},{4,5},{5,4},{6,7},{7,6},{8,9},{9,8},{10,11... | collective-permute-start | bytes 2949128 | tf_op jit(solution)/shard_map/ppermute | solution.py:251
  116.7 0.2 fusion
  116.9 1.6 %collective-permute-start.8 = (f32[1920,128]{1,0:T(8,128)S(1)}, f32[1920,128]{1,0:T(8,128)S(1)}, u32[]{:S(2)}, u32[]{:S(2)}) collective-permute-start(f32[1920,128]{1,0:T(8,128)S(1)} %fusion), channel_id=1, source_target_pairs={{0,2},{1,7},{2,4},{3,1},{4,6},{5,3},{6,0},{7,5},{8,10},{9,15},{10,... | collective-permute-start | bytes 2949128 | tf_op jit(solution)/shard_map/ppermute | solution.py:254
  118.6 3.2 %collective-permute-done.20.refs_1_ = f32[1536,128]{1,0:T(8,128)S(1)} collective-permute-done((f32[1536,128]{1,0:T(8,128)S(1)}, f32[1536,128]{1,0:T(8,128)S(1)}, u32[]{:S(2)}, u32[]{:S(2)}) %collective-permute-start.20) | collective-permute-done | bytes 786464 | tf_op jit(solution)/shard_map/ppermute | solution.py:254
  121.9 0.8 shard_map.91.refs_3_
  122.7 0.1 bitcast_add_fusion.1.refs_0_
  122.8 9.5 %collective-permute-done.8.refs_1_ = f32[1920,128]{1,0:T(8,128)S(1)} collective-permute-done((f32[1920,128]{1,0:T(8,128)S(1)}, f32[1920,128]{1,0:T(8,128)S(1)}, u32[]{:S(2)}, u32[]{:S(2)}) %collective-permute-start.8) | collective-permute-done | bytes 983072 | tf_op jit(solution)/shard_map/ppermute | solution.py:254
  132.4 0.8 shard_map.92
  (38 shorter events, 0.6 us)
Async XLA Ops:
  3.3 21.7 %all-to-all-start = ((f32[32,17,1,128]{3,2,1,0:T(1,128)}), f32[32,17,1,128]{3,2,1,0:T(1,128)S(1)}, u32[]{:S(2)}, u32[]{:S(2)}) async-start(f32[32,17,1,128]{3,2,1,0:T(1,128)} %get-tuple-element.38), calls=%async_computation | async-start | bytes 557056 | tf_op jit(solution)/shard_map/all_to_all | solution.py:208
  15.2 1.1 copy-start
  16.3 1.1 copy-start.1
  17.5 1.1 copy-start.2
  18.6 0.7 copy-start.4
  19.3 5.6 %copy-start.7 = (s32[32]{0:T(128)S(1)}, s32[32]{0:T(128)}, u32[]{:S(2)}) copy-start(s32[32]{0:T(128)} %parent_ref.1) | copy-start | bytes 388
  26.5 16.1 %all-to-all-start.1 = ((f32[32,16,128]{2,1,0:T(8,128)}), f32[32,16,128]{2,1,0:T(8,128)S(1)}, u32[]{:S(2)}, u32[]{:S(2)}) async-start(f32[32,16,128]{2,1,0:T(8,128)} %shard_map.75), calls=%async_computation.1 | async-start | bytes 524288 | tf_op jit(solution)/shard_map/all_to_all | solution.py:215
  33.0 9.6 %copy-start.3 = (bf16[768,512]{1,0:T(8,128)(2,1)S(1)}, bf16[768,512]{1,0:T(8,128)(2,1)}, u32[]{:S(2)}) copy-start(bf16[768,512]{1,0:T(8,128)(2,1)} %q_hbm.5) | copy-start | bytes 2359300
  33.0 9.6 %copy-start.5 = (f32[8,768]{1,0:T(8,128)S(1)}, f32[8,768]{1,0:T(8,128)}, u32[]{:S(2)}) copy-start(f32[8,768]{1,0:T(8,128)} %get-tuple-element.42.running_ref) | copy-start | bytes 73732
  33.0 9.6 %copy-start.6 = (f32[512]{0:T(512)S(1)}, f32[512]{0:T(512)}, u32[]{:S(2)}) copy-start(f32[512]{0:T(512)} %param.12) | copy-start | bytes 6148
  42.7 4.1 %slice-start = ((s8[6291456]{0:T(1024)(128)(4,1)}), s8[4194304]{0:T(1024)(128)(4,1)S(1)}, s32[]{:S(2)}) async-start(s8[6291456]{0:T(1024)(128)(4,1)} %bitcast.50), calls=%async_computation.2 | async-start | bytes 8388608
  42.7 1.3 copy-start.8
  44.0 2.8 %slice-start.1 = ((s8[6291456]{0:T(1024)(128)(4,1)}), s8[2097152]{0:T(1024)(128)(4,1)S(1)}, s32[]{:S(2)}) async-start(s8[6291456]{0:T(1024)(128)(4,1)} %bitcast.50), calls=%async_computation.3 | async-start | bytes 4194304
  47.3 5.7 %collective-permute-start = (f32[1160,128]{1,0:T(8,128)S(1)}, f32[1160,128]{1,0:T(8,128)S(1)}, u32[]{:S(2)}, u32[]{:S(2)}) collective-permute-start(f32[1160,128]{1,0:T(8,128)S(1)} %bitcast.64), channel_id=1, source_target_pairs={{0,1},{1,0},{2,3},{3,2},{4,5},{5,4},{6,7},{7,6},{8,9},{9,8},{10,11... | collective-permute-start | bytes 1781768 | tf_op jit(solution)/shard_map/ppermute | solution.py:251
  51.6 4.3 %collective-permute-start.1 = (f32[1536,128]{1,0:T(8,128)S(1)}, f32[1536,128]{1,0:T(8,128)S(1)}, u32[]{:S(2)}, u32[]{:S(2)}) collective-permute-start(f32[1536,128]{1,0:T(8,128)S(1)} %bitcast.60), channel_id=1, source_target_pairs={{0,1},{1,0},{2,3},{3,2},{4,5},{5,4},{6,7},{7,6},{8,9},{9,8},{10,11... | collective-permute-start | bytes 2359304 | tf_op jit(solution)/shard_map/ppermute | solution.py:251
  52.4 4.7 %collective-permute-start.2 = (f32[1920,128]{1,0:T(8,128)S(1)}, f32[1920,128]{1,0:T(8,128)S(1)}, u32[]{:S(2)}, u32[]{:S(2)}) collective-permute-start(f32[1920,128]{1,0:T(8,128)S(1)} %bitcast.56), channel_id=1, source_target_pairs={{0,1},{1,0},{2,3},{3,2},{4,5},{5,4},{6,7},{7,6},{8,9},{9,8},{10,11... | collective-permute-start | bytes 2949128 | tf_op jit(solution)/shard_map/ppermute | solution.py:251
  53.1 9.7 %collective-permute-start.10 = (f32[1160,128]{1,0:T(8,128)S(1)}, f32[1160,128]{1,0:T(8,128)S(1)}, u32[]{:S(2)}, u32[]{:S(2)}) collective-permute-start(f32[1160,128]{1,0:T(8,128)S(1)} %bitcast_add_fusion.11.refs_0_), channel_id=1, source_target_pairs={{0,2},{1,7},{2,4},{3,1},{4,6},{5,3},{6,0},{7,5},{8,10},{9,15},{10,... | collective-permute-start | bytes 1781768 | tf_op jit(solution)/shard_map/ppermute | solution.py:254
  56.0 15.2 %collective-permute-start.16 = (f32[1536,128]{1,0:T(8,128)S(1)}, f32[1536,128]{1,0:T(8,128)S(1)}, u32[]{:S(2)}, u32[]{:S(2)}) collective-permute-start(f32[1536,128]{1,0:T(8,128)S(1)} %bitcast_add_fusion.7.refs_1_), channel_id=1, source_target_pairs={{0,2},{1,7},{2,4},{3,1},{4,6},{5,3},{6,0},{7,5},{8,10},{9,15},{10,... | collective-permute-start | bytes 2359304 | tf_op jit(solution)/shard_map/ppermute | solution.py:254
  57.7 15.6 %collective-permute-start.9 = (f32[1160,128]{1,0:T(8,128)S(1)}, f32[1160,128]{1,0:T(8,128)S(1)}, u32[]{:S(2)}, u32[]{:S(2)}) collective-permute-start(f32[1160,128]{1,0:T(8,128)S(1)} %bitcast.62), channel_id=1, source_target_pairs={{0,1},{1,0},{2,3},{3,2},{4,5},{5,4},{6,7},{7,6},{8,9},{9,8},{10,11... | collective-permute-start | bytes 1781768 | tf_op jit(solution)/shard_map/ppermute | solution.py:251
  58.4 15.2 %collective-permute-start.15 = (f32[1536,128]{1,0:T(8,128)S(1)}, f32[1536,128]{1,0:T(8,128)S(1)}, u32[]{:S(2)}, u32[]{:S(2)}) collective-permute-start(f32[1536,128]{1,0:T(8,128)S(1)} %bitcast.59), channel_id=1, source_target_pairs={{0,1},{1,0},{2,3},{3,2},{4,5},{5,4},{6,7},{7,6},{8,9},{9,8},{10,11... | collective-permute-start | bytes 2359304 | tf_op jit(solution)/shard_map/ppermute | solution.py:251
  59.0 22.7 %collective-permute-start.4 = (f32[1920,128]{1,0:T(8,128)S(1)}, f32[1920,128]{1,0:T(8,128)S(1)}, u32[]{:S(2)}, u32[]{:S(2)}) collective-permute-start(f32[1920,128]{1,0:T(8,128)S(1)} %bitcast_add_fusion.3.refs_2_), channel_id=1, source_target_pairs={{0,2},{1,7},{2,4},{3,1},{4,6},{5,3},{6,0},{7,5},{8,10},{9,15},{10,... | collective-permute-start | bytes 2949128 | tf_op jit(solution)/shard_map/ppermute | solution.py:254
  62.8 13.1 %collective-permute-start.3 = (f32[1920,128]{1,0:T(8,128)S(1)}, f32[1920,128]{1,0:T(8,128)S(1)}, u32[]{:S(2)}, u32[]{:S(2)}) collective-permute-start(f32[1920,128]{1,0:T(8,128)S(1)} %bitcast.54), channel_id=1, source_target_pairs={{0,1},{1,0},{2,3},{3,2},{4,5},{5,4},{6,7},{7,6},{8,9},{9,8},{10,11... | collective-permute-start | bytes 2949128 | tf_op jit(solution)/shard_map/ppermute | solution.py:251
  71.2 19.0 %collective-permute-start.13 = (f32[1160,128]{1,0:T(8,128)S(1)}, f32[1160,128]{1,0:T(8,128)S(1)}, u32[]{:S(2)}, u32[]{:S(2)}) collective-permute-start(f32[1160,128]{1,0:T(8,128)S(1)} %bitcast.61), channel_id=1, source_target_pairs={{0,1},{1,0},{2,3},{3,2},{4,5},{5,4},{6,7},{7,6},{8,9},{9,8},{10,11... | collective-permute-start | bytes 1781768 | tf_op jit(solution)/shard_map/ppermute | solution.py:251
  73.4 17.0 %collective-permute-start.19 = (f32[1536,128]{1,0:T(8,128)S(1)}, f32[1536,128]{1,0:T(8,128)S(1)}, u32[]{:S(2)}, u32[]{:S(2)}) collective-permute-start(f32[1536,128]{1,0:T(8,128)S(1)} %bitcast.57), channel_id=1, source_target_pairs={{0,1},{1,0},{2,3},{3,2},{4,5},{5,4},{6,7},{7,6},{8,9},{9,8},{10,11... | collective-permute-start | bytes 2359304 | tf_op jit(solution)/shard_map/ppermute | solution.py:251
  73.6 14.5 %collective-permute-start.11 = (f32[1160,128]{1,0:T(8,128)S(1)}, f32[1160,128]{1,0:T(8,128)S(1)}, u32[]{:S(2)}, u32[]{:S(2)}) collective-permute-start(f32[1160,128]{1,0:T(8,128)S(1)} %fusion.5), channel_id=1, source_target_pairs={{0,2},{1,7},{2,4},{3,1},{4,6},{5,3},{6,0},{7,5},{8,10},{9,15},{10,... | collective-permute-start | bytes 1781768 | tf_op jit(solution)/shard_map/ppermute | solution.py:254
  75.9 20.6 %collective-permute-start.17 = (f32[1536,128]{1,0:T(8,128)S(1)}, f32[1536,128]{1,0:T(8,128)S(1)}, u32[]{:S(2)}, u32[]{:S(2)}) collective-permute-start(f32[1536,128]{1,0:T(8,128)S(1)} %fusion.3), channel_id=1, source_target_pairs={{0,2},{1,7},{2,4},{3,1},{4,6},{5,3},{6,0},{7,5},{8,10},{9,15},{10,... | collective-permute-start | bytes 2359304 | tf_op jit(solution)/shard_map/ppermute | solution.py:254
  81.9 32.4 %collective-permute-start.5 = (f32[1920,128]{1,0:T(8,128)S(1)}, f32[1920,128]{1,0:T(8,128)S(1)}, u32[]{:S(2)}, u32[]{:S(2)}) collective-permute-start(f32[1920,128]{1,0:T(8,128)S(1)} %fusion.1), channel_id=1, source_target_pairs={{0,2},{1,7},{2,4},{3,1},{4,6},{5,3},{6,0},{7,5},{8,10},{9,15},{10,... | collective-permute-start | bytes 2949128 | tf_op jit(solution)/shard_map/ppermute | solution.py:254
  88.1 28.6 %collective-permute-start.7 = (f32[1920,128]{1,0:T(8,128)S(1)}, f32[1920,128]{1,0:T(8,128)S(1)}, u32[]{:S(2)}, u32[]{:S(2)}) collective-permute-start(f32[1920,128]{1,0:T(8,128)S(1)} %bitcast.53), channel_id=1, source_target_pairs={{0,1},{1,0},{2,3},{3,2},{4,5},{5,4},{6,7},{7,6},{8,9},{9,8},{10,11... | collective-permute-start | bytes 2949128 | tf_op jit(solution)/shard_map/ppermute | solution.py:251
  90.2 10.5 %collective-permute-start.12 = (f32[1160,128]{1,0:T(8,128)S(1)}, f32[1160,128]{1,0:T(8,128)S(1)}, u32[]{:S(2)}, u32[]{:S(2)}) collective-permute-start(f32[1160,128]{1,0:T(8,128)S(1)} %bitcast.63), channel_id=1, source_target_pairs={{0,1},{1,0},{2,3},{3,2},{4,5},{5,4},{6,7},{7,6},{8,9},{9,8},{10,11... | collective-permute-start | bytes 1781768 | tf_op jit(solution)/shard_map/ppermute | solution.py:251
  90.4 23.0 %collective-permute-start.14 = (f32[1160,128]{1,0:T(8,128)S(1)}, f32[1160,128]{1,0:T(8,128)S(1)}, u32[]{:S(2)}, u32[]{:S(2)}) collective-permute-start(f32[1160,128]{1,0:T(8,128)S(1)} %fusion.4), channel_id=1, source_target_pairs={{0,2},{1,7},{2,4},{3,1},{4,6},{5,3},{6,0},{7,5},{8,10},{9,15},{10,... | collective-permute-start | bytes 1781768 | tf_op jit(solution)/shard_map/ppermute | solution.py:254
  96.7 25.2 %collective-permute-start.20 = (f32[1536,128]{1,0:T(8,128)S(1)}, f32[1536,128]{1,0:T(8,128)S(1)}, u32[]{:S(2)}, u32[]{:S(2)}) collective-permute-start(f32[1536,128]{1,0:T(8,128)S(1)} %fusion.2), channel_id=1, source_target_pairs={{0,2},{1,7},{2,4},{3,1},{4,6},{5,3},{6,0},{7,5},{8,10},{9,15},{10,... | collective-permute-start | bytes 2359304 | tf_op jit(solution)/shard_map/ppermute | solution.py:254
  100.7 17.8 %collective-permute-start.18 = (f32[1536,128]{1,0:T(8,128)S(1)}, f32[1536,128]{1,0:T(8,128)S(1)}, u32[]{:S(2)}, u32[]{:S(2)}) collective-permute-start(f32[1536,128]{1,0:T(8,128)S(1)} %bitcast.58), channel_id=1, source_target_pairs={{0,1},{1,0},{2,3},{3,2},{4,5},{5,4},{6,7},{7,6},{8,9},{9,8},{10,11... | collective-permute-start | bytes 2359304 | tf_op jit(solution)/shard_map/ppermute | solution.py:251
  115.0 7.7 %collective-permute-start.6 = (f32[1920,128]{1,0:T(8,128)S(1)}, f32[1920,128]{1,0:T(8,128)S(1)}, u32[]{:S(2)}, u32[]{:S(2)}) collective-permute-start(f32[1920,128]{1,0:T(8,128)S(1)} %bitcast.55), channel_id=1, source_target_pairs={{0,1},{1,0},{2,3},{3,2},{4,5},{5,4},{6,7},{7,6},{8,9},{9,8},{10,11... | collective-permute-start | bytes 2949128 | tf_op jit(solution)/shard_map/ppermute | solution.py:251
  116.9 15.5 %collective-permute-start.8 = (f32[1920,128]{1,0:T(8,128)S(1)}, f32[1920,128]{1,0:T(8,128)S(1)}, u32[]{:S(2)}, u32[]{:S(2)}) collective-permute-start(f32[1920,128]{1,0:T(8,128)S(1)} %fusion), channel_id=1, source_target_pairs={{0,2},{1,7},{2,4},{3,1},{4,6},{5,3},{6,0},{7,5},{8,10},{9,15},{10,... | collective-permute-start | bytes 2949128 | tf_op jit(solution)/shard_map/ppermute | solution.py:254

commit v10 on v9

--- a/solution.py
+++ b/solution.py
@@ -95,19 +95,21 @@
 
 
 def mix_kernel(
-    place_ref, q_hbm, prefix_ref, early_ref, late_ref, running_ref, gain_ref, _,
+    place_ref, q_hbm, prefix_ref, early_hbm, late_ref, running_ref, gain_ref, _,
     out_ref, squares_out_ref,
-    q_ref, sems,
+    q_ref, early_ref, sems,
 ):
     heads = [slice(128 * h, 128 * h + 128) for h in range(4)]
-    inputs = load(sems, *[(q_hbm.at[:, cols], q_ref.at[:, cols]) for cols in heads])
+    inputs = load(sems, *[(q_hbm.at[:, cols], q_ref.at[:, cols]) for cols in heads[2:] + heads[:2]], (early_hbm, early_ref))
     parts, share, width = out_ref.shape
     growth = jnp.exp(running_ref[...].T)
     squares = None
-    for h in range(4):
-        cols = slice(128 * h, 128 * h + 128)
+    for h in (2, 3, 0, 1):
+        cols = heads[h]
         high, low = split(prefix_ref[h])
-        inputs[h].wait()
+        inputs[(h + 2) % 4].wait()
+        if h == 0:
+            inputs[4].wait()
         q = q_ref[:, cols]
         inner = (early_ref if h < 2 else late_ref)[:, 128 * (h % 2) : 128 * (h % 2) + 128]
         both = dot(q, jnp.concatenate([high, low], axis=1))
@@ -229,10 +231,10 @@
     features, squares = call(
         mix_kernel,
         [((8, share, width), BF16), ((8, 8, 128), F32)],
-        [SMEM, HBM, VMEM, VMEM, VMEM, VMEM, VMEM, HBM],
-        scratch=[pltpu.VMEM(q.shape, BF16), dma((4,))],
+        [SMEM, HBM, VMEM, HBM, VMEM, VMEM, VMEM, HBM],
+        scratch=[pltpu.VMEM(q.shape, BF16), pltpu.VMEM(early.shape, F32), dma((5,))],
         flops=2**34,
-        vmem=50 * 2**20,
+        vmem=51 * 2**20,
     )(places, q, prefix, early, late, running, gain.reshape(1, width), w)
 
     def project(start, size, extra, first, after):

time: 134 us -> 133 us (level)
    unnamed x22 -> x20, local copies, waits for them, and re-layouts: 5.44 us -> 4.16 us
where the time goes in v10:
time: 133 us
  waiting for transfers between devices  54.2 us (41%)
  starting transfers between devices  47.6 us (36%)
  Pallas kernels  25 us (19%)
  local copies, waits for them, and re-layouts  4.16 us (3%)
  other arithmetic  1.49 us (1%)
    ppermute x9, waiting for transfers between devices, per_device(): arrived = [lax.ppermute(total, 'head', RING) for total in totals]  45.8 us
    ppermute x9, starting transfers between devices, per_device(): arrived = [lax.ppermute(total, 'head', RING) for total in totals]  17.5 us
    all_to_all x1, starting transfers between devices, per_device(): everyone = lax.all_to_all(chunks, 'seg', 0, 0, tiled=True)  11.9 us
    ppermute x12, starting transfers between devices, per_device(): lax.ppermute(send[0], 'head', SWAP)  11.7 us
    pallas_call x12, Pallas kernels, project(): call(functools.partial(project_kernel, start, size, first), [((1, size //...  7.03 us
    all_to_all x1, starting transfers between devices, per_device(): prefix = lax.all_to_all(mine, 'seg', 0, 0, tiled=True).reshape(4, 128, 128)  6.46 us
    pallas_call x1, Pallas kernels, per_device(): call(functools.partial(within_kernel, 2), [((length, width // 2), F32)],...  4.92 us
    all_to_all x1, waiting for transfers between devices, per_device(): prefix = lax.all_to_all(mine, 'seg', 0, 0, tiled=True).reshape(4, 128, 128)  4.68 us
  transfers between devices with their start and end apart: 23, of which 10 were waited for; matrix products, arithmetic and copies ran while one was open for 1% of the time, Pallas kernels for 11%

profile of v10, /device:TPU:1, one launch (start us, length us, event | category | flops | bytes accessed | tf_op | source)
XLA Modules:
  0.0 132.9 jit_solution(5474349289851095663)
XLA Ops:
  0.0 3.3 %shard_map.73 = (f32[32,17,1,128]{3,2,1,0:T(1,128)}, f32[8,768]{1,0:T(8,128)}) custom-call(f32[4,768]{1,0:T(4,128)} %decay_hbm.1, bf16[768,512]{1,0:T(8,128)(2,1)} %k_hbm.5, bf16[768,512]{1,0:T(8,128)(2,1)} %v_hbm.5), custom_call_target="tpu_custom_call" | custom-call | flops 268435456 | bytes 1048576 | tf_op jit(solution)/shard_map/pallas_call | solution.py:203
  3.3 11.9 %all-to-all-start = ((f32[32,17,1,128]{3,2,1,0:T(1,128)}), f32[32,17,1,128]{3,2,1,0:T(1,128)S(1)}, u32[]{:S(2)}, u32[]{:S(2)}) async-start(f32[32,17,1,128]{3,2,1,0:T(1,128)} %get-tuple-element.38), calls=%async_computation | async-start | bytes 557056 | tf_op jit(solution)/shard_map/all_to_all | solution.py:210
  15.2 1.1 copy-done
  16.3 1.1 copy-done.1
  17.5 1.1 copy-done.2
  18.6 0.7 copy-done.4
  19.3 2.0 %shard_map.74.early_hbm = f32[768,256]{1,0:T(8,128)S(1)} custom-call(bf16[768,512]{1,0:T(8,128)(2,1)S(1)} %copy-done.2, bf16[768,512]{1,0:T(8,128)(2,1)S(1)} %copy-done, bf16[768,512]{1,0:T(8,128)(2,1)S(1)} %copy-done.1, f32[8,768]{1,0:T(8,128)S(1)} %copy-done.4), custom_call_target="tpu_custom_call" | custom-call | flops 1073741824 | bytes 1048576 | tf_op jit(solution)/shard_map/pallas_call | solution.py:212
  21.3 3.7 %all-to-all-done.all_ref = f32[32,17,1,128]{3,2,1,0:T(1,128)S(1)} async-done(((f32[32,17,1,128]{3,2,1,0:T(1,128)}), f32[32,17,1,128]{3,2,1,0:T(1,128)S(1)}, u32[]{:S(2)}, u32[]{:S(2)}) %all-to-all-start) | async-done | bytes 278560 | tf_op jit(solution)/shard_map/all_to_all | solution.py:210
  25.0 1.6 %shard_map.75 = f32[32,16,128]{2,1,0:T(8,128)} custom-call(s32[32]{0:T(128)S(1)} %copy-done.7, f32[32,17,1,128]{3,2,1,0:T(1,128)S(1)} %all-to-all-done.all_ref), custom_call_target="tpu_custom_call" | custom-call | flops 268435456 | bytes 1048576 | tf_op jit(solution)/shard_map/pallas_call | solution.py:216
  26.5 6.5 %all-to-all-start.1 = ((f32[32,16,128]{2,1,0:T(8,128)}), f32[32,16,128]{2,1,0:T(8,128)S(1)}, u32[]{:S(2)}, u32[]{:S(2)}) async-start(f32[32,16,128]{2,1,0:T(8,128)} %shard_map.75), calls=%async_computation.1 | async-start | bytes 524288 | tf_op jit(solution)/shard_map/all_to_all | solution.py:217
  33.0 4.9 %shard_map.76.late_ref = f32[768,256]{1,0:T(8,128)} custom-call(bf16[768,512]{1,0:T(8,128)(2,1)} %q_hbm.5, bf16[768,512]{1,0:T(8,128)(2,1)} %k_hbm.5, bf16[768,512]{1,0:T(8,128)(2,1)} %v_hbm.5, f32[8,768]{1,0:T(8,128)} %get-tuple-element.42.running_ref), custom_call_target="tpu_custom_call" | custom-call | flops 1073741824 | bytes 1048576 | tf_op jit(solution)/shard_map/pallas_call | solution.py:218
  38.0 4.7 %all-to-all-done.1 = f32[32,16,128]{2,1,0:T(8,128)S(1)} async-done(((f32[32,16,128]{2,1,0:T(8,128)}), f32[32,16,128]{2,1,0:T(8,128)S(1)}, u32[]{:S(2)}, u32[]{:S(2)}) %all-to-all-start.1) | async-done | bytes 262176 | tf_op jit(solution)/shard_map/all_to_all | solution.py:217
  42.7 3.6 %shard_map.77 = (bf16[8,96,512]{2,1,0:T(8,128)(2,1)S(1)}, f32[8,8,128]{2,1,0:T(8,128)S(1)}) custom-call(s32[8]{0:T(128)S(1)} %compare_select_fusion.place_ref, bf16[768,512]{1,0:T(8,128)(2,1)S(1)} %copy-done.3, f32[4,128,128]{2,1,0:T(8,128)S(1)} %bitcast.52, f32[768,256]{1,0:T(8,128)S(1)} %shard_map.74.early_hbm, f32[768,256]{1,0:T(8,128)} %shard_map.76.late_ref, ...), custom_call_target="tpu_custom_call" | custom-call | flops 17179869184 | bytes 1048576 | tf_op jit(solution)/shard_map/pallas_call | solution.py:231
  46.3 0.5 shard_map.78
  46.8 3.7 %collective-permute-start = (f32[1160,128]{1,0:T(8,128)S(1)}, f32[1160,128]{1,0:T(8,128)S(1)}, u32[]{:S(2)}, u32[]{:S(2)}) collective-permute-start(f32[1160,128]{1,0:T(8,128)S(1)} %bitcast.64), channel_id=1, source_target_pairs={{0,1},{1,0},{2,3},{3,2},{4,5},{5,4},{6,7},{7,6},{8,9},{9,8},{10,11... | collective-permute-start | bytes 1781768 | tf_op jit(solution)/shard_map/ppermute | solution.py:253
  50.6 0.6 shard_map.79
  51.2 0.1 collective-permute-start.1
  51.3 0.7 shard_map.80
  52.0 0.6 collective-permute-start.2
  52.6 2.8 %collective-permute-start.10 = (f32[1160,128]{1,0:T(8,128)S(1)}, f32[1160,128]{1,0:T(8,128)S(1)}, u32[]{:S(2)}, u32[]{:S(2)}) collective-permute-start(f32[1160,128]{1,0:T(8,128)S(1)} %bitcast_add_fusion.11.refs_0_), channel_id=1, source_target_pairs={{0,2},{1,7},{2,4},{3,1},{4,6},{5,3},{6,0},{7,5},{8,10},{9,15},{10,... | collective-permute-start | bytes 1781768 | tf_op jit(solution)/shard_map/ppermute | solution.py:256
  55.5 1.1 collective-permute-start.16
  56.6 0.1 bitcast_add_fusion.3.refs_2_
  56.8 0.5 shard_map.84
  57.3 0.1 collective-permute-start.9
  57.4 0.6 shard_map.88
  58.0 0.6 collective-permute-start.15
  58.5 1.1 collective-permute-start.4
  59.6 0.7 shard_map.81
  60.3 2.0 %collective-permute-done.10.refs_0_ = f32[1160,128]{1,0:T(8,128)S(1)} collective-permute-done((f32[1160,128]{1,0:T(8,128)S(1)}, f32[1160,128]{1,0:T(8,128)S(1)}, u32[]{:S(2)}, u32[]{:S(2)}) %collective-permute-start.10) | collective-permute-done | bytes 593952 | tf_op jit(solution)/shard_map/ppermute | solution.py:256
  62.3 1.6 %collective-permute-start.3 = (f32[1920,128]{1,0:T(8,128)S(1)}, f32[1920,128]{1,0:T(8,128)S(1)}, u32[]{:S(2)}, u32[]{:S(2)}) collective-permute-start(f32[1920,128]{1,0:T(8,128)S(1)} %bitcast.54), channel_id=1, source_target_pairs={{0,1},{1,0},{2,3},{3,2},{4,5},{5,4},{6,7},{7,6},{8,9},{9,8},{10,11... | collective-permute-start | bytes 2949128 | tf_op jit(solution)/shard_map/ppermute | solution.py:253
  63.9 0.5 shard_map.86
  64.4 6.4 %collective-permute-done.16.refs_0_ = f32[1536,128]{1,0:T(8,128)S(1)} collective-permute-done((f32[1536,128]{1,0:T(8,128)S(1)}, f32[1536,128]{1,0:T(8,128)S(1)}, u32[]{:S(2)}, u32[]{:S(2)}) %collective-permute-start.16) | collective-permute-done | bytes 786464 | tf_op jit(solution)/shard_map/ppermute | solution.py:256
  70.7 1.6 %collective-permute-start.13 = (f32[1160,128]{1,0:T(8,128)S(1)}, f32[1160,128]{1,0:T(8,128)S(1)}, u32[]{:S(2)}, u32[]{:S(2)}) collective-permute-start(f32[1160,128]{1,0:T(8,128)S(1)} %bitcast.61), channel_id=1, source_target_pairs={{0,1},{1,0},{2,3},{3,2},{4,5},{5,4},{6,7},{7,6},{8,9},{9,8},{10,11... | collective-permute-start | bytes 1781768 | tf_op jit(solution)/shard_map/ppermute | solution.py:253
  72.3 0.6 shard_map.90
  72.9 0.1 collective-permute-start.19
  73.0 0.1 fusion.5
  73.1 2.1 %collective-permute-start.11 = (f32[1160,128]{1,0:T(8,128)S(1)}, f32[1160,128]{1,0:T(8,128)S(1)}, u32[]{:S(2)}, u32[]{:S(2)}) collective-permute-start(f32[1160,128]{1,0:T(8,128)S(1)} %fusion.5), channel_id=1, source_target_pairs={{0,2},{1,7},{2,4},{3,1},{4,6},{5,3},{6,0},{7,5},{8,10},{9,15},{10,... | collective-permute-start | bytes 1781768 | tf_op jit(solution)/shard_map/ppermute | solution.py:256
  75.3 0.2 fusion.3
  75.4 0.1 collective-permute-start.17
  75.5 5.8 %collective-permute-done.4.refs_0_ = f32[1920,128]{1,0:T(8,128)S(1)} collective-permute-done((f32[1920,128]{1,0:T(8,128)S(1)}, f32[1920,128]{1,0:T(8,128)S(1)}, u32[]{:S(2)}, u32[]{:S(2)}) %collective-permute-start.4) | collective-permute-done | bytes 983072 | tf_op jit(solution)/shard_map/ppermute | solution.py:256
  81.3 0.2 fusion.1
  81.5 3.2 %collective-permute-start.5 = (f32[1920,128]{1,0:T(8,128)S(1)}, f32[1920,128]{1,0:T(8,128)S(1)}, u32[]{:S(2)}, u32[]{:S(2)}) collective-permute-start(f32[1920,128]{1,0:T(8,128)S(1)} %fusion.1), channel_id=1, source_target_pairs={{0,2},{1,7},{2,4},{3,1},{4,6},{5,3},{6,0},{7,5},{8,10},{9,15},{10,... | collective-permute-start | bytes 2949128 | tf_op jit(solution)/shard_map/ppermute | solution.py:256
  84.7 0.7 shard_map.83
  85.4 2.3 %collective-permute-done.11.refs_0_ = f32[1160,128]{1,0:T(8,128)S(1)} collective-permute-done((f32[1160,128]{1,0:T(8,128)S(1)}, f32[1160,128]{1,0:T(8,128)S(1)}, u32[]{:S(2)}, u32[]{:S(2)}) %collective-permute-start.11) | collective-permute-done | bytes 593952 | tf_op jit(solution)/shard_map/ppermute | solution.py:256
  87.6 1.6 %collective-permute-start.7 = (f32[1920,128]{1,0:T(8,128)S(1)}, f32[1920,128]{1,0:T(8,128)S(1)}, u32[]{:S(2)}, u32[]{:S(2)}) collective-permute-start(f32[1920,128]{1,0:T(8,128)S(1)} %bitcast.53), channel_id=1, source_target_pairs={{0,1},{1,0},{2,3},{3,2},{4,5},{5,4},{6,7},{7,6},{8,9},{9,8},{10,11... | collective-permute-start | bytes 2949128 | tf_op jit(solution)/shard_map/ppermute | solution.py:253
  89.2 0.5 shard_map.85
  89.7 0.1 collective-permute-start.12
  89.9 2.1 %collective-permute-start.14 = (f32[1160,128]{1,0:T(8,128)S(1)}, f32[1160,128]{1,0:T(8,128)S(1)}, u32[]{:S(2)}, u32[]{:S(2)}) collective-permute-start(f32[1160,128]{1,0:T(8,128)S(1)} %fusion.4), channel_id=1, source_target_pairs={{0,2},{1,7},{2,4},{3,1},{4,6},{5,3},{6,0},{7,5},{8,10},{9,15},{10,... | collective-permute-start | bytes 1781768 | tf_op jit(solution)/shard_map/ppermute | solution.py:256
  92.0 4.0 %collective-permute-done.17.refs_0_ = f32[1536,128]{1,0:T(8,128)S(1)} collective-permute-done((f32[1536,128]{1,0:T(8,128)S(1)}, f32[1536,128]{1,0:T(8,128)S(1)}, u32[]{:S(2)}, u32[]{:S(2)}) %collective-permute-start.17) | collective-permute-done | bytes 786464 | tf_op jit(solution)/shard_map/ppermute | solution.py:256
  96.1 0.1 fusion.2
  96.2 3.4 %collective-permute-start.20 = (f32[1536,128]{1,0:T(8,128)S(1)}, f32[1536,128]{1,0:T(8,128)S(1)}, u32[]{:S(2)}, u32[]{:S(2)}) collective-permute-start(f32[1536,128]{1,0:T(8,128)S(1)} %fusion.2), channel_id=1, source_target_pairs={{0,2},{1,7},{2,4},{3,1},{4,6},{5,3},{6,0},{7,5},{8,10},{9,15},{10,... | collective-permute-start | bytes 2359304 | tf_op jit(solution)/shard_map/ppermute | solution.py:256
  99.6 0.6 shard_map.89
  100.2 0.1 collective-permute-start.18
  100.4 12.6 %collective-permute-done.14.refs_1_ = f32[1160,128]{1,0:T(8,128)S(1)} collective-permute-done((f32[1160,128]{1,0:T(8,128)S(1)}, f32[1160,128]{1,0:T(8,128)S(1)}, u32[]{:S(2)}, u32[]{:S(2)}) %collective-permute-start.14) | collective-permute-done | bytes 593952 | tf_op jit(solution)/shard_map/ppermute | solution.py:256
  113.0 0.9 shard_map.87
  113.9 0.7 shard_map.82
  114.6 1.7 %collective-permute-start.6 = (f32[1920,128]{1,0:T(8,128)S(1)}, f32[1920,128]{1,0:T(8,128)S(1)}, u32[]{:S(2)}, u32[]{:S(2)}) collective-permute-start(f32[1920,128]{1,0:T(8,128)S(1)} %bitcast.55), channel_id=1, source_target_pairs={{0,1},{1,0},{2,3},{3,2},{4,5},{5,4},{6,7},{7,6},{8,9},{9,8},{10,11... | collective-permute-start | bytes 2949128 | tf_op jit(solution)/shard_map/ppermute | solution.py:253
  116.2 0.2 fusion
  116.4 1.6 %collective-permute-start.8 = (f32[1920,128]{1,0:T(8,128)S(1)}, f32[1920,128]{1,0:T(8,128)S(1)}, u32[]{:S(2)}, u32[]{:S(2)}) collective-permute-start(f32[1920,128]{1,0:T(8,128)S(1)} %fusion), channel_id=1, source_target_pairs={{0,2},{1,7},{2,4},{3,1},{4,6},{5,3},{6,0},{7,5},{8,10},{9,15},{10,... | collective-permute-start | bytes 2949128 | tf_op jit(solution)/shard_map/ppermute | solution.py:256
  118.1 3.2 %collective-permute-done.20.refs_1_ = f32[1536,128]{1,0:T(8,128)S(1)} collective-permute-done((f32[1536,128]{1,0:T(8,128)S(1)}, f32[1536,128]{1,0:T(8,128)S(1)}, u32[]{:S(2)}, u32[]{:S(2)}) %collective-permute-start.20) | collective-permute-done | bytes 786464 | tf_op jit(solution)/shard_map/ppermute | solution.py:256
  121.4 0.8 shard_map.91.refs_3_
  122.2 0.1 bitcast_add_fusion.1.refs_0_
  122.4 9.5 %collective-permute-done.8.refs_1_ = f32[1920,128]{1,0:T(8,128)S(1)} collective-permute-done((f32[1920,128]{1,0:T(8,128)S(1)}, f32[1920,128]{1,0:T(8,128)S(1)}, u32[]{:S(2)}, u32[]{:S(2)}) %collective-permute-start.8) | collective-permute-done | bytes 983072 | tf_op jit(solution)/shard_map/ppermute | solution.py:256
  131.9 0.8 shard_map.92
  (36 shorter events, 0.5 us)
Async XLA Ops:
  3.3 21.7 %all-to-all-start = ((f32[32,17,1,128]{3,2,1,0:T(1,128)}), f32[32,17,1,128]{3,2,1,0:T(1,128)S(1)}, u32[]{:S(2)}, u32[]{:S(2)}) async-start(f32[32,17,1,128]{3,2,1,0:T(1,128)} %get-tuple-element.38), calls=%async_computation | async-start | bytes 557056 | tf_op jit(solution)/shard_map/all_to_all | solution.py:210
  15.2 1.1 copy-start
  16.3 1.1 copy-start.1
  17.5 1.1 copy-start.2
  18.6 0.7 copy-start.4
  19.3 5.6 %copy-start.7 = (s32[32]{0:T(128)S(1)}, s32[32]{0:T(128)}, u32[]{:S(2)}) copy-start(s32[32]{0:T(128)} %parent_ref.1) | copy-start | bytes 388
  26.5 16.1 %all-to-all-start.1 = ((f32[32,16,128]{2,1,0:T(8,128)}), f32[32,16,128]{2,1,0:T(8,128)S(1)}, u32[]{:S(2)}, u32[]{:S(2)}) async-start(f32[32,16,128]{2,1,0:T(8,128)} %shard_map.75), calls=%async_computation.1 | async-start | bytes 524288 | tf_op jit(solution)/shard_map/all_to_all | solution.py:217
  33.0 9.6 %copy-start.3 = (bf16[768,512]{1,0:T(8,128)(2,1)S(1)}, bf16[768,512]{1,0:T(8,128)(2,1)}, u32[]{:S(2)}) copy-start(bf16[768,512]{1,0:T(8,128)(2,1)} %q_hbm.5) | copy-start | bytes 2359300
  33.0 9.6 %copy-start.5 = (f32[8,768]{1,0:T(8,128)S(1)}, f32[8,768]{1,0:T(8,128)}, u32[]{:S(2)}) copy-start(f32[8,768]{1,0:T(8,128)} %get-tuple-element.42.running_ref) | copy-start | bytes 73732
  33.0 9.6 %copy-start.6 = (f32[512]{0:T(512)S(1)}, f32[512]{0:T(512)}, u32[]{:S(2)}) copy-start(f32[512]{0:T(512)} %param.12) | copy-start | bytes 6148
  42.7 3.7 %slice-start = ((s8[6291456]{0:T(1024)(128)(4,1)}), s8[4194304]{0:T(1024)(128)(4,1)S(1)}, s32[]{:S(2)}) async-start(s8[6291456]{0:T(1024)(128)(4,1)} %bitcast.50), calls=%async_computation.2 | async-start | bytes 8388608
  42.7 3.7 %slice-start.1 = ((s8[6291456]{0:T(1024)(128)(4,1)}), s8[2097152]{0:T(1024)(128)(4,1)S(1)}, s32[]{:S(2)}) async-start(s8[6291456]{0:T(1024)(128)(4,1)} %bitcast.50), calls=%async_computation.3 | async-start | bytes 4194304
  46.8 5.7 %collective-permute-start = (f32[1160,128]{1,0:T(8,128)S(1)}, f32[1160,128]{1,0:T(8,128)S(1)}, u32[]{:S(2)}, u32[]{:S(2)}) collective-permute-start(f32[1160,128]{1,0:T(8,128)S(1)} %bitcast.64), channel_id=1, source_target_pairs={{0,1},{1,0},{2,3},{3,2},{4,5},{5,4},{6,7},{7,6},{8,9},{9,8},{10,11... | collective-permute-start | bytes 1781768 | tf_op jit(solution)/shard_map/ppermute | solution.py:253
  51.2 4.3 %collective-permute-start.1 = (f32[1536,128]{1,0:T(8,128)S(1)}, f32[1536,128]{1,0:T(8,128)S(1)}, u32[]{:S(2)}, u32[]{:S(2)}) collective-permute-start(f32[1536,128]{1,0:T(8,128)S(1)} %bitcast.60), channel_id=1, source_target_pairs={{0,1},{1,0},{2,3},{3,2},{4,5},{5,4},{6,7},{7,6},{8,9},{9,8},{10,11... | collective-permute-start | bytes 2359304 | tf_op jit(solution)/shard_map/ppermute | solution.py:253
  52.0 4.7 %collective-permute-start.2 = (f32[1920,128]{1,0:T(8,128)S(1)}, f32[1920,128]{1,0:T(8,128)S(1)}, u32[]{:S(2)}, u32[]{:S(2)}) collective-permute-start(f32[1920,128]{1,0:T(8,128)S(1)} %bitcast.56), channel_id=1, source_target_pairs={{0,1},{1,0},{2,3},{3,2},{4,5},{5,4},{6,7},{7,6},{8,9},{9,8},{10,11... | collective-permute-start | bytes 2949128 | tf_op jit(solution)/shard_map/ppermute | solution.py:253
  52.6 9.7 %collective-permute-start.10 = (f32[1160,128]{1,0:T(8,128)S(1)}, f32[1160,128]{1,0:T(8,128)S(1)}, u32[]{:S(2)}, u32[]{:S(2)}) collective-permute-start(f32[1160,128]{1,0:T(8,128)S(1)} %bitcast_add_fusion.11.refs_0_), channel_id=1, source_target_pairs={{0,2},{1,7},{2,4},{3,1},{4,6},{5,3},{6,0},{7,5},{8,10},{9,15},{10,... | collective-permute-start | bytes 1781768 | tf_op jit(solution)/shard_map/ppermute | solution.py:256
  55.5 15.2 %collective-permute-start.16 = (f32[1536,128]{1,0:T(8,128)S(1)}, f32[1536,128]{1,0:T(8,128)S(1)}, u32[]{:S(2)}, u32[]{:S(2)}) collective-permute-start(f32[1536,128]{1,0:T(8,128)S(1)} %bitcast_add_fusion.7.refs_1_), channel_id=1, source_target_pairs={{0,2},{1,7},{2,4},{3,1},{4,6},{5,3},{6,0},{7,5},{8,10},{9,15},{10,... | collective-permute-start | bytes 2359304 | tf_op jit(solution)/shard_map/ppermute | solution.py:256
  57.3 15.6 %collective-permute-start.9 = (f32[1160,128]{1,0:T(8,128)S(1)}, f32[1160,128]{1,0:T(8,128)S(1)}, u32[]{:S(2)}, u32[]{:S(2)}) collective-permute-start(f32[1160,128]{1,0:T(8,128)S(1)} %bitcast.62), channel_id=1, source_target_pairs={{0,1},{1,0},{2,3},{3,2},{4,5},{5,4},{6,7},{7,6},{8,9},{9,8},{10,11... | collective-permute-start | bytes 1781768 | tf_op jit(solution)/shard_map/ppermute | solution.py:253
  58.0 15.2 %collective-permute-start.15 = (f32[1536,128]{1,0:T(8,128)S(1)}, f32[1536,128]{1,0:T(8,128)S(1)}, u32[]{:S(2)}, u32[]{:S(2)}) collective-permute-start(f32[1536,128]{1,0:T(8,128)S(1)} %bitcast.59), channel_id=1, source_target_pairs={{0,1},{1,0},{2,3},{3,2},{4,5},{5,4},{6,7},{7,6},{8,9},{9,8},{10,11... | collective-permute-start | bytes 2359304 | tf_op jit(solution)/shard_map/ppermute | solution.py:253
  58.5 22.7 %collective-permute-start.4 = (f32[1920,128]{1,0:T(8,128)S(1)}, f32[1920,128]{1,0:T(8,128)S(1)}, u32[]{:S(2)}, u32[]{:S(2)}) collective-permute-start(f32[1920,128]{1,0:T(8,128)S(1)} %bitcast_add_fusion.3.refs_2_), channel_id=1, source_target_pairs={{0,2},{1,7},{2,4},{3,1},{4,6},{5,3},{6,0},{7,5},{8,10},{9,15},{10,... | collective-permute-start | bytes 2949128 | tf_op jit(solution)/shard_map/ppermute | solution.py:256
  62.3 13.1 %collective-permute-start.3 = (f32[1920,128]{1,0:T(8,128)S(1)}, f32[1920,128]{1,0:T(8,128)S(1)}, u32[]{:S(2)}, u32[]{:S(2)}) collective-permute-start(f32[1920,128]{1,0:T(8,128)S(1)} %bitcast.54), channel_id=1, source_target_pairs={{0,1},{1,0},{2,3},{3,2},{4,5},{5,4},{6,7},{7,6},{8,9},{9,8},{10,11... | collective-permute-start | bytes 2949128 | tf_op jit(solution)/shard_map/ppermute | solution.py:253
  70.7 19.0 %collective-permute-start.13 = (f32[1160,128]{1,0:T(8,128)S(1)}, f32[1160,128]{1,0:T(8,128)S(1)}, u32[]{:S(2)}, u32[]{:S(2)}) collective-permute-start(f32[1160,128]{1,0:T(8,128)S(1)} %bitcast.61), channel_id=1, source_target_pairs={{0,1},{1,0},{2,3},{3,2},{4,5},{5,4},{6,7},{7,6},{8,9},{9,8},{10,11... | collective-permute-start | bytes 1781768 | tf_op jit(solution)/shard_map/ppermute | solution.py:253
  72.9 17.0 %collective-permute-start.19 = (f32[1536,128]{1,0:T(8,128)S(1)}, f32[1536,128]{1,0:T(8,128)S(1)}, u32[]{:S(2)}, u32[]{:S(2)}) collective-permute-start(f32[1536,128]{1,0:T(8,128)S(1)} %bitcast.57), channel_id=1, source_target_pairs={{0,1},{1,0},{2,3},{3,2},{4,5},{5,4},{6,7},{7,6},{8,9},{9,8},{10,11... | collective-permute-start | bytes 2359304 | tf_op jit(solution)/shard_map/ppermute | solution.py:253
  73.1 14.5 %collective-permute-start.11 = (f32[1160,128]{1,0:T(8,128)S(1)}, f32[1160,128]{1,0:T(8,128)S(1)}, u32[]{:S(2)}, u32[]{:S(2)}) collective-permute-start(f32[1160,128]{1,0:T(8,128)S(1)} %fusion.5), channel_id=1, source_target_pairs={{0,2},{1,7},{2,4},{3,1},{4,6},{5,3},{6,0},{7,5},{8,10},{9,15},{10,... | collective-permute-start | bytes 1781768 | tf_op jit(solution)/shard_map/ppermute | solution.py:256
  75.4 20.6 %collective-permute-start.17 = (f32[1536,128]{1,0:T(8,128)S(1)}, f32[1536,128]{1,0:T(8,128)S(1)}, u32[]{:S(2)}, u32[]{:S(2)}) collective-permute-start(f32[1536,128]{1,0:T(8,128)S(1)} %fusion.3), channel_id=1, source_target_pairs={{0,2},{1,7},{2,4},{3,1},{4,6},{5,3},{6,0},{7,5},{8,10},{9,15},{10,... | collective-permute-start | bytes 2359304 | tf_op jit(solution)/shard_map/ppermute | solution.py:256
  81.5 32.4 %collective-permute-start.5 = (f32[1920,128]{1,0:T(8,128)S(1)}, f32[1920,128]{1,0:T(8,128)S(1)}, u32[]{:S(2)}, u32[]{:S(2)}) collective-permute-start(f32[1920,128]{1,0:T(8,128)S(1)} %fusion.1), channel_id=1, source_target_pairs={{0,2},{1,7},{2,4},{3,1},{4,6},{5,3},{6,0},{7,5},{8,10},{9,15},{10,... | collective-permute-start | bytes 2949128 | tf_op jit(solution)/shard_map/ppermute | solution.py:256
  87.6 28.6 %collective-permute-start.7 = (f32[1920,128]{1,0:T(8,128)S(1)}, f32[1920,128]{1,0:T(8,128)S(1)}, u32[]{:S(2)}, u32[]{:S(2)}) collective-permute-start(f32[1920,128]{1,0:T(8,128)S(1)} %bitcast.53), channel_id=1, source_target_pairs={{0,1},{1,0},{2,3},{3,2},{4,5},{5,4},{6,7},{7,6},{8,9},{9,8},{10,11... | collective-permute-start | bytes 2949128 | tf_op jit(solution)/shard_map/ppermute | solution.py:253
  89.7 10.5 %collective-permute-start.12 = (f32[1160,128]{1,0:T(8,128)S(1)}, f32[1160,128]{1,0:T(8,128)S(1)}, u32[]{:S(2)}, u32[]{:S(2)}) collective-permute-start(f32[1160,128]{1,0:T(8,128)S(1)} %bitcast.63), channel_id=1, source_target_pairs={{0,1},{1,0},{2,3},{3,2},{4,5},{5,4},{6,7},{7,6},{8,9},{9,8},{10,11... | collective-permute-start | bytes 1781768 | tf_op jit(solution)/shard_map/ppermute | solution.py:253
  89.9 23.0 %collective-permute-start.14 = (f32[1160,128]{1,0:T(8,128)S(1)}, f32[1160,128]{1,0:T(8,128)S(1)}, u32[]{:S(2)}, u32[]{:S(2)}) collective-permute-start(f32[1160,128]{1,0:T(8,128)S(1)} %fusion.4), channel_id=1, source_target_pairs={{0,2},{1,7},{2,4},{3,1},{4,6},{5,3},{6,0},{7,5},{8,10},{9,15},{10,... | collective-permute-start | bytes 1781768 | tf_op jit(solution)/shard_map/ppermute | solution.py:256
  96.2 25.2 %collective-permute-start.20 = (f32[1536,128]{1,0:T(8,128)S(1)}, f32[1536,128]{1,0:T(8,128)S(1)}, u32[]{:S(2)}, u32[]{:S(2)}) collective-permute-start(f32[1536,128]{1,0:T(8,128)S(1)} %fusion.2), channel_id=1, source_target_pairs={{0,2},{1,7},{2,4},{3,1},{4,6},{5,3},{6,0},{7,5},{8,10},{9,15},{10,... | collective-permute-start | bytes 2359304 | tf_op jit(solution)/shard_map/ppermute | solution.py:256
  100.2 17.8 %collective-permute-start.18 = (f32[1536,128]{1,0:T(8,128)S(1)}, f32[1536,128]{1,0:T(8,128)S(1)}, u32[]{:S(2)}, u32[]{:S(2)}) collective-permute-start(f32[1536,128]{1,0:T(8,128)S(1)} %bitcast.58), channel_id=1, source_target_pairs={{0,1},{1,0},{2,3},{3,2},{4,5},{5,4},{6,7},{7,6},{8,9},{9,8},{10,11... | collective-permute-start | bytes 2359304 | tf_op jit(solution)/shard_map/ppermute | solution.py:253
  114.6 7.7 %collective-permute-start.6 = (f32[1920,128]{1,0:T(8,128)S(1)}, f32[1920,128]{1,0:T(8,128)S(1)}, u32[]{:S(2)}, u32[]{:S(2)}) collective-permute-start(f32[1920,128]{1,0:T(8,128)S(1)} %bitcast.55), channel_id=1, source_target_pairs={{0,1},{1,0},{2,3},{3,2},{4,5},{5,4},{6,7},{7,6},{8,9},{9,8},{10,11... | collective-permute-start | bytes 2949128 | tf_op jit(solution)/shard_map/ppermute | solution.py:253
  116.4 15.5 %collective-permute-start.8 = (f32[1920,128]{1,0:T(8,128)S(1)}, f32[1920,128]{1,0:T(8,128)S(1)}, u32[]{:S(2)}, u32[]{:S(2)}) collective-permute-start(f32[1920,128]{1,0:T(8,128)S(1)} %fusion), channel_id=1, source_target_pairs={{0,2},{1,7},{2,4},{3,1},{4,6},{5,3},{6,0},{7,5},{8,10},{9,15},{10,... | collective-permute-start | bytes 2949128 | tf_op jit(solution)/shard_map/ppermute | solution.py:256

commit v11 on v9

--- a/solution.py
+++ b/solution.py
@@ -232,7 +232,7 @@
         [SMEM, HBM, VMEM, VMEM, VMEM, VMEM, VMEM, HBM],
         scratch=[pltpu.VMEM(q.shape, BF16), dma((4,))],
         flops=2**34,
-        vmem=50 * 2**20,
+        vmem=51 * 2**20,
     )(places, q, prefix, early, late, running, gain.reshape(1, width), w)
 
     def project(start, size, extra, first, after):

time: 134 us -> 133 us (level)
    unnamed x22 -> x20, local copies, waits for them, and re-layouts: 5.44 us -> 4.16 us
where the time goes in v11:
time: 133 us
  waiting for transfers between devices  54.2 us (41%)
  starting transfers between devices  47.6 us (36%)
  Pallas kernels  24.9 us (19%)
  local copies, waits for them, and re-layouts  4.16 us (3%)
  other arithmetic  1.49 us (1%)
    ppermute x9, waiting for transfers between devices, per_device(): arrived = [lax.ppermute(total, 'head', RING) for total in totals]  45.8 us
    ppermute x9, starting transfers between devices, per_device(): arrived = [lax.ppermute(total, 'head', RING) for total in totals]  17.5 us
    all_to_all x1, starting transfers between devices, per_device(): everyone = lax.all_to_all(chunks, 'seg', 0, 0, tiled=True)  11.9 us
    ppermute x12, starting transfers between devices, per_device(): lax.ppermute(send[0], 'head', SWAP)  11.7 us
    pallas_call x12, Pallas kernels, project(): call(functools.partial(project_kernel, start, size, first), [((1, size //...  7.03 us
    all_to_all x1, starting transfers between devices, per_device(): prefix = lax.all_to_all(mine, 'seg', 0, 0, tiled=True).reshape(4, 128, 128)  6.46 us
    pallas_call x1, Pallas kernels, per_device(): call(functools.partial(within_kernel, 2), [((length, width // 2), F32)],...  4.92 us
    all_to_all x1, waiting for transfers between devices, per_device(): prefix = lax.all_to_all(mine, 'seg', 0, 0, tiled=True).reshape(4, 128, 128)  4.68 us
  transfers between devices with their start and end apart: 23, of which 10 were waited for; matrix products, arithmetic and copies ran while one was open for 1% of the time, Pallas kernels for 11%

profile of v11, /device:TPU:1, one launch (start us, length us, event | category | flops | bytes accessed | tf_op | source)
XLA Modules:
  0.0 132.9 jit_solution(11606209066733006604)
XLA Ops:
  0.0 3.3 %shard_map.73 = (f32[32,17,1,128]{3,2,1,0:T(1,128)}, f32[8,768]{1,0:T(8,128)}) custom-call(f32[4,768]{1,0:T(4,128)} %decay_hbm.1, bf16[768,512]{1,0:T(8,128)(2,1)} %k_hbm.5, bf16[768,512]{1,0:T(8,128)(2,1)} %v_hbm.5), custom_call_target="tpu_custom_call" | custom-call | flops 268435456 | bytes 1048576 | tf_op jit(solution)/shard_map/pallas_call | solution.py:201
  3.3 11.9 %all-to-all-start = ((f32[32,17,1,128]{3,2,1,0:T(1,128)}), f32[32,17,1,128]{3,2,1,0:T(1,128)S(1)}, u32[]{:S(2)}, u32[]{:S(2)}) async-start(f32[32,17,1,128]{3,2,1,0:T(1,128)} %get-tuple-element.38), calls=%async_computation | async-start | bytes 557056 | tf_op jit(solution)/shard_map/all_to_all | solution.py:208
  15.2 1.1 copy-done
  16.3 1.1 copy-done.1
  17.5 1.1 copy-done.2
  18.6 0.7 copy-done.4
  19.3 2.0 %shard_map.74.early_ref = f32[768,256]{1,0:T(8,128)S(1)} custom-call(bf16[768,512]{1,0:T(8,128)(2,1)S(1)} %copy-done.2, bf16[768,512]{1,0:T(8,128)(2,1)S(1)} %copy-done, bf16[768,512]{1,0:T(8,128)(2,1)S(1)} %copy-done.1, f32[8,768]{1,0:T(8,128)S(1)} %copy-done.4), custom_call_target="tpu_custom_call" | custom-call | flops 1073741824 | bytes 1048576 | tf_op jit(solution)/shard_map/pallas_call | solution.py:210
  21.3 3.7 %all-to-all-done.all_ref = f32[32,17,1,128]{3,2,1,0:T(1,128)S(1)} async-done(((f32[32,17,1,128]{3,2,1,0:T(1,128)}), f32[32,17,1,128]{3,2,1,0:T(1,128)S(1)}, u32[]{:S(2)}, u32[]{:S(2)}) %all-to-all-start) | async-done | bytes 278560 | tf_op jit(solution)/shard_map/all_to_all | solution.py:208
  25.0 1.6 %shard_map.75 = f32[32,16,128]{2,1,0:T(8,128)} custom-call(s32[32]{0:T(128)S(1)} %copy-done.7, f32[32,17,1,128]{3,2,1,0:T(1,128)S(1)} %all-to-all-done.all_ref), custom_call_target="tpu_custom_call" | custom-call | flops 268435456 | bytes 1048576 | tf_op jit(solution)/shard_map/pallas_call | solution.py:214
  26.5 6.5 %all-to-all-start.1 = ((f32[32,16,128]{2,1,0:T(8,128)}), f32[32,16,128]{2,1,0:T(8,128)S(1)}, u32[]{:S(2)}, u32[]{:S(2)}) async-start(f32[32,16,128]{2,1,0:T(8,128)} %shard_map.75), calls=%async_computation.1 | async-start | bytes 524288 | tf_op jit(solution)/shard_map/all_to_all | solution.py:215
  33.0 4.9 %shard_map.76.late_ref = f32[768,256]{1,0:T(8,128)} custom-call(bf16[768,512]{1,0:T(8,128)(2,1)} %q_hbm.5, bf16[768,512]{1,0:T(8,128)(2,1)} %k_hbm.5, bf16[768,512]{1,0:T(8,128)(2,1)} %v_hbm.5, f32[8,768]{1,0:T(8,128)} %get-tuple-element.42.running_ref), custom_call_target="tpu_custom_call" | custom-call | flops 1073741824 | bytes 1048576 | tf_op jit(solution)/shard_map/pallas_call | solution.py:216
  38.0 4.7 %all-to-all-done.1 = f32[32,16,128]{2,1,0:T(8,128)S(1)} async-done(((f32[32,16,128]{2,1,0:T(8,128)}), f32[32,16,128]{2,1,0:T(8,128)S(1)}, u32[]{:S(2)}, u32[]{:S(2)}) %all-to-all-start.1) | async-done | bytes 262176 | tf_op jit(solution)/shard_map/all_to_all | solution.py:215
  42.7 3.6 %shard_map.77 = (bf16[8,96,512]{2,1,0:T(8,128)(2,1)S(1)}, f32[8,8,128]{2,1,0:T(8,128)S(1)}) custom-call(s32[8]{0:T(128)S(1)} %compare_select_fusion.place_ref, bf16[768,512]{1,0:T(8,128)(2,1)S(1)} %copy-done.3, f32[4,128,128]{2,1,0:T(8,128)S(1)} %bitcast.52, f32[768,256]{1,0:T(8,128)S(1)} %shard_map.74.early_ref, f32[768,256]{1,0:T(8,128)} %shard_map.76.late_ref, ...), custom_call_target="tpu_custom_call" | custom-call | flops 17179869184 | bytes 1048576 | tf_op jit(solution)/shard_map/pallas_call | solution.py:229
  46.3 0.5 shard_map.78
  46.8 3.7 %collective-permute-start = (f32[1160,128]{1,0:T(8,128)S(1)}, f32[1160,128]{1,0:T(8,128)S(1)}, u32[]{:S(2)}, u32[]{:S(2)}) collective-permute-start(f32[1160,128]{1,0:T(8,128)S(1)} %bitcast.64), channel_id=1, source_target_pairs={{0,1},{1,0},{2,3},{3,2},{4,5},{5,4},{6,7},{7,6},{8,9},{9,8},{10,11... | collective-permute-start | bytes 1781768 | tf_op jit(solution)/shard_map/ppermute | solution.py:251
  50.5 0.6 shard_map.79
  51.1 0.1 collective-permute-start.1
  51.2 0.7 shard_map.80
  51.9 0.6 collective-permute-start.2
  52.6 2.8 %collective-permute-start.10 = (f32[1160,128]{1,0:T(8,128)S(1)}, f32[1160,128]{1,0:T(8,128)S(1)}, u32[]{:S(2)}, u32[]{:S(2)}) collective-permute-start(f32[1160,128]{1,0:T(8,128)S(1)} %bitcast_add_fusion.11.refs_0_), channel_id=1, source_target_pairs={{0,2},{1,7},{2,4},{3,1},{4,6},{5,3},{6,0},{7,5},{8,10},{9,15},{10,... | collective-permute-start | bytes 1781768 | tf_op jit(solution)/shard_map/ppermute | solution.py:254
  55.5 1.1 collective-permute-start.16
  56.6 0.1 bitcast_add_fusion.3.refs_2_
  56.7 0.5 shard_map.84
  57.2 0.1 collective-permute-start.9
  57.3 0.6 shard_map.88
  57.9 0.6 collective-permute-start.15
  58.5 1.1 collective-permute-start.4
  59.5 0.7 shard_map.81
  60.2 2.0 %collective-permute-done.10.refs_0_ = f32[1160,128]{1,0:T(8,128)S(1)} collective-permute-done((f32[1160,128]{1,0:T(8,128)S(1)}, f32[1160,128]{1,0:T(8,128)S(1)}, u32[]{:S(2)}, u32[]{:S(2)}) %collective-permute-start.10) | collective-permute-done | bytes 593952 | tf_op jit(solution)/shard_map/ppermute | solution.py:254
  62.3 1.6 %collective-permute-start.3 = (f32[1920,128]{1,0:T(8,128)S(1)}, f32[1920,128]{1,0:T(8,128)S(1)}, u32[]{:S(2)}, u32[]{:S(2)}) collective-permute-start(f32[1920,128]{1,0:T(8,128)S(1)} %bitcast.54), channel_id=1, source_target_pairs={{0,1},{1,0},{2,3},{3,2},{4,5},{5,4},{6,7},{7,6},{8,9},{9,8},{10,11... | collective-permute-start | bytes 2949128 | tf_op jit(solution)/shard_map/ppermute | solution.py:251
  63.8 0.5 shard_map.86
  64.3 6.4 %collective-permute-done.16.refs_0_ = f32[1536,128]{1,0:T(8,128)S(1)} collective-permute-done((f32[1536,128]{1,0:T(8,128)S(1)}, f32[1536,128]{1,0:T(8,128)S(1)}, u32[]{:S(2)}, u32[]{:S(2)}) %collective-permute-start.16) | collective-permute-done | bytes 786464 | tf_op jit(solution)/shard_map/ppermute | solution.py:254
  70.7 1.6 %collective-permute-start.13 = (f32[1160,128]{1,0:T(8,128)S(1)}, f32[1160,128]{1,0:T(8,128)S(1)}, u32[]{:S(2)}, u32[]{:S(2)}) collective-permute-start(f32[1160,128]{1,0:T(8,128)S(1)} %bitcast.61), channel_id=1, source_target_pairs={{0,1},{1,0},{2,3},{3,2},{4,5},{5,4},{6,7},{7,6},{8,9},{9,8},{10,11... | collective-permute-start | bytes 1781768 | tf_op jit(solution)/shard_map/ppermute | solution.py:251
  72.3 0.6 shard_map.90
  72.8 0.1 collective-permute-start.19
  72.9 0.1 fusion.5
  73.1 2.1 %collective-permute-start.11 = (f32[1160,128]{1,0:T(8,128)S(1)}, f32[1160,128]{1,0:T(8,128)S(1)}, u32[]{:S(2)}, u32[]{:S(2)}) collective-permute-start(f32[1160,128]{1,0:T(8,128)S(1)} %fusion.5), channel_id=1, source_target_pairs={{0,2},{1,7},{2,4},{3,1},{4,6},{5,3},{6,0},{7,5},{8,10},{9,15},{10,... | collective-permute-start | bytes 1781768 | tf_op jit(solution)/shard_map/ppermute | solution.py:254
  75.2 0.2 fusion.3
  75.4 0.1 collective-permute-start.17
  75.5 5.8 %collective-permute-done.4.refs_0_ = f32[1920,128]{1,0:T(8,128)S(1)} collective-permute-done((f32[1920,128]{1,0:T(8,128)S(1)}, f32[1920,128]{1,0:T(8,128)S(1)}, u32[]{:S(2)}, u32[]{:S(2)}) %collective-permute-start.4) | collective-permute-done | bytes 983072 | tf_op jit(solution)/shard_map/ppermute | solution.py:254
  81.2 0.2 fusion.1
  81.4 3.2 %collective-permute-start.5 = (f32[1920,128]{1,0:T(8,128)S(1)}, f32[1920,128]{1,0:T(8,128)S(1)}, u32[]{:S(2)}, u32[]{:S(2)}) collective-permute-start(f32[1920,128]{1,0:T(8,128)S(1)} %fusion.1), channel_id=1, source_target_pairs={{0,2},{1,7},{2,4},{3,1},{4,6},{5,3},{6,0},{7,5},{8,10},{9,15},{10,... | collective-permute-start | bytes 2949128 | tf_op jit(solution)/shard_map/ppermute | solution.py:254
  84.6 0.7 shard_map.83
  85.3 2.3 %collective-permute-done.11.refs_0_ = f32[1160,128]{1,0:T(8,128)S(1)} collective-permute-done((f32[1160,128]{1,0:T(8,128)S(1)}, f32[1160,128]{1,0:T(8,128)S(1)}, u32[]{:S(2)}, u32[]{:S(2)}) %collective-permute-start.11) | collective-permute-done | bytes 593952 | tf_op jit(solution)/shard_map/ppermute | solution.py:254
  87.6 1.6 %collective-permute-start.7 = (f32[1920,128]{1,0:T(8,128)S(1)}, f32[1920,128]{1,0:T(8,128)S(1)}, u32[]{:S(2)}, u32[]{:S(2)}) collective-permute-start(f32[1920,128]{1,0:T(8,128)S(1)} %bitcast.53), channel_id=1, source_target_pairs={{0,1},{1,0},{2,3},{3,2},{4,5},{5,4},{6,7},{7,6},{8,9},{9,8},{10,11... | collective-permute-start | bytes 2949128 | tf_op jit(solution)/shard_map/ppermute | solution.py:251
  89.1 0.5 shard_map.85
  89.6 0.1 collective-permute-start.12
  89.9 2.1 %collective-permute-start.14 = (f32[1160,128]{1,0:T(8,128)S(1)}, f32[1160,128]{1,0:T(8,128)S(1)}, u32[]{:S(2)}, u32[]{:S(2)}) collective-permute-start(f32[1160,128]{1,0:T(8,128)S(1)} %fusion.4), channel_id=1, source_target_pairs={{0,2},{1,7},{2,4},{3,1},{4,6},{5,3},{6,0},{7,5},{8,10},{9,15},{10,... | collective-permute-start | bytes 1781768 | tf_op jit(solution)/shard_map/ppermute | solution.py:254
  92.0 4.0 %collective-permute-done.17.refs_0_ = f32[1536,128]{1,0:T(8,128)S(1)} collective-permute-done((f32[1536,128]{1,0:T(8,128)S(1)}, f32[1536,128]{1,0:T(8,128)S(1)}, u32[]{:S(2)}, u32[]{:S(2)}) %collective-permute-start.17) | collective-permute-done | bytes 786464 | tf_op jit(solution)/shard_map/ppermute | solution.py:254
  96.0 0.1 fusion.2
  96.1 3.4 %collective-permute-start.20 = (f32[1536,128]{1,0:T(8,128)S(1)}, f32[1536,128]{1,0:T(8,128)S(1)}, u32[]{:S(2)}, u32[]{:S(2)}) collective-permute-start(f32[1536,128]{1,0:T(8,128)S(1)} %fusion.2), channel_id=1, source_target_pairs={{0,2},{1,7},{2,4},{3,1},{4,6},{5,3},{6,0},{7,5},{8,10},{9,15},{10,... | collective-permute-start | bytes 2359304 | tf_op jit(solution)/shard_map/ppermute | solution.py:254
  99.6 0.6 shard_map.89
  100.2 0.1 collective-permute-start.18
  100.3 12.6 %collective-permute-done.14.refs_1_ = f32[1160,128]{1,0:T(8,128)S(1)} collective-permute-done((f32[1160,128]{1,0:T(8,128)S(1)}, f32[1160,128]{1,0:T(8,128)S(1)}, u32[]{:S(2)}, u32[]{:S(2)}) %collective-permute-start.14) | collective-permute-done | bytes 593952 | tf_op jit(solution)/shard_map/ppermute | solution.py:254
  112.9 0.9 shard_map.87
  113.8 0.7 shard_map.82
  114.5 1.7 %collective-permute-start.6 = (f32[1920,128]{1,0:T(8,128)S(1)}, f32[1920,128]{1,0:T(8,128)S(1)}, u32[]{:S(2)}, u32[]{:S(2)}) collective-permute-start(f32[1920,128]{1,0:T(8,128)S(1)} %bitcast.55), channel_id=1, source_target_pairs={{0,1},{1,0},{2,3},{3,2},{4,5},{5,4},{6,7},{7,6},{8,9},{9,8},{10,11... | collective-permute-start | bytes 2949128 | tf_op jit(solution)/shard_map/ppermute | solution.py:251
  116.2 0.2 fusion
  116.3 1.6 %collective-permute-start.8 = (f32[1920,128]{1,0:T(8,128)S(1)}, f32[1920,128]{1,0:T(8,128)S(1)}, u32[]{:S(2)}, u32[]{:S(2)}) collective-permute-start(f32[1920,128]{1,0:T(8,128)S(1)} %fusion), channel_id=1, source_target_pairs={{0,2},{1,7},{2,4},{3,1},{4,6},{5,3},{6,0},{7,5},{8,10},{9,15},{10,... | collective-permute-start | bytes 2949128 | tf_op jit(solution)/shard_map/ppermute | solution.py:254
  118.1 3.2 %collective-permute-done.20.refs_1_ = f32[1536,128]{1,0:T(8,128)S(1)} collective-permute-done((f32[1536,128]{1,0:T(8,128)S(1)}, f32[1536,128]{1,0:T(8,128)S(1)}, u32[]{:S(2)}, u32[]{:S(2)}) %collective-permute-start.20) | collective-permute-done | bytes 786464 | tf_op jit(solution)/shard_map/ppermute | solution.py:254
  121.3 0.8 shard_map.91.refs_3_
  122.2 0.1 bitcast_add_fusion.1.refs_0_
  122.3 9.5 %collective-permute-done.8.refs_1_ = f32[1920,128]{1,0:T(8,128)S(1)} collective-permute-done((f32[1920,128]{1,0:T(8,128)S(1)}, f32[1920,128]{1,0:T(8,128)S(1)}, u32[]{:S(2)}, u32[]{:S(2)}) %collective-permute-start.8) | collective-permute-done | bytes 983072 | tf_op jit(solution)/shard_map/ppermute | solution.py:254
  131.9 0.8 shard_map.92
  (36 shorter events, 0.5 us)
Async XLA Ops:
  3.3 21.7 %all-to-all-start = ((f32[32,17,1,128]{3,2,1,0:T(1,128)}), f32[32,17,1,128]{3,2,1,0:T(1,128)S(1)}, u32[]{:S(2)}, u32[]{:S(2)}) async-start(f32[32,17,1,128]{3,2,1,0:T(1,128)} %get-tuple-element.38), calls=%async_computation | async-start | bytes 557056 | tf_op jit(solution)/shard_map/all_to_all | solution.py:208
  15.2 1.1 copy-start
  16.3 1.1 copy-start.1
  17.5 1.1 copy-start.2
  18.6 0.7 copy-start.4
  19.3 5.6 %copy-start.7 = (s32[32]{0:T(128)S(1)}, s32[32]{0:T(128)}, u32[]{:S(2)}) copy-start(s32[32]{0:T(128)} %parent_ref.1) | copy-start | bytes 388
  26.5 16.1 %all-to-all-start.1 = ((f32[32,16,128]{2,1,0:T(8,128)}), f32[32,16,128]{2,1,0:T(8,128)S(1)}, u32[]{:S(2)}, u32[]{:S(2)}) async-start(f32[32,16,128]{2,1,0:T(8,128)} %shard_map.75), calls=%async_computation.1 | async-start | bytes 524288 | tf_op jit(solution)/shard_map/all_to_all | solution.py:215
  33.0 9.6 %copy-start.3 = (bf16[768,512]{1,0:T(8,128)(2,1)S(1)}, bf16[768,512]{1,0:T(8,128)(2,1)}, u32[]{:S(2)}) copy-start(bf16[768,512]{1,0:T(8,128)(2,1)} %q_hbm.5) | copy-start | bytes 2359300
  33.0 9.6 %copy-start.5 = (f32[8,768]{1,0:T(8,128)S(1)}, f32[8,768]{1,0:T(8,128)}, u32[]{:S(2)}) copy-start(f32[8,768]{1,0:T(8,128)} %get-tuple-element.42.running_ref) | copy-start | bytes 73732
  33.0 9.6 %copy-start.6 = (f32[512]{0:T(512)S(1)}, f32[512]{0:T(512)}, u32[]{:S(2)}) copy-start(f32[512]{0:T(512)} %param.12) | copy-start | bytes 6148
  42.7 3.6 %slice-start = ((s8[6291456]{0:T(1024)(128)(4,1)}), s8[4194304]{0:T(1024)(128)(4,1)S(1)}, s32[]{:S(2)}) async-start(s8[6291456]{0:T(1024)(128)(4,1)} %bitcast.50), calls=%async_computation.2 | async-start | bytes 8388608
  42.7 3.6 %slice-start.1 = ((s8[6291456]{0:T(1024)(128)(4,1)}), s8[2097152]{0:T(1024)(128)(4,1)S(1)}, s32[]{:S(2)}) async-start(s8[6291456]{0:T(1024)(128)(4,1)} %bitcast.50), calls=%async_computation.3 | async-start | bytes 4194304
  46.8 5.7 %collective-permute-start = (f32[1160,128]{1,0:T(8,128)S(1)}, f32[1160,128]{1,0:T(8,128)S(1)}, u32[]{:S(2)}, u32[]{:S(2)}) collective-permute-start(f32[1160,128]{1,0:T(8,128)S(1)} %bitcast.64), channel_id=1, source_target_pairs={{0,1},{1,0},{2,3},{3,2},{4,5},{5,4},{6,7},{7,6},{8,9},{9,8},{10,11... | collective-permute-start | bytes 1781768 | tf_op jit(solution)/shard_map/ppermute | solution.py:251
  51.1 4.3 %collective-permute-start.1 = (f32[1536,128]{1,0:T(8,128)S(1)}, f32[1536,128]{1,0:T(8,128)S(1)}, u32[]{:S(2)}, u32[]{:S(2)}) collective-permute-start(f32[1536,128]{1,0:T(8,128)S(1)} %bitcast.60), channel_id=1, source_target_pairs={{0,1},{1,0},{2,3},{3,2},{4,5},{5,4},{6,7},{7,6},{8,9},{9,8},{10,11... | collective-permute-start | bytes 2359304 | tf_op jit(solution)/shard_map/ppermute | solution.py:251
  51.9 4.7 %collective-permute-start.2 = (f32[1920,128]{1,0:T(8,128)S(1)}, f32[1920,128]{1,0:T(8,128)S(1)}, u32[]{:S(2)}, u32[]{:S(2)}) collective-permute-start(f32[1920,128]{1,0:T(8,128)S(1)} %bitcast.56), channel_id=1, source_target_pairs={{0,1},{1,0},{2,3},{3,2},{4,5},{5,4},{6,7},{7,6},{8,9},{9,8},{10,11... | collective-permute-start | bytes 2949128 | tf_op jit(solution)/shard_map/ppermute | solution.py:251
  52.6 9.7 %collective-permute-start.10 = (f32[1160,128]{1,0:T(8,128)S(1)}, f32[1160,128]{1,0:T(8,128)S(1)}, u32[]{:S(2)}, u32[]{:S(2)}) collective-permute-start(f32[1160,128]{1,0:T(8,128)S(1)} %bitcast_add_fusion.11.refs_0_), channel_id=1, source_target_pairs={{0,2},{1,7},{2,4},{3,1},{4,6},{5,3},{6,0},{7,5},{8,10},{9,15},{10,... | collective-permute-start | bytes 1781768 | tf_op jit(solution)/shard_map/ppermute | solution.py:254
  55.5 15.2 %collective-permute-start.16 = (f32[1536,128]{1,0:T(8,128)S(1)}, f32[1536,128]{1,0:T(8,128)S(1)}, u32[]{:S(2)}, u32[]{:S(2)}) collective-permute-start(f32[1536,128]{1,0:T(8,128)S(1)} %bitcast_add_fusion.7.refs_1_), channel_id=1, source_target_pairs={{0,2},{1,7},{2,4},{3,1},{4,6},{5,3},{6,0},{7,5},{8,10},{9,15},{10,... | collective-permute-start | bytes 2359304 | tf_op jit(solution)/shard_map/ppermute | solution.py:254
  57.2 15.6 %collective-permute-start.9 = (f32[1160,128]{1,0:T(8,128)S(1)}, f32[1160,128]{1,0:T(8,128)S(1)}, u32[]{:S(2)}, u32[]{:S(2)}) collective-permute-start(f32[1160,128]{1,0:T(8,128)S(1)} %bitcast.62), channel_id=1, source_target_pairs={{0,1},{1,0},{2,3},{3,2},{4,5},{5,4},{6,7},{7,6},{8,9},{9,8},{10,11... | collective-permute-start | bytes 1781768 | tf_op jit(solution)/shard_map/ppermute | solution.py:251
  57.9 15.2 %collective-permute-start.15 = (f32[1536,128]{1,0:T(8,128)S(1)}, f32[1536,128]{1,0:T(8,128)S(1)}, u32[]{:S(2)}, u32[]{:S(2)}) collective-permute-start(f32[1536,128]{1,0:T(8,128)S(1)} %bitcast.59), channel_id=1, source_target_pairs={{0,1},{1,0},{2,3},{3,2},{4,5},{5,4},{6,7},{7,6},{8,9},{9,8},{10,11... | collective-permute-start | bytes 2359304 | tf_op jit(solution)/shard_map/ppermute | solution.py:251
  58.5 22.7 %collective-permute-start.4 = (f32[1920,128]{1,0:T(8,128)S(1)}, f32[1920,128]{1,0:T(8,128)S(1)}, u32[]{:S(2)}, u32[]{:S(2)}) collective-permute-start(f32[1920,128]{1,0:T(8,128)S(1)} %bitcast_add_fusion.3.refs_2_), channel_id=1, source_target_pairs={{0,2},{1,7},{2,4},{3,1},{4,6},{5,3},{6,0},{7,5},{8,10},{9,15},{10,... | collective-permute-start | bytes 2949128 | tf_op jit(solution)/shard_map/ppermute | solution.py:254
  62.3 13.1 %collective-permute-start.3 = (f32[1920,128]{1,0:T(8,128)S(1)}, f32[1920,128]{1,0:T(8,128)S(1)}, u32[]{:S(2)}, u32[]{:S(2)}) collective-permute-start(f32[1920,128]{1,0:T(8,128)S(1)} %bitcast.54), channel_id=1, source_target_pairs={{0,1},{1,0},{2,3},{3,2},{4,5},{5,4},{6,7},{7,6},{8,9},{9,8},{10,11... | collective-permute-start | bytes 2949128 | tf_op jit(solution)/shard_map/ppermute | solution.py:251
  70.7 19.0 %collective-permute-start.13 = (f32[1160,128]{1,0:T(8,128)S(1)}, f32[1160,128]{1,0:T(8,128)S(1)}, u32[]{:S(2)}, u32[]{:S(2)}) collective-permute-start(f32[1160,128]{1,0:T(8,128)S(1)} %bitcast.61), channel_id=1, source_target_pairs={{0,1},{1,0},{2,3},{3,2},{4,5},{5,4},{6,7},{7,6},{8,9},{9,8},{10,11... | collective-permute-start | bytes 1781768 | tf_op jit(solution)/shard_map/ppermute | solution.py:251
  72.8 17.0 %collective-permute-start.19 = (f32[1536,128]{1,0:T(8,128)S(1)}, f32[1536,128]{1,0:T(8,128)S(1)}, u32[]{:S(2)}, u32[]{:S(2)}) collective-permute-start(f32[1536,128]{1,0:T(8,128)S(1)} %bitcast.57), channel_id=1, source_target_pairs={{0,1},{1,0},{2,3},{3,2},{4,5},{5,4},{6,7},{7,6},{8,9},{9,8},{10,11... | collective-permute-start | bytes 2359304 | tf_op jit(solution)/shard_map/ppermute | solution.py:251
  73.1 14.5 %collective-permute-start.11 = (f32[1160,128]{1,0:T(8,128)S(1)}, f32[1160,128]{1,0:T(8,128)S(1)}, u32[]{:S(2)}, u32[]{:S(2)}) collective-permute-start(f32[1160,128]{1,0:T(8,128)S(1)} %fusion.5), channel_id=1, source_target_pairs={{0,2},{1,7},{2,4},{3,1},{4,6},{5,3},{6,0},{7,5},{8,10},{9,15},{10,... | collective-permute-start | bytes 1781768 | tf_op jit(solution)/shard_map/ppermute | solution.py:254
  75.4 20.6 %collective-permute-start.17 = (f32[1536,128]{1,0:T(8,128)S(1)}, f32[1536,128]{1,0:T(8,128)S(1)}, u32[]{:S(2)}, u32[]{:S(2)}) collective-permute-start(f32[1536,128]{1,0:T(8,128)S(1)} %fusion.3), channel_id=1, source_target_pairs={{0,2},{1,7},{2,4},{3,1},{4,6},{5,3},{6,0},{7,5},{8,10},{9,15},{10,... | collective-permute-start | bytes 2359304 | tf_op jit(solution)/shard_map/ppermute | solution.py:254
  81.4 32.4 %collective-permute-start.5 = (f32[1920,128]{1,0:T(8,128)S(1)}, f32[1920,128]{1,0:T(8,128)S(1)}, u32[]{:S(2)}, u32[]{:S(2)}) collective-permute-start(f32[1920,128]{1,0:T(8,128)S(1)} %fusion.1), channel_id=1, source_target_pairs={{0,2},{1,7},{2,4},{3,1},{4,6},{5,3},{6,0},{7,5},{8,10},{9,15},{10,... | collective-permute-start | bytes 2949128 | tf_op jit(solution)/shard_map/ppermute | solution.py:254
  87.6 28.6 %collective-permute-start.7 = (f32[1920,128]{1,0:T(8,128)S(1)}, f32[1920,128]{1,0:T(8,128)S(1)}, u32[]{:S(2)}, u32[]{:S(2)}) collective-permute-start(f32[1920,128]{1,0:T(8,128)S(1)} %bitcast.53), channel_id=1, source_target_pairs={{0,1},{1,0},{2,3},{3,2},{4,5},{5,4},{6,7},{7,6},{8,9},{9,8},{10,11... | collective-permute-start | bytes 2949128 | tf_op jit(solution)/shard_map/ppermute | solution.py:251
  89.6 10.5 %collective-permute-start.12 = (f32[1160,128]{1,0:T(8,128)S(1)}, f32[1160,128]{1,0:T(8,128)S(1)}, u32[]{:S(2)}, u32[]{:S(2)}) collective-permute-start(f32[1160,128]{1,0:T(8,128)S(1)} %bitcast.63), channel_id=1, source_target_pairs={{0,1},{1,0},{2,3},{3,2},{4,5},{5,4},{6,7},{7,6},{8,9},{9,8},{10,11... | collective-permute-start | bytes 1781768 | tf_op jit(solution)/shard_map/ppermute | solution.py:251
  89.9 23.0 %collective-permute-start.14 = (f32[1160,128]{1,0:T(8,128)S(1)}, f32[1160,128]{1,0:T(8,128)S(1)}, u32[]{:S(2)}, u32[]{:S(2)}) collective-permute-start(f32[1160,128]{1,0:T(8,128)S(1)} %fusion.4), channel_id=1, source_target_pairs={{0,2},{1,7},{2,4},{3,1},{4,6},{5,3},{6,0},{7,5},{8,10},{9,15},{10,... | collective-permute-start | bytes 1781768 | tf_op jit(solution)/shard_map/ppermute | solution.py:254
  96.1 25.2 %collective-permute-start.20 = (f32[1536,128]{1,0:T(8,128)S(1)}, f32[1536,128]{1,0:T(8,128)S(1)}, u32[]{:S(2)}, u32[]{:S(2)}) collective-permute-start(f32[1536,128]{1,0:T(8,128)S(1)} %fusion.2), channel_id=1, source_target_pairs={{0,2},{1,7},{2,4},{3,1},{4,6},{5,3},{6,0},{7,5},{8,10},{9,15},{10,... | collective-permute-start | bytes 2359304 | tf_op jit(solution)/shard_map/ppermute | solution.py:254
  100.2 17.8 %collective-permute-start.18 = (f32[1536,128]{1,0:T(8,128)S(1)}, f32[1536,128]{1,0:T(8,128)S(1)}, u32[]{:S(2)}, u32[]{:S(2)}) collective-permute-start(f32[1536,128]{1,0:T(8,128)S(1)} %bitcast.58), channel_id=1, source_target_pairs={{0,1},{1,0},{2,3},{3,2},{4,5},{5,4},{6,7},{7,6},{8,9},{9,8},{10,11... | collective-permute-start | bytes 2359304 | tf_op jit(solution)/shard_map/ppermute | solution.py:251
  114.5 7.7 %collective-permute-start.6 = (f32[1920,128]{1,0:T(8,128)S(1)}, f32[1920,128]{1,0:T(8,128)S(1)}, u32[]{:S(2)}, u32[]{:S(2)}) collective-permute-start(f32[1920,128]{1,0:T(8,128)S(1)} %bitcast.55), channel_id=1, source_target_pairs={{0,1},{1,0},{2,3},{3,2},{4,5},{5,4},{6,7},{7,6},{8,9},{9,8},{10,11... | collective-permute-start | bytes 2949128 | tf_op jit(solution)/shard_map/ppermute | solution.py:251
  116.3 15.5 %collective-permute-start.8 = (f32[1920,128]{1,0:T(8,128)S(1)}, f32[1920,128]{1,0:T(8,128)S(1)}, u32[]{:S(2)}, u32[]{:S(2)}) collective-permute-start(f32[1920,128]{1,0:T(8,128)S(1)} %fusion), channel_id=1, source_target_pairs={{0,2},{1,7},{2,4},{3,1},{4,6},{5,3},{6,0},{7,5},{8,10},{9,15},{10,... | collective-permute-start | bytes 2949128 | tf_op jit(solution)/shard_map/ppermute | solution.py:254
